TPU v7x, 32 devices: a whole 2x2x4 slice. The times are simulated.
32 devices in a mesh: date: 4 (over y, x), strip: 8 (over z, core).
Axes of the slice: x: 2, y: 2, z: 4, core: 2. Of those that a mesh axis runs over, the one named last changes fastest.
Arguments:
- slc: bfloat16 [2, 128, 256, 2048], P(None, 'date', None, 'strip'), may hold values from -180 to 180
- range_kernel: bfloat16 [128, 256, 256], P('date'), may hold values from -2.5 to 2.5, as said below
- azimuth_kernel: bfloat16 [128, 272, 2048], P('date', None, 'strip'), may hold values from -2.5 to 2.5, as said below
Outputs:
- coherence: float32 [16, 128, 2, 128, 128], P('date', 'strip')
Inputs may be any that keep to these rules, and one draw needn't show every extreme that they name: range_kernel[d, r, s] is zero unless s - r lies in a run of 8 consecutive values that begins between -8 and 1; the run depends on r but not on d, and runs beginning at -8 and at 1 both occur. azimuth_kernel[d, k, a] is zero unless k - (a mod 256) lies in a run of 8 consecutive values that begins between 0 and 9; the run depends on a but not on d; in every strip the first pixel's run begins at 0 and the last pixel's at 9.
All inputs are finite; a program needn't handle non-finite values.
Results may differ from a plain program's by a relative error of at most 0.00051.
Values may be sent and summed in bfloat16 or wider, within the bound.
No kernel may reach another device: no remote copies, remote signals or barrier semaphores. Data moves between devices by JAX's collectives and lax.ppermute only.
A program may use at most 192 MiB of HBM per device.

v0:
```python
import jax
import jax.numpy as jnp
from jax import lax
from jax.sharding import PartitionSpec as P

HALO = 8
WIN = 32


epsilon = 1e-06


def with_halo(value, sides, width):
    for axis, dim in sides:
        devices, length = (lax.axis_size(axis), value.shape[dim])
        up = [(i, (i + 1) % devices) for i in range(devices - 1)]
        down = [(j, i) for i, j in up]
        last = lax.slice_in_dim(value, length - width, length, axis=dim)
        initial = lax.slice_in_dim(value, 0, width, axis=dim)
        before = lax.ppermute(last, axis, up)
        after = lax.ppermute(initial, axis, down)
        value = jnp.concatenate([before, value, after], axis=dim)
    return value


def coherence_of(moment, date_count):
    real_part = moment[..., :date_count, :date_count] + moment[..., date_count:, date_count:]
    imag_part = moment[..., date_count:, :date_count] - moment[..., :date_count, date_count:]
    power_sum = jnp.diagonal(real_part, axis1=-2, axis2=-1) + epsilon
    inverse_root = lax.rsqrt(power_sum)
    pair_scale = inverse_root[..., :, None] * inverse_root[..., None, :]
    return jnp.stack([real_part * pair_scale, imag_part * pair_scale], axis=-3)


def block_gram(pixels):
    return jnp.einsum("uvip,uvjp->uvij", pixels, pixels, preferred_element_type=jnp.float32)


def on_device(slc, range_kernel, azimuth_kernel):
    ranged = jnp.einsum(
        "drs,cdsa->cdra", range_kernel, slc, preferred_element_type=jnp.float32
    ).astype(jnp.bfloat16)
    extended = with_halo(ranged, (("strip", 3),), HALO)
    shifted = jnp.einsum(
        "cdrp,dpa->cdra", extended, azimuth_kernel, preferred_element_type=jnp.float32
    ).astype(jnp.bfloat16)
    margin = WIN // 4
    half_window = WIN // 2
    regrouped = lax.all_to_all(shifted, "date", split_axis=2, concat_axis=1, tiled=True)
    pixel_grid = with_halo(regrouped, (("date", 2), ("strip", 3)), margin)
    date_count = pixel_grid.shape[1]
    range_blocks = pixel_grid.shape[2] // half_window
    az_blocks = pixel_grid.shape[3] // half_window
    blocks = pixel_grid.reshape(2 * date_count, range_blocks, half_window, az_blocks, half_window)
    blocks = jnp.transpose(blocks, (1, 3, 0, 2, 4)).reshape(
        range_blocks, az_blocks, 2 * date_count, half_window * half_window
    )
    moment = block_gram(blocks[:-1, :-1]) + block_gram(blocks[1:, :-1])
    moment = moment + block_gram(blocks[:-1, 1:]) + block_gram(blocks[1:, 1:])
    return coherence_of(moment, date_count)


def solution(mesh):
    in_specs = (P(None, "date", None, "strip"), P("date", None, None), P("date", None, "strip"))
    out_specs = P("date", "strip", None, None, None)
    return jax.shard_map(
        on_device, mesh=mesh, in_specs=in_specs, out_specs=out_specs, check_vma=False
    )
```

profile of v0, /device:TPU:0, one launch (start us, length us, event | category | flops | bytes accessed | tf_op | source)
XLA Modules:
  0.0 446.0 jit_solution(13482411422651867326)
XLA Ops:
  0.0 6.1 %convert_bitcast_fusion.1 = bf16[2,32,256,256]{2,3,0,1:T(8,128)(2,1)S(1)} fusion(bf16[2,32,256,256]{3,2,1,0:T(8,128)(2,1)} %param.3, bf16[32,256,256]{2,1,0:T(8,128)(2,1)} %param.4), kind=kOutput, calls=%fused_computation.21 | convolution fusion | flops 2151677952 | bytes 20971520 | tf_op jit(solution)/shard_map/drs,cdsa->cdra/dot_general | solution.py:40
  6.2 2.4 collective-permute-start
  8.5 1.3 collective-permute-start.1
  9.8 0.0 collective-permute-done
  9.9 4.3 collective-permute-done.1
  14.2 9.3 %convert_bitcast_fusion = bf16[2,32,256,256]{3,2,0,1:T(8,128)(2,1)} fusion(bf16[2,32,256,8]{2,3,0,1:T(8,128)(2,1)S(1)} %collective-permute-done.1, bf16[2,32,256,256]{2,3,0,1:T(8,128)(2,1)S(1)} %convert_bitcast_fusion.1, bf16[2,32,256,8]{2,3,0,1:T(8,128)(2,1)S(1)} %collective-permute-done, bf16[32,272,256]{2,1,0:T(8,128)(2,1)} %param.5), kind=kOutput, calls=%fused_computation.20 | convolution fusion | flops 2312634368 | bytes 21757952 | tf_op jit(solution)/shard_map/cdrp,dpa->cdra/dot_general | solution.py:44
  23.5 12.4 %copy.35 = bf16[2,32,256,256]{3,0,1,2:T(2,128)(2,1)S(1)} copy(bf16[2,32,256,256]{3,2,0,1:T(8,128)(2,1)} %convert_bitcast_fusion) | data formatting | bytes 16777216 | tf_op jit(solution)/shard_map/convert_element_type | solution.py:46
  35.9 93.8 %all_to_all.18 = bf16[2,32,256,256]{3,0,1,2:T(2,128)(2,1)} all-to-all(bf16[2,32,256,256]{3,0,1,2:T(2,128)(2,1)S(1)} %copy.35), channel_id=1, replica_groups=mesh['date'=4,'strip'=8] {'date'}, dimensions={2} | all-to-all | bytes 16777216 | tf_op jit(solution)/shard_map/all_to_all | solution.py:49
  129.6 11.5 %copy.36 = bf16[2,32,256,256]{3,2,1,0:T(8,128)(2,1)} copy(bf16[2,32,256,256]{3,0,1,2:T(2,128)(2,1)} %all_to_all.18) | data formatting | bytes 16777216 | tf_op jit(solution)/shard_map/all_to_all | solution.py:49
  141.2 8.3 %copy.37 = bf16[2,4,32,64,256]{4,3,2,1,0:T(8,128)(2,1)} copy(bf16[2,4,32,64,256]{4,3,1,2,0:T(8,128)(2,1)} %bitcast.45) | data formatting | bytes 16777216 | tf_op jit(solution)/shard_map/all_to_all | solution.py:49
  149.5 1.7 fusion.25
  151.2 3.2 collective-permute-start.2
  154.4 1.5 collective-permute-start.3
  155.9 19.2 %collective-permute-done.2 = bf16[2,128,8,256]{3,2,1,0:T(8,128)(2,1)S(1)} collective-permute-done((bf16[2,128,8,256]{3,2,1,0:T(8,128)(2,1)S(1)}, bf16[2,128,8,256]{3,2,1,0:T(8,128)(2,1)S(1)}, u32[]{:S(2)}, u32[]{:S(2)}) %collective-permute-start.2) | collective-permute-done | bytes 1048608 | tf_op jit(solution)/shard_map/ppermute | solution.py:20
  175.1 24.4 %collective-permute-done.3 = bf16[2,128,8,256]{3,2,1,0:T(8,128)(2,1)S(1)} collective-permute-done((bf16[2,128,8,256]{3,2,1,0:T(8,128)(2,1)S(1)}, bf16[2,128,8,256]{3,2,1,0:T(8,128)(2,1)S(1)}, u32[]{:S(2)}, u32[]{:S(2)}) %collective-permute-start.3) | collective-permute-done | bytes 1048608 | tf_op jit(solution)/shard_map/ppermute | solution.py:21
  199.5 8.7 %pad_maximum_fusion.1 = bf16[2,128,80,256]{3,2,1,0:T(8,128)(2,1)} fusion(bf16[2,128,8,256]{3,2,1,0:T(8,128)(2,1)S(1)} %collective-permute-done.3, bf16[2,128,64,256]{3,2,1,0:T(8,128)(2,1)} %bitcast.37, bf16[2,128,8,256]{3,2,1,0:T(8,128)(2,1)S(1)} %collective-permute-done.2), kind=kLoop, calls=%fused_computation.3 | loop fusion | flops 31457280 | bytes 20971520 | tf_op jit(solution)/shard_map/concatenate | solution.py:22
  208.2 10.4 %fusion.24 = (bf16[2,128,80,8]{3,2,1,0:T(8,128)(2,1)}, bf16[2,128,80,8]{3,2,1,0:T(8,128)(2,1)}) fusion(bf16[2,128,80,256]{3,2,1,0:T(8,128)(2,1)} %pad_maximum_fusion.1), kind=kLoop, calls=%fused_computation.33 | loop fusion | bytes 1310720 | tf_op jit(solution)/shard_map/slice | solution.py:18
  218.7 4.6 %copy.38 = bf16[2,128,80,8]{1,3,2,0:T(8,128)(2,1)S(1)} copy(bf16[2,128,80,8]{3,2,1,0:T(8,128)(2,1)} %get-tuple-element.5) | data formatting | bytes 655360 | tf_op jit(solution)/shard_map/slice | solution.py:18
  223.3 4.5 %collective-permute-start.4 = (bf16[2,128,80,8]{1,3,2,0:T(8,128)(2,1)S(1)}, bf16[2,128,80,8]{1,3,2,0:T(8,128)(2,1)S(1)}, u32[]{:S(2)}, u32[]{:S(2)}) collective-permute-start(bf16[2,128,80,8]{1,3,2,0:T(8,128)(2,1)S(1)} %copy.38), channel_id=1, source_target_pairs={{0,1},{1,2},{2,3},{3,4},{4,5},{5,6},{6,7},{8,9},{9,10},{10,11},{11... | collective-permute-start | bytes 983048 | tf_op jit(solution)/shard_map/ppermute | solution.py:20
  227.8 4.6 %copy.39 = bf16[2,128,80,8]{1,3,2,0:T(8,128)(2,1)S(1)} copy(bf16[2,128,80,8]{3,2,1,0:T(8,128)(2,1)} %get-tuple-element.6) | data formatting | bytes 655360 | tf_op jit(solution)/shard_map/slice | solution.py:19
  232.4 1.3 collective-permute-start.5
  233.7 0.5 or_bitcast_fusion
  234.2 0.0 collective-permute-done.4
  234.2 3.9 copy.40
  238.1 4.7 %collective-permute-done.5 = bf16[2,128,80,8]{1,3,2,0:T(8,128)(2,1)S(1)} collective-permute-done((bf16[2,128,80,8]{1,3,2,0:T(8,128)(2,1)S(1)}, bf16[2,128,80,8]{1,3,2,0:T(8,128)(2,1)S(1)}, u32[]{:S(2)}, u32[]{:S(2)}) %collective-permute-start.5) | collective-permute-done | bytes 327712 | tf_op jit(solution)/shard_map/ppermute | solution.py:21
  242.9 3.8 copy.41
  246.6 18.6 %pad_maximum_fusion = bf16[2,128,80,272]{3,2,1,0:T(8,128)(2,1)} fusion(bf16[2,128,80,8]{3,2,1,0:T(8,128)(2,1)} %copy.41, bf16[2,128,8,256]{3,2,1,0:T(8,128)(2,1)S(1)} %collective-permute-done.3, bf16[2,128,64,256]{3,2,1,0:T(8,128)(2,1)} %bitcast.38, bf16[2,128,8,256]{3,2,1,0:T(8,128)(2,1)S(1)} %collective-permute-done.2, bf16[2,128,80,8]{3,2,1,0:T(8,128)(2,1)} %copy.40), kind=kLoop, calls=%fused_computation.2 | loop fusion | flops 55705600 | bytes 22282240 | tf_op jit(solution)/shard_map/concatenate | solution.py:22
  265.3 26.8 %copy.42 = bf16[2,128,80,272]{1,0,3,2:T(2,128)(2,1)} copy(bf16[2,128,80,272]{3,2,1,0:T(8,128)(2,1)} %pad_maximum_fusion) | data formatting | bytes 22282240 | tf_op jit(solution)/shard_map/concatenate | solution.py:22
  292.1 24.6 %reshape.14 = bf16[256,5,16,17,16]{0,4,3,2,1:T(8,128)(2,1)} reshape(bf16[2,128,80,272]{1,0,3,2:T(2,128)(2,1)} %copy.42) | data formatting | bytes 22282240 | tf_op jit(solution)/shard_map/reshape | solution.py:54
  316.7 10.4 %copy.43 = bf16[5,17,256,16,16]{2,4,3,1,0:T(8,128)(2,1)} copy(bf16[5,17,256,16,16]{2,4,1,3,0:T(8,128)(2,1)} %bitcast.39) | data formatting | bytes 22282240 | tf_op jit(solution)/shard_map/transpose | solution.py:55
  327.1 12.0 %fusion.11 = f32[4,16,256,256]{3,2,1,0:T(8,128)} fusion(bf16[5,17,256,256]{2,3,1,0:T(8,128)(2,1)} %bitcast.40), kind=kOutput, calls=%fused_computation.15 | convolution fusion | flops 2147483648 | bytes 36306944 | tf_op jit(solution)/shard_map/uvip,uvjp->uvij/dot_general | solution.py:36
  339.1 12.0 %fusion.7 = f32[4,16,256,256]{3,2,1,0:T(8,128)} fusion(bf16[5,17,256,256]{2,3,1,0:T(8,128)(2,1)} %bitcast.41), kind=kOutput, calls=%fused_computation.11 | convolution fusion | flops 2147483648 | bytes 36306944 | tf_op jit(solution)/shard_map/uvip,uvjp->uvij/dot_general | solution.py:36
  351.1 12.0 %fusion.9 = f32[4,16,256,256]{3,2,1,0:T(8,128)} fusion(bf16[5,17,256,256]{2,3,1,0:T(8,128)(2,1)} %bitcast.42), kind=kOutput, calls=%fused_computation.13 | convolution fusion | flops 2147483648 | bytes 36306944 | tf_op jit(solution)/shard_map/uvip,uvjp->uvij/dot_general | solution.py:36
  363.1 7.8 %fusion.34 = bf16[4,16,256,256]{2,3,1,0:T(8,128)(2,1)} fusion(bf16[5,17,256,256]{2,3,1,0:T(8,128)(2,1)} %bitcast.43), kind=kLoop, calls=%fused_computation.10.clone.1 | loop fusion | bytes 16777216 | tf_op jit(solution)/shard_map/uvip,uvjp->uvij/dot_general | solution.py:36
  370.8 36.0 %add_add_fusion = f32[4,16,256,256]{3,2,1,0:T(8,128)} fusion(f32[4,16,256,256]{3,2,1,0:T(8,128)} %fusion.7, f32[4,16,256,256]{3,2,1,0:T(8,128)} %fusion.11, f32[4,16,256,256]{3,2,1,0:T(8,128)} %fusion.9, bf16[5,17,256,256]{2,3,1,0:T(8,128)(2,1)} %bitcast.44, bf16[4,16,256,256]{2,3,1,0:T(8,128)(2,1)} %fusion.34), kind=kOutput, calls=%fused_computation.1 | convolution fusion | flops 2160066560 | bytes 86638592 | tf_op jit(solution)/shard_map/uvip,uvjp->uvij/dot_general | solution.py:36
  406.9 6.6 %slice_add_fusion = f32[4,16,128,128]{3,2,1,0:T(8,128)} fusion(f32[4,16,256,256]{3,2,1,0:T(8,128)} %add_add_fusion), kind=kLoop, calls=%fused_computation.28 | loop fusion | flops 1048576 | bytes 12582912 | tf_op jit(solution)/shard_map/add | solution.py:27
  413.5 0.0 copy-start
  413.5 18.3 %copy.48 = f32[4,16,128,128]{1,0,3,2:T(4,128)} copy(f32[4,16,128,128]{3,2,1,0:T(8,128)} %slice_add_fusion) | data formatting | bytes 8388608 | tf_op jit(solution)/shard_map/add | solution.py:27
  431.7 0.0 copy-done
  431.8 1.9 gather_fusion
  433.6 0.1 rsqrt_bitcast_fusion
  433.7 0.1 copy.49
  433.8 7.1 %fusion.20 = (f32[4,16,1,128,128]{4,3,1,0,2:T(8,128)S(1)}, f32[4,16,1,128,128]{4,3,1,0,2:T(8,128)S(1)}) fusion(f32[4,16,128]{2,1,0:T(8,128)S(1)} %copy.49, f32[4,16,256,256]{3,2,1,0:T(8,128)} %add_add_fusion), kind=kLoop, calls=%fused_computation.25 | loop fusion | flops 5242880 | bytes 25231360 | tf_op jit(solution)/shard_map/stack | solution.py:32
  440.9 1.1 pad_maximum_fusion.2
  442.0 4.0 copy.51
  (1 shorter events, 0.0 us)
Async XLA Ops:
  6.2 3.7 collective-permute-start
  8.5 5.6 %collective-permute-start.1 = (bf16[2,32,256,8]{2,3,0,1:T(8,128)(2,1)S(1)}, bf16[2,32,256,8]{2,3,0,1:T(8,128)(2,1)S(1)}, u32[]{:S(2)}, u32[]{:S(2)}) collective-permute-start(bf16[2,32,256,8]{2,3,0,1:T(8,128)(2,1)S(1)} %get-tuple-element.10), channel_id=1, source_target_pairs={{1,0},{2,1},{3,2},{4,3},{5,4},{6,5},{7,6},{9,8},{10,9},{11,10},{12... | collective-permute-start | bytes 786440 | tf_op jit(solution)/shard_map/ppermute | solution.py:21
  151.2 23.9 %collective-permute-start.2 = (bf16[2,128,8,256]{3,2,1,0:T(8,128)(2,1)S(1)}, bf16[2,128,8,256]{3,2,1,0:T(8,128)(2,1)S(1)}, u32[]{:S(2)}, u32[]{:S(2)}) collective-permute-start(bf16[2,128,8,256]{3,2,1,0:T(8,128)(2,1)S(1)} %get-tuple-element.7), channel_id=1, source_target_pairs={{0,8},{8,16},{16,24},{1,9},{9,17},{17,25},{2,10},{10,18},{18,26},{... | collective-permute-start | bytes 3145736 | tf_op jit(solution)/shard_map/ppermute | solution.py:20
  154.4 45.1 %collective-permute-start.3 = (bf16[2,128,8,256]{3,2,1,0:T(8,128)(2,1)S(1)}, bf16[2,128,8,256]{3,2,1,0:T(8,128)(2,1)S(1)}, u32[]{:S(2)}, u32[]{:S(2)}) collective-permute-start(bf16[2,128,8,256]{3,2,1,0:T(8,128)(2,1)S(1)} %get-tuple-element.8), channel_id=1, source_target_pairs={{8,0},{16,8},{24,16},{9,1},{17,9},{25,17},{10,2},{18,10},{26,18},{... | collective-permute-start | bytes 3145736 | tf_op jit(solution)/shard_map/ppermute | solution.py:21
  223.3 10.9 %collective-permute-start.4 = (bf16[2,128,80,8]{1,3,2,0:T(8,128)(2,1)S(1)}, bf16[2,128,80,8]{1,3,2,0:T(8,128)(2,1)S(1)}, u32[]{:S(2)}, u32[]{:S(2)}) collective-permute-start(bf16[2,128,80,8]{1,3,2,0:T(8,128)(2,1)S(1)} %copy.38), channel_id=1, source_target_pairs={{0,1},{1,2},{2,3},{3,4},{4,5},{5,6},{6,7},{8,9},{9,10},{10,11},{11... | collective-permute-start | bytes 983048 | tf_op jit(solution)/shard_map/ppermute | solution.py:20
  232.4 10.5 %collective-permute-start.5 = (bf16[2,128,80,8]{1,3,2,0:T(8,128)(2,1)S(1)}, bf16[2,128,80,8]{1,3,2,0:T(8,128)(2,1)S(1)}, u32[]{:S(2)}, u32[]{:S(2)}) collective-permute-start(bf16[2,128,80,8]{1,3,2,0:T(8,128)(2,1)S(1)} %copy.39), channel_id=1, source_target_pairs={{1,0},{2,1},{3,2},{4,3},{5,4},{6,5},{7,6},{9,8},{10,9},{11,10},{12... | collective-permute-start | bytes 983048 | tf_op jit(solution)/shard_map/ppermute | solution.py:21
  413.5 18.3 %copy-start = (s32[128]{0:T(128)S(1)}, s32[128]{0:T(128)}, u32[]{:S(2)}) copy-start(s32[128]{0:T(128)} %or_bitcast_fusion) | copy-start | bytes 1540
where the time goes:
time: 453 us; the launch traced here: 446 us
  local copies, waits for them, and re-layouts  155 us (34%)
  blocking collectives  93.8 us (21%)
  matrix products  87.4 us (19%)
  waiting for transfers between devices  52.6 us (12%)
  other arithmetic  42.8 us (9%)
  starting transfers between devices  14.2 us (3%)
    all_to_all x1, blocking collectives, on_device(): lax.all_to_all(shifted, 'date', split_axis=2, concat_axis=1, tiled=True)  93.8 us
    dot_general x4, matrix products, block_gram(): jnp.einsum('uvip,uvjp->uvij', pixels, pixels, preferred_element_type=jnp....  72 us
    ppermute x3, waiting for transfers between devices, with_halo(): after = lax.ppermute(initial, axis, down)  33.4 us
    concatenate x2, other arithmetic, with_halo(): value = jnp.concatenate([before, value, after], axis=dim)  27.4 us
    concatenate x1, local copies, waits for them, and re-layouts, with_halo(): value = jnp.concatenate([before, value, after], axis=dim)  26.8 us
    reshape x1, local copies, waits for them, and re-layouts, on_device(): pixel_grid.reshape(2 * date_count, range_blocks, half_window, az_blocks,...  24.6 us
    all_to_all x2, local copies, waits for them, and re-layouts, on_device(): lax.all_to_all(shifted, 'date', split_axis=2, concat_axis=1, tiled=True)  19.8 us
    ppermute x3, waiting for transfers between devices, with_halo(): before = lax.ppermute(last, axis, up)  19.2 us
  transfers between devices with their start and end apart: 6, of which 4 were waited for; matrix products, arithmetic and copies ran while one was open for 2% of the time, Pallas kernels for 0%

commit v1 on v0

v1 whole, which is shorter than its diff:
```python
import functools

import jax
import jax.numpy as jnp
from jax import lax
from jax.experimental import pallas as pl
from jax.experimental.pallas import tpu as pltpu
from jax.sharding import PartitionSpec as P

HALO = 8
SIDE = 16
PIX = SIDE * SIDE
LANES = 128
SUB = 8
DBLK = 16
EPS = 1e-06
VMEM = 56 * 1024 * 1024

bf16 = jnp.bfloat16
f32 = jnp.float32


def params():
    return pltpu.CompilerParams(vmem_limit_bytes=VMEM)


def block_transpose(rows):
    group = lax.broadcasted_iota(jnp.int32, rows[0].shape, 1) // SIDE
    for step in (4, 2, 1):
        low = (group & step) == 0
        later = list(rows)
        for r in range(8):
            if r & step == 0:
                a, b = rows[r], rows[r + step]
                later[r] = jnp.where(low, a, pltpu.roll(b, SIDE * step, 1))
                later[r + step] = jnp.where(low, pltpu.roll(a, LANES - SIDE * step, 1), b)
        rows = later
    return rows


def interior_kernel(spans, dest_rows, me_ref, slc_ref, rk_ref, ak_ref, *refs):
    *outs, plane = refs
    step, steps = pl.program_id(0), pl.num_programs(0)
    per_step, n_rows = slc_ref.shape[1], slc_ref.shape[2]
    lines = 2 * DBLK
    partners = len(outs) // len(spans)
    row_blocks = outs[0].shape[0]
    halves = plane.shape[0]

    @pl.when(step == 0)
    def _():
        zero = jnp.zeros((halves, SUB * lines, LANES), f32)
        plane[:, : SUB * lines, :] = zero
        plane[:, (SUB + n_rows) * lines :, :] = zero

    for i in range(per_step):
        kernel = ak_ref[i].astype(f32)[HALO : HALO + n_rows]
        kernel = pltpu.roll(kernel, HALO, 1).astype(bf16)
        for c in range(2):
            ranged = jnp.dot(rk_ref[i], slc_ref[c, i], preferred_element_type=f32).astype(bf16)
            moved = jnp.dot(ranged, kernel, preferred_element_type=f32)
            line = SUB * lines + c * DBLK + step * per_step + i
            for h in range(halves):
                plane[h, pl.ds(line, n_rows, stride=lines), :] = moved[:, h * LANES : (h + 1) * LANES]

    @pl.when(step == steps - 1)
    def _():
        me = me_ref[0]
        for k in range(partners):
            base = (me ^ k) * dest_rows

            def blocks(j, carry):
                first = base + j * SIDE
                for half in range(2):
                    for h in range(halves):
                        rows = []
                        for r in range(8):
                            start = pl.multiple_of((first + half * 8 + r) * lines, lines)
                            rows.append(plane[h, pl.ds(start, lines), :].astype(bf16))
                        cols = block_transpose(rows)
                        for g in range(8):
                            column = h * 8 + g
                            for s, (lo, hi) in enumerate(spans):
                                if lo <= column < hi:
                                    out = outs[s * partners + k]
                                    for c in range(2):
                                        out[j, column - lo, c, :, half * LANES : (half + 1) * LANES] = cols[g][
                                            c * DBLK : (c + 1) * DBLK
                                        ]
                return carry

            lax.fori_loop(0, row_blocks, blocks, 0)


def interior(me, slc, rk, ak, part, spans, partners):
    n_rows, n_az = slc.shape[2], slc.shape[3]
    dest_rows = n_rows // partners
    row_blocks = dest_rows // SIDE + 1
    per_step = 2
    steps = DBLK // per_step
    shapes = [
        jax.ShapeDtypeStruct((row_blocks, hi - lo, 2, DBLK, PIX), bf16)
        for lo, hi in spans
        for _ in range(partners)
    ]
    grid = pltpu.PrefetchScalarGridSpec(
        num_scalar_prefetch=1,
        grid=(steps,),
        in_specs=[
            pl.BlockSpec((2, per_step, n_rows, n_az), lambda t, m: (0, part * steps + t, 0, 0)),
            pl.BlockSpec((per_step, n_rows, n_rows), lambda t, m: (part * steps + t, 0, 0)),
            pl.BlockSpec((per_step, ak.shape[1], n_az), lambda t, m: (part * steps + t, 0, 0)),
        ],
        out_specs=[pl.BlockSpec(s.shape, lambda t, m: (0, 0, 0, 0, 0)) for s in shapes],
        scratch_shapes=[pltpu.VMEM((n_az // LANES, (n_rows + 2 * SUB) * 2 * DBLK, LANES), f32)],
    )
    flat = pl.pallas_call(
        functools.partial(interior_kernel, spans, dest_rows),
        grid_spec=grid,
        out_shape=shapes,
        compiler_params=params(),
        cost_estimate=pl.CostEstimate(flops=DBLK * 8 * 256**3, bytes_accessed=16 << 20, transcendentals=0),
        name=f"interior_{part}",
    )(me, slc, rk, ak)
    return [flat[s * partners : (s + 1) * partners] for s in range(len(spans))]


def rim_kernel(dest_rows, me_ref, edge_ref, rk_ref, ak_ref, *refs):
    *outs, plane = refs
    step, steps = pl.program_id(0), pl.num_programs(0)
    per_step, n_rows = rk_ref.shape[0], rk_ref.shape[1]
    n_dates = outs[0].shape[2]
    lines = 2 * n_dates
    row_blocks = outs[0].shape[0]
    eighths = n_rows // 8

    @pl.when(step == 0)
    def _():
        zero = jnp.zeros((lines, LANES), f32)
        plane[:lines, :] = zero
        plane[(eighths + 1) * lines :, :] = zero

    row = lax.broadcasted_iota(jnp.int32, (n_rows, 2 * LANES), 0)
    lane = lax.broadcasted_iota(jnp.int32, (n_rows, 2 * LANES), 1)
    own = (row % 8) == (lane % LANES) // SIDE
    gather = (
        lax.broadcasted_iota(jnp.int32, (eighths, n_rows), 1) // 8
        == lax.broadcasted_iota(jnp.int32, (eighths, n_rows), 0)
    ).astype(f32).astype(bf16)
    for i in range(per_step):
        ranged = jnp.dot(rk_ref[i], edge_ref[i], preferred_element_type=f32).astype(bf16)
        moved = jnp.dot(ranged, ak_ref[i], preferred_element_type=f32)
        moved = jnp.where(own, moved, 0.0).astype(bf16)
        packed = jnp.dot(gather, moved, preferred_element_type=f32)
        for c in range(2):
            line = lines + c * n_dates + step * per_step + i
            plane[pl.ds(line, eighths, stride=lines), :] = packed[:, c * LANES : (c + 1) * LANES]

    @pl.when(step == steps - 1)
    def _():
        me = me_ref[0]
        for k in range(len(outs)):
            base = (me ^ k) * (dest_rows // 8)
            for j in range(row_blocks):
                for half in range(2):
                    start = pl.multiple_of((base + 2 * j + half) * lines, lines)
                    values = plane[pl.ds(start, lines), :].astype(bf16)
                    for c in range(2):
                        outs[k][j, c, :, half * LANES : (half + 1) * LANES] = values[
                            c * n_dates : (c + 1) * n_dates
                        ]


def rim(me, edge, rk, ak_edge, partners):
    n_dates, n_rows = rk.shape[0], rk.shape[1]
    dest_rows = n_rows // partners
    row_blocks = dest_rows // SIDE + 1
    per_step = 4
    shape = jax.ShapeDtypeStruct((row_blocks, 2, n_dates, PIX), bf16)
    grid = pltpu.PrefetchScalarGridSpec(
        num_scalar_prefetch=1,
        grid=(n_dates // per_step,),
        in_specs=[
            pl.BlockSpec((per_step, n_rows, LANES), lambda t, m: (t, 0, 0)),
            pl.BlockSpec((per_step, n_rows, n_rows), lambda t, m: (t, 0, 0)),
            pl.BlockSpec((per_step, LANES, 2 * LANES), lambda t, m: (t, 0, 0)),
        ],
        out_specs=[pl.BlockSpec(shape.shape, lambda t, m: (0, 0, 0, 0))] * partners,
        scratch_shapes=[pltpu.VMEM(((n_rows // 8 + 2) * 2 * n_dates, LANES), f32)],
    )
    return pl.pallas_call(
        functools.partial(rim_kernel, dest_rows),
        grid_spec=grid,
        out_shape=[shape] * partners,
        compiler_params=params(),
        cost_estimate=pl.CostEstimate(flops=n_dates * 256**3, bytes_accessed=10 << 20, transcendentals=0),
        name="rim",
    )(me, edge, rk, ak_edge)


def block_moment(pixels):
    n = pixels.shape[0] // 2
    m = lax.dot_general(pixels, pixels, (((1,), (1,)), ((), ())), preferred_element_type=f32)
    return m[:n, :n] + m[n:, n:], m[n:, :n] - m[:n, n:]


def store_coherence(out, index, real, imag):
    n = real.shape[0]
    eye = lax.broadcasted_iota(jnp.int32, (n, n), 0) == lax.broadcasted_iota(jnp.int32, (n, n), 1)
    diagonal = jnp.where(eye, real, 0.0)
    column = lax.rsqrt(jnp.sum(diagonal, axis=1, keepdims=True) + EPS)
    row = lax.rsqrt(jnp.sum(diagonal, axis=0, keepdims=True) + EPS)
    scale = column * row
    out[(*index, 0)] = real * scale
    out[(*index, 1)] = imag * scale


def column_sums(read, scratch, row_blocks, emit):
    before = None
    for j in range(row_blocks):
        read(j, scratch.at[j])
        now = block_moment(scratch[j])
        if before is not None:
            emit(j - 1, before[0] + now[0], before[1] + now[1])
        before = now


def rim_gram_kernel(partners, me_ref, *refs):
    own, before, after = (refs[i * partners : (i + 1) * partners] for i in range(3))
    out, pixels = refs[3 * partners :]
    row_blocks, _, n, _ = own[0].shape
    me = me_ref[0]
    total = n * partners
    for end in range(2):

        def read(j, scratch):
            for k in range(partners):
                for c in range(2):
                    left, right = (before[k], own[k]) if end == 0 else (own[k], after[k])
                    lane = lax.broadcasted_iota(jnp.int32, (n, PIX), 1)
                    value = jnp.where(lane % SIDE < 8, left[j, c], right[j, c])
                    at = pl.multiple_of(c * total + (me ^ k) * n, SIDE)
                    scratch[pl.ds(at, n), :] = value

        def emit(u, real, imag):
            out[end, u, 0] = real
            out[end, u, 1] = imag

        column_sums(read, pixels, row_blocks, emit)


def rim_gram(me, own, before, after):
    partners = len(own)
    row_blocks, _, n, _ = own[0].shape
    total = n * partners
    whole = pl.BlockSpec(memory_space=pltpu.VMEM)
    return pl.pallas_call(
        functools.partial(rim_gram_kernel, partners),
        in_specs=[pl.BlockSpec(memory_space=pltpu.SMEM)] + [whole] * (3 * partners),
        out_specs=whole,
        out_shape=jax.ShapeDtypeStruct((2, row_blocks - 1, 2, total, total), f32),
        scratch_shapes=[pltpu.VMEM((row_blocks, 2 * total, PIX), bf16)],
        compiler_params=params(),
        cost_estimate=pl.CostEstimate(flops=20 * 256**3, bytes_accessed=4 << 20, transcendentals=0),
        name="rim_gram",
    )(me, *own, *before, *after)


def gram_kernel(partners, parts, columns, closing, me_ref, *refs):
    pieces = refs[: partners * parts]
    state, end = refs[partners * parts : partners * parts + 2]
    out, state_out, held, pixels = refs[-4:]
    step = pl.program_id(0)
    row_blocks = pieces[0].shape[0]
    me = me_ref[0]
    total = pixels.shape[1] // 2

    @pl.when(step == 0)
    def _():
        held[...] = state[0]

    def work():
        def read(j, scratch):
            for k in range(partners):
                for p in range(parts):
                    for c in range(2):
                        at = pl.multiple_of(c * total + (me ^ k) * (parts * DBLK) + p * DBLK, DBLK)
                        scratch[pl.ds(at, DBLK), :] = pieces[k * parts + p][j, 0, c]

        def emit(u, real, imag):
            store_coherence(out, (u, 0), held[u, 0] + real, held[u, 1] + imag)
            held[u, 0] = real
            held[u, 1] = imag

        column_sums(read, pixels, row_blocks, emit)

    if closing:
        pl.when(step < columns)(work)

        @pl.when(step == columns)
        def _():
            for u in range(row_blocks - 1):
                store_coherence(out, (u, 0), held[u, 0] + end[0, u, 0], held[u, 1] + end[0, u, 1])
    else:
        work()

    @pl.when(step == pl.num_programs(0) - 1)
    def _():
        state_out[0] = held[...]


def gram(me, pieces, offsets, columns, first, state, state_at, ends, result, out_shape, closing):
    partners, parts = len(pieces), len(pieces[0])
    row_blocks = pieces[0][0].shape[0]
    total = out_shape.shape[-1]
    grid_steps = columns + (1 if closing else 0)

    def piece_spec(p):
        return pl.BlockSpec(
            (row_blocks, 1, 2, DBLK, PIX),
            lambda t, m: (0, offsets[p] + jnp.minimum(t, columns - 1), 0, 0, 0),
        )

    state_block = (1, row_blocks - 1, 2, total, total)
    in_specs = [piece_spec(p) for _ in range(partners) for p in range(parts)]
    in_specs += [
        pl.BlockSpec(state_block, lambda t, m: (state_at, 0, 0, 0, 0)),
        pl.BlockSpec(state_block, lambda t, m: (1, 0, 0, 0, 0)),
    ]
    operands = [x for k in pieces for x in k] + [state, ends]
    aliases = {}
    if result is not None:
        in_specs.append(pl.BlockSpec(memory_space=pl.ANY))
        aliases = {1 + len(operands): 0}
        operands.append(result)
    grid = pltpu.PrefetchScalarGridSpec(
        num_scalar_prefetch=1,
        grid=(grid_steps,),
        in_specs=in_specs,
        out_specs=[
            pl.BlockSpec((row_blocks - 1, 1, 2, total, total), lambda t, m: (0, first - 1 + t, 0, 0, 0)),
            pl.BlockSpec(state_block, lambda t, m: (0, 0, 0, 0, 0)),
        ],
        scratch_shapes=[
            pltpu.VMEM((row_blocks - 1, 2, total, total), f32),
            pltpu.VMEM((row_blocks, 2 * total, PIX), bf16),
        ],
    )
    return pl.pallas_call(
        functools.partial(gram_kernel, partners, parts, columns, closing),
        grid_spec=grid,
        out_shape=[out_shape, jax.ShapeDtypeStruct(state_block, f32)],
        input_output_aliases=aliases,
        compiler_params=params(),
        cost_estimate=pl.CostEstimate(flops=columns * 10 * 256**3, bytes_accessed=columns << 21, transcendentals=0),
        name=f"gram_{first}",
    )(me, *operands)


def shift(value, axis, by):
    n = lax.axis_size(axis)
    pairs = [(i, i + by) for i in range(n) if 0 <= i + by < n]
    return lax.ppermute(value, axis, pairs)


def exchange(blocks):
    n = lax.axis_size("date")
    got = [blocks[0]]
    for k in range(1, n):
        got.append(lax.ppermute(blocks[k], "date", [(i, i ^ k) for i in range(n)]))
    return got


def edge_operands(slc, ak):
    n_az = slc.shape[3]
    first, last = slc[..., :SUB], slc[..., n_az - SUB :]
    left, right = shift(last, "strip", 1), shift(first, "strip", -1)
    pad = jnp.zeros((*slc.shape[:3], 16), bf16)
    edge = jnp.concatenate([slc[..., n_az - 16 :], right, left, slc[..., :16], pad], axis=3)
    edge = jnp.concatenate([edge[0], edge[1]], axis=2)
    at_end = ak[:, n_az - 8 : n_az + 16, n_az - 8 :]
    at_start = ak[:, :24, :8]
    block = jnp.concatenate(
        [
            jnp.pad(at_end, ((0, 0), (0, 0), (0, 8))),
            jnp.pad(at_start, ((0, 0), (0, 0), (8, 0))),
        ],
        axis=1,
    )
    block = jnp.tile(block, (1, 1, 8))
    weights = jnp.concatenate(
        [
            jnp.pad(block, ((0, 0), (0, 16), (0, LANES))),
            jnp.pad(block, ((0, 0), (0, 16), (LANES, 0))),
        ],
        axis=1,
    )
    return edge, weights


def on_device(slc, range_kernel, azimuth_kernel):
    partners = lax.axis_size("date")
    n_dates, n_rows, n_az = slc.shape[1:]
    total = n_dates * partners
    columns = n_az // SIDE
    me = lax.axis_index("date").astype(jnp.int32).reshape(1)
    parts = n_dates // DBLK
    bounds = [1, 6, 10, 13, columns]
    spans = list(zip(bounds[:-1], bounds[1:]))

    sent = []
    for part in range(parts - 1):
        sent.append(interior(me, slc, range_kernel, azimuth_kernel, part, [(1, columns)], partners))
    early = [exchange(s[0]) for s in sent]
    edge, weights = edge_operands(slc, azimuth_kernel)
    last = interior(me, slc, range_kernel, azimuth_kernel, parts - 1, spans, partners)
    rims = exchange(rim(me, edge, range_kernel, weights, partners))
    before = [shift(x, "strip", 1) for x in rims]
    after = [shift(x, "strip", -1) for x in rims]
    late = [exchange(x) for x in last]
    ends = rim_gram(me, rims, before, after)

    dest_windows = n_rows // partners // SIDE
    out_shape = jax.ShapeDtypeStruct((dest_windows, columns, 2, total, total), f32)
    result, state = None, ends
    for s, (lo, hi) in enumerate(spans):
        pieces = [[e[k] for e in early] + [late[s][k]] for k in range(partners)]
        offsets = [lo - 1] * (parts - 1) + [0]
        result, state = gram(
            me, pieces, offsets, hi - lo, lo, state, 0, ends, result, out_shape, closing=s == len(spans) - 1
        )
    return result


def solution(mesh):
    in_specs = (P(None, "date", None, "strip"), P("date", None, None), P("date", None, "strip"))
    out_specs = P("date", "strip", None, None, None)
    return jax.shard_map(on_device, mesh=mesh, in_specs=in_specs, out_specs=out_specs, check_vma=False)
```

time: 453 us -> 249 us (0.55)
  local copies, waits for them, and re-layouts: 155 us -> 56.5 us
  blocking collectives: 93.8 us -> 0 us
  matrix products: 87.4 us -> 0 us
  Pallas kernels: 0 us -> 81.4 us
  other arithmetic: 42.8 us -> 4.23 us
  starting transfers between devices: 14.2 us -> 44 us
  waiting for transfers between devices: 52.6 us -> 57.8 us
    all_to_all x1 -> x0, blocking collectives: 93.8 us -> none  [on_device(): lax.all_to_all(shifted, 'date', split_axis=2, concat_axis=1, tiled=True)]
    dot_general x6 -> x0, matrix products: 87.4 us -> none  [the longest x4 72 us: block_gram(): jnp.einsum('uvip,uvjp->uvij', pixels, pixels, preferred_element_type=jnp....]
    pallas_call x0 -> x8, Pallas kernels: none -> 81.4 us  [the longest x2 44.5 us: interior(): pl.pallas_call(functools.partial(interior_kernel, spans, dest_rows), grid...]
    ppermute x6 -> x28, starting transfers between devices: 14.2 us -> 44 us  [the longest x18 23.7 us: exchange(): got.append(lax.ppermute(blocks[k], 'date', [(i, i ^ k) for i in range(n)]))]
    reshape x1 -> x0, local copies, waits for them, and re-layouts: 24.6 us -> none  [on_device(): pixel_grid.reshape(2 * date_count, range_blocks, half_window, az_blocks,...]
    concatenate x3, other arithmetic: 27.9 us -> 4.23 us  [the longest x1 2.49 us: edge_operands(): edge = jnp.concatenate([edge[0], edge[1]], axis=2)]
    all_to_all x2 -> x0, local copies, waits for them, and re-layouts: 19.8 us -> none  [on_device(): lax.all_to_all(shifted, 'date', split_axis=2, concat_axis=1, tiled=True)]
    add x1 -> x0, local copies, waits for them, and re-layouts: 18.3 us -> none  [coherence_of(): moment[..., :date_count, :date_count]]
  transfers between devices with their start and end apart: 6 -> 28, of which waited for: 4 -> 8; matrix products, arithmetic and copies ran while one was open for 2% -> 20% of each run, Pallas kernels for 0% -> 31%
where the time goes in v1:
time: 249 us; the launch traced here: 245 us
  Pallas kernels  81.4 us (33%)
  waiting for transfers between devices  57.8 us (23%)
  local copies, waits for them, and re-layouts  56.5 us (23%)
  starting transfers between devices  44 us (18%)
  other arithmetic  4.23 us (2%)
    ppermute x18, waiting for transfers between devices, exchange(): got.append(lax.ppermute(blocks[k], 'date', [(i, i ^ k) for i in range(n)]))  52 us
    pallas_call x2, Pallas kernels, interior(): pl.pallas_call(functools.partial(interior_kernel, spans, dest_rows), grid...  44.5 us
    ppermute x18, starting transfers between devices, exchange(): got.append(lax.ppermute(blocks[k], 'date', [(i, i ^ k) for i in range(n)]))  23.7 us
    pallas_call x4, Pallas kernels, gram(): pl.pallas_call(functools.partial(gram_kernel, partners, parts, columns, c...  22.4 us
    concatenate x1, local copies, waits for them, and re-layouts, edge_operands(): jnp.concatenate([slc[..., n_az - 16:], right, left, slc[..., :16], pad],...  20.8 us
    ppermute x10, starting transfers between devices, shift(): return lax.ppermute(value, axis, pairs)  20.2 us
    pallas_call x1, Pallas kernels, rim(): pl.pallas_call(functools.partial(rim_kernel, dest_rows), grid_spec=grid,...  11.3 us
    unnamed x64, local copies, waits for them, and re-layouts  9.17 us
  transfers between devices with their start and end apart: 28, of which 8 were waited for; matrix products, arithmetic and copies ran while one was open for 20% of the time, Pallas kernels for 31%

profile of v1, /device:TPU:0, one launch (start us, length us, event | category | flops | bytes accessed | tf_op | source)
XLA Modules:
  0.0 244.6 jit_solution(17390175058943275091)
XLA Ops:
  0.0 6.4 %fusion.7 = (bf16[2,32,256,8]{3,2,1,0:T(8,128)(2,1)}, bf16[2,32,256,8]{3,2,1,0:T(8,128)(2,1)}) fusion(bf16[2,32,256,256]{3,2,1,0:T(8,128)(2,1)} %slc_ref.3), kind=kLoop, calls=%fused_computation.14 | loop fusion | bytes 1048576 | tf_op jit(solution)/shard_map/slice | solution.py:376
  6.4 3.6 %copy.18 = bf16[2,32,256,8]{2,3,1,0:T(8,128)(2,1)S(1)} copy(bf16[2,32,256,8]{3,2,1,0:T(8,128)(2,1)} %get-tuple-element.70) | data formatting | bytes 524288
  10.0 1.3 collective-permute-start.15
  11.3 3.6 %copy.19 = bf16[2,32,256,8]{2,3,1,0:T(8,128)(2,1)S(1)} copy(bf16[2,32,256,8]{3,2,1,0:T(8,128)(2,1)} %get-tuple-element.69) | data formatting | bytes 524288
  14.9 3.0 %collective-permute-start.16 = (bf16[2,32,256,8]{2,3,1,0:T(8,128)(2,1)S(1)}, bf16[2,32,256,8]{2,3,1,0:T(8,128)(2,1)S(1)}, u32[]{:S(2)}, u32[]{:S(2)}) collective-permute-start(bf16[2,32,256,8]{2,3,1,0:T(8,128)(2,1)S(1)} %copy.19), channel_id=1, source_target_pairs={{0,1},{1,2},{2,3},{3,4},{4,5},{5,6},{6,7},{8,9},{9,10},{10,11},{11... | collective-permute-start | bytes 786440 | tf_op jit(solution)/shard_map/ppermute | solution.py:363
  18.0 22.3 %interior_1.1 = (bf16[5,5,2,16,256]{4,3,2,1,0:T(8,128)(2,1)}, bf16[5,5,2,16,256]{4,3,2,1,0:T(8,128)(2,1)}, bf16[5,5,2,16,256]{4,3,2,1,0:T(8,128)(2,1)}, bf16[5,5...) custom-call(s32[1]{0:T(128)} %bitcast.me_ref, ...), custom_call_target="tpu_custom_call" | custom-call | flops 2147483648 | bytes 16777216 | tf_op jit(solution)/shard_map/interior_1/pallas_call | solution.py:117
  40.3 2.9 %collective-permute-start.12 = (bf16[5,5,2,16,256]{4,3,2,1,0:T(8,128)(2,1)}, bf16[5,5,2,16,256]{4,3,2,1,0:T(8,128)(2,1)S(1)}, u32[]{:S(2)}, u32[]{:S(2)}) collective-permute-start(bf16[5,5,2,16,256]{4,3,2,1,0:T(8,128)(2,1)} %get-tuple-element.53), channel_id=1, source_target_pairs={{0,8},{8,0},{16,24},{24,16},{1,9},{9,1},{17,25},{25,17},{2,10},{10... | collective-permute-start | bytes 1228808 | tf_op jit(solution)/shard_map/ppermute | solution.py:370
  43.2 1.5 collective-permute-start.10
  45.3 6.4 %fusion.6 = (bf16[2,32,256,16]{3,2,1,0:T(8,128)(2,1)}, bf16[2,32,256,16]{3,2,1,0:T(8,128)(2,1)}) fusion(bf16[2,32,256,256]{3,2,1,0:T(8,128)(2,1)} %slc_ref.3), kind=kLoop, calls=%fused_computation.13 | loop fusion | bytes 2097152 | tf_op jit(solution)/shard_map/slice | solution.py:379
  51.7 1.1 fusion.8
  53.7 1.6 fusion.2.ak_ref
  55.4 22.1 %interior_0.1 = (bf16[5,15,2,16,256]{4,3,2,1,0:T(8,128)(2,1)}, bf16[5,15,2,16,256]{4,3,2,1,0:T(8,128)(2,1)}, bf16[5,15,2,16,256]{4,3,2,1,0:T(8,128)(2,1)}, bf16[5,15,2,16,256]{4,3,2,1,0:T(8,128)(2,1)}) custom-call(s32[1]{0:T(128)} %bitcast.me_ref, bf16[2,32,256,256]{3,2,1,0:T(8,128)(2,1)} %slc_ref.3, bf16[32,256,256]{2,1,0:T(8,128)(2,1)} %rk_ref.5, ...), custom_call_target="tpu_custom_call" | custom-call | flops 2147483648 | bytes 16777216 | tf_op jit(solution)/shard_map/interior_0/pallas_call | solution.py:117
  77.6 3.2 %copy.12 = bf16[2,32,256,8]{3,2,1,0:T(8,128)(2,1)} copy(bf16[2,32,256,8]{2,3,1,0:T(8,128)(2,1)S(1)} %collective-permute-done.15) | data formatting | bytes 524288 | tf_op jit(solution)/shard_map/ppermute | solution.py:363
  80.8 2.9 %collective-permute-start.14 = (bf16[5,5,2,16,256]{4,3,2,1,0:T(8,128)(2,1)}, bf16[5,5,2,16,256]{4,3,2,1,0:T(8,128)(2,1)S(1)}, u32[]{:S(2)}, u32[]{:S(2)}) collective-permute-start(bf16[5,5,2,16,256]{4,3,2,1,0:T(8,128)(2,1)} %get-tuple-element.55), channel_id=1, source_target_pairs={{0,24},{8,16},{16,8},{24,0},{1,25},{9,17},{17,9},{25,1},{2,26},{10... | collective-permute-start | bytes 1228808 | tf_op jit(solution)/shard_map/ppermute | solution.py:370
  83.6 3.1 %copy.13 = bf16[2,32,256,8]{3,2,1,0:T(8,128)(2,1)} copy(bf16[2,32,256,8]{2,3,1,0:T(8,128)(2,1)S(1)} %collective-permute-done.16) | data formatting | bytes 524288 | tf_op jit(solution)/shard_map/ppermute | solution.py:363
  86.8 3.0 %broadcast_in_dim.3 = bf16[2,32,256,16]{3,2,1,0:T(8,128)(2,1)} broadcast(bf16[]{:T(256)} %constant.8.clone.1), dimensions={} | broadcast | bytes 524290 | tf_op jit(solution)/shard_map/broadcast_in_dim | solution.py:378
  89.8 20.8 %concatenate.12 = bf16[2,32,256,64]{3,2,1,0:T(8,128)(2,1)} concatenate(bf16[2,32,256,16]{3,2,1,0:T(8,128)(2,1)} %get-tuple-element.68, bf16[2,32,256,8]{3,2,1,0:T(8,128)(2,1)} %copy.12, bf16[2,32,256,8]{3,2,1,0:T(8,128)(2,1)} %copy.13, bf16[2,32,256,16]{3,2,1,0:T(8,128)(2,1)} %get-tuple-element.67, bf16[2,32,256,16]{3,2,1,0:T(8,128)(2,1)} %broadcast_in_dim.3), dimensions={3} | concatenate | bytes 4194304 | tf_op jit(solution)/shard_map/concatenate | solution.py:379
  110.8 2.0 collective-permute-start.9
  112.7 2.7 %slice_bitcast_fusion.1 = (bf16[32,256,64]{2,1,0:T(8,128)(2,1)S(1)}, bf16[32,256,64]{2,1,0:T(8,128)(2,1)S(1)}) fusion(bf16[2,32,256,64]{3,2,1,0:T(8,128)(2,1)} %concatenate.12), kind=kLoop, calls=%fused_computation.6 | loop fusion | bytes 4194304 | tf_op jit(solution)/shard_map/squeeze | solution.py:380
  115.5 6.7 %collective-permute-done.11.refs_7_ = bf16[5,4,2,16,256]{4,3,2,1,0:T(8,128)(2,1)S(1)} collective-permute-done((bf16[5,4,2,16,256]{4,3,2,1,0:T(8,128)(2,1)S(1)}, bf16[5,4,2,16,256]{4,3,2,1,0:T(8,128)(2,1)S(1)}, u32[]{:S(2)}, u32[]{:S(2)}) %collective-permute-start.11) | collective-permute-done | bytes 327712 | tf_op jit(solution)/shard_map/ppermute | solution.py:370
  122.7 5.5 %collective-permute-done.9.refs_3_ = bf16[5,4,2,16,256]{4,3,2,1,0:T(8,128)(2,1)S(1)} collective-permute-done((bf16[5,4,2,16,256]{4,3,2,1,0:T(8,128)(2,1)S(1)}, bf16[5,4,2,16,256]{4,3,2,1,0:T(8,128)(2,1)S(1)}, u32[]{:S(2)}, u32[]{:S(2)}) %collective-permute-start.9) | collective-permute-done | bytes 327712 | tf_op jit(solution)/shard_map/ppermute | solution.py:370
  128.3 1.5 collective-permute-start.2
  129.8 2.5 %pad_maximum_fusion.edge_ref = bf16[32,256,128]{2,1,0:T(8,128)(2,1)} fusion(bf16[32,256,64]{2,1,0:T(8,128)(2,1)S(1)} %get-tuple-element.74, bf16[32,256,64]{2,1,0:T(8,128)(2,1)S(1)} %get-tuple-element.73), kind=kLoop, calls=%fused_computation.7 | loop fusion | flops 4194304 | bytes 4194304 | tf_op jit(solution)/shard_map/concatenate | solution.py:380
  132.3 11.3 %rim.1 = (bf16[5,2,32,256]{3,2,1,0:T(8,128)(2,1)}, bf16[5,2,32,256]{3,2,1,0:T(8,128)(2,1)}, bf16[5,2,32,256]{3,2,1,0:T(8,128)(2,1)}, bf16[5,2,32,256]{3,2,1,0:T(8,128)(2,1)}) custom-call(s32[1]{0:T(128)} %bitcast.me_ref, bf16[32,256,128]{2,1,0:T(8,128)(2,1)} %pad_maximum_fusion.edge_ref, bf16[32,256,256]{2,1,0:T(8,128)(2,1)} %rk_ref.5, ...), custom_call_target="tpu_custom_call" | custom-call | flops 536870912 | bytes 10485760 | tf_op jit(solution)/shard_map/rim/pallas_call | solution.py:191
  143.7 2.0 collective-permute-start.17
  145.6 1.5 collective-permute-start.18
  147.2 36.1 %collective-permute-done.17.refs_1_ = bf16[5,2,32,256]{3,2,1,0:T(8,128)(2,1)S(1)} collective-permute-done((bf16[5,2,32,256]{3,2,1,0:T(8,128)(2,1)}, bf16[5,2,32,256]{3,2,1,0:T(8,128)(2,1)S(1)}, u32[]{:S(2)}, u32[]{:S(2)}) %collective-permute-start.17) | collective-permute-done | bytes 163872 | tf_op jit(solution)/shard_map/ppermute | solution.py:370
  183.3 1.5 collective-permute-start.19
  184.9 1.3 collective-permute-start.20
  186.2 3.5 %collective-permute-done.19.refs_3_ = bf16[5,2,32,256]{3,2,1,0:T(8,128)(2,1)S(1)} collective-permute-done((bf16[5,2,32,256]{3,2,1,0:T(8,128)(2,1)}, bf16[5,2,32,256]{3,2,1,0:T(8,128)(2,1)S(1)}, u32[]{:S(2)}, u32[]{:S(2)}) %collective-permute-start.19) | collective-permute-done | bytes 163872 | tf_op jit(solution)/shard_map/ppermute | solution.py:370
  189.7 1.3 collective-permute-start.24
  191.0 3.0 %collective-permute-start.21 = (bf16[5,2,32,256]{3,2,1,0:T(8,128)(2,1)S(1)}, bf16[5,2,32,256]{3,2,1,0:T(8,128)(2,1)S(1)}, u32[]{:S(2)}, u32[]{:S(2)}) collective-permute-start(bf16[5,2,32,256]{3,2,1,0:T(8,128)(2,1)S(1)} %collective-permute-done.17.refs_1_), channel_id=1, source_target_pairs={{0,1},{1,2},{2,3},{3,4},{4,5},{5,6},{6,7},{8,9},{9,10},{10,11},{11... | collective-permute-start | bytes 491528 | tf_op jit(solution)/shard_map/ppermute | solution.py:363
  194.1 4.3 %collective-permute-start.22 = (bf16[5,2,32,256]{3,2,1,0:T(8,128)(2,1)S(1)}, bf16[5,2,32,256]{3,2,1,0:T(8,128)(2,1)S(1)}, u32[]{:S(2)}, u32[]{:S(2)}) collective-permute-start(bf16[5,2,32,256]{3,2,1,0:T(8,128)(2,1)S(1)} %collective-permute-done.18.refs_2_), channel_id=1, source_target_pairs={{0,1},{1,2},{2,3},{3,4},{4,5},{5,6},{6,7},{8,9},{9,10},{10,11},{11... | collective-permute-start | bytes 491528 | tf_op jit(solution)/shard_map/ppermute | solution.py:363
  198.4 1.9 collective-permute-start.23
  200.4 1.3 collective-permute-start.25
  201.7 1.3 collective-permute-start.26
  203.0 2.1 collective-permute-done.25.refs_9_
  205.2 1.5 collective-permute-start.27
  207.4 1.5 collective-permute-start.7
  208.9 2.9 %collective-permute-done.27.refs_11_ = bf16[5,2,32,256]{3,2,1,0:T(8,128)(2,1)S(1)} collective-permute-done((bf16[5,2,32,256]{3,2,1,0:T(8,128)(2,1)S(1)}, bf16[5,2,32,256]{3,2,1,0:T(8,128)(2,1)S(1)}, u32[]{:S(2)}, u32[]{:S(2)}) %collective-permute-start.27) | collective-permute-done | bytes 163872 | tf_op jit(solution)/shard_map/ppermute | solution.py:363
  211.8 1.5 collective-permute-start.8
  213.3 1.5 collective-permute-start.1
  215.4 1.6 collective-permute-start.5
  217.0 3.2 %rim_gram.1.refs_8_.refs_9_ = f32[2,4,2,128,128]{4,3,2,1,0:T(8,128)} custom-call(s32[1]{0:T(128)} %bitcast.me_ref, bf16[5,2,32,256]{3,2,1,0:T(8,128)(2,1)} %get-tuple-element.56.refs_0_, bf16[5,2,32,256]{3,2,1,0:T(8,128)(2,1)} %copy-done.15, bf16[5,2,32,256]{3,2,1,0:T(8,128)(2,1)} %copy-done.16, bf16[5,2,32,256]{3,2,1,0:T(8,128)(2,1)} %copy-done.17, ...), custom_call_target="tpu_custom_call" | custom-call | flops 335544320 | bytes 4194304 | tf_op jit(solution)/shard_map/rim_gram/pallas_call | solution.py:257
  220.2 6.8 %gram_1.1 = (f32[4,16,2,128,128]{4,3,2,1,0:T(8,128)}, f32[1,4,2,128,128]{4,3,2,1,0:T(8,128)}) custom-call(s32[1]{0:T(128)} %bitcast.me_ref, bf16[5,15,2,16,256]{4,3,2,1,0:T(8,128)(2,1)} %get-tuple-element.36.refs_0_, bf16[5,5,2,16,256]{4,3,2,1,0:T(8,128)(2,1)} %get-tuple-element.52.refs_1_, bf16[5,15,2,16,256]{4,3,2,1,0:T(8,128)(2,1)} %copy-done, ...), custom_call_target="tpu_custom_call" | custom-call | flops 838860800 | bytes 10485760 | tf_op jit(solution)/shard_map/gram_1/pallas_call | solution.py:349
  227.0 5.5 %gram_6.1 = (f32[4,16,2,128,128]{4,3,2,1,0:T(8,128)}, f32[1,4,2,128,128]{4,3,2,1,0:T(8,128)}) custom-call(s32[1]{0:T(128)} %bitcast.me_ref, bf16[5,15,2,16,256]{4,3,2,1,0:T(8,128)(2,1)} %get-tuple-element.36.refs_0_, bf16[5,4,2,16,256]{4,3,2,1,0:T(8,128)(2,1)} %get-tuple-element.48.refs_1_, ...), custom_call_target="tpu_custom_call", output_to_operand_aliasing={{0}: (11, {})} | custom-call | flops 671088640 | bytes 8388608 | tf_op jit(solution)/shard_map/gram_6/pallas_call | solution.py:349
  233.4 4.9 %gram_10.1 = (f32[4,16,2,128,128]{4,3,2,1,0:T(8,128)}, f32[1,4,2,128,128]{4,3,2,1,0:T(8,128)}) custom-call(s32[1]{0:T(128)} %bitcast.me_ref, bf16[5,15,2,16,256]{4,3,2,1,0:T(8,128)(2,1)} %get-tuple-element.36.refs_0_, bf16[5,3,2,16,256]{4,3,2,1,0:T(8,128)(2,1)} %get-tuple-element.44.refs_1_, ...), custom_call_target="tpu_custom_call", output_to_operand_aliasing={{0}: (11, {})} | custom-call | flops 503316480 | bytes 6291456 | tf_op jit(solution)/shard_map/gram_10/pallas_call | solution.py:349
  239.2 5.2 %gram_13.1 = (f32[4,16,2,128,128]{4,3,2,1,0:T(8,128)}, f32[1,4,2,128,128]{4,3,2,1,0:T(8,128)}) custom-call(s32[1]{0:T(128)} %bitcast.me_ref, bf16[5,15,2,16,256]{4,3,2,1,0:T(8,128)(2,1)} %get-tuple-element.36.refs_0_, bf16[5,3,2,16,256]{4,3,2,1,0:T(8,128)(2,1)} %get-tuple-element.37.refs_1_, ...), custom_call_target="tpu_custom_call", output_to_operand_aliasing={{0}: (11, {})} | custom-call | flops 503316480 | bytes 6291456 | tf_op jit(solution)/shard_map/gram_13/pallas_call | solution.py:349
  (93 shorter events, 5.5 us)
Async XLA Ops:
  10.0 67.5 %collective-permute-start.15 = (bf16[2,32,256,8]{2,3,1,0:T(8,128)(2,1)S(1)}, bf16[2,32,256,8]{2,3,1,0:T(8,128)(2,1)S(1)}, u32[]{:S(2)}, u32[]{:S(2)}) collective-permute-start(bf16[2,32,256,8]{2,3,1,0:T(8,128)(2,1)S(1)} %copy.18), channel_id=1, source_target_pairs={{1,0},{2,1},{3,2},{4,3},{5,4},{6,5},{7,6},{9,8},{10,9},{11,10},{12... | collective-permute-start | bytes 786440 | tf_op jit(solution)/shard_map/ppermute | solution.py:363
  14.9 65.9 %collective-permute-start.16 = (bf16[2,32,256,8]{2,3,1,0:T(8,128)(2,1)S(1)}, bf16[2,32,256,8]{2,3,1,0:T(8,128)(2,1)S(1)}, u32[]{:S(2)}, u32[]{:S(2)}) collective-permute-start(bf16[2,32,256,8]{2,3,1,0:T(8,128)(2,1)S(1)} %copy.19), channel_id=1, source_target_pairs={{0,1},{1,2},{2,3},{3,4},{4,5},{5,6},{6,7},{8,9},{9,10},{10,11},{11... | collective-permute-start | bytes 786440 | tf_op jit(solution)/shard_map/ppermute | solution.py:363
  40.3 89.5 %collective-permute-start.12 = (bf16[5,5,2,16,256]{4,3,2,1,0:T(8,128)(2,1)}, bf16[5,5,2,16,256]{4,3,2,1,0:T(8,128)(2,1)S(1)}, u32[]{:S(2)}, u32[]{:S(2)}) collective-permute-start(bf16[5,5,2,16,256]{4,3,2,1,0:T(8,128)(2,1)} %get-tuple-element.53), channel_id=1, source_target_pairs={{0,8},{8,0},{16,24},{24,16},{1,9},{9,1},{17,25},{25,17},{2,10},{10... | collective-permute-start | bytes 1228808 | tf_op jit(solution)/shard_map/ppermute | solution.py:370
  43.2 67.5 %collective-permute-start.10 = (bf16[5,4,2,16,256]{4,3,2,1,0:T(8,128)(2,1)}, bf16[5,4,2,16,256]{4,3,2,1,0:T(8,128)(2,1)S(1)}, u32[]{:S(2)}, u32[]{:S(2)}) collective-permute-start(bf16[5,4,2,16,256]{4,3,2,1,0:T(8,128)(2,1)} %get-tuple-element.50), channel_id=1, source_target_pairs={{0,16},{8,24},{16,0},{24,8},{1,17},{9,25},{17,1},{25,9},{2,18},{10... | collective-permute-start | bytes 983048 | tf_op jit(solution)/shard_map/ppermute | solution.py:370
  44.7 65.9 %collective-permute-start.6 = (bf16[5,3,2,16,256]{4,3,2,1,0:T(8,128)(2,1)}, bf16[5,3,2,16,256]{4,3,2,1,0:T(8,128)(2,1)S(1)}, u32[]{:S(2)}, u32[]{:S(2)}) collective-permute-start(bf16[5,3,2,16,256]{4,3,2,1,0:T(8,128)(2,1)} %get-tuple-element.45), channel_id=1, source_target_pairs={{0,8},{8,0},{16,24},{24,16},{1,9},{9,1},{17,25},{25,17},{2,10},{10... | collective-permute-start | bytes 737288 | tf_op jit(solution)/shard_map/ppermute | solution.py:370
  77.5 66.1 %collective-permute-start.13 = (bf16[5,5,2,16,256]{4,3,2,1,0:T(8,128)(2,1)}, bf16[5,5,2,16,256]{4,3,2,1,0:T(8,128)(2,1)S(1)}, u32[]{:S(2)}, u32[]{:S(2)}) collective-permute-start(bf16[5,5,2,16,256]{4,3,2,1,0:T(8,128)(2,1)} %get-tuple-element.54), channel_id=1, source_target_pairs={{0,16},{8,24},{16,0},{24,8},{1,17},{9,25},{17,1},{25,9},{2,18},{10... | collective-permute-start | bytes 1228808 | tf_op jit(solution)/shard_map/ppermute | solution.py:370
  80.8 64.9 %collective-permute-start.14 = (bf16[5,5,2,16,256]{4,3,2,1,0:T(8,128)(2,1)}, bf16[5,5,2,16,256]{4,3,2,1,0:T(8,128)(2,1)S(1)}, u32[]{:S(2)}, u32[]{:S(2)}) collective-permute-start(bf16[5,5,2,16,256]{4,3,2,1,0:T(8,128)(2,1)} %get-tuple-element.55), channel_id=1, source_target_pairs={{0,24},{8,16},{16,8},{24,0},{1,25},{9,17},{17,9},{25,1},{2,26},{10... | collective-permute-start | bytes 1228808 | tf_op jit(solution)/shard_map/ppermute | solution.py:370
  89.8 20.8 %copy-start.27 = (bf16[5,4,2,16,256]{4,3,2,1,0:T(8,128)(2,1)S(1)}, bf16[5,4,2,16,256]{4,3,2,1,0:T(8,128)(2,1)}, u32[]{:S(2)}) copy-start(bf16[5,4,2,16,256]{4,3,2,1,0:T(8,128)(2,1)} %get-tuple-element.51) | copy-start | bytes 983044
  89.8 21.0 %copy-start.26 = (bf16[5,4,2,16,256]{4,3,2,1,0:T(8,128)(2,1)S(1)}, bf16[5,4,2,16,256]{4,3,2,1,0:T(8,128)(2,1)}, u32[]{:S(2)}) copy-start(bf16[5,4,2,16,256]{4,3,2,1,0:T(8,128)(2,1)} %get-tuple-element.49) | copy-start | bytes 983044
  110.6 11.6 %collective-permute-start.11 = (bf16[5,4,2,16,256]{4,3,2,1,0:T(8,128)(2,1)S(1)}, bf16[5,4,2,16,256]{4,3,2,1,0:T(8,128)(2,1)S(1)}, u32[]{:S(2)}, u32[]{:S(2)}) collective-permute-start(bf16[5,4,2,16,256]{4,3,2,1,0:T(8,128)(2,1)S(1)} %copy-done.27), channel_id=1, source_target_pairs={{0,24},{8,16},{16,8},{24,0},{1,25},{9,17},{17,9},{25,1},{2,26},{10... | collective-permute-start | bytes 983048 | tf_op jit(solution)/shard_map/ppermute | solution.py:370
  110.8 17.5 %collective-permute-start.9 = (bf16[5,4,2,16,256]{4,3,2,1,0:T(8,128)(2,1)S(1)}, bf16[5,4,2,16,256]{4,3,2,1,0:T(8,128)(2,1)S(1)}, u32[]{:S(2)}, u32[]{:S(2)}) collective-permute-start(bf16[5,4,2,16,256]{4,3,2,1,0:T(8,128)(2,1)S(1)} %copy-done.26), channel_id=1, source_target_pairs={{0,8},{8,0},{16,24},{24,16},{1,9},{9,1},{17,25},{25,17},{2,10},{10... | collective-permute-start | bytes 983048 | tf_op jit(solution)/shard_map/ppermute | solution.py:370
  122.2 21.4 %copy-start.7 = (bf16[5,4,2,16,256]{4,3,2,1,0:T(8,128)(2,1)}, bf16[5,4,2,16,256]{4,3,2,1,0:T(8,128)(2,1)S(1)}, u32[]{:S(2)}) copy-start(bf16[5,4,2,16,256]{4,3,2,1,0:T(8,128)(2,1)S(1)} %collective-permute-done.11.refs_7_) | copy-start | bytes 983044
  122.2 91.1 %collective-permute-start = (bf16[5,15,2,16,256]{4,3,2,1,0:T(8,128)(2,1)}, bf16[5,15,2,16,256]{4,3,2,1,0:T(8,128)(2,1)S(1)}, u32[]{:S(2)}, u32[]{:S(2)}) collective-permute-start(bf16[5,15,2,16,256]{4,3,2,1,0:T(8,128)(2,1)} %get-tuple-element.38), channel_id=1, source_target_pairs={{0,8},{8,0},{16,24},{24,16},{1,9},{9,1},{17,25},{25,17},{2,10},{10... | collective-permute-start | bytes 3686408 | tf_op jit(solution)/shard_map/ppermute | solution.py:370
  128.3 15.4 %copy-start.8 = (bf16[5,4,2,16,256]{4,3,2,1,0:T(8,128)(2,1)}, bf16[5,4,2,16,256]{4,3,2,1,0:T(8,128)(2,1)S(1)}, u32[]{:S(2)}) copy-start(bf16[5,4,2,16,256]{4,3,2,1,0:T(8,128)(2,1)S(1)} %collective-permute-done.9.refs_3_) | copy-start | bytes 983044
  128.3 86.5 %collective-permute-start.2 = (bf16[5,15,2,16,256]{4,3,2,1,0:T(8,128)(2,1)}, bf16[5,15,2,16,256]{4,3,2,1,0:T(8,128)(2,1)S(1)}, u32[]{:S(2)}, u32[]{:S(2)}) collective-permute-start(bf16[5,15,2,16,256]{4,3,2,1,0:T(8,128)(2,1)} %get-tuple-element.40), channel_id=1, source_target_pairs={{0,16},{8,24},{16,0},{24,8},{1,17},{9,25},{17,1},{25,9},{2,18},{10... | collective-permute-start | bytes 3686408 | tf_op jit(solution)/shard_map/ppermute | solution.py:370
  129.8 13.8 %copy-start.3 = (bf16[5,5,2,16,256]{4,3,2,1,0:T(8,128)(2,1)}, bf16[5,5,2,16,256]{4,3,2,1,0:T(8,128)(2,1)S(1)}, u32[]{:S(2)}) copy-start(bf16[5,5,2,16,256]{4,3,2,1,0:T(8,128)(2,1)S(1)} %collective-permute-done.12.refs_3_) | copy-start | bytes 1228804
  129.8 85.6 %collective-permute-start.4 = (bf16[5,15,2,16,256]{4,3,2,1,0:T(8,128)(2,1)}, bf16[5,15,2,16,256]{4,3,2,1,0:T(8,128)(2,1)S(1)}, u32[]{:S(2)}, u32[]{:S(2)}) collective-permute-start(bf16[5,15,2,16,256]{4,3,2,1,0:T(8,128)(2,1)} %get-tuple-element.42), channel_id=1, source_target_pairs={{0,24},{8,16},{16,8},{24,0},{1,25},{9,17},{17,9},{25,1},{2,26},{10... | collective-permute-start | bytes 3686408 | tf_op jit(solution)/shard_map/ppermute | solution.py:370
  132.3 82.4 %copy-start.29 = (bf16[5,3,2,16,256]{4,3,2,1,0:T(8,128)(2,1)S(1)}, bf16[5,3,2,16,256]{4,3,2,1,0:T(8,128)(2,1)}, u32[]{:S(2)}) copy-start(bf16[5,3,2,16,256]{4,3,2,1,0:T(8,128)(2,1)} %get-tuple-element.41) | copy-start | bytes 737284
  132.3 83.0 %copy-start.28 = (bf16[5,3,2,16,256]{4,3,2,1,0:T(8,128)(2,1)S(1)}, bf16[5,3,2,16,256]{4,3,2,1,0:T(8,128)(2,1)}, u32[]{:S(2)}) copy-start(bf16[5,3,2,16,256]{4,3,2,1,0:T(8,128)(2,1)} %get-tuple-element.43) | copy-start | bytes 737284
  143.7 76.5 %copy-start.4 = (bf16[5,5,2,16,256]{4,3,2,1,0:T(8,128)(2,1)}, bf16[5,5,2,16,256]{4,3,2,1,0:T(8,128)(2,1)S(1)}, u32[]{:S(2)}) copy-start(bf16[5,5,2,16,256]{4,3,2,1,0:T(8,128)(2,1)S(1)} %collective-permute-done.13.refs_5_) | copy-start | bytes 1228804
  143.7 39.6 %collective-permute-start.17 = (bf16[5,2,32,256]{3,2,1,0:T(8,128)(2,1)}, bf16[5,2,32,256]{3,2,1,0:T(8,128)(2,1)S(1)}, u32[]{:S(2)}, u32[]{:S(2)}) collective-permute-start(bf16[5,2,32,256]{3,2,1,0:T(8,128)(2,1)} %get-tuple-element.57), channel_id=1, source_target_pairs={{0,8},{8,0},{16,24},{24,16},{1,9},{9,1},{17,25},{25,17},{2,10},{10... | collective-permute-start | bytes 491528 | tf_op jit(solution)/shard_map/ppermute | solution.py:370
  145.6 74.6 %copy-start.5 = (bf16[5,5,2,16,256]{4,3,2,1,0:T(8,128)(2,1)}, bf16[5,5,2,16,256]{4,3,2,1,0:T(8,128)(2,1)S(1)}, u32[]{:S(2)}) copy-start(bf16[5,5,2,16,256]{4,3,2,1,0:T(8,128)(2,1)S(1)} %collective-permute-done.14.refs_7_) | copy-start | bytes 1228804
  145.6 39.3 %collective-permute-start.18 = (bf16[5,2,32,256]{3,2,1,0:T(8,128)(2,1)}, bf16[5,2,32,256]{3,2,1,0:T(8,128)(2,1)S(1)}, u32[]{:S(2)}, u32[]{:S(2)}) collective-permute-start(bf16[5,2,32,256]{3,2,1,0:T(8,128)(2,1)} %get-tuple-element.58), channel_id=1, source_target_pairs={{0,16},{8,24},{16,0},{24,8},{1,17},{9,25},{17,1},{25,9},{2,18},{10... | collective-permute-start | bytes 491528 | tf_op jit(solution)/shard_map/ppermute | solution.py:370
  183.3 33.6 %copy-start.15 = (bf16[5,2,32,256]{3,2,1,0:T(8,128)(2,1)}, bf16[5,2,32,256]{3,2,1,0:T(8,128)(2,1)S(1)}, u32[]{:S(2)}) copy-start(bf16[5,2,32,256]{3,2,1,0:T(8,128)(2,1)S(1)} %collective-permute-done.17.refs_1_) | copy-start | bytes 491524
  183.3 6.4 %collective-permute-start.19 = (bf16[5,2,32,256]{3,2,1,0:T(8,128)(2,1)}, bf16[5,2,32,256]{3,2,1,0:T(8,128)(2,1)S(1)}, u32[]{:S(2)}, u32[]{:S(2)}) collective-permute-start(bf16[5,2,32,256]{3,2,1,0:T(8,128)(2,1)} %get-tuple-element.59), channel_id=1, source_target_pairs={{0,24},{8,16},{16,8},{24,0},{1,25},{9,17},{17,9},{25,1},{2,26},{10... | collective-permute-start | bytes 491528 | tf_op jit(solution)/shard_map/ppermute | solution.py:370
  184.9 32.0 %copy-start.16 = (bf16[5,2,32,256]{3,2,1,0:T(8,128)(2,1)}, bf16[5,2,32,256]{3,2,1,0:T(8,128)(2,1)S(1)}, u32[]{:S(2)}) copy-start(bf16[5,2,32,256]{3,2,1,0:T(8,128)(2,1)S(1)} %collective-permute-done.18.refs_2_) | copy-start | bytes 491524
  184.9 6.1 %collective-permute-start.20 = (bf16[5,2,32,256]{3,2,1,0:T(8,128)(2,1)}, bf16[5,2,32,256]{3,2,1,0:T(8,128)(2,1)S(1)}, u32[]{:S(2)}, u32[]{:S(2)}) collective-permute-start(bf16[5,2,32,256]{3,2,1,0:T(8,128)(2,1)} %get-tuple-element.56.refs_0_), channel_id=1, source_target_pairs={{0,1},{1,2},{2,3},{3,4},{4,5},{5,6},{6,7},{8,9},{9,10},{10,11},{11... | collective-permute-start | bytes 491528 | tf_op jit(solution)/shard_map/ppermute | solution.py:363
  189.7 27.2 %copy-start.17 = (bf16[5,2,32,256]{3,2,1,0:T(8,128)(2,1)}, bf16[5,2,32,256]{3,2,1,0:T(8,128)(2,1)S(1)}, u32[]{:S(2)}) copy-start(bf16[5,2,32,256]{3,2,1,0:T(8,128)(2,1)S(1)} %collective-permute-done.19.refs_3_) | copy-start | bytes 491524
  189.7 4.4 %collective-permute-start.24 = (bf16[5,2,32,256]{3,2,1,0:T(8,128)(2,1)}, bf16[5,2,32,256]{3,2,1,0:T(8,128)(2,1)S(1)}, u32[]{:S(2)}, u32[]{:S(2)}) collective-permute-start(bf16[5,2,32,256]{3,2,1,0:T(8,128)(2,1)} %get-tuple-element.56.refs_0_), channel_id=1, source_target_pairs={{1,0},{2,1},{3,2},{4,3},{5,4},{6,5},{7,6},{9,8},{10,9},{11,10},{12... | collective-permute-start | bytes 491528 | tf_op jit(solution)/shard_map/ppermute | solution.py:363
  191.0 25.9 %copy-start.18 = (bf16[5,2,32,256]{3,2,1,0:T(8,128)(2,1)}, bf16[5,2,32,256]{3,2,1,0:T(8,128)(2,1)S(1)}, u32[]{:S(2)}) copy-start(bf16[5,2,32,256]{3,2,1,0:T(8,128)(2,1)S(1)} %collective-permute-done.20.refs_4_) | copy-start | bytes 491524
  191.0 7.4 %collective-permute-start.21 = (bf16[5,2,32,256]{3,2,1,0:T(8,128)(2,1)S(1)}, bf16[5,2,32,256]{3,2,1,0:T(8,128)(2,1)S(1)}, u32[]{:S(2)}, u32[]{:S(2)}) collective-permute-start(bf16[5,2,32,256]{3,2,1,0:T(8,128)(2,1)S(1)} %collective-permute-done.17.refs_1_), channel_id=1, source_target_pairs={{0,1},{1,2},{2,3},{3,4},{4,5},{5,6},{6,7},{8,9},{9,10},{10,11},{11... | collective-permute-start | bytes 491528 | tf_op jit(solution)/shard_map/ppermute | solution.py:363
  194.1 22.8 %copy-start.19 = (bf16[5,2,32,256]{3,2,1,0:T(8,128)(2,1)}, bf16[5,2,32,256]{3,2,1,0:T(8,128)(2,1)S(1)}, u32[]{:S(2)}) copy-start(bf16[5,2,32,256]{3,2,1,0:T(8,128)(2,1)S(1)} %collective-permute-done.24.refs_8_) | copy-start | bytes 491524
  194.1 6.3 %collective-permute-start.22 = (bf16[5,2,32,256]{3,2,1,0:T(8,128)(2,1)S(1)}, bf16[5,2,32,256]{3,2,1,0:T(8,128)(2,1)S(1)}, u32[]{:S(2)}, u32[]{:S(2)}) collective-permute-start(bf16[5,2,32,256]{3,2,1,0:T(8,128)(2,1)S(1)} %collective-permute-done.18.refs_2_), channel_id=1, source_target_pairs={{0,1},{1,2},{2,3},{3,4},{4,5},{5,6},{6,7},{8,9},{9,10},{10,11},{11... | collective-permute-start | bytes 491528 | tf_op jit(solution)/shard_map/ppermute | solution.py:363
  198.4 18.5 %copy-start.20 = (bf16[5,2,32,256]{3,2,1,0:T(8,128)(2,1)}, bf16[5,2,32,256]{3,2,1,0:T(8,128)(2,1)S(1)}, u32[]{:S(2)}) copy-start(bf16[5,2,32,256]{3,2,1,0:T(8,128)(2,1)S(1)} %collective-permute-done.21.refs_5_) | copy-start | bytes 491524
  198.4 3.3 %collective-permute-start.23 = (bf16[5,2,32,256]{3,2,1,0:T(8,128)(2,1)S(1)}, bf16[5,2,32,256]{3,2,1,0:T(8,128)(2,1)S(1)}, u32[]{:S(2)}, u32[]{:S(2)}) collective-permute-start(bf16[5,2,32,256]{3,2,1,0:T(8,128)(2,1)S(1)} %collective-permute-done.19.refs_3_), channel_id=1, source_target_pairs={{0,1},{1,2},{2,3},{3,4},{4,5},{5,6},{6,7},{8,9},{9,10},{10,11},{11... | collective-permute-start | bytes 491528 | tf_op jit(solution)/shard_map/ppermute | solution.py:363
  200.4 16.6 %copy-start.21 = (bf16[5,2,32,256]{3,2,1,0:T(8,128)(2,1)}, bf16[5,2,32,256]{3,2,1,0:T(8,128)(2,1)S(1)}, u32[]{:S(2)}) copy-start(bf16[5,2,32,256]{3,2,1,0:T(8,128)(2,1)S(1)} %collective-permute-done.22.refs_6_) | copy-start | bytes 491524
  200.4 4.8 %collective-permute-start.25 = (bf16[5,2,32,256]{3,2,1,0:T(8,128)(2,1)S(1)}, bf16[5,2,32,256]{3,2,1,0:T(8,128)(2,1)S(1)}, u32[]{:S(2)}, u32[]{:S(2)}) collective-permute-start(bf16[5,2,32,256]{3,2,1,0:T(8,128)(2,1)S(1)} %collective-permute-done.17.refs_1_), channel_id=1, source_target_pairs={{1,0},{2,1},{3,2},{4,3},{5,4},{6,5},{7,6},{9,8},{10,9},{11,10},{12... | collective-permute-start | bytes 491528 | tf_op jit(solution)/shard_map/ppermute | solution.py:363
  201.7 15.2 %copy-start.22 = (bf16[5,2,32,256]{3,2,1,0:T(8,128)(2,1)}, bf16[5,2,32,256]{3,2,1,0:T(8,128)(2,1)S(1)}, u32[]{:S(2)}) copy-start(bf16[5,2,32,256]{3,2,1,0:T(8,128)(2,1)S(1)} %collective-permute-done.23.refs_7_) | copy-start | bytes 491524
  201.7 5.6 %collective-permute-start.26 = (bf16[5,2,32,256]{3,2,1,0:T(8,128)(2,1)S(1)}, bf16[5,2,32,256]{3,2,1,0:T(8,128)(2,1)S(1)}, u32[]{:S(2)}, u32[]{:S(2)}) collective-permute-start(bf16[5,2,32,256]{3,2,1,0:T(8,128)(2,1)S(1)} %collective-permute-done.18.refs_2_), channel_id=1, source_target_pairs={{1,0},{2,1},{3,2},{4,3},{5,4},{6,5},{7,6},{9,8},{10,9},{11,10},{12... | collective-permute-start | bytes 491528 | tf_op jit(solution)/shard_map/ppermute | solution.py:363
  205.1 11.8 %copy-start.23 = (bf16[5,2,32,256]{3,2,1,0:T(8,128)(2,1)}, bf16[5,2,32,256]{3,2,1,0:T(8,128)(2,1)S(1)}, u32[]{:S(2)}) copy-start(bf16[5,2,32,256]{3,2,1,0:T(8,128)(2,1)S(1)} %collective-permute-done.25.refs_9_) | copy-start | bytes 491524
  205.2 6.6 %collective-permute-start.27 = (bf16[5,2,32,256]{3,2,1,0:T(8,128)(2,1)S(1)}, bf16[5,2,32,256]{3,2,1,0:T(8,128)(2,1)S(1)}, u32[]{:S(2)}, u32[]{:S(2)}) collective-permute-start(bf16[5,2,32,256]{3,2,1,0:T(8,128)(2,1)S(1)} %collective-permute-done.19.refs_3_), channel_id=1, source_target_pairs={{1,0},{2,1},{3,2},{4,3},{5,4},{6,5},{7,6},{9,8},{10,9},{11,10},{12... | collective-permute-start | bytes 491528 | tf_op jit(solution)/shard_map/ppermute | solution.py:363
  207.4 9.6 %copy-start.24 = (bf16[5,2,32,256]{3,2,1,0:T(8,128)(2,1)}, bf16[5,2,32,256]{3,2,1,0:T(8,128)(2,1)S(1)}, u32[]{:S(2)}) copy-start(bf16[5,2,32,256]{3,2,1,0:T(8,128)(2,1)S(1)} %collective-permute-done.26.refs_10_) | copy-start | bytes 491524
  207.4 25.2 %collective-permute-start.7 = (bf16[5,3,2,16,256]{4,3,2,1,0:T(8,128)(2,1)}, bf16[5,3,2,16,256]{4,3,2,1,0:T(8,128)(2,1)S(1)}, u32[]{:S(2)}, u32[]{:S(2)}) collective-permute-start(bf16[5,3,2,16,256]{4,3,2,1,0:T(8,128)(2,1)} %get-tuple-element.46), channel_id=1, source_target_pairs={{0,16},{8,24},{16,0},{24,8},{1,17},{9,25},{17,1},{25,9},{2,18},{10... | collective-permute-start | bytes 737288 | tf_op jit(solution)/shard_map/ppermute | solution.py:370
  211.8 20.8 %collective-permute-start.8 = (bf16[5,3,2,16,256]{4,3,2,1,0:T(8,128)(2,1)}, bf16[5,3,2,16,256]{4,3,2,1,0:T(8,128)(2,1)S(1)}, u32[]{:S(2)}, u32[]{:S(2)}) collective-permute-start(bf16[5,3,2,16,256]{4,3,2,1,0:T(8,128)(2,1)} %get-tuple-element.47), channel_id=1, source_target_pairs={{0,24},{8,16},{16,8},{24,0},{1,25},{9,17},{17,9},{25,1},{2,26},{10... | collective-permute-start | bytes 737288 | tf_op jit(solution)/shard_map/ppermute | solution.py:370
  213.3 6.9 %copy-start = (bf16[5,15,2,16,256]{4,3,2,1,0:T(8,128)(2,1)}, bf16[5,15,2,16,256]{4,3,2,1,0:T(8,128)(2,1)S(1)}, u32[]{:S(2)}) copy-start(bf16[5,15,2,16,256]{4,3,2,1,0:T(8,128)(2,1)S(1)} %collective-permute-done.refs_2_) | copy-start | bytes 3686404
  213.3 25.0 %collective-permute-start.1 = (bf16[5,3,2,16,256]{4,3,2,1,0:T(8,128)(2,1)}, bf16[5,3,2,16,256]{4,3,2,1,0:T(8,128)(2,1)S(1)}, u32[]{:S(2)}, u32[]{:S(2)}) collective-permute-start(bf16[5,3,2,16,256]{4,3,2,1,0:T(8,128)(2,1)} %get-tuple-element.39), channel_id=1, source_target_pairs={{0,8},{8,0},{16,24},{24,16},{1,9},{9,1},{17,25},{25,17},{2,10},{10... | collective-permute-start | bytes 737288 | tf_op jit(solution)/shard_map/ppermute | solution.py:370
  214.8 23.5 %collective-permute-start.3 = (bf16[5,3,2,16,256]{4,3,2,1,0:T(8,128)(2,1)S(1)}, bf16[5,3,2,16,256]{4,3,2,1,0:T(8,128)(2,1)S(1)}, u32[]{:S(2)}, u32[]{:S(2)}) collective-permute-start(bf16[5,3,2,16,256]{4,3,2,1,0:T(8,128)(2,1)S(1)} %copy-done.29), channel_id=1, source_target_pairs={{0,16},{8,24},{16,0},{24,8},{1,17},{9,25},{17,1},{25,9},{2,18},{10... | collective-permute-start | bytes 737288 | tf_op jit(solution)/shard_map/ppermute | solution.py:370
  215.4 23.0 %collective-permute-start.5 = (bf16[5,3,2,16,256]{4,3,2,1,0:T(8,128)(2,1)S(1)}, bf16[5,3,2,16,256]{4,3,2,1,0:T(8,128)(2,1)S(1)}, u32[]{:S(2)}, u32[]{:S(2)}) collective-permute-start(bf16[5,3,2,16,256]{4,3,2,1,0:T(8,128)(2,1)S(1)} %copy-done.28), channel_id=1, source_target_pairs={{0,24},{8,16},{16,8},{24,0},{1,25},{9,17},{17,9},{25,1},{2,26},{10... | collective-permute-start | bytes 737288 | tf_op jit(solution)/shard_map/ppermute | solution.py:370
  (10 other events, 28.9 us)

commit v2 on v0

v2 whole, which is shorter than its diff:
```python
import functools

import jax
import jax.numpy as jnp
from jax import lax
from jax.experimental import pallas as pl
from jax.experimental.pallas import tpu as pltpu
from jax.sharding import PartitionSpec as P

HALO = 8
SIDE = 16
PIX = SIDE * SIDE
LANES = 128
SUB = 8
DBLK = 16
EPS = 1e-06
VMEM = 56 * 1024 * 1024
COST = pl.CostEstimate(flops=1, bytes_accessed=1, transcendentals=0)

bf16 = jnp.bfloat16
f32 = jnp.float32


def params():
    return pltpu.CompilerParams(vmem_limit_bytes=VMEM)


def gather_groups(rows):
    group = lax.broadcasted_iota(jnp.int32, rows[0].shape, 1) // SIDE
    turned = [rows[0]] + [pltpu.roll(rows[r], SIDE * r, 1) for r in range(1, 8)]
    held = [turned[-i % 8] for i in range(8)]
    for step in (1, 2, 4):
        low = (group & step) == 0
        held = [jnp.where(low, held[i], held[(i - step) % 8]) for i in range(8)]
    return held


def interior_kernel(spans, dest_rows, part, per_step, me_ref, slc_any, rk_any, ak_any, *refs):
    own_ref, first_ref, last_ref, *refs = refs
    *refs, slc_ref, rk_ref, ak_ref, turned, plane, ranged, in_sems, out_sems = refs
    outs, stage = refs[: len(refs) - len(spans)], refs[len(refs) - len(spans) :]
    steps = DBLK // per_step
    n_rows, n_az = slc_ref.shape[2:]
    lines = 2 * DBLK
    partners = len(outs) // len(spans)
    row_blocks = outs[0].shape[0]
    halves = plane.shape[0]

    def fetch(step):
        here = pl.ds(step * per_step, per_step)
        there = pl.ds(part * DBLK + step * per_step, per_step)
        return [
            pltpu.make_async_copy(rk_any.at[there], rk_ref.at[here], in_sems.at[step, 0]),
            pltpu.make_async_copy(slc_any.at[0, there], slc_ref.at[0, here], in_sems.at[step, 1]),
            pltpu.make_async_copy(slc_any.at[1, there], slc_ref.at[1, here], in_sems.at[step, 2]),
            pltpu.make_async_copy(ak_any.at[there], ak_ref.at[here], in_sems.at[step, 3]),
        ]

    def start(step, carry):
        for copy in fetch(step):
            copy.start()
        return carry

    def wait(step):
        for copy in fetch(step):
            copy.wait()

    def along_range(step):
        for n in range(per_step):
            i = step * per_step + n
            for c in range(2):
                value = jnp.dot(rk_ref[i], slc_ref[c, i], preferred_element_type=f32)
                ranged[i, c * n_rows : (c + 1) * n_rows, :] = value.astype(bf16)

    def prepare(step):
        for n in range(per_step):
            i = step * per_step + n
            kernel = ak_ref[i].astype(f32)[HALO : HALO + n_rows]
            turned[i] = pltpu.roll(kernel, HALO, 1).astype(bf16)

    def along_azimuth(step):
        for n in range(per_step):
            i = step * per_step + n
            moved = jnp.dot(ranged[i], turned[i], preferred_element_type=f32)
            for c in range(2):
                line = SUB * lines + c * DBLK + i
                for h in range(halves):
                    plane[h, pl.ds(line, n_rows, stride=lines), :] = moved[
                        c * n_rows : (c + 1) * n_rows, h * LANES : (h + 1) * LANES
                    ]

    lax.fori_loop(0, steps, start, 0)
    zero = jnp.zeros((SUB * lines, LANES), f32)
    for h in range(halves):
        plane[h, : SUB * lines, :] = zero
        plane[h, (SUB + n_rows) * lines :, :] = zero
    wait(0)
    along_range(0)
    prepare(0)

    def resample(step, carry):
        later = jnp.minimum(step + 1, steps - 1)
        pl.when(step + 1 < steps)(lambda: wait(later))
        along_azimuth(step)
        along_range(later)
        prepare(later)
        return carry

    lax.fori_loop(0, steps, resample, 0)

    me = me_ref[0]
    copies = [
        pltpu.make_async_copy(stage[n // partners].at[n % partners], outs[n], out_sems.at[n]) for n in range(len(outs))
    ]

    for k in [*range(1, partners), 0]:
        base = (me ^ k) * dest_rows

        def blocks(j, carry):
            for half in range(2):
                for h in range(halves):
                    rows = []
                    for r in range(8):
                        at = pl.multiple_of((base + j * SIDE + half * 8 + r) * lines, lines)
                        rows.append(plane[h, pl.ds(at, lines), :].astype(bf16))
                    cols = gather_groups(rows)
                    for g in range(8):
                        column = h * 8 + g
                        for s, (lo, hi) in enumerate(spans):
                            if lo <= column < hi:
                                for c in range(2):
                                    stage[s][k, j, column - lo, c, :, half * LANES : (half + 1) * LANES] = cols[g][
                                        c * DBLK : (c + 1) * DBLK
                                    ]
            return carry

        lax.fori_loop(0, row_blocks, blocks, 0)
        for s in range(len(spans)):
            copies[s * partners + k].start()

    pick_row = lax.broadcasted_iota(jnp.int32, (2 * SIDE, n_az), 0)
    pick_col = lax.broadcasted_iota(jnp.int32, (2 * SIDE, n_az), 1)
    pick = (pick_col == jnp.where(pick_row < SIDE, pick_row, pick_row + n_az - 2 * SIDE)).astype(f32).astype(bf16)

    def edges(step, carry):
        for n in range(4):
            i = step * 4 + n
            both = lax.dot_general(pick, ranged[i], (((1,), (1,)), ((), ())), preferred_element_type=f32)
            parts = [both[:, c * n_rows : (c + 1) * n_rows] for c in range(2)]
            for c in range(2):
                own_ref[i, c] = parts[c].astype(bf16)
            first_ref[i] = jnp.concatenate([p[:SUB] for p in parts], axis=0).astype(bf16)
            last_ref[i] = jnp.concatenate([p[2 * SIDE - SUB :] for p in parts], axis=0).astype(bf16)
        return carry

    lax.fori_loop(0, DBLK // 4, edges, 0)
    for copy in copies:
        copy.wait()


def interior(me, slc, rk, ak, part, spans, partners):
    n_rows, n_az = slc.shape[2], slc.shape[3]
    dest_rows = n_rows // partners
    row_blocks = dest_rows // SIDE + 1
    per_step = 2
    steps = DBLK // per_step
    shapes = [
        jax.ShapeDtypeStruct((row_blocks, hi - lo, 2, DBLK, PIX), bf16)
        for lo, hi in spans
        for _ in range(partners)
    ]
    edge_shapes = [
        jax.ShapeDtypeStruct((DBLK, 2, 2 * SIDE, n_rows), bf16),
        jax.ShapeDtypeStruct((DBLK, 2 * SUB, n_rows), bf16),
        jax.ShapeDtypeStruct((DBLK, 2 * SUB, n_rows), bf16),
    ]
    whole = pl.BlockSpec(memory_space=pltpu.VMEM)
    anywhere = pl.BlockSpec(memory_space=pl.ANY)
    own, first, last, *flat = pl.pallas_call(
        functools.partial(interior_kernel, spans, dest_rows, part, per_step),
        in_specs=[pl.BlockSpec(memory_space=pltpu.SMEM)] + [anywhere] * 3,
        out_specs=[whole] * 3 + [anywhere] * len(shapes),
        out_shape=edge_shapes + shapes,
        scratch_shapes=[pltpu.VMEM((partners, *x.shape), bf16) for x in shapes[::partners]]
        + [
            pltpu.VMEM((2, DBLK, n_rows, n_az), bf16),
            pltpu.VMEM((DBLK, n_rows, n_rows), bf16),
            pltpu.VMEM((DBLK, *ak.shape[1:]), bf16),
            pltpu.VMEM((DBLK, n_rows, n_az), bf16),
            pltpu.VMEM((n_az // LANES, (n_rows + 2 * SUB) * 2 * DBLK, LANES), f32),
            pltpu.VMEM((DBLK, 2 * n_rows, n_az), bf16),
            pltpu.SemaphoreType.DMA((steps, 4)),
            pltpu.SemaphoreType.DMA((len(shapes),)),
        ],
        compiler_params=params(),
        cost_estimate=COST,
        name=f"interior_{part}",
    )(me, slc, rk, ak)
    return own, first, last, [flat[s * partners : (s + 1) * partners] for s in range(len(spans))]


def rim_kernel(dest_rows, parts, me_ref, *refs):
    operands, outs, plane = refs[: 4 * parts], refs[4 * parts : -1], refs[-1]
    step, steps = pl.program_id(0), pl.num_programs(0)
    per_step, n_az = operands[0].shape[0], operands[3].shape[2]
    n_rows = operands[0].shape[3]
    n_dates = outs[0].shape[2]
    lines = 2 * n_dates
    row_blocks = outs[0].shape[0]
    eighths = n_rows // 8

    @pl.when(step == 0)
    def _():
        zero = jnp.zeros((lines, LANES), f32)
        plane[:lines, :] = zero
        plane[(eighths + 1) * lines :, :] = zero

    row = lax.broadcasted_iota(jnp.int32, (n_rows, LANES), 0)
    lane = lax.broadcasted_iota(jnp.int32, (n_rows, LANES), 1)
    own = (row % 8) == lane // SIDE
    gather = (
        lax.broadcasted_iota(jnp.int32, (eighths, n_rows), 1) // 8
        == lax.broadcasted_iota(jnp.int32, (eighths, n_rows), 0)
    ).astype(f32).astype(bf16)
    pick_row = lax.broadcasted_iota(jnp.int32, (n_az, LANES), 0)
    pick_col = lax.broadcasted_iota(jnp.int32, (n_az, LANES), 1) % SIDE
    pick = (pick_row == jnp.where(pick_col < 8, pick_col + n_az - 8, pick_col - 8)).astype(f32).astype(bf16)
    zero = jnp.zeros((SUB, LANES), f32)
    items = [(p, i) for p in range(parts) for i in range(per_step)]
    weights = [jnp.dot(operands[4 * p + 3][i], pick, preferred_element_type=f32) for p, i in items]
    moved = []
    for (p, i), w in zip(items, weights):
        edge, left, right, _ = operands[4 * p : 4 * p + 4]
        for c in range(2):
            ends = [
                jnp.concatenate([x, zero] if c == 0 else [zero, x], axis=0)
                for x in (w[:SUB], w[n_az + SUB :])
            ]
            weight = jnp.concatenate([w[SUB : 3 * SUB], w[n_az - SUB : n_az + SUB], *ends], axis=0).astype(bf16)
            value = jnp.concatenate([edge[i, c], left[i], right[i]], axis=0)
            moved.append(lax.dot_general(value, weight, (((0,), (0,)), ((), ())), preferred_element_type=f32))
    moved = [jnp.where(own, x, 0.0).astype(bf16) for x in moved]
    packed = [jnp.dot(gather, x, preferred_element_type=f32) for x in moved]
    for n, (p, i) in enumerate(items):
        for c in range(2):
            line = lines + c * n_dates + p * DBLK + step * per_step + i
            plane[pl.ds(line, eighths, stride=lines), :] = packed[2 * n + c]

    @pl.when(step == steps - 1)
    def _():
        me = me_ref[0]
        for k in range(len(outs)):
            base = (me ^ k) * (dest_rows // 8)
            for j in range(row_blocks):
                for half in range(2):
                    start = pl.multiple_of((base + 2 * j + half) * lines, lines)
                    values = plane[pl.ds(start, lines), :].astype(bf16)
                    for c in range(2):
                        outs[k][j, c, :, half * LANES : (half + 1) * LANES] = values[
                            c * n_dates : (c + 1) * n_dates
                        ]


def rim(me, own, left, right, ak, partners):
    parts = len(own)
    n_rows = own[0].shape[3]
    n_dates = parts * DBLK
    dest_rows = n_rows // partners
    row_blocks = dest_rows // SIDE + 1
    per_step = 2
    steps = DBLK // per_step
    shape = jax.ShapeDtypeStruct((row_blocks, 2, n_dates, PIX), bf16)

    def ak_spec(p):
        return pl.BlockSpec((per_step, *ak.shape[1:]), lambda t, m: (p * steps + t, 0, 0))

    in_specs, operands = [], []
    for p in range(parts):
        in_specs += [
            pl.BlockSpec((per_step, 2, 2 * SIDE, n_rows), lambda t, m: (t, 0, 0, 0)),
            pl.BlockSpec((per_step, 2 * SUB, n_rows), lambda t, m: (t, 0, 0)),
            pl.BlockSpec((per_step, 2 * SUB, n_rows), lambda t, m: (t, 0, 0)),
            ak_spec(p),
        ]
        operands += [own[p], left[p], right[p], ak]
    grid = pltpu.PrefetchScalarGridSpec(
        num_scalar_prefetch=1,
        grid=(steps,),
        in_specs=in_specs,
        out_specs=[pl.BlockSpec(shape.shape, lambda t, m: (0, 0, 0, 0))] * partners,
        scratch_shapes=[pltpu.VMEM(((n_rows // 8 + 2) * 2 * n_dates, LANES), f32)],
    )
    return pl.pallas_call(
        functools.partial(rim_kernel, dest_rows, parts),
        grid_spec=grid,
        out_shape=[shape] * partners,
        compiler_params=params(),
        cost_estimate=COST,
        name="rim",
    )(me, *operands)


def block_moment(pixels):
    n = pixels.shape[0] // 2
    m = lax.dot_general(pixels, pixels, (((1,), (1,)), ((), ())), preferred_element_type=f32)
    return m[:n, :n] + m[n:, n:], m[n:, :n] - m[:n, n:]


def store_coherence(out, index, real, imag):
    n = real.shape[0]
    eye = lax.broadcasted_iota(jnp.int32, (n, n), 0) == lax.broadcasted_iota(jnp.int32, (n, n), 1)
    diagonal = jnp.where(eye, real, 0.0)
    column = lax.rsqrt(jnp.sum(diagonal, axis=1, keepdims=True) + EPS)
    row = lax.rsqrt(jnp.sum(diagonal, axis=0, keepdims=True) + EPS)
    scale = column * row
    out[(*index, 0)] = real * scale
    out[(*index, 1)] = imag * scale


def column_sums(read, scratch, row_blocks, emit):
    before = None
    for j in range(row_blocks):
        read(j, scratch.at[j])
        now = block_moment(scratch[j])
        if before is not None:
            emit(j - 1, before[0] + now[0], before[1] + now[1])
        before = now


def rim_gram_kernel(me_ref, own, before, after, state, result_in, result, out, window, pixels, sem):
    del result_in
    partners, row_blocks, _, n, _ = own.shape
    me = me_ref[0]
    total = n * partners
    lane = lax.broadcasted_iota(jnp.int32, (n, PIX), 1)
    copy = pltpu.make_async_copy(window, result.at[:, 0], sem)
    for end in range(2):

        def read(j, scratch):
            for k in range(partners):
                for c in range(2):
                    left, right = (before, own) if end == 0 else (own, after)
                    value = jnp.where(lane % SIDE < 8, left[k, j, c], right[k, j, c])
                    at = pl.multiple_of(c * total + (me ^ k) * n, SIDE)
                    scratch[pl.ds(at, n), :] = value

        def emit(u, real, imag):
            if end == 0:
                store_coherence(window, (u,), state[u, 0] + real, state[u, 1] + imag)
            else:
                out[u, 0] = real
                out[u, 1] = imag

        column_sums(read, pixels.at[end], row_blocks, emit)
        if end == 0:
            copy.start()
    copy.wait()


def rim_gram(me, own, before, after, state, result):
    partners, row_blocks, _, n, _ = own.shape
    total = n * partners
    whole = pl.BlockSpec(memory_space=pltpu.VMEM)
    anywhere = pl.BlockSpec(memory_space=pl.ANY)
    return pl.pallas_call(
        rim_gram_kernel,
        in_specs=[pl.BlockSpec(memory_space=pltpu.SMEM)] + [whole] * 4 + [anywhere],
        out_specs=[anywhere, whole],
        out_shape=[
            jax.ShapeDtypeStruct(result.shape, f32),
            jax.ShapeDtypeStruct(state.shape, f32),
        ],
        input_output_aliases={5: 0},
        scratch_shapes=[
            pltpu.VMEM(state.shape, f32),
            pltpu.VMEM((2, row_blocks, 2 * total, PIX), bf16),
            pltpu.SemaphoreType.DMA,
        ],
        compiler_params=params(),
        cost_estimate=COST,
        name="rim_gram",
    )(me, own, before, after, state, result)


def gram_kernel(partners, parts, offsets, columns, first, opening, closing, *refs):
    pieces, refs = refs[: partners * parts], refs[partners * parts :]
    if not opening:
        state, end, _, *refs = refs
    result, *refs = refs
    if opening:
        first_out, *refs = refs
    state_out, held, kept, *blocks, stage, pixels, in_sems, out_sems, state_sems = refs
    row_blocks = pieces[0].shape[0]
    me = lax.axis_index("date").astype(jnp.int32)
    total = pixels.shape[1] // 2

    def fetch(column):
        return [
            pltpu.make_async_copy(
                pieces[n].at[:, offsets[n % parts] + column], blocks[n].at[column], in_sems.at[column, n]
            )
            for n in range(partners * parts)
        ]

    def write(window):
        return pltpu.make_async_copy(stage.at[window], result.at[:, first - 1 + window], out_sems.at[window])

    def start(column, carry):
        for copy in fetch(column):
            copy.start()
        return carry

    if not opening:
        state_in = pltpu.make_async_copy(state, held, state_sems.at[0])
        state_in.start()
    lax.fori_loop(0, columns, start, 0)
    if closing:
        end_in = pltpu.make_async_copy(end, kept, state_sems.at[1])
        end_in.start()
    if opening:
        first_copy = pltpu.make_async_copy(kept, first_out, state_sems.at[1])
    else:
        state_in.wait()

    def work(column, carry):
        for copy in fetch(column):
            copy.wait()

        def read(j, scratch):
            for k in range(partners):
                for p in range(parts):
                    for c in range(2):
                        at = pl.multiple_of(c * total + (me ^ k) * (parts * DBLK) + p * DBLK, DBLK)
                        scratch[pl.ds(at, DBLK), :] = blocks[k * parts + p][column, j, c]

        def emit(u, real, imag):
            store_coherence(stage.at[column], (u,), held[u, 0] + real, held[u, 1] + imag)
            held[u, 0] = real
            held[u, 1] = imag

        column_sums(read, pixels, row_blocks, emit)
        if opening:

            @pl.when(column == 0)
            def _():
                kept[...] = held[...]
                first_copy.start()

            pl.when(column > 0)(write(column).start)
        else:
            write(column).start()
        return carry

    lax.fori_loop(0, columns, work, 0)
    if closing:
        end_in.wait()
        for u in range(row_blocks - 1):
            store_coherence(stage.at[columns], (u,), held[u, 0] + kept[u, 0], held[u, 1] + kept[u, 1])
        write(columns).start()
    else:
        state_copy = pltpu.make_async_copy(held, state_out, state_sems.at[0])
        state_copy.start()
    for window in range(1 if opening else 0, columns + (1 if closing else 0)):
        write(window).wait()
    if opening:
        first_copy.wait()
    if not closing:
        state_copy.wait()


def gram(pieces, offsets, columns, first, state, end, result, out_shape, closing):
    partners, parts = len(pieces), len(pieces[0])
    row_blocks = pieces[0][0].shape[0]
    total = out_shape.shape[-1]
    opening = state is None
    sums = jax.ShapeDtypeStruct((row_blocks - 1, 2, total, total), f32)
    anywhere = pl.BlockSpec(memory_space=pl.ANY)
    operands = [x for k in pieces for x in k]
    aliases = {}
    if not opening:
        aliases = {len(operands) + 2: 0}
        operands += [state, end, result]
    n_out = 2 if opening else 1
    return pl.pallas_call(
        functools.partial(gram_kernel, partners, parts, offsets, columns, first, opening, closing),
        in_specs=[anywhere] * len(operands),
        out_specs=[anywhere] * (1 + n_out),
        out_shape=[out_shape] + [sums] * n_out,
        input_output_aliases=aliases,
        scratch_shapes=[pltpu.VMEM(sums.shape, f32)] * 2
        + [pltpu.VMEM((columns, row_blocks, 2, DBLK, PIX), bf16)] * (partners * parts)
        + [
            pltpu.VMEM((columns + (1 if closing else 0), *sums.shape), f32),
            pltpu.VMEM((row_blocks, 2 * total, PIX), bf16),
            pltpu.SemaphoreType.DMA((columns, partners * parts)),
            pltpu.SemaphoreType.DMA((columns + 1,)),
            pltpu.SemaphoreType.DMA((2,)),
        ],
        compiler_params=params(),
        cost_estimate=COST,
        name=f"gram_{first}",
    )(*operands)


def shift(value, axis, by):
    n = lax.axis_size(axis)
    pairs = [(i, i + by) for i in range(n) if 0 <= i + by < n]
    return lax.ppermute(value, axis, pairs)


def exchange(blocks, ahead=None, gates=()):
    n = lax.axis_size("date")
    got = [blocks[0]]
    for k in range(1, n):
        block = blocks[k]
        if ahead is not None:
            block = after(block, ahead[k])
        if k == n - 1 and gates:
            block = after(block, *gates)
        got.append(lax.ppermute(block, "date", [(i, i ^ k) for i in range(n)]))
    return got


def after(value, *others):
    return lax.optimization_barrier((value, *others))[0]


def on_device(slc, range_kernel, azimuth_kernel):
    partners = lax.axis_size("date")
    n_dates, n_rows, n_az = slc.shape[1:]
    total = n_dates * partners
    columns = n_az // SIDE
    me = lax.axis_index("date").astype(jnp.int32).reshape(1)
    parts = n_dates // DBLK
    bounds = [1, 7, 12, columns]
    spans = list(zip(bounds[:-1], bounds[1:]))

    dest_windows = n_rows // partners // SIDE
    out_shape = jax.ShapeDtypeStruct((dest_windows, columns, 2, total, total), f32)

    own, left, right, sent = [], [], [], []
    turn = me
    for part in range(parts):
        part_spans = spans if part == parts - 1 else [(1, columns)]
        edge, first, last, out = interior(turn, slc, range_kernel, azimuth_kernel, part, part_spans, partners)
        turn = after(me, first)
        own.append(edge)
        left.append(shift(last, "strip", 1))
        right.append(shift(first, "strip", -1))
        sent.append(out)
    early = [exchange(s[0]) for s in sent[:-1]]
    rims = jnp.stack(exchange(rim(me, own, left, right, azimuth_kernel, partners)))
    above, below = shift(rims, "strip", 1), shift(rims, "strip", -1)

    def column_gram(s, state, end, result):
        lo, hi = spans[s]
        pieces = [[e[k] for e in early] + [late[s][k]] for k in range(partners)]
        offsets = [lo - 1] * (parts - 1) + [0]
        closing = s == len(spans) - 1
        return gram(pieces, offsets, hi - lo, lo, state, end, result, out_shape, closing)

    late = [exchange(sent[-1][0], early[-1] if early else None)]
    late.append(exchange(sent[-1][1], late[0]))
    result, opening, state = column_gram(0, None, None, None)
    result, end = rim_gram(me, rims, above, below, opening, result)
    for s in range(1, len(spans) - 1):
        result, state = column_gram(s, state, end, result)
        late.append(exchange(sent[-1][s + 1], late[s], gates=(state,)))
    result, state = column_gram(len(spans) - 1, state, end, result)
    return result


def solution(mesh):
    in_specs = (P(None, "date", None, "strip"), P("date", None, None), P("date", None, "strip"))
    out_specs = P("date", "strip", None, None, None)
    return jax.shard_map(on_device, mesh=mesh, in_specs=in_specs, out_specs=out_specs, check_vma=False)
```

time: 453 us -> 143 us (0.32); the launches traced: 446 us -> 143 us
  local copies, waits for them, and re-layouts: 155 us -> 3.04 us
  blocking collectives: 93.8 us -> 0 us
  matrix products: 87.4 us -> 0 us
  Pallas kernels: 0 us -> 59.8 us
  other arithmetic: 42.8 us -> 1 us
  starting transfers between devices: 14.2 us -> 34.9 us
  waiting for transfers between devices: 52.6 us -> 43.5 us
    all_to_all x1 -> x0, blocking collectives: 93.8 us -> none  [on_device(): lax.all_to_all(shifted, 'date', split_axis=2, concat_axis=1, tiled=True)]
    dot_general x6 -> x0, matrix products: 87.4 us -> none  [the longest x4 72 us: block_gram(): jnp.einsum('uvip,uvjp->uvij', pixels, pixels, preferred_element_type=jnp....]
    pallas_call x0 -> x7, Pallas kernels: none -> 59.8 us  [the longest x2 31.3 us: interior(): pl.pallas_call(functools.partial(interior_kernel, spans, dest_rows, part,...]
    concatenate x3 -> x0, other arithmetic: 27.9 us -> none  [the longest x2 27.4 us: with_halo(): value = jnp.concatenate([before, value, after], axis=dim)]
    concatenate x1 -> x0, local copies, waits for them, and re-layouts: 26.8 us -> none  [with_halo(): value = jnp.concatenate([before, value, after], axis=dim)]
    reshape x1 -> x0, local copies, waits for them, and re-layouts: 24.6 us -> none  [on_device(): pixel_grid.reshape(2 * date_count, range_blocks, half_window, az_blocks,...]
    slice x5 -> x0, local copies, waits for them, and re-layouts: 21.3 us -> none  [the longest x4 16.8 us: with_halo(): last = lax.slice_in_dim(value, length - width, length, axis=dim)]
    ppermute x6 -> x21, starting transfers between devices: 14.2 us -> 34.9 us  [the longest x15 21.4 us: exchange(): got.append(lax.ppermute(block, 'date', [(i, i ^ k) for i in range(n)]))]
  transfers between devices with their start and end apart: 6 -> 21, of which waited for: 4 -> 10; matrix products, arithmetic and copies ran while one was open for 2% -> 1% of each run, Pallas kernels for 0% -> 28%
where the time goes in v2:
time: 143 us
  Pallas kernels  59.8 us (42%)
  waiting for transfers between devices  43.5 us (30%)
  starting transfers between devices  34.9 us (24%)
  local copies, waits for them, and re-layouts  3.04 us (2%)
    ppermute x15, waiting for transfers between devices, exchange(): got.append(lax.ppermute(block, 'date', [(i, i ^ k) for i in range(n)]))  40.1 us
    pallas_call x2, Pallas kernels, interior(): pl.pallas_call(functools.partial(interior_kernel, spans, dest_rows, part,...  31.3 us
    ppermute x15, starting transfers between devices, exchange(): got.append(lax.ppermute(block, 'date', [(i, i ^ k) for i in range(n)]))  21.4 us
    pallas_call x3, Pallas kernels, gram(): pl.pallas_call(functools.partial(gram_kernel, partners, parts, offsets, c...  15.3 us
    ppermute x6, starting transfers between devices, shift(): return lax.ppermute(value, axis, pairs)  13.5 us
    pallas_call x1, Pallas kernels, rim(): pl.pallas_call(functools.partial(rim_kernel, dest_rows, parts), grid_spec...  9.37 us
    pallas_call x1, Pallas kernels, rim_gram(): pl.pallas_call(rim_gram_kernel, in_specs=[pl.BlockSpec(memory_space=pltpu...  3.88 us
    ppermute x6, waiting for transfers between devices, shift(): return lax.ppermute(value, axis, pairs)  3.37 us
  transfers between devices with their start and end apart: 21, of which 10 were waited for; matrix products, arithmetic and copies ran while one was open for 1% of the time, Pallas kernels for 28%

profile of v2, /device:TPU:0, one launch (start us, length us, event | category | flops | bytes accessed | tf_op | source)
XLA Modules:
  0.0 142.5 jit_solution(11772015812013126046)
XLA Ops:
  0.0 15.6 %interior_0.1 = (bf16[16,2,32,256]{3,2,1,0:T(8,128)(2,1)}, bf16[16,16,256]{2,1,0:T(8,128)(2,1)}, bf16[16,16,256]{2,1,0:T(8,128)(2,1)}, bf16[5,15,2,16,256]{4,3,2...) custom-call(s32[1]{0:T(128)} %bitcast.me_ref, ...), custom_call_target="tpu_custom_call" | custom-call | flops 1 | bytes 1 | tf_op jit(solution)/shard_map/interior_0/pallas_call | solution.py:179
  15.6 4.0 %collective-permute-start.8 = (bf16[5,15,2,16,256]{4,3,2,1,0:T(8,128)(2,1)}, bf16[5,15,2,16,256]{4,3,2,1,0:T(8,128)(2,1)S(1)}, u32[]{:S(2)}, u32[]{:S(2)}) collective-permute-start(bf16[5,15,2,16,256]{4,3,2,1,0:T(8,128)(2,1)} %get-tuple-element.68), channel_id=1, source_target_pairs={{0,24},{8,16},{16,8},{24,0},{1,25},{9,17},{17,9},{25,1},{2,26},{10... | collective-permute-start | bytes 3686408 | tf_op jit(solution)/shard_map/ppermute | solution.py:520
  19.6 0.5 collective-permute-start.4
  20.1 0.1 collective-permute-start
  20.2 1.3 collective-permute-start.11
  21.5 1.3 collective-permute-start.12
  22.8 15.7 %interior_1.1 = (bf16[16,2,32,256]{3,2,1,0:T(8,128)(2,1)}, bf16[16,16,256]{2,1,0:T(8,128)(2,1)}, bf16[16,16,256]{2,1,0:T(8,128)(2,1)}, bf16[5,6,2,16,256]{4,3,2,...) custom-call(s32[1]{0:T(128)} %bitcast.me_ref, ...), custom_call_target="tpu_custom_call" | custom-call | flops 1 | bytes 1 | tf_op jit(solution)/shard_map/interior_1/pallas_call | solution.py:179
  38.5 0.0 collective-permute-done.11.refs_1_
  38.5 5.2 %collective-permute-start.13 = (bf16[16,16,256]{2,1,0:T(8,128)(2,1)}, bf16[16,16,256]{2,1,0:T(8,128)(2,1)S(1)}, u32[]{:S(2)}, u32[]{:S(2)}) collective-permute-start(bf16[16,16,256]{2,1,0:T(8,128)(2,1)} %get-tuple-element.81), channel_id=1, source_target_pairs={{0,1},{1,2},{2,3},{3,4},{4,5},{5,6},{6,7},{8,9},{9,10},{10,11},{11... | collective-permute-start | bytes 393224 | tf_op jit(solution)/shard_map/ppermute | solution.py:508
  43.8 1.3 collective-permute-start.14
  45.1 0.0 collective-permute-done.13.refs_5_
  45.1 3.4 %collective-permute-done.14.refs_6_ = bf16[16,16,256]{2,1,0:T(8,128)(2,1)S(1)} collective-permute-done((bf16[16,16,256]{2,1,0:T(8,128)(2,1)}, bf16[16,16,256]{2,1,0:T(8,128)(2,1)S(1)}, u32[]{:S(2)}, u32[]{:S(2)}) %collective-permute-start.14) | collective-permute-done | bytes 131104 | tf_op jit(solution)/shard_map/ppermute | solution.py:508
  48.5 0.6 copy-done.17
  49.1 9.4 %rim.1 = (bf16[5,2,32,256]{3,2,1,0:T(8,128)(2,1)}, bf16[5,2,32,256]{3,2,1,0:T(8,128)(2,1)}, bf16[5,2,32,256]{3,2,1,0:T(8,128)(2,1)}, bf16[5,2,32,256]{3,2,1,0:T(8,128)(2,1)}) custom-call(s32[1]{0:T(128)} %bitcast.me_ref, bf16[16,2,32,256]{3,2,1,0:T(8,128)(2,1)} %get-tuple-element.78.refs_0_, bf16[16,16,256]{2,1,0:T(8,128)(2,1)} %copy-done.14, ...), custom_call_target="tpu_custom_call" | custom-call | flops 1 | bytes 1 | tf_op jit(solution)/shard_map/rim/pallas_call | solution.py:293
  58.5 1.5 %collective-permute-start.15 = (bf16[5,2,32,256]{3,2,1,0:T(8,128)(2,1)}, bf16[5,2,32,256]{3,2,1,0:T(8,128)(2,1)S(1)}, u32[]{:S(2)}, u32[]{:S(2)}) collective-permute-start(bf16[5,2,32,256]{3,2,1,0:T(8,128)(2,1)} %get-tuple-element.84), channel_id=1, source_target_pairs={{0,8},{8,0},{16,24},{24,16},{1,9},{9,1},{17,25},{25,17},{2,10},{10... | collective-permute-start | bytes 491528 | tf_op jit(solution)/shard_map/ppermute | solution.py:520
  60.0 1.5 %collective-permute-start.16 = (bf16[5,2,32,256]{3,2,1,0:T(8,128)(2,1)}, bf16[5,2,32,256]{3,2,1,0:T(8,128)(2,1)S(1)}, u32[]{:S(2)}, u32[]{:S(2)}) collective-permute-start(bf16[5,2,32,256]{3,2,1,0:T(8,128)(2,1)} %get-tuple-element.85), channel_id=1, source_target_pairs={{0,16},{8,24},{16,0},{24,8},{1,17},{9,25},{17,1},{25,9},{2,18},{10... | collective-permute-start | bytes 491528 | tf_op jit(solution)/shard_map/ppermute | solution.py:520
  61.5 0.5 collective-permute-start.17
  62.0 11.2 %collective-permute-done.4.refs_4_ = bf16[5,15,2,16,256]{4,3,2,1,0:T(8,128)(2,1)S(1)} collective-permute-done((bf16[5,15,2,16,256]{4,3,2,1,0:T(8,128)(2,1)}, bf16[5,15,2,16,256]{4,3,2,1,0:T(8,128)(2,1)S(1)}, u32[]{:S(2)}, u32[]{:S(2)}) %collective-permute-start.4) | collective-permute-done | bytes 1228832 | tf_op jit(solution)/shard_map/ppermute | solution.py:520
  73.3 2.7 %collective-permute-start.9 = (bf16[5,6,2,16,256]{4,3,2,1,0:T(8,128)(2,1)}, bf16[5,6,2,16,256]{4,3,2,1,0:T(8,128)(2,1)S(1)}, u32[]{:S(2)}, u32[]{:S(2)}) collective-permute-start(bf16[5,6,2,16,256]{4,3,2,1,0:T(8,128)(2,1)} %get-tuple-element.72), channel_id=1, source_target_pairs={{0,24},{8,16},{16,8},{24,0},{1,25},{9,17},{17,9},{25,1},{2,26},{10... | collective-permute-start | bytes 1474568 | tf_op jit(solution)/shard_map/ppermute | solution.py:520
  75.9 0.0 collective-permute-done.refs_2_
  75.9 0.5 collective-permute-start.5
  76.5 1.6 %collective-permute-done.15 = bf16[5,2,32,256]{3,2,1,0:T(8,128)(2,1)S(1)} collective-permute-done((bf16[5,2,32,256]{3,2,1,0:T(8,128)(2,1)}, bf16[5,2,32,256]{3,2,1,0:T(8,128)(2,1)S(1)}, u32[]{:S(2)}, u32[]{:S(2)}) %collective-permute-start.15) | collective-permute-done | bytes 163872 | tf_op jit(solution)/shard_map/ppermute | solution.py:520
  78.1 1.5 %collective-permute-start.1 = (bf16[5,6,2,16,256]{4,3,2,1,0:T(8,128)(2,1)}, bf16[5,6,2,16,256]{4,3,2,1,0:T(8,128)(2,1)S(1)}, u32[]{:S(2)}, u32[]{:S(2)}) collective-permute-start(bf16[5,6,2,16,256]{4,3,2,1,0:T(8,128)(2,1)} %get-tuple-element.58), channel_id=1, source_target_pairs={{0,8},{8,0},{16,24},{24,16},{1,9},{9,1},{17,25},{25,17},{2,10},{10... | collective-permute-start | bytes 1474568 | tf_op jit(solution)/shard_map/ppermute | solution.py:520
  79.6 0.0 collective-permute-done.16
  79.6 1.6 %collective-permute-done.17 = bf16[5,2,32,256]{3,2,1,0:T(8,128)(2,1)S(1)} collective-permute-done((bf16[5,2,32,256]{3,2,1,0:T(8,128)(2,1)}, bf16[5,2,32,256]{3,2,1,0:T(8,128)(2,1)S(1)}, u32[]{:S(2)}, u32[]{:S(2)}) %collective-permute-start.17) | collective-permute-done | bytes 163872 | tf_op jit(solution)/shard_map/ppermute | solution.py:520
  81.2 1.0 pad_maximum_fusion.own
  82.2 1.3 collective-permute-start.19
  83.5 3.1 %collective-permute-start.18 = (bf16[4,5,2,32,256]{4,3,2,1,0:T(8,128)(2,1)S(1)}, bf16[4,5,2,32,256]{4,3,2,1,0:T(8,128)(2,1)S(1)}, u32[]{:S(2)}, u32[]{:S(2)}) collective-permute-start(bf16[4,5,2,32,256]{4,3,2,1,0:T(8,128)(2,1)S(1)} %pad_maximum_fusion.own), channel_id=1, source_target_pairs={{0,1},{1,2},{2,3},{3,4},{4,5},{5,6},{6,7},{8,9},{9,10},{10,11},{11... | collective-permute-start | bytes 1966088 | tf_op jit(solution)/shard_map/ppermute | solution.py:508
  86.6 5.1 %collective-permute-done.9.refs_7_ = bf16[5,6,2,16,256]{4,3,2,1,0:T(8,128)(2,1)S(1)} collective-permute-done((bf16[5,6,2,16,256]{4,3,2,1,0:T(8,128)(2,1)}, bf16[5,6,2,16,256]{4,3,2,1,0:T(8,128)(2,1)S(1)}, u32[]{:S(2)}, u32[]{:S(2)}) %collective-permute-start.9) | collective-permute-done | bytes 491552 | tf_op jit(solution)/shard_map/ppermute | solution.py:520
  91.6 2.9 %collective-permute-start.10 = (bf16[5,5,2,16,256]{4,3,2,1,0:T(8,128)(2,1)}, bf16[5,5,2,16,256]{4,3,2,1,0:T(8,128)(2,1)S(1)}, u32[]{:S(2)}, u32[]{:S(2)}) collective-permute-start(bf16[5,5,2,16,256]{4,3,2,1,0:T(8,128)(2,1)} %get-tuple-element.73), channel_id=1, source_target_pairs={{0,24},{8,16},{16,8},{24,0},{1,25},{9,17},{17,9},{25,1},{2,26},{10... | collective-permute-start | bytes 1228808 | tf_op jit(solution)/shard_map/ppermute | solution.py:520
  94.6 7.4 %collective-permute-done.5.refs_5_ = bf16[5,6,2,16,256]{4,3,2,1,0:T(8,128)(2,1)S(1)} collective-permute-done((bf16[5,6,2,16,256]{4,3,2,1,0:T(8,128)(2,1)S(1)}, bf16[5,6,2,16,256]{4,3,2,1,0:T(8,128)(2,1)S(1)}, u32[]{:S(2)}, u32[]{:S(2)}) %collective-permute-start.5) | collective-permute-done | bytes 491552 | tf_op jit(solution)/shard_map/ppermute | solution.py:520
  102.0 2.0 %collective-permute-start.6 = (bf16[5,5,2,16,256]{4,3,2,1,0:T(8,128)(2,1)}, bf16[5,5,2,16,256]{4,3,2,1,0:T(8,128)(2,1)S(1)}, u32[]{:S(2)}, u32[]{:S(2)}) collective-permute-start(bf16[5,5,2,16,256]{4,3,2,1,0:T(8,128)(2,1)} %get-tuple-element.66), channel_id=1, source_target_pairs={{0,16},{8,24},{16,0},{24,8},{1,17},{9,25},{17,1},{25,9},{2,18},{10... | collective-permute-start | bytes 1228808 | tf_op jit(solution)/shard_map/ppermute | solution.py:520
  104.0 0.2 collective-permute-start.2
  104.2 0.6 copy-done.8
  104.8 5.7 %gram_1.1 = (f32[4,16,2,128,128]{4,3,2,1,0:T(8,128)}, f32[4,2,128,128]{3,2,1,0:T(8,128)}, f32[4,2,128,128]{3,2,1,0:T(8,128)}) custom-call(bf16[5,15,2,16,256]{4,3,2,1,0:T(8,128)(2,1)} %get-tuple-element.50.refs_0_, bf16[5,6,2,16,256]{4,3,2,1,0:T(8,128)(2,1)} %get-tuple-element.76.refs_1_, bf16[5,15,2,16,256]{4,3,2,1,0:T(8,128)(2,1)} %copy-done.2, ...), custom_call_target="tpu_custom_call" | custom-call | flops 1 | bytes 1 | tf_op jit(solution)/shard_map/gram_1/pallas_call | solution.py:484
  110.6 0.8 copy-done.4
  111.4 0.2 copy-done.5
  111.6 3.9 %rim_gram.1 = (f32[4,16,2,128,128]{4,3,2,1,0:T(8,128)}, f32[4,2,128,128]{3,2,1,0:T(8,128)}) custom-call(s32[1]{0:T(128)} %bitcast.me_ref, bf16[4,5,2,32,256]{4,3,2,1,0:T(8,128)(2,1)} %copy-done.3, bf16[4,5,2,32,256]{4,3,2,1,0:T(8,128)(2,1)} %copy-done.5, bf16[4,5,2,32,256]{4,3,2,1,0:T(8,128)(2,1)} %copy-done.4, ...), custom_call_target="tpu_custom_call", output_to_operand_aliasing={{0}: (5, {})} | custom-call | flops 1 | bytes 1 | tf_op jit(solution)/shard_map/rim_gram/pallas_call | solution.py:365
  115.5 3.4 %collective-permute-done.6.refs_5_ = bf16[5,5,2,16,256]{4,3,2,1,0:T(8,128)(2,1)S(1)} collective-permute-done((bf16[5,5,2,16,256]{4,3,2,1,0:T(8,128)(2,1)}, bf16[5,5,2,16,256]{4,3,2,1,0:T(8,128)(2,1)S(1)}, u32[]{:S(2)}, u32[]{:S(2)}) %collective-permute-start.6) | collective-permute-done | bytes 409632 | tf_op jit(solution)/shard_map/ppermute | solution.py:520
  118.9 1.7 %collective-permute-start.7 = (bf16[5,4,2,16,256]{4,3,2,1,0:T(8,128)(2,1)S(1)}, bf16[5,4,2,16,256]{4,3,2,1,0:T(8,128)(2,1)S(1)}, u32[]{:S(2)}, u32[]{:S(2)}) collective-permute-start(bf16[5,4,2,16,256]{4,3,2,1,0:T(8,128)(2,1)S(1)} %copy-done.21), channel_id=1, source_target_pairs={{0,16},{8,24},{16,0},{24,8},{1,17},{9,25},{17,1},{25,9},{2,18},{10... | collective-permute-start | bytes 983048 | tf_op jit(solution)/shard_map/ppermute | solution.py:520
  120.6 1.5 %collective-permute-start.3 = (bf16[5,4,2,16,256]{4,3,2,1,0:T(8,128)(2,1)S(1)}, bf16[5,4,2,16,256]{4,3,2,1,0:T(8,128)(2,1)S(1)}, u32[]{:S(2)}, u32[]{:S(2)}) collective-permute-start(bf16[5,4,2,16,256]{4,3,2,1,0:T(8,128)(2,1)S(1)} %copy-done.20), channel_id=1, source_target_pairs={{0,8},{8,0},{16,24},{24,16},{1,9},{9,1},{17,25},{25,17},{2,10},{10... | collective-permute-start | bytes 983048 | tf_op jit(solution)/shard_map/ppermute | solution.py:520
  122.1 5.1 %gram_7.1 = (f32[4,16,2,128,128]{4,3,2,1,0:T(8,128)}, f32[4,2,128,128]{3,2,1,0:T(8,128)}) custom-call(bf16[5,15,2,16,256]{4,3,2,1,0:T(8,128)(2,1)} %get-tuple-element.50.refs_0_, bf16[5,5,2,16,256]{4,3,2,1,0:T(8,128)(2,1)} %get-tuple-element.75.refs_1_, bf16[5,15,2,16,256]{4,3,2,1,0:T(8,128)(2,1)} %copy-done.2, ...), custom_call_target="tpu_custom_call", output_to_operand_aliasing={{0}: (10, {})} | custom-call | flops 1 | bytes 1 | tf_op jit(solution)/shard_map/gram_7/pallas_call | solution.py:484
  127.2 0.4 collective-permute-start.20
  127.5 1.1 collective-permute-done.7.refs_5_
  128.6 1.9 %collective-permute-done.3.refs_3_ = bf16[5,4,2,16,256]{4,3,2,1,0:T(8,128)(2,1)S(1)} collective-permute-done((bf16[5,4,2,16,256]{4,3,2,1,0:T(8,128)(2,1)S(1)}, bf16[5,4,2,16,256]{4,3,2,1,0:T(8,128)(2,1)S(1)}, u32[]{:S(2)}, u32[]{:S(2)}) %collective-permute-start.3) | collective-permute-done | bytes 327712 | tf_op jit(solution)/shard_map/ppermute | solution.py:520
  130.5 6.7 %collective-permute-done.20.refs_7_ = bf16[5,4,2,16,256]{4,3,2,1,0:T(8,128)(2,1)S(1)} collective-permute-done((bf16[5,4,2,16,256]{4,3,2,1,0:T(8,128)(2,1)S(1)}, bf16[5,4,2,16,256]{4,3,2,1,0:T(8,128)(2,1)S(1)}, u32[]{:S(2)}, u32[]{:S(2)}) %collective-permute-start.20) | collective-permute-done | bytes 327712 | tf_op jit(solution)/shard_map/ppermute | solution.py:520
  137.3 0.7 copy-done.13
  138.0 4.5 %gram_12.1 = (f32[4,16,2,128,128]{4,3,2,1,0:T(8,128)}, f32[4,2,128,128]{3,2,1,0:T(8,128)}) custom-call(bf16[5,15,2,16,256]{4,3,2,1,0:T(8,128)(2,1)} %get-tuple-element.50.refs_0_, bf16[5,4,2,16,256]{4,3,2,1,0:T(8,128)(2,1)} %get-tuple-element.53.refs_1_, bf16[5,15,2,16,256]{4,3,2,1,0:T(8,128)(2,1)} %copy-done.2, ...), custom_call_target="tpu_custom_call", output_to_operand_aliasing={{0}: (10, {})} | custom-call | flops 1 | bytes 1 | tf_op jit(solution)/shard_map/gram_12/pallas_call | solution.py:484
  (46 shorter events, 0.1 us)
Async XLA Ops:
  15.6 45.9 %collective-permute-start.8 = (bf16[5,15,2,16,256]{4,3,2,1,0:T(8,128)(2,1)}, bf16[5,15,2,16,256]{4,3,2,1,0:T(8,128)(2,1)S(1)}, u32[]{:S(2)}, u32[]{:S(2)}) collective-permute-start(bf16[5,15,2,16,256]{4,3,2,1,0:T(8,128)(2,1)} %get-tuple-element.68), channel_id=1, source_target_pairs={{0,24},{8,16},{16,8},{24,0},{1,25},{9,17},{17,9},{25,1},{2,26},{10... | collective-permute-start | bytes 3686408 | tf_op jit(solution)/shard_map/ppermute | solution.py:520
  19.6 53.7 %collective-permute-start.4 = (bf16[5,15,2,16,256]{4,3,2,1,0:T(8,128)(2,1)}, bf16[5,15,2,16,256]{4,3,2,1,0:T(8,128)(2,1)S(1)}, u32[]{:S(2)}, u32[]{:S(2)}) collective-permute-start(bf16[5,15,2,16,256]{4,3,2,1,0:T(8,128)(2,1)} %get-tuple-element.61), channel_id=1, source_target_pairs={{0,16},{8,24},{16,0},{24,8},{1,17},{9,25},{17,1},{25,9},{2,18},{10... | collective-permute-start | bytes 3686408 | tf_op jit(solution)/shard_map/ppermute | solution.py:520
  20.1 55.8 %collective-permute-start = (bf16[5,15,2,16,256]{4,3,2,1,0:T(8,128)(2,1)}, bf16[5,15,2,16,256]{4,3,2,1,0:T(8,128)(2,1)S(1)}, u32[]{:S(2)}, u32[]{:S(2)}) collective-permute-start(bf16[5,15,2,16,256]{4,3,2,1,0:T(8,128)(2,1)} %get-tuple-element.54), channel_id=1, source_target_pairs={{0,8},{8,0},{16,24},{24,16},{1,9},{9,1},{17,25},{25,17},{2,10},{10... | collective-permute-start | bytes 3686408 | tf_op jit(solution)/shard_map/ppermute | solution.py:520
  20.2 18.3 %collective-permute-start.11 = (bf16[16,16,256]{2,1,0:T(8,128)(2,1)}, bf16[16,16,256]{2,1,0:T(8,128)(2,1)S(1)}, u32[]{:S(2)}, u32[]{:S(2)}) collective-permute-start(bf16[16,16,256]{2,1,0:T(8,128)(2,1)} %get-tuple-element.79), channel_id=1, source_target_pairs={{0,1},{1,2},{2,3},{3,4},{4,5},{5,6},{6,7},{8,9},{9,10},{10,11},{11... | collective-permute-start | bytes 393224 | tf_op jit(solution)/shard_map/ppermute | solution.py:508
  21.5 22.3 %collective-permute-start.12 = (bf16[16,16,256]{2,1,0:T(8,128)(2,1)}, bf16[16,16,256]{2,1,0:T(8,128)(2,1)S(1)}, u32[]{:S(2)}, u32[]{:S(2)}) collective-permute-start(bf16[16,16,256]{2,1,0:T(8,128)(2,1)} %get-tuple-element.51), channel_id=1, source_target_pairs={{1,0},{2,1},{3,2},{4,3},{5,4},{6,5},{7,6},{9,8},{10,9},{11,10},{12... | collective-permute-start | bytes 393224 | tf_op jit(solution)/shard_map/ppermute | solution.py:508
  38.5 10.0 %copy-start.14 = (bf16[16,16,256]{2,1,0:T(8,128)(2,1)}, bf16[16,16,256]{2,1,0:T(8,128)(2,1)S(1)}, u32[]{:S(2)}) copy-start(bf16[16,16,256]{2,1,0:T(8,128)(2,1)S(1)} %collective-permute-done.11.refs_1_) | copy-start | bytes 393220
  38.5 6.6 %collective-permute-start.13 = (bf16[16,16,256]{2,1,0:T(8,128)(2,1)}, bf16[16,16,256]{2,1,0:T(8,128)(2,1)S(1)}, u32[]{:S(2)}, u32[]{:S(2)}) collective-permute-start(bf16[16,16,256]{2,1,0:T(8,128)(2,1)} %get-tuple-element.81), channel_id=1, source_target_pairs={{0,1},{1,2},{2,3},{3,4},{4,5},{5,6},{6,7},{8,9},{9,10},{10,11},{11... | collective-permute-start | bytes 393224 | tf_op jit(solution)/shard_map/ppermute | solution.py:508
  43.8 4.7 %copy-start.15 = (bf16[16,16,256]{2,1,0:T(8,128)(2,1)}, bf16[16,16,256]{2,1,0:T(8,128)(2,1)S(1)}, u32[]{:S(2)}) copy-start(bf16[16,16,256]{2,1,0:T(8,128)(2,1)S(1)} %collective-permute-done.12.refs_2_) | copy-start | bytes 393220
  43.8 4.7 %collective-permute-start.14 = (bf16[16,16,256]{2,1,0:T(8,128)(2,1)}, bf16[16,16,256]{2,1,0:T(8,128)(2,1)S(1)}, u32[]{:S(2)}, u32[]{:S(2)}) collective-permute-start(bf16[16,16,256]{2,1,0:T(8,128)(2,1)} %get-tuple-element.82), channel_id=1, source_target_pairs={{1,0},{2,1},{3,2},{4,3},{5,4},{6,5},{7,6},{9,8},{10,9},{11,10},{12... | collective-permute-start | bytes 393224 | tf_op jit(solution)/shard_map/ppermute | solution.py:508
  45.1 3.4 %copy-start.16 = (bf16[16,16,256]{2,1,0:T(8,128)(2,1)}, bf16[16,16,256]{2,1,0:T(8,128)(2,1)S(1)}, u32[]{:S(2)}) copy-start(bf16[16,16,256]{2,1,0:T(8,128)(2,1)S(1)} %collective-permute-done.13.refs_5_) | copy-start | bytes 393220
  48.5 0.7 copy-start.17
  49.1 26.8 %copy-start.18 = (bf16[5,6,2,16,256]{4,3,2,1,0:T(8,128)(2,1)S(1)}, bf16[5,6,2,16,256]{4,3,2,1,0:T(8,128)(2,1)}, u32[]{:S(2)}) copy-start(bf16[5,6,2,16,256]{4,3,2,1,0:T(8,128)(2,1)} %get-tuple-element.65) | copy-start | bytes 1474564
  58.5 19.6 %collective-permute-start.15 = (bf16[5,2,32,256]{3,2,1,0:T(8,128)(2,1)}, bf16[5,2,32,256]{3,2,1,0:T(8,128)(2,1)S(1)}, u32[]{:S(2)}, u32[]{:S(2)}) collective-permute-start(bf16[5,2,32,256]{3,2,1,0:T(8,128)(2,1)} %get-tuple-element.84), channel_id=1, source_target_pairs={{0,8},{8,0},{16,24},{24,16},{1,9},{9,1},{17,25},{25,17},{2,10},{10... | collective-permute-start | bytes 491528 | tf_op jit(solution)/shard_map/ppermute | solution.py:520
  60.0 19.6 %collective-permute-start.16 = (bf16[5,2,32,256]{3,2,1,0:T(8,128)(2,1)}, bf16[5,2,32,256]{3,2,1,0:T(8,128)(2,1)S(1)}, u32[]{:S(2)}, u32[]{:S(2)}) collective-permute-start(bf16[5,2,32,256]{3,2,1,0:T(8,128)(2,1)} %get-tuple-element.85), channel_id=1, source_target_pairs={{0,16},{8,24},{16,0},{24,8},{1,17},{9,25},{17,1},{25,9},{2,18},{10... | collective-permute-start | bytes 491528 | tf_op jit(solution)/shard_map/ppermute | solution.py:520
  61.5 42.6 %copy-start = (bf16[5,15,2,16,256]{4,3,2,1,0:T(8,128)(2,1)}, bf16[5,15,2,16,256]{4,3,2,1,0:T(8,128)(2,1)S(1)}, u32[]{:S(2)}) copy-start(bf16[5,15,2,16,256]{4,3,2,1,0:T(8,128)(2,1)S(1)} %collective-permute-done.8.refs_6_) | copy-start | bytes 3686404
  61.5 19.6 %collective-permute-start.17 = (bf16[5,2,32,256]{3,2,1,0:T(8,128)(2,1)}, bf16[5,2,32,256]{3,2,1,0:T(8,128)(2,1)S(1)}, u32[]{:S(2)}, u32[]{:S(2)}) collective-permute-start(bf16[5,2,32,256]{3,2,1,0:T(8,128)(2,1)} %get-tuple-element.86), channel_id=1, source_target_pairs={{0,24},{8,16},{16,8},{24,0},{1,25},{9,17},{17,9},{25,1},{2,26},{10... | collective-permute-start | bytes 491528 | tf_op jit(solution)/shard_map/ppermute | solution.py:520
  73.3 30.9 %copy-start.1 = (bf16[5,15,2,16,256]{4,3,2,1,0:T(8,128)(2,1)}, bf16[5,15,2,16,256]{4,3,2,1,0:T(8,128)(2,1)S(1)}, u32[]{:S(2)}) copy-start(bf16[5,15,2,16,256]{4,3,2,1,0:T(8,128)(2,1)S(1)} %collective-permute-done.4.refs_4_) | copy-start | bytes 3686404
  73.3 18.4 %collective-permute-start.9 = (bf16[5,6,2,16,256]{4,3,2,1,0:T(8,128)(2,1)}, bf16[5,6,2,16,256]{4,3,2,1,0:T(8,128)(2,1)S(1)}, u32[]{:S(2)}, u32[]{:S(2)}) collective-permute-start(bf16[5,6,2,16,256]{4,3,2,1,0:T(8,128)(2,1)} %get-tuple-element.72), channel_id=1, source_target_pairs={{0,24},{8,16},{16,8},{24,0},{1,25},{9,17},{17,9},{25,1},{2,26},{10... | collective-permute-start | bytes 1474568 | tf_op jit(solution)/shard_map/ppermute | solution.py:520
  75.9 28.3 %copy-start.2 = (bf16[5,15,2,16,256]{4,3,2,1,0:T(8,128)(2,1)}, bf16[5,15,2,16,256]{4,3,2,1,0:T(8,128)(2,1)S(1)}, u32[]{:S(2)}) copy-start(bf16[5,15,2,16,256]{4,3,2,1,0:T(8,128)(2,1)S(1)} %collective-permute-done.refs_2_) | copy-start | bytes 3686404
  75.9 26.1 %collective-permute-start.5 = (bf16[5,6,2,16,256]{4,3,2,1,0:T(8,128)(2,1)S(1)}, bf16[5,6,2,16,256]{4,3,2,1,0:T(8,128)(2,1)S(1)}, u32[]{:S(2)}, u32[]{:S(2)}) collective-permute-start(bf16[5,6,2,16,256]{4,3,2,1,0:T(8,128)(2,1)S(1)} %copy-done.18), channel_id=1, source_target_pairs={{0,16},{8,24},{16,0},{24,8},{1,17},{9,25},{17,1},{25,9},{2,18},{10... | collective-permute-start | bytes 1474568 | tf_op jit(solution)/shard_map/ppermute | solution.py:520
  78.1 25.9 %collective-permute-start.1 = (bf16[5,6,2,16,256]{4,3,2,1,0:T(8,128)(2,1)}, bf16[5,6,2,16,256]{4,3,2,1,0:T(8,128)(2,1)S(1)}, u32[]{:S(2)}, u32[]{:S(2)}) collective-permute-start(bf16[5,6,2,16,256]{4,3,2,1,0:T(8,128)(2,1)} %get-tuple-element.58), channel_id=1, source_target_pairs={{0,8},{8,0},{16,24},{24,16},{1,9},{9,1},{17,25},{25,17},{2,10},{10... | collective-permute-start | bytes 1474568 | tf_op jit(solution)/shard_map/ppermute | solution.py:520
  82.2 28.4 %copy-start.3 = (bf16[4,5,2,32,256]{4,3,2,1,0:T(8,128)(2,1)}, bf16[4,5,2,32,256]{4,3,2,1,0:T(8,128)(2,1)S(1)}, u32[]{:S(2)}) copy-start(bf16[4,5,2,32,256]{4,3,2,1,0:T(8,128)(2,1)S(1)} %pad_maximum_fusion.own) | copy-start | bytes 1966084
  82.2 28.3 %collective-permute-start.19 = (bf16[4,5,2,32,256]{4,3,2,1,0:T(8,128)(2,1)S(1)}, bf16[4,5,2,32,256]{4,3,2,1,0:T(8,128)(2,1)S(1)}, u32[]{:S(2)}, u32[]{:S(2)}) collective-permute-start(bf16[4,5,2,32,256]{4,3,2,1,0:T(8,128)(2,1)S(1)} %pad_maximum_fusion.own), channel_id=1, source_target_pairs={{1,0},{2,1},{3,2},{4,3},{5,4},{6,5},{7,6},{9,8},{10,9},{11,10},{12... | collective-permute-start | bytes 1966088 | tf_op jit(solution)/shard_map/ppermute | solution.py:508
  83.5 27.1 %collective-permute-start.18 = (bf16[4,5,2,32,256]{4,3,2,1,0:T(8,128)(2,1)S(1)}, bf16[4,5,2,32,256]{4,3,2,1,0:T(8,128)(2,1)S(1)}, u32[]{:S(2)}, u32[]{:S(2)}) collective-permute-start(bf16[4,5,2,32,256]{4,3,2,1,0:T(8,128)(2,1)S(1)} %pad_maximum_fusion.own), channel_id=1, source_target_pairs={{0,1},{1,2},{2,3},{3,4},{4,5},{5,6},{6,7},{8,9},{9,10},{10,11},{11... | collective-permute-start | bytes 1966088 | tf_op jit(solution)/shard_map/ppermute | solution.py:508
  91.6 12.6 %copy-start.6 = (bf16[5,6,2,16,256]{4,3,2,1,0:T(8,128)(2,1)}, bf16[5,6,2,16,256]{4,3,2,1,0:T(8,128)(2,1)S(1)}, u32[]{:S(2)}) copy-start(bf16[5,6,2,16,256]{4,3,2,1,0:T(8,128)(2,1)S(1)} %collective-permute-done.9.refs_7_) | copy-start | bytes 1474564
  91.6 23.8 %collective-permute-start.10 = (bf16[5,5,2,16,256]{4,3,2,1,0:T(8,128)(2,1)}, bf16[5,5,2,16,256]{4,3,2,1,0:T(8,128)(2,1)S(1)}, u32[]{:S(2)}, u32[]{:S(2)}) collective-permute-start(bf16[5,5,2,16,256]{4,3,2,1,0:T(8,128)(2,1)} %get-tuple-element.73), channel_id=1, source_target_pairs={{0,24},{8,16},{16,8},{24,0},{1,25},{9,17},{17,9},{25,1},{2,26},{10... | collective-permute-start | bytes 1228808 | tf_op jit(solution)/shard_map/ppermute | solution.py:520
  102.0 2.2 %copy-start.7 = (bf16[5,6,2,16,256]{4,3,2,1,0:T(8,128)(2,1)}, bf16[5,6,2,16,256]{4,3,2,1,0:T(8,128)(2,1)S(1)}, u32[]{:S(2)}) copy-start(bf16[5,6,2,16,256]{4,3,2,1,0:T(8,128)(2,1)S(1)} %collective-permute-done.5.refs_5_) | copy-start | bytes 1474564
  102.0 16.9 %collective-permute-start.6 = (bf16[5,5,2,16,256]{4,3,2,1,0:T(8,128)(2,1)}, bf16[5,5,2,16,256]{4,3,2,1,0:T(8,128)(2,1)S(1)}, u32[]{:S(2)}, u32[]{:S(2)}) collective-permute-start(bf16[5,5,2,16,256]{4,3,2,1,0:T(8,128)(2,1)} %get-tuple-element.66), channel_id=1, source_target_pairs={{0,16},{8,24},{16,0},{24,8},{1,17},{9,25},{17,1},{25,9},{2,18},{10... | collective-permute-start | bytes 1228808 | tf_op jit(solution)/shard_map/ppermute | solution.py:520
  104.0 0.8 copy-start.8
  104.0 16.6 %collective-permute-start.2 = (bf16[5,5,2,16,256]{4,3,2,1,0:T(8,128)(2,1)}, bf16[5,5,2,16,256]{4,3,2,1,0:T(8,128)(2,1)}, u32[]{:S(2)}, u32[]{:S(2)}) collective-permute-start(bf16[5,5,2,16,256]{4,3,2,1,0:T(8,128)(2,1)} %get-tuple-element.59), channel_id=1, source_target_pairs={{0,8},{8,0},{16,24},{24,16},{1,9},{9,1},{17,25},{25,17},{2,10},{10... | collective-permute-start | bytes 1228808 | tf_op jit(solution)/shard_map/ppermute | solution.py:520
  110.5 0.8 copy-start.4
  110.5 1.0 copy-start.5
  111.6 7.3 %copy-start.21 = (bf16[5,4,2,16,256]{4,3,2,1,0:T(8,128)(2,1)S(1)}, bf16[5,4,2,16,256]{4,3,2,1,0:T(8,128)(2,1)}, u32[]{:S(2)}) copy-start(bf16[5,4,2,16,256]{4,3,2,1,0:T(8,128)(2,1)} %get-tuple-element.67) | copy-start | bytes 983044
  111.6 9.0 %copy-start.20 = (bf16[5,4,2,16,256]{4,3,2,1,0:T(8,128)(2,1)S(1)}, bf16[5,4,2,16,256]{4,3,2,1,0:T(8,128)(2,1)}, u32[]{:S(2)}) copy-start(bf16[5,4,2,16,256]{4,3,2,1,0:T(8,128)(2,1)} %get-tuple-element.60) | copy-start | bytes 983044
  115.5 6.6 %copy-start.9 = (bf16[5,5,2,16,256]{4,3,2,1,0:T(8,128)(2,1)}, bf16[5,5,2,16,256]{4,3,2,1,0:T(8,128)(2,1)S(1)}, u32[]{:S(2)}) copy-start(bf16[5,5,2,16,256]{4,3,2,1,0:T(8,128)(2,1)S(1)} %collective-permute-done.10.refs_7_) | copy-start | bytes 1228804
  118.9 3.2 %copy-start.10 = (bf16[5,5,2,16,256]{4,3,2,1,0:T(8,128)(2,1)}, bf16[5,5,2,16,256]{4,3,2,1,0:T(8,128)(2,1)S(1)}, u32[]{:S(2)}) copy-start(bf16[5,5,2,16,256]{4,3,2,1,0:T(8,128)(2,1)S(1)} %collective-permute-done.6.refs_5_) | copy-start | bytes 1228804
  118.9 9.7 %collective-permute-start.7 = (bf16[5,4,2,16,256]{4,3,2,1,0:T(8,128)(2,1)S(1)}, bf16[5,4,2,16,256]{4,3,2,1,0:T(8,128)(2,1)S(1)}, u32[]{:S(2)}, u32[]{:S(2)}) collective-permute-start(bf16[5,4,2,16,256]{4,3,2,1,0:T(8,128)(2,1)S(1)} %copy-done.21), channel_id=1, source_target_pairs={{0,16},{8,24},{16,0},{24,8},{1,17},{9,25},{17,1},{25,9},{2,18},{10... | collective-permute-start | bytes 983048 | tf_op jit(solution)/shard_map/ppermute | solution.py:520
  120.6 9.9 %collective-permute-start.3 = (bf16[5,4,2,16,256]{4,3,2,1,0:T(8,128)(2,1)S(1)}, bf16[5,4,2,16,256]{4,3,2,1,0:T(8,128)(2,1)S(1)}, u32[]{:S(2)}, u32[]{:S(2)}) collective-permute-start(bf16[5,4,2,16,256]{4,3,2,1,0:T(8,128)(2,1)S(1)} %copy-done.20), channel_id=1, source_target_pairs={{0,8},{8,0},{16,24},{24,16},{1,9},{9,1},{17,25},{25,17},{2,10},{10... | collective-permute-start | bytes 983048 | tf_op jit(solution)/shard_map/ppermute | solution.py:520
  122.1 5.1 %copy-start.19 = (bf16[5,4,2,16,256]{4,3,2,1,0:T(8,128)(2,1)S(1)}, bf16[5,4,2,16,256]{4,3,2,1,0:T(8,128)(2,1)}, u32[]{:S(2)}) copy-start(bf16[5,4,2,16,256]{4,3,2,1,0:T(8,128)(2,1)} %get-tuple-element.92) | copy-start | bytes 983044
  127.2 10.1 %collective-permute-start.20 = (bf16[5,4,2,16,256]{4,3,2,1,0:T(8,128)(2,1)S(1)}, bf16[5,4,2,16,256]{4,3,2,1,0:T(8,128)(2,1)S(1)}, u32[]{:S(2)}, u32[]{:S(2)}) collective-permute-start(bf16[5,4,2,16,256]{4,3,2,1,0:T(8,128)(2,1)S(1)} %copy-done.19), channel_id=1, source_target_pairs={{0,24},{8,16},{16,8},{24,0},{1,25},{9,17},{17,9},{25,1},{2,26},{10... | collective-permute-start | bytes 983048 | tf_op jit(solution)/shard_map/ppermute | solution.py:520
  128.6 8.6 %copy-start.11 = (bf16[5,4,2,16,256]{4,3,2,1,0:T(8,128)(2,1)}, bf16[5,4,2,16,256]{4,3,2,1,0:T(8,128)(2,1)S(1)}, u32[]{:S(2)}) copy-start(bf16[5,4,2,16,256]{4,3,2,1,0:T(8,128)(2,1)S(1)} %collective-permute-done.7.refs_5_) | copy-start | bytes 983044
  130.5 6.7 %copy-start.12 = (bf16[5,4,2,16,256]{4,3,2,1,0:T(8,128)(2,1)}, bf16[5,4,2,16,256]{4,3,2,1,0:T(8,128)(2,1)S(1)}, u32[]{:S(2)}) copy-start(bf16[5,4,2,16,256]{4,3,2,1,0:T(8,128)(2,1)S(1)} %collective-permute-done.3.refs_3_) | copy-start | bytes 983044
  137.2 0.7 copy-start.13

commit v3 on v2

--- a/solution.py
+++ b/solution.py
@@ -25,12 +25,20 @@
     return pltpu.CompilerParams(vmem_limit_bytes=VMEM)
 
 
-def gather_groups(rows):
-    group = lax.broadcasted_iota(jnp.int32, rows[0].shape, 1) // SIDE
+def odd_tiles(rows):
+    tiles = -(-rows // SUB)
+    return (tiles + 1 - tiles % 2) * SUB
+
+
+def group_masks(shape):
+    group = lax.broadcasted_iota(jnp.int32, shape, 1) // SIDE
+    return [(group & step) == 0 for step in (1, 2, 4)]
+
+
+def gather_groups(rows, masks):
     turned = [rows[0]] + [pltpu.roll(rows[r], SIDE * r, 1) for r in range(1, 8)]
     held = [turned[-i % 8] for i in range(8)]
-    for step in (1, 2, 4):
-        low = (group & step) == 0
+    for step, low in zip((1, 2, 4), masks):
         held = [jnp.where(low, held[i], held[(i - step) % 8]) for i in range(8)]
     return held
 
@@ -41,7 +49,7 @@
     outs, stage = refs[: len(refs) - len(spans)], refs[len(refs) - len(spans) :]
     steps = DBLK // per_step
     n_rows, n_az = slc_ref.shape[2:]
-    lines = 2 * DBLK
+    lines, pitch = 2 * DBLK, odd_tiles(2 * DBLK)
     partners = len(outs) // len(spans)
     row_blocks = outs[0].shape[0]
     halves = plane.shape[0]
@@ -83,17 +91,17 @@
             i = step * per_step + n
             moved = jnp.dot(ranged[i], turned[i], preferred_element_type=f32)
             for c in range(2):
-                line = SUB * lines + c * DBLK + i
+                line = SUB * pitch + c * DBLK + i
                 for h in range(halves):
-                    plane[h, pl.ds(line, n_rows, stride=lines), :] = moved[
+                    plane[h, pl.ds(line, n_rows, stride=pitch), :] = moved[
                         c * n_rows : (c + 1) * n_rows, h * LANES : (h + 1) * LANES
                     ]
 
     lax.fori_loop(0, steps, start, 0)
-    zero = jnp.zeros((SUB * lines, LANES), f32)
+    zero = jnp.zeros((SUB * pitch, LANES), f32)
     for h in range(halves):
-        plane[h, : SUB * lines, :] = zero
-        plane[h, (SUB + n_rows) * lines :, :] = zero
+        plane[h, : SUB * pitch, :] = zero
+        plane[h, (SUB + n_rows) * pitch :, :] = zero
     wait(0)
     along_range(0)
     prepare(0)
@@ -109,6 +117,7 @@
     lax.fori_loop(0, steps, resample, 0)
 
     me = me_ref[0]
+    masks = group_masks((lines, LANES))
     copies = [
         pltpu.make_async_copy(stage[n // partners].at[n % partners], outs[n], out_sems.at[n]) for n in range(len(outs))
     ]
@@ -121,9 +130,9 @@
                 for h in range(halves):
                     rows = []
                     for r in range(8):
-                        at = pl.multiple_of((base + j * SIDE + half * 8 + r) * lines, lines)
+                        at = pl.multiple_of((base + j * SIDE + half * 8 + r) * pitch, SUB)
                         rows.append(plane[h, pl.ds(at, lines), :].astype(bf16))
-                    cols = gather_groups(rows)
+                    cols = gather_groups(rows, masks)
                     for g in range(8):
                         column = h * 8 + g
                         for s, (lo, hi) in enumerate(spans):
@@ -187,7 +196,7 @@
             pltpu.VMEM((DBLK, n_rows, n_rows), bf16),
             pltpu.VMEM((DBLK, *ak.shape[1:]), bf16),
             pltpu.VMEM((DBLK, n_rows, n_az), bf16),
-            pltpu.VMEM((n_az // LANES, (n_rows + 2 * SUB) * 2 * DBLK, LANES), f32),
+            pltpu.VMEM((n_az // LANES, (n_rows + 2 * SUB) * odd_tiles(2 * DBLK), LANES), f32),
             pltpu.VMEM((DBLK, 2 * n_rows, n_az), bf16),
             pltpu.SemaphoreType.DMA((steps, 4)),
             pltpu.SemaphoreType.DMA((len(shapes),)),
@@ -205,15 +214,15 @@
     per_step, n_az = operands[0].shape[0], operands[3].shape[2]
     n_rows = operands[0].shape[3]
     n_dates = outs[0].shape[2]
-    lines = 2 * n_dates
+    lines, pitch = 2 * n_dates, odd_tiles(2 * n_dates)
     row_blocks = outs[0].shape[0]
     eighths = n_rows // 8
 
     @pl.when(step == 0)
     def _():
-        zero = jnp.zeros((lines, LANES), f32)
-        plane[:lines, :] = zero
-        plane[(eighths + 1) * lines :, :] = zero
+        zero = jnp.zeros((pitch, LANES), f32)
+        plane[:pitch, :] = zero
+        plane[(eighths + 1) * pitch :, :] = zero
 
     row = lax.broadcasted_iota(jnp.int32, (n_rows, LANES), 0)
     lane = lax.broadcasted_iota(jnp.int32, (n_rows, LANES), 1)
@@ -243,8 +252,8 @@
     packed = [jnp.dot(gather, x, preferred_element_type=f32) for x in moved]
     for n, (p, i) in enumerate(items):
         for c in range(2):
-            line = lines + c * n_dates + p * DBLK + step * per_step + i
-            plane[pl.ds(line, eighths, stride=lines), :] = packed[2 * n + c]
+            line = pitch + c * n_dates + p * DBLK + step * per_step + i
+            plane[pl.ds(line, eighths, stride=pitch), :] = packed[2 * n + c]
 
     @pl.when(step == steps - 1)
     def _():
@@ -253,7 +262,7 @@
             base = (me ^ k) * (dest_rows // 8)
             for j in range(row_blocks):
                 for half in range(2):
-                    start = pl.multiple_of((base + 2 * j + half) * lines, lines)
+                    start = pl.multiple_of((base + 2 * j + half) * pitch, SUB)
                     values = plane[pl.ds(start, lines), :].astype(bf16)
                     for c in range(2):
                         outs[k][j, c, :, half * LANES : (half + 1) * LANES] = values[
@@ -288,7 +297,7 @@
         grid=(steps,),
         in_specs=in_specs,
         out_specs=[pl.BlockSpec(shape.shape, lambda t, m: (0, 0, 0, 0))] * partners,
-        scratch_shapes=[pltpu.VMEM(((n_rows // 8 + 2) * 2 * n_dates, LANES), f32)],
+        scratch_shapes=[pltpu.VMEM(((n_rows // 8 + 2) * odd_tiles(2 * n_dates), LANES), f32)],
     )
     return pl.pallas_call(
         functools.partial(rim_kernel, dest_rows, parts),
@@ -515,7 +524,7 @@
         block = blocks[k]
         if ahead is not None:
             block = after(block, ahead[k])
-        if k == n - 1 and gates:
+        if k == 1 and gates:
             block = after(block, *gates)
         got.append(lax.ppermute(block, "date", [(i, i ^ k) for i in range(n)]))
     return got
@@ -565,7 +574,7 @@
     result, end = rim_gram(me, rims, above, below, opening, result)
     for s in range(1, len(spans) - 1):
         result, state = column_gram(s, state, end, result)
-        late.append(exchange(sent[-1][s + 1], late[s], gates=(state,)))
+        late.append(exchange(sent[-1][s + 1], late[s], gates=(end,)))
     result, state = column_gram(len(spans) - 1, state, end, result)
     return result
 

time: 143 us -> 134 us (0.937)
  Pallas kernels: 59.8 us -> 50.7 us
  starting transfers between devices: 34.9 us -> 36.8 us
    pallas_call x2, Pallas kernels: 31.3 us -> 22.4 us  [interior(): pl.pallas_call(functools.partial(interior_kernel, spans, dest_rows, part,...]
    ppermute x15, starting transfers between devices: 21.4 us -> 23.3 us  [exchange(): got.append(lax.ppermute(block, 'date', [(i, i ^ k) for i in range(n)]))]
  transfers between devices with their start and end apart: 21 -> 21, of which waited for: 10 -> 9; matrix products, arithmetic and copies ran while one was open for 1% -> 1% of each run, Pallas kernels for 28% -> 26%
where the time goes in v3:
time: 134 us
  Pallas kernels  50.7 us (38%)
  waiting for transfers between devices  42.3 us (32%)
  starting transfers between devices  36.8 us (27%)
  local copies, waits for them, and re-layouts  3.04 us (2%)
    ppermute x15, waiting for transfers between devices, exchange(): got.append(lax.ppermute(block, 'date', [(i, i ^ k) for i in range(n)]))  38.9 us
    ppermute x15, starting transfers between devices, exchange(): got.append(lax.ppermute(block, 'date', [(i, i ^ k) for i in range(n)]))  23.3 us
    pallas_call x2, Pallas kernels, interior(): pl.pallas_call(functools.partial(interior_kernel, spans, dest_rows, part,...  22.4 us
    pallas_call x3, Pallas kernels, gram(): pl.pallas_call(functools.partial(gram_kernel, partners, parts, offsets, c...  15.2 us
    ppermute x6, starting transfers between devices, shift(): return lax.ppermute(value, axis, pairs)  13.5 us
    pallas_call x1, Pallas kernels, rim(): pl.pallas_call(functools.partial(rim_kernel, dest_rows, parts), grid_spec...  9.15 us
    pallas_call x1, Pallas kernels, rim_gram(): pl.pallas_call(rim_gram_kernel, in_specs=[pl.BlockSpec(memory_space=pltpu...  3.9 us
    ppermute x6, waiting for transfers between devices, shift(): return lax.ppermute(value, axis, pairs)  3.38 us
  transfers between devices with their start and end apart: 21, of which 9 were waited for; matrix products, arithmetic and copies ran while one was open for 1% of the time, Pallas kernels for 26%

profile of v3, /device:TPU:0, one launch (start us, length us, event | category | flops | bytes accessed | tf_op | source)
XLA Modules:
  0.0 134.1 jit_solution(12976345971236442107)
XLA Ops:
  0.0 11.2 %interior_0.1 = (bf16[16,2,32,256]{3,2,1,0:T(8,128)(2,1)}, bf16[16,16,256]{2,1,0:T(8,128)(2,1)}, bf16[16,16,256]{2,1,0:T(8,128)(2,1)}, bf16[5,15,2,16,256]{4,3,2...) custom-call(s32[1]{0:T(128)} %bitcast.me_ref, ...), custom_call_target="tpu_custom_call" | custom-call | flops 1 | bytes 1 | tf_op jit(solution)/shard_map/interior_0/pallas_call | solution.py:188
  11.2 4.0 %collective-permute-start.14 = (bf16[5,15,2,16,256]{4,3,2,1,0:T(8,128)(2,1)}, bf16[5,15,2,16,256]{4,3,2,1,0:T(8,128)(2,1)S(1)}, u32[]{:S(2)}, u32[]{:S(2)}) collective-permute-start(bf16[5,15,2,16,256]{4,3,2,1,0:T(8,128)(2,1)} %get-tuple-element.74), channel_id=1, source_target_pairs={{0,24},{8,16},{16,8},{24,0},{1,25},{9,17},{17,9},{25,1},{2,26},{10... | collective-permute-start | bytes 3686408 | tf_op jit(solution)/shard_map/ppermute | solution.py:529
  15.1 0.5 collective-permute-start.12
  15.6 0.1 collective-permute-start
  15.8 1.3 collective-permute-start.3
  17.1 1.3 collective-permute-start.4
  18.4 11.2 %interior_1.1 = (bf16[16,2,32,256]{3,2,1,0:T(8,128)(2,1)}, bf16[16,16,256]{2,1,0:T(8,128)(2,1)}, bf16[16,16,256]{2,1,0:T(8,128)(2,1)}, bf16[5,6,2,16,256]{4,3,2,...) custom-call(s32[1]{0:T(128)} %bitcast.me_ref, ...), custom_call_target="tpu_custom_call" | custom-call | flops 1 | bytes 1 | tf_op jit(solution)/shard_map/interior_1/pallas_call | solution.py:188
  29.6 5.2 %collective-permute-start.5 = (bf16[16,16,256]{2,1,0:T(8,128)(2,1)}, bf16[16,16,256]{2,1,0:T(8,128)(2,1)S(1)}, u32[]{:S(2)}, u32[]{:S(2)}) collective-permute-start(bf16[16,16,256]{2,1,0:T(8,128)(2,1)} %get-tuple-element.64), channel_id=1, source_target_pairs={{0,1},{1,2},{2,3},{3,4},{4,5},{5,6},{6,7},{8,9},{9,10},{10,11},{11... | collective-permute-start | bytes 393224 | tf_op jit(solution)/shard_map/ppermute | solution.py:517
  34.8 0.0 collective-permute-done.4.refs_2_
  34.9 1.3 collective-permute-start.6
  36.2 0.0 collective-permute-done.5.refs_5_
  36.2 3.4 %collective-permute-done.6.refs_6_ = bf16[16,16,256]{2,1,0:T(8,128)(2,1)S(1)} collective-permute-done((bf16[16,16,256]{2,1,0:T(8,128)(2,1)}, bf16[16,16,256]{2,1,0:T(8,128)(2,1)S(1)}, u32[]{:S(2)}, u32[]{:S(2)}) %collective-permute-start.6) | collective-permute-done | bytes 131104 | tf_op jit(solution)/shard_map/ppermute | solution.py:517
  39.6 0.6 copy-done.17
  40.2 9.1 %rim.1 = (bf16[5,2,32,256]{3,2,1,0:T(8,128)(2,1)}, bf16[5,2,32,256]{3,2,1,0:T(8,128)(2,1)}, bf16[5,2,32,256]{3,2,1,0:T(8,128)(2,1)}, bf16[5,2,32,256]{3,2,1,0:T(8,128)(2,1)}) custom-call(s32[1]{0:T(128)} %bitcast.me_ref, bf16[16,2,32,256]{3,2,1,0:T(8,128)(2,1)} %get-tuple-element.61.refs_0_, bf16[16,16,256]{2,1,0:T(8,128)(2,1)} %copy-done.14, ...), custom_call_target="tpu_custom_call" | custom-call | flops 1 | bytes 1 | tf_op jit(solution)/shard_map/rim/pallas_call | solution.py:302
  49.4 1.5 %collective-permute-start.7 = (bf16[5,2,32,256]{3,2,1,0:T(8,128)(2,1)}, bf16[5,2,32,256]{3,2,1,0:T(8,128)(2,1)S(1)}, u32[]{:S(2)}, u32[]{:S(2)}) collective-permute-start(bf16[5,2,32,256]{3,2,1,0:T(8,128)(2,1)} %get-tuple-element.67), channel_id=1, source_target_pairs={{0,8},{8,0},{16,24},{24,16},{1,9},{9,1},{17,25},{25,17},{2,10},{10... | collective-permute-start | bytes 491528 | tf_op jit(solution)/shard_map/ppermute | solution.py:529
  50.9 1.5 %collective-permute-start.8 = (bf16[5,2,32,256]{3,2,1,0:T(8,128)(2,1)}, bf16[5,2,32,256]{3,2,1,0:T(8,128)(2,1)S(1)}, u32[]{:S(2)}, u32[]{:S(2)}) collective-permute-start(bf16[5,2,32,256]{3,2,1,0:T(8,128)(2,1)} %get-tuple-element.68), channel_id=1, source_target_pairs={{0,16},{8,24},{16,0},{24,8},{1,17},{9,25},{17,1},{25,9},{2,18},{10... | collective-permute-start | bytes 491528 | tf_op jit(solution)/shard_map/ppermute | solution.py:529
  52.4 0.0 collective-permute-done.14.refs_6_
  52.4 0.5 collective-permute-start.9
  52.9 15.9 %collective-permute-done.12.refs_4_ = bf16[5,15,2,16,256]{4,3,2,1,0:T(8,128)(2,1)S(1)} collective-permute-done((bf16[5,15,2,16,256]{4,3,2,1,0:T(8,128)(2,1)}, bf16[5,15,2,16,256]{4,3,2,1,0:T(8,128)(2,1)S(1)}, u32[]{:S(2)}, u32[]{:S(2)}) %collective-permute-start.12) | collective-permute-done | bytes 1228832 | tf_op jit(solution)/shard_map/ppermute | solution.py:529
  68.8 2.7 %collective-permute-start.15 = (bf16[5,6,2,16,256]{4,3,2,1,0:T(8,128)(2,1)}, bf16[5,6,2,16,256]{4,3,2,1,0:T(8,128)(2,1)S(1)}, u32[]{:S(2)}, u32[]{:S(2)}) collective-permute-start(bf16[5,6,2,16,256]{4,3,2,1,0:T(8,128)(2,1)} %get-tuple-element.76), channel_id=1, source_target_pairs={{0,24},{8,16},{16,8},{24,0},{1,25},{9,17},{17,9},{25,1},{2,26},{10... | collective-permute-start | bytes 1474568 | tf_op jit(solution)/shard_map/ppermute | solution.py:529
  71.4 0.0 collective-permute-done.refs_2_
  71.5 0.5 collective-permute-start.13
  72.0 1.6 %collective-permute-done.7 = bf16[5,2,32,256]{3,2,1,0:T(8,128)(2,1)S(1)} collective-permute-done((bf16[5,2,32,256]{3,2,1,0:T(8,128)(2,1)}, bf16[5,2,32,256]{3,2,1,0:T(8,128)(2,1)S(1)}, u32[]{:S(2)}, u32[]{:S(2)}) %collective-permute-start.7) | collective-permute-done | bytes 163872 | tf_op jit(solution)/shard_map/ppermute | solution.py:529
  73.6 1.5 %collective-permute-start.1 = (bf16[5,6,2,16,256]{4,3,2,1,0:T(8,128)(2,1)}, bf16[5,6,2,16,256]{4,3,2,1,0:T(8,128)(2,1)S(1)}, u32[]{:S(2)}, u32[]{:S(2)}) collective-permute-start(bf16[5,6,2,16,256]{4,3,2,1,0:T(8,128)(2,1)} %get-tuple-element.58), channel_id=1, source_target_pairs={{0,8},{8,0},{16,24},{24,16},{1,9},{9,1},{17,25},{25,17},{2,10},{10... | collective-permute-start | bytes 1474568 | tf_op jit(solution)/shard_map/ppermute | solution.py:529
  75.1 1.6 %collective-permute-done.9 = bf16[5,2,32,256]{3,2,1,0:T(8,128)(2,1)S(1)} collective-permute-done((bf16[5,2,32,256]{3,2,1,0:T(8,128)(2,1)}, bf16[5,2,32,256]{3,2,1,0:T(8,128)(2,1)S(1)}, u32[]{:S(2)}, u32[]{:S(2)}) %collective-permute-start.9) | collective-permute-done | bytes 163872 | tf_op jit(solution)/shard_map/ppermute | solution.py:529
  76.7 1.0 pad_maximum_fusion.own
  77.7 1.3 collective-permute-start.11
  79.0 3.1 %collective-permute-start.10 = (bf16[4,5,2,32,256]{4,3,2,1,0:T(8,128)(2,1)S(1)}, bf16[4,5,2,32,256]{4,3,2,1,0:T(8,128)(2,1)S(1)}, u32[]{:S(2)}, u32[]{:S(2)}) collective-permute-start(bf16[4,5,2,32,256]{4,3,2,1,0:T(8,128)(2,1)S(1)} %pad_maximum_fusion.own), channel_id=1, source_target_pairs={{0,1},{1,2},{2,3},{3,4},{4,5},{5,6},{6,7},{8,9},{9,10},{10,11},{11... | collective-permute-start | bytes 1966088 | tf_op jit(solution)/shard_map/ppermute | solution.py:517
  82.1 5.1 %collective-permute-done.15.refs_7_ = bf16[5,6,2,16,256]{4,3,2,1,0:T(8,128)(2,1)S(1)} collective-permute-done((bf16[5,6,2,16,256]{4,3,2,1,0:T(8,128)(2,1)}, bf16[5,6,2,16,256]{4,3,2,1,0:T(8,128)(2,1)S(1)}, u32[]{:S(2)}, u32[]{:S(2)}) %collective-permute-start.15) | collective-permute-done | bytes 491552 | tf_op jit(solution)/shard_map/ppermute | solution.py:529
  87.2 2.9 %collective-permute-start.19 = (bf16[5,5,2,16,256]{4,3,2,1,0:T(8,128)(2,1)}, bf16[5,5,2,16,256]{4,3,2,1,0:T(8,128)(2,1)S(1)}, u32[]{:S(2)}, u32[]{:S(2)}) collective-permute-start(bf16[5,5,2,16,256]{4,3,2,1,0:T(8,128)(2,1)} %get-tuple-element.87), channel_id=1, source_target_pairs={{0,24},{8,16},{16,8},{24,0},{1,25},{9,17},{17,9},{25,1},{2,26},{10... | collective-permute-start | bytes 1228808 | tf_op jit(solution)/shard_map/ppermute | solution.py:529
  90.1 7.4 %collective-permute-done.13.refs_5_ = bf16[5,6,2,16,256]{4,3,2,1,0:T(8,128)(2,1)S(1)} collective-permute-done((bf16[5,6,2,16,256]{4,3,2,1,0:T(8,128)(2,1)S(1)}, bf16[5,6,2,16,256]{4,3,2,1,0:T(8,128)(2,1)S(1)}, u32[]{:S(2)}, u32[]{:S(2)}) %collective-permute-start.13) | collective-permute-done | bytes 491552 | tf_op jit(solution)/shard_map/ppermute | solution.py:529
  97.5 2.0 %collective-permute-start.17 = (bf16[5,5,2,16,256]{4,3,2,1,0:T(8,128)(2,1)}, bf16[5,5,2,16,256]{4,3,2,1,0:T(8,128)(2,1)S(1)}, u32[]{:S(2)}, u32[]{:S(2)}) collective-permute-start(bf16[5,5,2,16,256]{4,3,2,1,0:T(8,128)(2,1)} %get-tuple-element.83), channel_id=1, source_target_pairs={{0,16},{8,24},{16,0},{24,8},{1,17},{9,25},{17,1},{25,9},{2,18},{10... | collective-permute-start | bytes 1228808 | tf_op jit(solution)/shard_map/ppermute | solution.py:529
  99.6 0.2 collective-permute-start.2
  99.7 0.6 copy-done.8
  100.3 5.7 %gram_1.1 = (f32[4,16,2,128,128]{4,3,2,1,0:T(8,128)}, f32[4,2,128,128]{3,2,1,0:T(8,128)}, f32[4,2,128,128]{3,2,1,0:T(8,128)}) custom-call(bf16[5,15,2,16,256]{4,3,2,1,0:T(8,128)(2,1)} %get-tuple-element.50.refs_0_, bf16[5,6,2,16,256]{4,3,2,1,0:T(8,128)(2,1)} %get-tuple-element.70.refs_1_, bf16[5,15,2,16,256]{4,3,2,1,0:T(8,128)(2,1)} %copy-done.2, ...), custom_call_target="tpu_custom_call" | custom-call | flops 1 | bytes 1 | tf_op jit(solution)/shard_map/gram_1/pallas_call | solution.py:493
  106.1 0.8 copy-done.4
  106.9 0.2 copy-done.5
  107.1 3.9 %rim_gram.1 = (f32[4,16,2,128,128]{4,3,2,1,0:T(8,128)}, f32[4,2,128,128]{3,2,1,0:T(8,128)}) custom-call(s32[1]{0:T(128)} %bitcast.me_ref, bf16[4,5,2,32,256]{4,3,2,1,0:T(8,128)(2,1)} %copy-done.3, bf16[4,5,2,32,256]{4,3,2,1,0:T(8,128)(2,1)} %copy-done.5, bf16[4,5,2,32,256]{4,3,2,1,0:T(8,128)(2,1)} %copy-done.4, ...), custom_call_target="tpu_custom_call", output_to_operand_aliasing={{0}: (5, {})} | custom-call | flops 1 | bytes 1 | tf_op jit(solution)/shard_map/rim_gram/pallas_call | solution.py:374
  111.1 1.5 %collective-permute-start.20 = (bf16[5,4,2,16,256]{4,3,2,1,0:T(8,128)(2,1)S(1)}, bf16[5,4,2,16,256]{4,3,2,1,0:T(8,128)(2,1)S(1)}, u32[]{:S(2)}, u32[]{:S(2)}) collective-permute-start(bf16[5,4,2,16,256]{4,3,2,1,0:T(8,128)(2,1)S(1)} %copy-done.21), channel_id=1, source_target_pairs={{0,24},{8,16},{16,8},{24,0},{1,25},{9,17},{17,9},{25,1},{2,26},{10... | collective-permute-start | bytes 983048 | tf_op jit(solution)/shard_map/ppermute | solution.py:529
  112.6 2.2 %collective-permute-done.17.refs_5_ = bf16[5,5,2,16,256]{4,3,2,1,0:T(8,128)(2,1)S(1)} collective-permute-done((bf16[5,5,2,16,256]{4,3,2,1,0:T(8,128)(2,1)}, bf16[5,5,2,16,256]{4,3,2,1,0:T(8,128)(2,1)S(1)}, u32[]{:S(2)}, u32[]{:S(2)}) %collective-permute-start.17) | collective-permute-done | bytes 409632 | tf_op jit(solution)/shard_map/ppermute | solution.py:529
  114.7 2.4 %collective-permute-start.18 = (bf16[5,4,2,16,256]{4,3,2,1,0:T(8,128)(2,1)S(1)}, bf16[5,4,2,16,256]{4,3,2,1,0:T(8,128)(2,1)S(1)}, u32[]{:S(2)}, u32[]{:S(2)}) collective-permute-start(bf16[5,4,2,16,256]{4,3,2,1,0:T(8,128)(2,1)S(1)} %copy-done.20), channel_id=1, source_target_pairs={{0,16},{8,24},{16,0},{24,8},{1,17},{9,25},{17,1},{25,9},{2,18},{10... | collective-permute-start | bytes 983048 | tf_op jit(solution)/shard_map/ppermute | solution.py:529
  117.2 1.5 %collective-permute-start.16 = (bf16[5,4,2,16,256]{4,3,2,1,0:T(8,128)(2,1)S(1)}, bf16[5,4,2,16,256]{4,3,2,1,0:T(8,128)(2,1)S(1)}, u32[]{:S(2)}, u32[]{:S(2)}) collective-permute-start(bf16[5,4,2,16,256]{4,3,2,1,0:T(8,128)(2,1)S(1)} %copy-done.19), channel_id=1, source_target_pairs={{0,8},{8,0},{16,24},{24,16},{1,9},{9,1},{17,25},{25,17},{2,10},{10... | collective-permute-start | bytes 983048 | tf_op jit(solution)/shard_map/ppermute | solution.py:529
  118.7 5.0 %gram_7.1 = (f32[4,16,2,128,128]{4,3,2,1,0:T(8,128)}, f32[4,2,128,128]{3,2,1,0:T(8,128)}) custom-call(bf16[5,15,2,16,256]{4,3,2,1,0:T(8,128)(2,1)} %get-tuple-element.50.refs_0_, bf16[5,5,2,16,256]{4,3,2,1,0:T(8,128)(2,1)} %get-tuple-element.89.refs_1_, bf16[5,15,2,16,256]{4,3,2,1,0:T(8,128)(2,1)} %copy-done.2, ...), custom_call_target="tpu_custom_call", output_to_operand_aliasing={{0}: (10, {})} | custom-call | flops 1 | bytes 1 | tf_op jit(solution)/shard_map/gram_7/pallas_call | solution.py:493
  123.8 4.8 %collective-permute-done.18.refs_5_ = bf16[5,4,2,16,256]{4,3,2,1,0:T(8,128)(2,1)S(1)} collective-permute-done((bf16[5,4,2,16,256]{4,3,2,1,0:T(8,128)(2,1)S(1)}, bf16[5,4,2,16,256]{4,3,2,1,0:T(8,128)(2,1)S(1)}, u32[]{:S(2)}, u32[]{:S(2)}) %collective-permute-start.18) | collective-permute-done | bytes 327712 | tf_op jit(solution)/shard_map/ppermute | solution.py:529
  128.5 0.3 collective-permute-done.16.refs_3_
  128.8 0.5 copy-done.12
  129.3 0.3 copy-done.13
  129.5 4.5 %gram_12.1 = (f32[4,16,2,128,128]{4,3,2,1,0:T(8,128)}, f32[4,2,128,128]{3,2,1,0:T(8,128)}) custom-call(bf16[5,15,2,16,256]{4,3,2,1,0:T(8,128)(2,1)} %get-tuple-element.50.refs_0_, bf16[5,4,2,16,256]{4,3,2,1,0:T(8,128)(2,1)} %get-tuple-element.53.refs_1_, bf16[5,15,2,16,256]{4,3,2,1,0:T(8,128)(2,1)} %copy-done.2, ...), custom_call_target="tpu_custom_call", output_to_operand_aliasing={{0}: (10, {})} | custom-call | flops 1 | bytes 1 | tf_op jit(solution)/shard_map/gram_12/pallas_call | solution.py:493
  (46 shorter events, 0.1 us)
Async XLA Ops:
  11.2 41.2 %collective-permute-start.14 = (bf16[5,15,2,16,256]{4,3,2,1,0:T(8,128)(2,1)}, bf16[5,15,2,16,256]{4,3,2,1,0:T(8,128)(2,1)S(1)}, u32[]{:S(2)}, u32[]{:S(2)}) collective-permute-start(bf16[5,15,2,16,256]{4,3,2,1,0:T(8,128)(2,1)} %get-tuple-element.74), channel_id=1, source_target_pairs={{0,24},{8,16},{16,8},{24,0},{1,25},{9,17},{17,9},{25,1},{2,26},{10... | collective-permute-start | bytes 3686408 | tf_op jit(solution)/shard_map/ppermute | solution.py:529
  15.1 53.7 %collective-permute-start.12 = (bf16[5,15,2,16,256]{4,3,2,1,0:T(8,128)(2,1)}, bf16[5,15,2,16,256]{4,3,2,1,0:T(8,128)(2,1)S(1)}, u32[]{:S(2)}, u32[]{:S(2)}) collective-permute-start(bf16[5,15,2,16,256]{4,3,2,1,0:T(8,128)(2,1)} %get-tuple-element.71), channel_id=1, source_target_pairs={{0,16},{8,24},{16,0},{24,8},{1,17},{9,25},{17,1},{25,9},{2,18},{10... | collective-permute-start | bytes 3686408 | tf_op jit(solution)/shard_map/ppermute | solution.py:529
  15.6 55.8 %collective-permute-start = (bf16[5,15,2,16,256]{4,3,2,1,0:T(8,128)(2,1)}, bf16[5,15,2,16,256]{4,3,2,1,0:T(8,128)(2,1)S(1)}, u32[]{:S(2)}, u32[]{:S(2)}) collective-permute-start(bf16[5,15,2,16,256]{4,3,2,1,0:T(8,128)(2,1)} %get-tuple-element.54), channel_id=1, source_target_pairs={{0,8},{8,0},{16,24},{24,16},{1,9},{9,1},{17,25},{25,17},{2,10},{10... | collective-permute-start | bytes 3686408 | tf_op jit(solution)/shard_map/ppermute | solution.py:529
  15.8 13.8 %collective-permute-start.3 = (bf16[16,16,256]{2,1,0:T(8,128)(2,1)}, bf16[16,16,256]{2,1,0:T(8,128)(2,1)S(1)}, u32[]{:S(2)}, u32[]{:S(2)}) collective-permute-start(bf16[16,16,256]{2,1,0:T(8,128)(2,1)} %get-tuple-element.62), channel_id=1, source_target_pairs={{0,1},{1,2},{2,3},{3,4},{4,5},{5,6},{6,7},{8,9},{9,10},{10,11},{11... | collective-permute-start | bytes 393224 | tf_op jit(solution)/shard_map/ppermute | solution.py:517
  17.1 17.8 %collective-permute-start.4 = (bf16[16,16,256]{2,1,0:T(8,128)(2,1)}, bf16[16,16,256]{2,1,0:T(8,128)(2,1)S(1)}, u32[]{:S(2)}, u32[]{:S(2)}) collective-permute-start(bf16[16,16,256]{2,1,0:T(8,128)(2,1)} %get-tuple-element.51), channel_id=1, source_target_pairs={{1,0},{2,1},{3,2},{4,3},{5,4},{6,5},{7,6},{9,8},{10,9},{11,10},{12... | collective-permute-start | bytes 393224 | tf_op jit(solution)/shard_map/ppermute | solution.py:517
  29.6 10.0 %copy-start.14 = (bf16[16,16,256]{2,1,0:T(8,128)(2,1)}, bf16[16,16,256]{2,1,0:T(8,128)(2,1)S(1)}, u32[]{:S(2)}) copy-start(bf16[16,16,256]{2,1,0:T(8,128)(2,1)S(1)} %collective-permute-done.3.refs_1_) | copy-start | bytes 393220
  29.6 6.6 %collective-permute-start.5 = (bf16[16,16,256]{2,1,0:T(8,128)(2,1)}, bf16[16,16,256]{2,1,0:T(8,128)(2,1)S(1)}, u32[]{:S(2)}, u32[]{:S(2)}) collective-permute-start(bf16[16,16,256]{2,1,0:T(8,128)(2,1)} %get-tuple-element.64), channel_id=1, source_target_pairs={{0,1},{1,2},{2,3},{3,4},{4,5},{5,6},{6,7},{8,9},{9,10},{10,11},{11... | collective-permute-start | bytes 393224 | tf_op jit(solution)/shard_map/ppermute | solution.py:517
  34.9 4.7 %copy-start.15 = (bf16[16,16,256]{2,1,0:T(8,128)(2,1)}, bf16[16,16,256]{2,1,0:T(8,128)(2,1)S(1)}, u32[]{:S(2)}) copy-start(bf16[16,16,256]{2,1,0:T(8,128)(2,1)S(1)} %collective-permute-done.4.refs_2_) | copy-start | bytes 393220
  34.9 4.7 %collective-permute-start.6 = (bf16[16,16,256]{2,1,0:T(8,128)(2,1)}, bf16[16,16,256]{2,1,0:T(8,128)(2,1)S(1)}, u32[]{:S(2)}, u32[]{:S(2)}) collective-permute-start(bf16[16,16,256]{2,1,0:T(8,128)(2,1)} %get-tuple-element.65), channel_id=1, source_target_pairs={{1,0},{2,1},{3,2},{4,3},{5,4},{6,5},{7,6},{9,8},{10,9},{11,10},{12... | collective-permute-start | bytes 393224 | tf_op jit(solution)/shard_map/ppermute | solution.py:517
  36.2 3.4 %copy-start.16 = (bf16[16,16,256]{2,1,0:T(8,128)(2,1)}, bf16[16,16,256]{2,1,0:T(8,128)(2,1)S(1)}, u32[]{:S(2)}) copy-start(bf16[16,16,256]{2,1,0:T(8,128)(2,1)S(1)} %collective-permute-done.5.refs_5_) | copy-start | bytes 393220
  39.6 0.7 copy-start.17
  40.2 31.2 %copy-start.18 = (bf16[5,6,2,16,256]{4,3,2,1,0:T(8,128)(2,1)S(1)}, bf16[5,6,2,16,256]{4,3,2,1,0:T(8,128)(2,1)}, u32[]{:S(2)}) copy-start(bf16[5,6,2,16,256]{4,3,2,1,0:T(8,128)(2,1)} %get-tuple-element.73) | copy-start | bytes 1474564
  49.4 24.3 %collective-permute-start.7 = (bf16[5,2,32,256]{3,2,1,0:T(8,128)(2,1)}, bf16[5,2,32,256]{3,2,1,0:T(8,128)(2,1)S(1)}, u32[]{:S(2)}, u32[]{:S(2)}) collective-permute-start(bf16[5,2,32,256]{3,2,1,0:T(8,128)(2,1)} %get-tuple-element.67), channel_id=1, source_target_pairs={{0,8},{8,0},{16,24},{24,16},{1,9},{9,1},{17,25},{25,17},{2,10},{10... | collective-permute-start | bytes 491528 | tf_op jit(solution)/shard_map/ppermute | solution.py:529
  50.9 24.2 %collective-permute-start.8 = (bf16[5,2,32,256]{3,2,1,0:T(8,128)(2,1)}, bf16[5,2,32,256]{3,2,1,0:T(8,128)(2,1)S(1)}, u32[]{:S(2)}, u32[]{:S(2)}) collective-permute-start(bf16[5,2,32,256]{3,2,1,0:T(8,128)(2,1)} %get-tuple-element.68), channel_id=1, source_target_pairs={{0,16},{8,24},{16,0},{24,8},{1,17},{9,25},{17,1},{25,9},{2,18},{10... | collective-permute-start | bytes 491528 | tf_op jit(solution)/shard_map/ppermute | solution.py:529
  52.4 47.3 %copy-start = (bf16[5,15,2,16,256]{4,3,2,1,0:T(8,128)(2,1)}, bf16[5,15,2,16,256]{4,3,2,1,0:T(8,128)(2,1)S(1)}, u32[]{:S(2)}) copy-start(bf16[5,15,2,16,256]{4,3,2,1,0:T(8,128)(2,1)S(1)} %collective-permute-done.14.refs_6_) | copy-start | bytes 3686404
  52.4 24.3 %collective-permute-start.9 = (bf16[5,2,32,256]{3,2,1,0:T(8,128)(2,1)}, bf16[5,2,32,256]{3,2,1,0:T(8,128)(2,1)S(1)}, u32[]{:S(2)}, u32[]{:S(2)}) collective-permute-start(bf16[5,2,32,256]{3,2,1,0:T(8,128)(2,1)} %get-tuple-element.69), channel_id=1, source_target_pairs={{0,24},{8,16},{16,8},{24,0},{1,25},{9,17},{17,9},{25,1},{2,26},{10... | collective-permute-start | bytes 491528 | tf_op jit(solution)/shard_map/ppermute | solution.py:529
  68.8 30.9 %copy-start.1 = (bf16[5,15,2,16,256]{4,3,2,1,0:T(8,128)(2,1)}, bf16[5,15,2,16,256]{4,3,2,1,0:T(8,128)(2,1)S(1)}, u32[]{:S(2)}) copy-start(bf16[5,15,2,16,256]{4,3,2,1,0:T(8,128)(2,1)S(1)} %collective-permute-done.12.refs_4_) | copy-start | bytes 3686404
  68.8 18.4 %collective-permute-start.15 = (bf16[5,6,2,16,256]{4,3,2,1,0:T(8,128)(2,1)}, bf16[5,6,2,16,256]{4,3,2,1,0:T(8,128)(2,1)S(1)}, u32[]{:S(2)}, u32[]{:S(2)}) collective-permute-start(bf16[5,6,2,16,256]{4,3,2,1,0:T(8,128)(2,1)} %get-tuple-element.76), channel_id=1, source_target_pairs={{0,24},{8,16},{16,8},{24,0},{1,25},{9,17},{17,9},{25,1},{2,26},{10... | collective-permute-start | bytes 1474568 | tf_op jit(solution)/shard_map/ppermute | solution.py:529
  71.5 28.3 %copy-start.2 = (bf16[5,15,2,16,256]{4,3,2,1,0:T(8,128)(2,1)}, bf16[5,15,2,16,256]{4,3,2,1,0:T(8,128)(2,1)S(1)}, u32[]{:S(2)}) copy-start(bf16[5,15,2,16,256]{4,3,2,1,0:T(8,128)(2,1)S(1)} %collective-permute-done.refs_2_) | copy-start | bytes 3686404
  71.5 26.1 %collective-permute-start.13 = (bf16[5,6,2,16,256]{4,3,2,1,0:T(8,128)(2,1)S(1)}, bf16[5,6,2,16,256]{4,3,2,1,0:T(8,128)(2,1)S(1)}, u32[]{:S(2)}, u32[]{:S(2)}) collective-permute-start(bf16[5,6,2,16,256]{4,3,2,1,0:T(8,128)(2,1)S(1)} %copy-done.18), channel_id=1, source_target_pairs={{0,16},{8,24},{16,0},{24,8},{1,17},{9,25},{17,1},{25,9},{2,18},{10... | collective-permute-start | bytes 1474568 | tf_op jit(solution)/shard_map/ppermute | solution.py:529
  73.6 25.9 %collective-permute-start.1 = (bf16[5,6,2,16,256]{4,3,2,1,0:T(8,128)(2,1)}, bf16[5,6,2,16,256]{4,3,2,1,0:T(8,128)(2,1)S(1)}, u32[]{:S(2)}, u32[]{:S(2)}) collective-permute-start(bf16[5,6,2,16,256]{4,3,2,1,0:T(8,128)(2,1)} %get-tuple-element.58), channel_id=1, source_target_pairs={{0,8},{8,0},{16,24},{24,16},{1,9},{9,1},{17,25},{25,17},{2,10},{10... | collective-permute-start | bytes 1474568 | tf_op jit(solution)/shard_map/ppermute | solution.py:529
  77.7 28.4 %copy-start.3 = (bf16[4,5,2,32,256]{4,3,2,1,0:T(8,128)(2,1)}, bf16[4,5,2,32,256]{4,3,2,1,0:T(8,128)(2,1)S(1)}, u32[]{:S(2)}) copy-start(bf16[4,5,2,32,256]{4,3,2,1,0:T(8,128)(2,1)S(1)} %pad_maximum_fusion.own) | copy-start | bytes 1966084
  77.7 28.3 %collective-permute-start.11 = (bf16[4,5,2,32,256]{4,3,2,1,0:T(8,128)(2,1)S(1)}, bf16[4,5,2,32,256]{4,3,2,1,0:T(8,128)(2,1)S(1)}, u32[]{:S(2)}, u32[]{:S(2)}) collective-permute-start(bf16[4,5,2,32,256]{4,3,2,1,0:T(8,128)(2,1)S(1)} %pad_maximum_fusion.own), channel_id=1, source_target_pairs={{1,0},{2,1},{3,2},{4,3},{5,4},{6,5},{7,6},{9,8},{10,9},{11,10},{12... | collective-permute-start | bytes 1966088 | tf_op jit(solution)/shard_map/ppermute | solution.py:517
  79.0 27.1 %collective-permute-start.10 = (bf16[4,5,2,32,256]{4,3,2,1,0:T(8,128)(2,1)S(1)}, bf16[4,5,2,32,256]{4,3,2,1,0:T(8,128)(2,1)S(1)}, u32[]{:S(2)}, u32[]{:S(2)}) collective-permute-start(bf16[4,5,2,32,256]{4,3,2,1,0:T(8,128)(2,1)S(1)} %pad_maximum_fusion.own), channel_id=1, source_target_pairs={{0,1},{1,2},{2,3},{3,4},{4,5},{5,6},{6,7},{8,9},{9,10},{10,11},{11... | collective-permute-start | bytes 1966088 | tf_op jit(solution)/shard_map/ppermute | solution.py:517
  87.2 12.6 %copy-start.6 = (bf16[5,6,2,16,256]{4,3,2,1,0:T(8,128)(2,1)}, bf16[5,6,2,16,256]{4,3,2,1,0:T(8,128)(2,1)S(1)}, u32[]{:S(2)}) copy-start(bf16[5,6,2,16,256]{4,3,2,1,0:T(8,128)(2,1)S(1)} %collective-permute-done.15.refs_7_) | copy-start | bytes 1474564
  87.2 23.9 %collective-permute-start.19 = (bf16[5,5,2,16,256]{4,3,2,1,0:T(8,128)(2,1)}, bf16[5,5,2,16,256]{4,3,2,1,0:T(8,128)(2,1)S(1)}, u32[]{:S(2)}, u32[]{:S(2)}) collective-permute-start(bf16[5,5,2,16,256]{4,3,2,1,0:T(8,128)(2,1)} %get-tuple-element.87), channel_id=1, source_target_pairs={{0,24},{8,16},{16,8},{24,0},{1,25},{9,17},{17,9},{25,1},{2,26},{10... | collective-permute-start | bytes 1228808 | tf_op jit(solution)/shard_map/ppermute | solution.py:529
  97.5 2.2 %copy-start.7 = (bf16[5,6,2,16,256]{4,3,2,1,0:T(8,128)(2,1)}, bf16[5,6,2,16,256]{4,3,2,1,0:T(8,128)(2,1)S(1)}, u32[]{:S(2)}) copy-start(bf16[5,6,2,16,256]{4,3,2,1,0:T(8,128)(2,1)S(1)} %collective-permute-done.13.refs_5_) | copy-start | bytes 1474564
  97.5 17.2 %collective-permute-start.17 = (bf16[5,5,2,16,256]{4,3,2,1,0:T(8,128)(2,1)}, bf16[5,5,2,16,256]{4,3,2,1,0:T(8,128)(2,1)S(1)}, u32[]{:S(2)}, u32[]{:S(2)}) collective-permute-start(bf16[5,5,2,16,256]{4,3,2,1,0:T(8,128)(2,1)} %get-tuple-element.83), channel_id=1, source_target_pairs={{0,16},{8,24},{16,0},{24,8},{1,17},{9,25},{17,1},{25,9},{2,18},{10... | collective-permute-start | bytes 1228808 | tf_op jit(solution)/shard_map/ppermute | solution.py:529
  99.6 0.8 copy-start.8
  99.6 17.6 %collective-permute-start.2 = (bf16[5,5,2,16,256]{4,3,2,1,0:T(8,128)(2,1)}, bf16[5,5,2,16,256]{4,3,2,1,0:T(8,128)(2,1)}, u32[]{:S(2)}, u32[]{:S(2)}) collective-permute-start(bf16[5,5,2,16,256]{4,3,2,1,0:T(8,128)(2,1)} %get-tuple-element.59), channel_id=1, source_target_pairs={{0,8},{8,0},{16,24},{24,16},{1,9},{9,1},{17,25},{25,17},{2,10},{10... | collective-permute-start | bytes 1228808 | tf_op jit(solution)/shard_map/ppermute | solution.py:529
  106.0 0.8 copy-start.4
  106.1 1.0 copy-start.5
  107.1 3.9 %copy-start.21 = (bf16[5,4,2,16,256]{4,3,2,1,0:T(8,128)(2,1)S(1)}, bf16[5,4,2,16,256]{4,3,2,1,0:T(8,128)(2,1)}, u32[]{:S(2)}) copy-start(bf16[5,4,2,16,256]{4,3,2,1,0:T(8,128)(2,1)} %get-tuple-element.88) | copy-start | bytes 983044
  107.1 7.6 %copy-start.20 = (bf16[5,4,2,16,256]{4,3,2,1,0:T(8,128)(2,1)S(1)}, bf16[5,4,2,16,256]{4,3,2,1,0:T(8,128)(2,1)}, u32[]{:S(2)}) copy-start(bf16[5,4,2,16,256]{4,3,2,1,0:T(8,128)(2,1)} %get-tuple-element.84) | copy-start | bytes 983044
  107.1 10.1 %copy-start.19 = (bf16[5,4,2,16,256]{4,3,2,1,0:T(8,128)(2,1)S(1)}, bf16[5,4,2,16,256]{4,3,2,1,0:T(8,128)(2,1)}, u32[]{:S(2)}) copy-start(bf16[5,4,2,16,256]{4,3,2,1,0:T(8,128)(2,1)} %get-tuple-element.80) | copy-start | bytes 983044
  111.0 7.7 %copy-start.9 = (bf16[5,5,2,16,256]{4,3,2,1,0:T(8,128)(2,1)}, bf16[5,5,2,16,256]{4,3,2,1,0:T(8,128)(2,1)S(1)}, u32[]{:S(2)}) copy-start(bf16[5,5,2,16,256]{4,3,2,1,0:T(8,128)(2,1)S(1)} %collective-permute-done.19.refs_7_) | copy-start | bytes 1228804
  111.1 12.7 %collective-permute-start.20 = (bf16[5,4,2,16,256]{4,3,2,1,0:T(8,128)(2,1)S(1)}, bf16[5,4,2,16,256]{4,3,2,1,0:T(8,128)(2,1)S(1)}, u32[]{:S(2)}, u32[]{:S(2)}) collective-permute-start(bf16[5,4,2,16,256]{4,3,2,1,0:T(8,128)(2,1)S(1)} %copy-done.21), channel_id=1, source_target_pairs={{0,24},{8,16},{16,8},{24,0},{1,25},{9,17},{17,9},{25,1},{2,26},{10... | collective-permute-start | bytes 983048 | tf_op jit(solution)/shard_map/ppermute | solution.py:529
  114.7 4.0 %copy-start.10 = (bf16[5,5,2,16,256]{4,3,2,1,0:T(8,128)(2,1)}, bf16[5,5,2,16,256]{4,3,2,1,0:T(8,128)(2,1)S(1)}, u32[]{:S(2)}) copy-start(bf16[5,5,2,16,256]{4,3,2,1,0:T(8,128)(2,1)S(1)} %collective-permute-done.17.refs_5_) | copy-start | bytes 1228804
  114.7 13.8 %collective-permute-start.18 = (bf16[5,4,2,16,256]{4,3,2,1,0:T(8,128)(2,1)S(1)}, bf16[5,4,2,16,256]{4,3,2,1,0:T(8,128)(2,1)S(1)}, u32[]{:S(2)}, u32[]{:S(2)}) collective-permute-start(bf16[5,4,2,16,256]{4,3,2,1,0:T(8,128)(2,1)S(1)} %copy-done.20), channel_id=1, source_target_pairs={{0,16},{8,24},{16,0},{24,8},{1,17},{9,25},{17,1},{25,9},{2,18},{10... | collective-permute-start | bytes 983048 | tf_op jit(solution)/shard_map/ppermute | solution.py:529
  117.2 11.6 %collective-permute-start.16 = (bf16[5,4,2,16,256]{4,3,2,1,0:T(8,128)(2,1)S(1)}, bf16[5,4,2,16,256]{4,3,2,1,0:T(8,128)(2,1)S(1)}, u32[]{:S(2)}, u32[]{:S(2)}) collective-permute-start(bf16[5,4,2,16,256]{4,3,2,1,0:T(8,128)(2,1)S(1)} %copy-done.19), channel_id=1, source_target_pairs={{0,8},{8,0},{16,24},{24,16},{1,9},{9,1},{17,25},{25,17},{2,10},{10... | collective-permute-start | bytes 983048 | tf_op jit(solution)/shard_map/ppermute | solution.py:529
  123.7 5.1 %copy-start.11 = (bf16[5,4,2,16,256]{4,3,2,1,0:T(8,128)(2,1)}, bf16[5,4,2,16,256]{4,3,2,1,0:T(8,128)(2,1)S(1)}, u32[]{:S(2)}) copy-start(bf16[5,4,2,16,256]{4,3,2,1,0:T(8,128)(2,1)S(1)} %collective-permute-done.20.refs_7_) | copy-start | bytes 983044
  128.5 0.8 copy-start.12
  128.8 0.7 copy-start.13

commit v4 on v3

--- a/solution.py
+++ b/solution.py
@@ -14,7 +14,7 @@
 SUB = 8
 DBLK = 16
 EPS = 1e-06
-VMEM = 56 * 1024 * 1024
+VMEM = 63 * 1024 * 1024
 COST = pl.CostEstimate(flops=1, bytes_accessed=1, transcendentals=0)
 
 bf16 = jnp.bfloat16
@@ -43,24 +43,32 @@
     return held
 
 
-def interior_kernel(spans, dest_rows, part, per_step, me_ref, slc_any, rk_any, ak_any, *refs):
-    own_ref, first_ref, last_ref, *refs = refs
+def interior_kernel(spans, targets, edged, dest_rows, part, per_step, me_ref, slc_any, rk_any, ak_any, *refs):
+    if edged:
+        own_ref, first_ref, last_ref, *refs = refs
     *refs, slc_ref, rk_ref, ak_ref, turned, plane, ranged, in_sems, out_sems = refs
     outs, stage = refs[: len(refs) - len(spans)], refs[len(refs) - len(spans) :]
     steps = DBLK // per_step
     n_rows, n_az = slc_ref.shape[2:]
     lines, pitch = 2 * DBLK, odd_tiles(2 * DBLK)
-    partners = len(outs) // len(spans)
+    n_targets = len(targets)
     row_blocks = outs[0].shape[0]
     halves = plane.shape[0]
+    me = me_ref[0]
+    taken, top = n_rows, 0
+    if n_targets == 1:
+        taken = min(n_rows, dest_rows + 2 * SIDE)
+        top = jnp.clip((me ^ targets[0]) * dest_rows - SIDE, 0, n_rows - taken)
+        top = pl.multiple_of(top, SIDE)
+    rows_in = pl.ds(top, taken)
 
     def fetch(step):
         here = pl.ds(step * per_step, per_step)
         there = pl.ds(part * DBLK + step * per_step, per_step)
         return [
-            pltpu.make_async_copy(rk_any.at[there], rk_ref.at[here], in_sems.at[step, 0]),
-            pltpu.make_async_copy(slc_any.at[0, there], slc_ref.at[0, here], in_sems.at[step, 1]),
-            pltpu.make_async_copy(slc_any.at[1, there], slc_ref.at[1, here], in_sems.at[step, 2]),
+            pltpu.make_async_copy(rk_any.at[there, rows_in], rk_ref.at[here, pl.ds(0, taken)], in_sems.at[step, 0]),
+            pltpu.make_async_copy(slc_any.at[0, there, rows_in], slc_ref.at[0, here, rows_in], in_sems.at[step, 1]),
+            pltpu.make_async_copy(slc_any.at[1, there, rows_in], slc_ref.at[1, here, rows_in], in_sems.at[step, 2]),
             pltpu.make_async_copy(ak_any.at[there], ak_ref.at[here], in_sems.at[step, 3]),
         ]
 
@@ -77,8 +85,8 @@
         for n in range(per_step):
             i = step * per_step + n
             for c in range(2):
-                value = jnp.dot(rk_ref[i], slc_ref[c, i], preferred_element_type=f32)
-                ranged[i, c * n_rows : (c + 1) * n_rows, :] = value.astype(bf16)
+                value = jnp.dot(rk_ref[i, :taken], slc_ref[c, i], preferred_element_type=f32)
+                ranged[i, c * taken : (c + 1) * taken, :] = value.astype(bf16)
 
     def prepare(step):
         for n in range(per_step):
@@ -89,12 +97,12 @@
     def along_azimuth(step):
         for n in range(per_step):
             i = step * per_step + n
-            moved = jnp.dot(ranged[i], turned[i], preferred_element_type=f32)
+            moved = jnp.dot(ranged[i, : 2 * taken], turned[i], preferred_element_type=f32)
             for c in range(2):
-                line = SUB * pitch + c * DBLK + i
+                line = (SUB + top) * pitch + c * DBLK + i
                 for h in range(halves):
-                    plane[h, pl.ds(line, n_rows, stride=pitch), :] = moved[
-                        c * n_rows : (c + 1) * n_rows, h * LANES : (h + 1) * LANES
+                    plane[h, pl.ds(line, taken, stride=pitch), :] = moved[
+                        c * taken : (c + 1) * taken, h * LANES : (h + 1) * LANES
                     ]
 
     lax.fori_loop(0, steps, start, 0)
@@ -102,6 +110,14 @@
     for h in range(halves):
         plane[h, : SUB * pitch, :] = zero
         plane[h, (SUB + n_rows) * pitch :, :] = zero
+    if taken < n_rows:
+
+        def clear(n, carry):
+            at = pl.multiple_of(jnp.where(n * SIDE < top, n * SIDE, n * SIDE + taken), SIDE)
+            slc_ref[:, :, pl.ds(at, SIDE), :] = jnp.zeros((2, DBLK, SIDE, n_az), bf16)
+            return carry
+
+        lax.fori_loop(0, (n_rows - taken) // SIDE, clear, 0)
     wait(0)
     along_range(0)
     prepare(0)
@@ -116,13 +132,13 @@
 
     lax.fori_loop(0, steps, resample, 0)
 
-    me = me_ref[0]
     masks = group_masks((lines, LANES))
     copies = [
-        pltpu.make_async_copy(stage[n // partners].at[n % partners], outs[n], out_sems.at[n]) for n in range(len(outs))
+        pltpu.make_async_copy(stage[n // n_targets].at[n % n_targets], outs[n], out_sems.at[n])
+        for n in range(len(outs))
     ]
 
-    for k in [*range(1, partners), 0]:
+    for t, k in enumerate(targets):
         base = (me ^ k) * dest_rows
 
         def blocks(j, carry):
@@ -138,14 +154,14 @@
                         for s, (lo, hi) in enumerate(spans):
                             if lo <= column < hi:
                                 for c in range(2):
-                                    stage[s][k, j, column - lo, c, :, half * LANES : (half + 1) * LANES] = cols[g][
+                                    stage[s][t, j, column - lo, c, :, half * LANES : (half + 1) * LANES] = cols[g][
                                         c * DBLK : (c + 1) * DBLK
                                     ]
             return carry
 
         lax.fori_loop(0, row_blocks, blocks, 0)
         for s in range(len(spans)):
-            copies[s * partners + k].start()
+            copies[s * n_targets + t].start()
 
     pick_row = lax.broadcasted_iota(jnp.int32, (2 * SIDE, n_az), 0)
     pick_col = lax.broadcasted_iota(jnp.int32, (2 * SIDE, n_az), 1)
@@ -162,12 +178,13 @@
             last_ref[i] = jnp.concatenate([p[2 * SIDE - SUB :] for p in parts], axis=0).astype(bf16)
         return carry
 
-    lax.fori_loop(0, DBLK // 4, edges, 0)
+    if edged:
+        lax.fori_loop(0, DBLK // 4, edges, 0)
     for copy in copies:
         copy.wait()
 
 
-def interior(me, slc, rk, ak, part, spans, partners):
+def interior(me, slc, rk, ak, part, spans, targets, edged, partners):
     n_rows, n_az = slc.shape[2], slc.shape[3]
     dest_rows = n_rows // partners
     row_blocks = dest_rows // SIDE + 1
@@ -176,21 +193,23 @@
     shapes = [
         jax.ShapeDtypeStruct((row_blocks, hi - lo, 2, DBLK, PIX), bf16)
         for lo, hi in spans
-        for _ in range(partners)
+        for _ in targets
     ]
     edge_shapes = [
         jax.ShapeDtypeStruct((DBLK, 2, 2 * SIDE, n_rows), bf16),
         jax.ShapeDtypeStruct((DBLK, 2 * SUB, n_rows), bf16),
         jax.ShapeDtypeStruct((DBLK, 2 * SUB, n_rows), bf16),
     ]
+    if not edged:
+        edge_shapes = []
     whole = pl.BlockSpec(memory_space=pltpu.VMEM)
     anywhere = pl.BlockSpec(memory_space=pl.ANY)
-    own, first, last, *flat = pl.pallas_call(
-        functools.partial(interior_kernel, spans, dest_rows, part, per_step),
+    outs = pl.pallas_call(
+        functools.partial(interior_kernel, spans, targets, edged, dest_rows, part, per_step),
         in_specs=[pl.BlockSpec(memory_space=pltpu.SMEM)] + [anywhere] * 3,
-        out_specs=[whole] * 3 + [anywhere] * len(shapes),
+        out_specs=[whole] * len(edge_shapes) + [anywhere] * len(shapes),
         out_shape=edge_shapes + shapes,
-        scratch_shapes=[pltpu.VMEM((partners, *x.shape), bf16) for x in shapes[::partners]]
+        scratch_shapes=[pltpu.VMEM((len(targets), *x.shape), bf16) for x in shapes[:: len(targets)]]
         + [
             pltpu.VMEM((2, DBLK, n_rows, n_az), bf16),
             pltpu.VMEM((DBLK, n_rows, n_rows), bf16),
@@ -203,9 +222,10 @@
         ],
         compiler_params=params(),
         cost_estimate=COST,
-        name=f"interior_{part}",
+        name=f"interior_{part}_{targets[0]}",
     )(me, slc, rk, ak)
-    return own, first, last, [flat[s * partners : (s + 1) * partners] for s in range(len(spans))]
+    flat = outs[len(edge_shapes) :]
+    return outs[: len(edge_shapes)], [flat[s * len(targets) : (s + 1) * len(targets)] for s in range(len(spans))]
 
 
 def rim_kernel(dest_rows, parts, me_ref, *refs):
@@ -541,7 +561,7 @@
     columns = n_az // SIDE
     me = lax.axis_index("date").astype(jnp.int32).reshape(1)
     parts = n_dates // DBLK
-    bounds = [1, 7, 12, columns]
+    bounds = [1, 7, 13, columns]
     spans = list(zip(bounds[:-1], bounds[1:]))
 
     dest_windows = n_rows // partners // SIDE
@@ -551,14 +571,27 @@
     turn = me
     for part in range(parts):
         part_spans = spans if part == parts - 1 else [(1, columns)]
-        edge, first, last, out = interior(turn, slc, range_kernel, azimuth_kernel, part, part_spans, partners)
+        source = (slc, range_kernel, azimuth_kernel, part, part_spans)
+        if part == 0:
+            _, lead = interior(turn, *source, [partners - 1], False, partners)
+            turn = after(me, lead[0][0])
+        targets = [*range(1, partners - 1 if part == 0 else partners), 0]
+        (edge, first, last), out = interior(turn, *source, targets, True, partners)
         turn = after(me, first)
         own.append(edge)
         left.append(shift(last, "strip", 1))
         right.append(shift(first, "strip", -1))
+        if part == 0:
+            out = [[x[-1], *x[:-1], y[0]] for x, y in zip(out, lead)]
+        else:
+            out = [[x[-1], *x[:-1]] for x in out]
         sent.append(out)
     early = [exchange(s[0]) for s in sent[:-1]]
-    rims = jnp.stack(exchange(rim(me, own, left, right, azimuth_kernel, partners)))
+    lead = [early[-1][-1]] if early else []
+    rims = exchange([after(x, *lead) for x in rim(me, own, left, right, azimuth_kernel, partners)])
+    first = [*sent[-1][0][:-1], after(sent[-1][0][-1], *rims)]
+    late = [exchange(first, early[-1] if early else None)]
+    rims = jnp.stack(rims)
     above, below = shift(rims, "strip", 1), shift(rims, "strip", -1)
 
     def column_gram(s, state, end, result):
@@ -568,7 +601,6 @@
         closing = s == len(spans) - 1
         return gram(pieces, offsets, hi - lo, lo, state, end, result, out_shape, closing)
 
-    late = [exchange(sent[-1][0], early[-1] if early else None)]
     late.append(exchange(sent[-1][1], late[0]))
     result, opening, state = column_gram(0, None, None, None)
     result, end = rim_gram(me, rims, above, below, opening, result)

time: 134 us -> 128 us (0.955)
  waiting for transfers between devices: 42.3 us -> 31.8 us
  Pallas kernels: 50.7 us -> 55.6 us
  local copies, waits for them, and re-layouts: 3.04 us -> 1.37 us
    ppermute x15, waiting for transfers between devices: 38.9 us -> 28.4 us  [exchange(): got.append(lax.ppermute(block, 'date', [(i, i ^ k) for i in range(n)]))]
    pallas_call x2 -> x3, Pallas kernels: 22.4 us -> 27.5 us  [interior(): pl.pallas_call(functools.partial(interior_kernel, spans, targets, edged,...]
    unnamed x44 -> x18, local copies, waits for them, and re-layouts: 3.04 us -> 1.37 us
  transfers between devices with their start and end apart: 21 -> 21, of which waited for: 9 -> 8; matrix products, arithmetic and copies ran while one was open for 1% -> 1% of each run, Pallas kernels for 26% -> 36%
where the time goes in v4:
time: 128 us
  Pallas kernels  55.6 us (43%)
  starting transfers between devices  37.8 us (30%)
  waiting for transfers between devices  31.8 us (25%)
  local copies, waits for them, and re-layouts  1.37 us (1%)
    ppermute x15, waiting for transfers between devices, exchange(): got.append(lax.ppermute(block, 'date', [(i, i ^ k) for i in range(n)]))  28.4 us
    pallas_call x3, Pallas kernels, interior(): pl.pallas_call(functools.partial(interior_kernel, spans, targets, edged,...  27.5 us
    ppermute x15, starting transfers between devices, exchange(): got.append(lax.ppermute(block, 'date', [(i, i ^ k) for i in range(n)]))  23.5 us
    pallas_call x3, Pallas kernels, gram(): pl.pallas_call(functools.partial(gram_kernel, partners, parts, offsets, c...  15.3 us
    ppermute x6, starting transfers between devices, shift(): return lax.ppermute(value, axis, pairs)  14.4 us
    pallas_call x1, Pallas kernels, rim(): pl.pallas_call(functools.partial(rim_kernel, dest_rows, parts), grid_spec...  9.05 us
    pallas_call x1, Pallas kernels, rim_gram(): pl.pallas_call(rim_gram_kernel, in_specs=[pl.BlockSpec(memory_space=pltpu...  3.81 us
    ppermute x6, waiting for transfers between devices, shift(): return lax.ppermute(value, axis, pairs)  3.38 us
  transfers between devices with their start and end apart: 21, of which 8 were waited for; matrix products, arithmetic and copies ran while one was open for 1% of the time, Pallas kernels for 36%

profile of v4, /device:TPU:0, one launch (start us, length us, event | category | flops | bytes accessed | tf_op | source)
XLA Modules:
  0.0 127.8 jit_solution(3292580937587189884)
XLA Ops:
  0.0 5.8 %interior_0_3.1 = bf16[5,15,2,16,256]{4,3,2,1,0:T(8,128)(2,1)} custom-call(s32[1]{0:T(128)} %bitcast.me_ref, bf16[2,32,256,256]{3,2,1,0:T(8,128)(2,1)} %slc_any.5, bf16[32,256,256]{2,1,0:T(8,128)(2,1)} %rk_any.5, bf16[32,272,256]{2,1,0:T(8,128)(2,1)} %refs_7_.1), custom_call_target="tpu_custom_call" | custom-call | flops 1 | bytes 1 | tf_op jit(solution)/shard_map/interior_0_3/pallas_call | solution.py:207
  5.8 4.0 %collective-permute-start.7 = (bf16[5,15,2,16,256]{4,3,2,1,0:T(8,128)(2,1)}, bf16[5,15,2,16,256]{4,3,2,1,0:T(8,128)(2,1)}, u32[]{:S(2)}, u32[]{:S(2)}) collective-permute-start(bf16[5,15,2,16,256]{4,3,2,1,0:T(8,128)(2,1)} %interior_0_3.1), channel_id=1, source_target_pairs={{0,24},{8,16},{16,8},{24,0},{1,25},{9,17},{17,9},{25,1},{2,26},{10... | collective-permute-start | bytes 3686408 | tf_op jit(solution)/shard_map/ppermute | solution.py:549
  9.8 10.4 %interior_0_1.1 = (bf16[16,2,32,256]{3,2,1,0:T(8,128)(2,1)}, bf16[16,16,256]{2,1,0:T(8,128)(2,1)}, bf16[16,16,256]{2,1,0:T(8,128)(2,1)}, bf16[5,15,2,16,256]{4,3...) custom-call(s32[1]{0:T(128)} %bitcast.me_ref, ...), custom_call_target="tpu_custom_call" | custom-call | flops 1 | bytes 1 | tf_op jit(solution)/shard_map/interior_0_1/pallas_call | solution.py:207
  20.2 0.6 collective-permute-start
  20.8 0.1 collective-permute-start.13
  20.9 1.3 %collective-permute-start.3 = (bf16[16,16,256]{2,1,0:T(8,128)(2,1)}, bf16[16,16,256]{2,1,0:T(8,128)(2,1)S(1)}, u32[]{:S(2)}, u32[]{:S(2)}) collective-permute-start(bf16[16,16,256]{2,1,0:T(8,128)(2,1)} %get-tuple-element.68), channel_id=1, source_target_pairs={{0,1},{1,2},{2,3},{3,4},{4,5},{5,6},{6,7},{8,9},{9,10},{10,11},{11... | collective-permute-start | bytes 393224 | tf_op jit(solution)/shard_map/ppermute | solution.py:537
  22.2 1.3 %collective-permute-start.4 = (bf16[16,16,256]{2,1,0:T(8,128)(2,1)}, bf16[16,16,256]{2,1,0:T(8,128)(2,1)S(1)}, u32[]{:S(2)}, u32[]{:S(2)}) collective-permute-start(bf16[16,16,256]{2,1,0:T(8,128)(2,1)} %get-tuple-element.57), channel_id=1, source_target_pairs={{1,0},{2,1},{3,2},{4,3},{5,4},{6,5},{7,6},{9,8},{10,9},{11,10},{12... | collective-permute-start | bytes 393224 | tf_op jit(solution)/shard_map/ppermute | solution.py:537
  23.5 11.3 %interior_1_1.1 = (bf16[16,2,32,256]{3,2,1,0:T(8,128)(2,1)}, bf16[16,16,256]{2,1,0:T(8,128)(2,1)}, bf16[16,16,256]{2,1,0:T(8,128)(2,1)}, bf16[5,6,2,16,256]{4,3,...) custom-call(s32[1]{0:T(128)} %bitcast.me_ref, ...), custom_call_target="tpu_custom_call" | custom-call | flops 1 | bytes 1 | tf_op jit(solution)/shard_map/interior_1_1/pallas_call | solution.py:207
  34.7 0.0 collective-permute-done.3.refs_1_
  34.8 5.3 %collective-permute-start.5 = (bf16[16,16,256]{2,1,0:T(8,128)(2,1)}, bf16[16,16,256]{2,1,0:T(8,128)(2,1)S(1)}, u32[]{:S(2)}, u32[]{:S(2)}) collective-permute-start(bf16[16,16,256]{2,1,0:T(8,128)(2,1)} %get-tuple-element.70), channel_id=1, source_target_pairs={{0,1},{1,2},{2,3},{3,4},{4,5},{5,6},{6,7},{8,9},{9,10},{10,11},{11... | collective-permute-start | bytes 393224 | tf_op jit(solution)/shard_map/ppermute | solution.py:537
  40.1 0.0 collective-permute-done.4.refs_2_
  40.1 1.3 %collective-permute-start.6 = (bf16[16,16,256]{2,1,0:T(8,128)(2,1)}, bf16[16,16,256]{2,1,0:T(8,128)(2,1)S(1)}, u32[]{:S(2)}, u32[]{:S(2)}) collective-permute-start(bf16[16,16,256]{2,1,0:T(8,128)(2,1)} %get-tuple-element.71), channel_id=1, source_target_pairs={{1,0},{2,1},{3,2},{4,3},{5,4},{6,5},{7,6},{9,8},{10,9},{11,10},{12... | collective-permute-start | bytes 393224 | tf_op jit(solution)/shard_map/ppermute | solution.py:537
  41.4 0.0 collective-permute-done.5.refs_5_
  41.4 3.4 %collective-permute-done.6.refs_6_ = bf16[16,16,256]{2,1,0:T(8,128)(2,1)S(1)} collective-permute-done((bf16[16,16,256]{2,1,0:T(8,128)(2,1)}, bf16[16,16,256]{2,1,0:T(8,128)(2,1)S(1)}, u32[]{:S(2)}, u32[]{:S(2)}) %collective-permute-start.6) | collective-permute-done | bytes 131104 | tf_op jit(solution)/shard_map/ppermute | solution.py:537
  44.8 0.6 copy-done.7
  45.4 9.1 %rim.1 = (bf16[5,2,32,256]{3,2,1,0:T(8,128)(2,1)}, bf16[5,2,32,256]{3,2,1,0:T(8,128)(2,1)}, bf16[5,2,32,256]{3,2,1,0:T(8,128)(2,1)}, bf16[5,2,32,256]{3,2,1,0:T(8,128)(2,1)}) custom-call(s32[1]{0:T(128)} %bitcast.me_ref, bf16[16,2,32,256]{3,2,1,0:T(8,128)(2,1)} %get-tuple-element.67.refs_0_, bf16[16,16,256]{2,1,0:T(8,128)(2,1)} %copy-done.4, ...), custom_call_target="tpu_custom_call" | custom-call | flops 1 | bytes 1 | tf_op jit(solution)/shard_map/rim/pallas_call | solution.py:322
  54.5 0.0 collective-permute-done.7.refs_6_
  54.5 2.5 %collective-permute-start.10 = (bf16[5,2,32,256]{3,2,1,0:T(8,128)(2,1)}, bf16[5,2,32,256]{3,2,1,0:T(8,128)(2,1)S(1)}, u32[]{:S(2)}, u32[]{:S(2)}) collective-permute-start(bf16[5,2,32,256]{3,2,1,0:T(8,128)(2,1)} %get-tuple-element.79), channel_id=1, source_target_pairs={{0,24},{8,16},{16,8},{24,0},{1,25},{9,17},{17,9},{25,1},{2,26},{10... | collective-permute-start | bytes 491528 | tf_op jit(solution)/shard_map/ppermute | solution.py:549
  57.0 0.5 collective-permute-start.9
  57.5 0.5 collective-permute-start.8
  58.0 6.8 %collective-permute-done.refs_2_ = bf16[5,15,2,16,256]{4,3,2,1,0:T(8,128)(2,1)} collective-permute-done((bf16[5,15,2,16,256]{4,3,2,1,0:T(8,128)(2,1)}, bf16[5,15,2,16,256]{4,3,2,1,0:T(8,128)(2,1)}, u32[]{:S(2)}, u32[]{:S(2)}) %collective-permute-start) | collective-permute-done | bytes 1228832 | tf_op jit(solution)/shard_map/ppermute | solution.py:549
  64.9 0.0 collective-permute-done.13.refs_4_
  64.9 1.5 %collective-permute-start.14 = (bf16[5,6,2,16,256]{4,3,2,1,0:T(8,128)(2,1)}, bf16[5,6,2,16,256]{4,3,2,1,0:T(8,128)(2,1)}, u32[]{:S(2)}, u32[]{:S(2)}) collective-permute-start(bf16[5,6,2,16,256]{4,3,2,1,0:T(8,128)(2,1)} %get-tuple-element.83), channel_id=1, source_target_pairs={{0,16},{8,24},{16,0},{24,8},{1,17},{9,25},{17,1},{25,9},{2,18},{10... | collective-permute-start | bytes 1474568 | tf_op jit(solution)/shard_map/ppermute | solution.py:549
  66.4 1.5 %collective-permute-start.1 = (bf16[5,6,2,16,256]{4,3,2,1,0:T(8,128)(2,1)}, bf16[5,6,2,16,256]{4,3,2,1,0:T(8,128)(2,1)}, u32[]{:S(2)}, u32[]{:S(2)}) collective-permute-start(bf16[5,6,2,16,256]{4,3,2,1,0:T(8,128)(2,1)} %get-tuple-element.64), channel_id=1, source_target_pairs={{0,8},{8,0},{16,24},{24,16},{1,9},{9,1},{17,25},{25,17},{2,10},{10... | collective-permute-start | bytes 1474568 | tf_op jit(solution)/shard_map/ppermute | solution.py:549
  67.9 0.0 collective-permute-done.10
  67.9 2.5 %collective-permute-done.9 = bf16[5,2,32,256]{3,2,1,0:T(8,128)(2,1)S(1)} collective-permute-done((bf16[5,2,32,256]{3,2,1,0:T(8,128)(2,1)}, bf16[5,2,32,256]{3,2,1,0:T(8,128)(2,1)S(1)}, u32[]{:S(2)}, u32[]{:S(2)}) %collective-permute-start.9) | collective-permute-done | bytes 163872 | tf_op jit(solution)/shard_map/ppermute | solution.py:549
  70.4 1.4 %collective-permute-done.8 = bf16[5,2,32,256]{3,2,1,0:T(8,128)(2,1)S(1)} collective-permute-done((bf16[5,2,32,256]{3,2,1,0:T(8,128)(2,1)}, bf16[5,2,32,256]{3,2,1,0:T(8,128)(2,1)S(1)}, u32[]{:S(2)}, u32[]{:S(2)}) %collective-permute-start.8) | collective-permute-done | bytes 163872 | tf_op jit(solution)/shard_map/ppermute | solution.py:549
  71.8 1.4 %collective-permute-start.15 = (bf16[5,6,2,16,256]{4,3,2,1,0:T(8,128)(2,1)}, bf16[5,6,2,16,256]{4,3,2,1,0:T(8,128)(2,1)}, u32[]{:S(2)}, u32[]{:S(2)}) collective-permute-start(bf16[5,6,2,16,256]{4,3,2,1,0:T(8,128)(2,1)} %get-tuple-element.86), channel_id=1, source_target_pairs={{0,24},{8,16},{16,8},{24,0},{1,25},{9,17},{17,9},{25,1},{2,26},{10... | collective-permute-start | bytes 1474568 | tf_op jit(solution)/shard_map/ppermute | solution.py:549
  73.3 1.0 pad_maximum_fusion.own
  74.3 1.3 %collective-permute-start.12 = (bf16[4,5,2,32,256]{4,3,2,1,0:T(8,128)(2,1)S(1)}, bf16[4,5,2,32,256]{4,3,2,1,0:T(8,128)(2,1)}, u32[]{:S(2)}, u32[]{:S(2)}) collective-permute-start(bf16[4,5,2,32,256]{4,3,2,1,0:T(8,128)(2,1)S(1)} %pad_maximum_fusion.own), channel_id=1, source_target_pairs={{1,0},{2,1},{3,2},{4,3},{5,4},{6,5},{7,6},{9,8},{10,9},{11,10},{12... | collective-permute-start | bytes 1966088 | tf_op jit(solution)/shard_map/ppermute | solution.py:537
  75.6 3.9 %collective-permute-start.11 = (bf16[4,5,2,32,256]{4,3,2,1,0:T(8,128)(2,1)S(1)}, bf16[4,5,2,32,256]{4,3,2,1,0:T(8,128)(2,1)}, u32[]{:S(2)}, u32[]{:S(2)}) collective-permute-start(bf16[4,5,2,32,256]{4,3,2,1,0:T(8,128)(2,1)S(1)} %pad_maximum_fusion.own), channel_id=1, source_target_pairs={{0,1},{1,2},{2,3},{3,4},{4,5},{5,6},{6,7},{8,9},{9,10},{10,11},{11... | collective-permute-start | bytes 1966088 | tf_op jit(solution)/shard_map/ppermute | solution.py:537
  79.5 2.3 %collective-permute-done.14.refs_5_ = bf16[5,6,2,16,256]{4,3,2,1,0:T(8,128)(2,1)} collective-permute-done((bf16[5,6,2,16,256]{4,3,2,1,0:T(8,128)(2,1)}, bf16[5,6,2,16,256]{4,3,2,1,0:T(8,128)(2,1)}, u32[]{:S(2)}, u32[]{:S(2)}) %collective-permute-start.14) | collective-permute-done | bytes 491552 | tf_op jit(solution)/shard_map/ppermute | solution.py:549
  81.7 2.0 %collective-permute-start.17 = (bf16[5,6,2,16,256]{4,3,2,1,0:T(8,128)(2,1)}, bf16[5,6,2,16,256]{4,3,2,1,0:T(8,128)(2,1)}, u32[]{:S(2)}, u32[]{:S(2)}) collective-permute-start(bf16[5,6,2,16,256]{4,3,2,1,0:T(8,128)(2,1)} %get-tuple-element.93), channel_id=1, source_target_pairs={{0,16},{8,24},{16,0},{24,8},{1,17},{9,25},{17,1},{25,9},{2,18},{10... | collective-permute-start | bytes 1474568 | tf_op jit(solution)/shard_map/ppermute | solution.py:549
  83.8 0.0 collective-permute-done.1.refs_3_
  83.8 1.5 %collective-permute-start.2 = (bf16[5,6,2,16,256]{4,3,2,1,0:T(8,128)(2,1)}, bf16[5,6,2,16,256]{4,3,2,1,0:T(8,128)(2,1)}, u32[]{:S(2)}, u32[]{:S(2)}) collective-permute-start(bf16[5,6,2,16,256]{4,3,2,1,0:T(8,128)(2,1)} %get-tuple-element.65), channel_id=1, source_target_pairs={{0,8},{8,0},{16,24},{24,16},{1,9},{9,1},{17,25},{25,17},{2,10},{10... | collective-permute-start | bytes 1474568 | tf_op jit(solution)/shard_map/ppermute | solution.py:549
  85.3 7.2 %collective-permute-done.15.refs_7_ = bf16[5,6,2,16,256]{4,3,2,1,0:T(8,128)(2,1)} collective-permute-done((bf16[5,6,2,16,256]{4,3,2,1,0:T(8,128)(2,1)}, bf16[5,6,2,16,256]{4,3,2,1,0:T(8,128)(2,1)}, u32[]{:S(2)}, u32[]{:S(2)}) %collective-permute-start.15) | collective-permute-done | bytes 491552 | tf_op jit(solution)/shard_map/ppermute | solution.py:549
  92.5 3.0 %collective-permute-start.19 = (bf16[5,6,2,16,256]{4,3,2,1,0:T(8,128)(2,1)}, bf16[5,6,2,16,256]{4,3,2,1,0:T(8,128)(2,1)}, u32[]{:S(2)}, u32[]{:S(2)}) collective-permute-start(bf16[5,6,2,16,256]{4,3,2,1,0:T(8,128)(2,1)} %get-tuple-element.97), channel_id=1, source_target_pairs={{0,24},{8,16},{16,8},{24,0},{1,25},{9,17},{17,9},{25,1},{2,26},{10... | collective-permute-start | bytes 1474568 | tf_op jit(solution)/shard_map/ppermute | solution.py:549
  95.4 5.7 %gram_1.1 = (f32[4,16,2,128,128]{4,3,2,1,0:T(8,128)}, f32[4,2,128,128]{3,2,1,0:T(8,128)}, f32[4,2,128,128]{3,2,1,0:T(8,128)}) custom-call(bf16[5,15,2,16,256]{4,3,2,1,0:T(8,128)(2,1)} %get-tuple-element.56.refs_0_, bf16[5,6,2,16,256]{4,3,2,1,0:T(8,128)(2,1)} %get-tuple-element.80.refs_1_, bf16[5,15,2,16,256]{4,3,2,1,0:T(8,128)(2,1)} %collective-permute-done.refs_2_, ...), custom_call_target="tpu_custom_call" | custom-call | flops 1 | bytes 1 | tf_op jit(solution)/shard_map/gram_1/pallas_call | solution.py:513
  101.2 0.0 collective-permute-done.12.after
  101.2 3.8 %rim_gram.1 = (f32[4,16,2,128,128]{4,3,2,1,0:T(8,128)}, f32[4,2,128,128]{3,2,1,0:T(8,128)}) custom-call(s32[1]{0:T(128)} %bitcast.me_ref, bf16[4,5,2,32,256]{4,3,2,1,0:T(8,128)(2,1)} %copy-done, bf16[4,5,2,32,256]{4,3,2,1,0:T(8,128)(2,1)} %collective-permute-done.11.before, ...), custom_call_target="tpu_custom_call", output_to_operand_aliasing={{0}: (5, {})} | custom-call | flops 1 | bytes 1 | tf_op jit(solution)/shard_map/rim_gram/pallas_call | solution.py:394
  105.0 0.6 collective-permute-start.18
  105.6 0.8 collective-permute-start.16
  106.5 7.1 %collective-permute-done.19.refs_7_ = bf16[5,6,2,16,256]{4,3,2,1,0:T(8,128)(2,1)} collective-permute-done((bf16[5,6,2,16,256]{4,3,2,1,0:T(8,128)(2,1)}, bf16[5,6,2,16,256]{4,3,2,1,0:T(8,128)(2,1)}, u32[]{:S(2)}, u32[]{:S(2)}) %collective-permute-start.19) | collective-permute-done | bytes 491552 | tf_op jit(solution)/shard_map/ppermute | solution.py:549
  113.6 3.0 %collective-permute-start.20 = (bf16[5,3,2,16,256]{4,3,2,1,0:T(8,128)(2,1)S(1)}, bf16[5,3,2,16,256]{4,3,2,1,0:T(8,128)(2,1)S(1)}, u32[]{:S(2)}, u32[]{:S(2)}) collective-permute-start(bf16[5,3,2,16,256]{4,3,2,1,0:T(8,128)(2,1)S(1)} %copy-done.8), channel_id=1, source_target_pairs={{0,24},{8,16},{16,8},{24,0},{1,25},{9,17},{17,9},{25,1},{2,26},{10... | collective-permute-start | bytes 737288 | tf_op jit(solution)/shard_map/ppermute | solution.py:549
  116.6 5.6 %gram_7.1 = (f32[4,16,2,128,128]{4,3,2,1,0:T(8,128)}, f32[4,2,128,128]{3,2,1,0:T(8,128)}) custom-call(bf16[5,15,2,16,256]{4,3,2,1,0:T(8,128)(2,1)} %get-tuple-element.56.refs_0_, bf16[5,6,2,16,256]{4,3,2,1,0:T(8,128)(2,1)} %get-tuple-element.99.refs_1_, bf16[5,15,2,16,256]{4,3,2,1,0:T(8,128)(2,1)} %collective-permute-done.refs_2_, ...), custom_call_target="tpu_custom_call", output_to_operand_aliasing={{0}: (10, {})} | custom-call | flops 1 | bytes 1 | tf_op jit(solution)/shard_map/gram_7/pallas_call | solution.py:513
  122.2 1.0 collective-permute-done.20.refs_7_
  123.2 0.7 copy-done.3
  123.9 3.9 %gram_13.1 = (f32[4,16,2,128,128]{4,3,2,1,0:T(8,128)}, f32[4,2,128,128]{3,2,1,0:T(8,128)}) custom-call(bf16[5,15,2,16,256]{4,3,2,1,0:T(8,128)(2,1)} %get-tuple-element.56.refs_0_, bf16[5,3,2,16,256]{4,3,2,1,0:T(8,128)(2,1)} %get-tuple-element.59.refs_1_, bf16[5,15,2,16,256]{4,3,2,1,0:T(8,128)(2,1)} %collective-permute-done.refs_2_, ...), custom_call_target="tpu_custom_call", output_to_operand_aliasing={{0}: (10, {})} | custom-call | flops 1 | bytes 1 | tf_op jit(solution)/shard_map/gram_13/pallas_call | solution.py:513
  (21 shorter events, 0.0 us)
Async XLA Ops:
  5.8 48.7 %collective-permute-start.7 = (bf16[5,15,2,16,256]{4,3,2,1,0:T(8,128)(2,1)}, bf16[5,15,2,16,256]{4,3,2,1,0:T(8,128)(2,1)}, u32[]{:S(2)}, u32[]{:S(2)}) collective-permute-start(bf16[5,15,2,16,256]{4,3,2,1,0:T(8,128)(2,1)} %interior_0_3.1), channel_id=1, source_target_pairs={{0,24},{8,16},{16,8},{24,0},{1,25},{9,17},{17,9},{25,1},{2,26},{10... | collective-permute-start | bytes 3686408 | tf_op jit(solution)/shard_map/ppermute | solution.py:549
  20.2 44.7 %collective-permute-start = (bf16[5,15,2,16,256]{4,3,2,1,0:T(8,128)(2,1)}, bf16[5,15,2,16,256]{4,3,2,1,0:T(8,128)(2,1)}, u32[]{:S(2)}, u32[]{:S(2)}) collective-permute-start(bf16[5,15,2,16,256]{4,3,2,1,0:T(8,128)(2,1)} %get-tuple-element.60), channel_id=1, source_target_pairs={{0,8},{8,0},{16,24},{24,16},{1,9},{9,1},{17,25},{25,17},{2,10},{10... | collective-permute-start | bytes 3686408 | tf_op jit(solution)/shard_map/ppermute | solution.py:549
  20.8 44.1 %collective-permute-start.13 = (bf16[5,15,2,16,256]{4,3,2,1,0:T(8,128)(2,1)}, bf16[5,15,2,16,256]{4,3,2,1,0:T(8,128)(2,1)}, u32[]{:S(2)}, u32[]{:S(2)}) collective-permute-start(bf16[5,15,2,16,256]{4,3,2,1,0:T(8,128)(2,1)} %get-tuple-element.81), channel_id=1, source_target_pairs={{0,16},{8,24},{16,0},{24,8},{1,17},{9,25},{17,1},{25,9},{2,18},{10... | collective-permute-start | bytes 3686408 | tf_op jit(solution)/shard_map/ppermute | solution.py:549
  20.9 13.9 %collective-permute-start.3 = (bf16[16,16,256]{2,1,0:T(8,128)(2,1)}, bf16[16,16,256]{2,1,0:T(8,128)(2,1)S(1)}, u32[]{:S(2)}, u32[]{:S(2)}) collective-permute-start(bf16[16,16,256]{2,1,0:T(8,128)(2,1)} %get-tuple-element.68), channel_id=1, source_target_pairs={{0,1},{1,2},{2,3},{3,4},{4,5},{5,6},{6,7},{8,9},{9,10},{10,11},{11... | collective-permute-start | bytes 393224 | tf_op jit(solution)/shard_map/ppermute | solution.py:537
  22.2 17.9 %collective-permute-start.4 = (bf16[16,16,256]{2,1,0:T(8,128)(2,1)}, bf16[16,16,256]{2,1,0:T(8,128)(2,1)S(1)}, u32[]{:S(2)}, u32[]{:S(2)}) collective-permute-start(bf16[16,16,256]{2,1,0:T(8,128)(2,1)} %get-tuple-element.57), channel_id=1, source_target_pairs={{1,0},{2,1},{3,2},{4,3},{5,4},{6,5},{7,6},{9,8},{10,9},{11,10},{12... | collective-permute-start | bytes 393224 | tf_op jit(solution)/shard_map/ppermute | solution.py:537
  34.8 10.0 %copy-start.4 = (bf16[16,16,256]{2,1,0:T(8,128)(2,1)}, bf16[16,16,256]{2,1,0:T(8,128)(2,1)S(1)}, u32[]{:S(2)}) copy-start(bf16[16,16,256]{2,1,0:T(8,128)(2,1)S(1)} %collective-permute-done.3.refs_1_) | copy-start | bytes 393220
  34.8 6.6 %collective-permute-start.5 = (bf16[16,16,256]{2,1,0:T(8,128)(2,1)}, bf16[16,16,256]{2,1,0:T(8,128)(2,1)S(1)}, u32[]{:S(2)}, u32[]{:S(2)}) collective-permute-start(bf16[16,16,256]{2,1,0:T(8,128)(2,1)} %get-tuple-element.70), channel_id=1, source_target_pairs={{0,1},{1,2},{2,3},{3,4},{4,5},{5,6},{6,7},{8,9},{9,10},{10,11},{11... | collective-permute-start | bytes 393224 | tf_op jit(solution)/shard_map/ppermute | solution.py:537
  40.1 4.7 %copy-start.5 = (bf16[16,16,256]{2,1,0:T(8,128)(2,1)}, bf16[16,16,256]{2,1,0:T(8,128)(2,1)S(1)}, u32[]{:S(2)}) copy-start(bf16[16,16,256]{2,1,0:T(8,128)(2,1)S(1)} %collective-permute-done.4.refs_2_) | copy-start | bytes 393220
  40.1 4.7 %collective-permute-start.6 = (bf16[16,16,256]{2,1,0:T(8,128)(2,1)}, bf16[16,16,256]{2,1,0:T(8,128)(2,1)S(1)}, u32[]{:S(2)}, u32[]{:S(2)}) collective-permute-start(bf16[16,16,256]{2,1,0:T(8,128)(2,1)} %get-tuple-element.71), channel_id=1, source_target_pairs={{1,0},{2,1},{3,2},{4,3},{5,4},{6,5},{7,6},{9,8},{10,9},{11,10},{12... | collective-permute-start | bytes 393224 | tf_op jit(solution)/shard_map/ppermute | solution.py:537
  41.4 3.4 %copy-start.6 = (bf16[16,16,256]{2,1,0:T(8,128)(2,1)}, bf16[16,16,256]{2,1,0:T(8,128)(2,1)S(1)}, u32[]{:S(2)}) copy-start(bf16[16,16,256]{2,1,0:T(8,128)(2,1)S(1)} %collective-permute-done.5.refs_5_) | copy-start | bytes 393220
  44.8 0.7 copy-start.7
  54.5 13.4 %collective-permute-start.10 = (bf16[5,2,32,256]{3,2,1,0:T(8,128)(2,1)}, bf16[5,2,32,256]{3,2,1,0:T(8,128)(2,1)S(1)}, u32[]{:S(2)}, u32[]{:S(2)}) collective-permute-start(bf16[5,2,32,256]{3,2,1,0:T(8,128)(2,1)} %get-tuple-element.79), channel_id=1, source_target_pairs={{0,24},{8,16},{16,8},{24,0},{1,25},{9,17},{17,9},{25,1},{2,26},{10... | collective-permute-start | bytes 491528 | tf_op jit(solution)/shard_map/ppermute | solution.py:549
  57.0 13.4 %collective-permute-start.9 = (bf16[5,2,32,256]{3,2,1,0:T(8,128)(2,1)}, bf16[5,2,32,256]{3,2,1,0:T(8,128)(2,1)S(1)}, u32[]{:S(2)}, u32[]{:S(2)}) collective-permute-start(bf16[5,2,32,256]{3,2,1,0:T(8,128)(2,1)} %get-tuple-element.77), channel_id=1, source_target_pairs={{0,16},{8,24},{16,0},{24,8},{1,17},{9,25},{17,1},{25,9},{2,18},{10... | collective-permute-start | bytes 491528 | tf_op jit(solution)/shard_map/ppermute | solution.py:549
  57.5 14.3 %collective-permute-start.8 = (bf16[5,2,32,256]{3,2,1,0:T(8,128)(2,1)}, bf16[5,2,32,256]{3,2,1,0:T(8,128)(2,1)S(1)}, u32[]{:S(2)}, u32[]{:S(2)}) collective-permute-start(bf16[5,2,32,256]{3,2,1,0:T(8,128)(2,1)} %get-tuple-element.75), channel_id=1, source_target_pairs={{0,8},{8,0},{16,24},{24,16},{1,9},{9,1},{17,25},{25,17},{2,10},{10... | collective-permute-start | bytes 491528 | tf_op jit(solution)/shard_map/ppermute | solution.py:549
  64.9 16.9 %collective-permute-start.14 = (bf16[5,6,2,16,256]{4,3,2,1,0:T(8,128)(2,1)}, bf16[5,6,2,16,256]{4,3,2,1,0:T(8,128)(2,1)}, u32[]{:S(2)}, u32[]{:S(2)}) collective-permute-start(bf16[5,6,2,16,256]{4,3,2,1,0:T(8,128)(2,1)} %get-tuple-element.83), channel_id=1, source_target_pairs={{0,16},{8,24},{16,0},{24,8},{1,17},{9,25},{17,1},{25,9},{2,18},{10... | collective-permute-start | bytes 1474568 | tf_op jit(solution)/shard_map/ppermute | solution.py:549
  66.4 17.4 %collective-permute-start.1 = (bf16[5,6,2,16,256]{4,3,2,1,0:T(8,128)(2,1)}, bf16[5,6,2,16,256]{4,3,2,1,0:T(8,128)(2,1)}, u32[]{:S(2)}, u32[]{:S(2)}) collective-permute-start(bf16[5,6,2,16,256]{4,3,2,1,0:T(8,128)(2,1)} %get-tuple-element.64), channel_id=1, source_target_pairs={{0,8},{8,0},{16,24},{24,16},{1,9},{9,1},{17,25},{25,17},{2,10},{10... | collective-permute-start | bytes 1474568 | tf_op jit(solution)/shard_map/ppermute | solution.py:549
  71.8 20.7 %collective-permute-start.15 = (bf16[5,6,2,16,256]{4,3,2,1,0:T(8,128)(2,1)}, bf16[5,6,2,16,256]{4,3,2,1,0:T(8,128)(2,1)}, u32[]{:S(2)}, u32[]{:S(2)}) collective-permute-start(bf16[5,6,2,16,256]{4,3,2,1,0:T(8,128)(2,1)} %get-tuple-element.86), channel_id=1, source_target_pairs={{0,24},{8,16},{16,8},{24,0},{1,25},{9,17},{17,9},{25,1},{2,26},{10... | collective-permute-start | bytes 1474568 | tf_op jit(solution)/shard_map/ppermute | solution.py:549
  74.3 26.9 %copy-start = (bf16[4,5,2,32,256]{4,3,2,1,0:T(8,128)(2,1)}, bf16[4,5,2,32,256]{4,3,2,1,0:T(8,128)(2,1)S(1)}, u32[]{:S(2)}) copy-start(bf16[4,5,2,32,256]{4,3,2,1,0:T(8,128)(2,1)S(1)} %pad_maximum_fusion.own) | copy-start | bytes 1966084
  74.3 26.9 %collective-permute-start.12 = (bf16[4,5,2,32,256]{4,3,2,1,0:T(8,128)(2,1)S(1)}, bf16[4,5,2,32,256]{4,3,2,1,0:T(8,128)(2,1)}, u32[]{:S(2)}, u32[]{:S(2)}) collective-permute-start(bf16[4,5,2,32,256]{4,3,2,1,0:T(8,128)(2,1)S(1)} %pad_maximum_fusion.own), channel_id=1, source_target_pairs={{1,0},{2,1},{3,2},{4,3},{5,4},{6,5},{7,6},{9,8},{10,9},{11,10},{12... | collective-permute-start | bytes 1966088 | tf_op jit(solution)/shard_map/ppermute | solution.py:537
  75.6 25.6 %collective-permute-start.11 = (bf16[4,5,2,32,256]{4,3,2,1,0:T(8,128)(2,1)S(1)}, bf16[4,5,2,32,256]{4,3,2,1,0:T(8,128)(2,1)}, u32[]{:S(2)}, u32[]{:S(2)}) collective-permute-start(bf16[4,5,2,32,256]{4,3,2,1,0:T(8,128)(2,1)S(1)} %pad_maximum_fusion.own), channel_id=1, source_target_pairs={{0,1},{1,2},{2,3},{3,4},{4,5},{5,6},{6,7},{8,9},{9,10},{10,11},{11... | collective-permute-start | bytes 1966088 | tf_op jit(solution)/shard_map/ppermute | solution.py:537
  81.7 23.3 %collective-permute-start.17 = (bf16[5,6,2,16,256]{4,3,2,1,0:T(8,128)(2,1)}, bf16[5,6,2,16,256]{4,3,2,1,0:T(8,128)(2,1)}, u32[]{:S(2)}, u32[]{:S(2)}) collective-permute-start(bf16[5,6,2,16,256]{4,3,2,1,0:T(8,128)(2,1)} %get-tuple-element.93), channel_id=1, source_target_pairs={{0,16},{8,24},{16,0},{24,8},{1,17},{9,25},{17,1},{25,9},{2,18},{10... | collective-permute-start | bytes 1474568 | tf_op jit(solution)/shard_map/ppermute | solution.py:549
  83.8 21.9 %collective-permute-start.2 = (bf16[5,6,2,16,256]{4,3,2,1,0:T(8,128)(2,1)}, bf16[5,6,2,16,256]{4,3,2,1,0:T(8,128)(2,1)}, u32[]{:S(2)}, u32[]{:S(2)}) collective-permute-start(bf16[5,6,2,16,256]{4,3,2,1,0:T(8,128)(2,1)} %get-tuple-element.65), channel_id=1, source_target_pairs={{0,8},{8,0},{16,24},{24,16},{1,9},{9,1},{17,25},{25,17},{2,10},{10... | collective-permute-start | bytes 1474568 | tf_op jit(solution)/shard_map/ppermute | solution.py:549
  92.5 21.1 %collective-permute-start.19 = (bf16[5,6,2,16,256]{4,3,2,1,0:T(8,128)(2,1)}, bf16[5,6,2,16,256]{4,3,2,1,0:T(8,128)(2,1)}, u32[]{:S(2)}, u32[]{:S(2)}) collective-permute-start(bf16[5,6,2,16,256]{4,3,2,1,0:T(8,128)(2,1)} %get-tuple-element.97), channel_id=1, source_target_pairs={{0,24},{8,16},{16,8},{24,0},{1,25},{9,17},{17,9},{25,1},{2,26},{10... | collective-permute-start | bytes 1474568 | tf_op jit(solution)/shard_map/ppermute | solution.py:549
  101.2 12.4 %copy-start.8 = (bf16[5,3,2,16,256]{4,3,2,1,0:T(8,128)(2,1)S(1)}, bf16[5,3,2,16,256]{4,3,2,1,0:T(8,128)(2,1)}, u32[]{:S(2)}) copy-start(bf16[5,3,2,16,256]{4,3,2,1,0:T(8,128)(2,1)} %get-tuple-element.98) | copy-start | bytes 737284
  105.0 17.1 %collective-permute-start.18 = (bf16[5,3,2,16,256]{4,3,2,1,0:T(8,128)(2,1)}, bf16[5,3,2,16,256]{4,3,2,1,0:T(8,128)(2,1)S(1)}, u32[]{:S(2)}, u32[]{:S(2)}) collective-permute-start(bf16[5,3,2,16,256]{4,3,2,1,0:T(8,128)(2,1)} %get-tuple-element.94), channel_id=1, source_target_pairs={{0,16},{8,24},{16,0},{24,8},{1,17},{9,25},{17,1},{25,9},{2,18},{10... | collective-permute-start | bytes 737288 | tf_op jit(solution)/shard_map/ppermute | solution.py:549
  105.6 16.6 %collective-permute-start.16 = (bf16[5,3,2,16,256]{4,3,2,1,0:T(8,128)(2,1)}, bf16[5,3,2,16,256]{4,3,2,1,0:T(8,128)(2,1)S(1)}, u32[]{:S(2)}, u32[]{:S(2)}) collective-permute-start(bf16[5,3,2,16,256]{4,3,2,1,0:T(8,128)(2,1)} %get-tuple-element.90), channel_id=1, source_target_pairs={{0,8},{8,0},{16,24},{24,16},{1,9},{9,1},{17,25},{25,17},{2,10},{10... | collective-permute-start | bytes 737288 | tf_op jit(solution)/shard_map/ppermute | solution.py:549
  113.6 9.6 %collective-permute-start.20 = (bf16[5,3,2,16,256]{4,3,2,1,0:T(8,128)(2,1)S(1)}, bf16[5,3,2,16,256]{4,3,2,1,0:T(8,128)(2,1)S(1)}, u32[]{:S(2)}, u32[]{:S(2)}) collective-permute-start(bf16[5,3,2,16,256]{4,3,2,1,0:T(8,128)(2,1)S(1)} %copy-done.8), channel_id=1, source_target_pairs={{0,24},{8,16},{16,8},{24,0},{1,25},{9,17},{17,9},{25,1},{2,26},{10... | collective-permute-start | bytes 737288 | tf_op jit(solution)/shard_map/ppermute | solution.py:549
  122.2 1.0 copy-start.1
  122.2 1.0 copy-start.2
  123.2 0.7 copy-start.3

commit v5 on v4

--- a/solution.py
+++ b/solution.py
@@ -14,7 +14,7 @@
 SUB = 8
 DBLK = 16
 EPS = 1e-06
-VMEM = 63 * 1024 * 1024
+VMEM = 62 * 1024 * 1024
 COST = pl.CostEstimate(flops=1, bytes_accessed=1, transcendentals=0)
 
 bf16 = jnp.bfloat16
@@ -547,6 +547,8 @@
         if k == 1 and gates:
             block = after(block, *gates)
         got.append(lax.ppermute(block, "date", [(i, i ^ k) for i in range(n)]))
+    if gates:
+        got = got[:1] + [pltpu.with_memory_space_constraint(x, pltpu.VMEM) for x in got[1:]]
     return got
 
 

time: 128 us -> 127 us (level)
  no operation moved by 1% of the time
where the time goes in v5:
time: 127 us
  Pallas kernels  55.5 us (44%)
  starting transfers between devices  37.8 us (30%)
  waiting for transfers between devices  31.8 us (25%)
    ppermute x15, waiting for transfers between devices, exchange(): got.append(lax.ppermute(block, 'date', [(i, i ^ k) for i in range(n)]))  28.5 us
    pallas_call x3, Pallas kernels, interior(): pl.pallas_call(functools.partial(interior_kernel, spans, targets, edged,...  27.4 us
    ppermute x15, starting transfers between devices, exchange(): got.append(lax.ppermute(block, 'date', [(i, i ^ k) for i in range(n)]))  23.4 us
    pallas_call x3, Pallas kernels, gram(): pl.pallas_call(functools.partial(gram_kernel, partners, parts, offsets, c...  15.2 us
    ppermute x6, starting transfers between devices, shift(): return lax.ppermute(value, axis, pairs)  14.4 us
    pallas_call x1, Pallas kernels, rim(): pl.pallas_call(functools.partial(rim_kernel, dest_rows, parts), grid_spec...  9.07 us
    pallas_call x1, Pallas kernels, rim_gram(): pl.pallas_call(rim_gram_kernel, in_specs=[pl.BlockSpec(memory_space=pltpu...  3.81 us
    ppermute x6, waiting for transfers between devices, shift(): return lax.ppermute(value, axis, pairs)  3.38 us
  transfers between devices with their start and end apart: 21, of which 8 were waited for; matrix products, arithmetic and copies ran while one was open for 1% of the time, Pallas kernels for 36%

profile of v5, /device:TPU:0, one launch (start us, length us, event | category | flops | bytes accessed | tf_op | source)
XLA Modules:
  0.0 127.0 jit_solution(13641646220146768031)
XLA Ops:
  0.0 5.8 %interior_0_3.1 = bf16[5,15,2,16,256]{4,3,2,1,0:T(8,128)(2,1)} custom-call(s32[1]{0:T(128)} %bitcast.me_ref, bf16[2,32,256,256]{3,2,1,0:T(8,128)(2,1)} %slc_any.5, bf16[32,256,256]{2,1,0:T(8,128)(2,1)} %rk_any.5, bf16[32,272,256]{2,1,0:T(8,128)(2,1)} %refs_7_.1), custom_call_target="tpu_custom_call" | custom-call | flops 1 | bytes 1 | tf_op jit(solution)/shard_map/interior_0_3/pallas_call | solution.py:207
  5.8 4.0 %collective-permute-start.7 = (bf16[5,15,2,16,256]{4,3,2,1,0:T(8,128)(2,1)}, bf16[5,15,2,16,256]{4,3,2,1,0:T(8,128)(2,1)S(1)}, u32[]{:S(2)}, u32[]{:S(2)}) collective-permute-start(bf16[5,15,2,16,256]{4,3,2,1,0:T(8,128)(2,1)} %interior_0_3.1), channel_id=1, source_target_pairs={{0,24},{8,16},{16,8},{24,0},{1,25},{9,17},{17,9},{25,1},{2,26},{10... | collective-permute-start | bytes 3686408 | tf_op jit(solution)/shard_map/ppermute | solution.py:549
  9.7 10.4 %interior_0_1.1 = (bf16[16,2,32,256]{3,2,1,0:T(8,128)(2,1)}, bf16[16,16,256]{2,1,0:T(8,128)(2,1)}, bf16[16,16,256]{2,1,0:T(8,128)(2,1)}, bf16[5,15,2,16,256]{4,3...) custom-call(s32[1]{0:T(128)} %bitcast.me_ref, ...), custom_call_target="tpu_custom_call" | custom-call | flops 1 | bytes 1 | tf_op jit(solution)/shard_map/interior_0_1/pallas_call | solution.py:207
  20.2 0.6 collective-permute-start
  20.8 0.1 collective-permute-start.13
  20.8 1.3 %collective-permute-start.3 = (bf16[16,16,256]{2,1,0:T(8,128)(2,1)}, bf16[16,16,256]{2,1,0:T(8,128)(2,1)S(1)}, u32[]{:S(2)}, u32[]{:S(2)}) collective-permute-start(bf16[16,16,256]{2,1,0:T(8,128)(2,1)} %get-tuple-element.68), channel_id=1, source_target_pairs={{0,1},{1,2},{2,3},{3,4},{4,5},{5,6},{6,7},{8,9},{9,10},{10,11},{11... | collective-permute-start | bytes 393224 | tf_op jit(solution)/shard_map/ppermute | solution.py:537
  22.1 1.3 %collective-permute-start.4 = (bf16[16,16,256]{2,1,0:T(8,128)(2,1)}, bf16[16,16,256]{2,1,0:T(8,128)(2,1)S(1)}, u32[]{:S(2)}, u32[]{:S(2)}) collective-permute-start(bf16[16,16,256]{2,1,0:T(8,128)(2,1)} %get-tuple-element.57), channel_id=1, source_target_pairs={{1,0},{2,1},{3,2},{4,3},{5,4},{6,5},{7,6},{9,8},{10,9},{11,10},{12... | collective-permute-start | bytes 393224 | tf_op jit(solution)/shard_map/ppermute | solution.py:537
  23.4 11.2 %interior_1_1.1 = (bf16[16,2,32,256]{3,2,1,0:T(8,128)(2,1)}, bf16[16,16,256]{2,1,0:T(8,128)(2,1)}, bf16[16,16,256]{2,1,0:T(8,128)(2,1)}, bf16[5,6,2,16,256]{4,3,...) custom-call(s32[1]{0:T(128)} %bitcast.me_ref, ...), custom_call_target="tpu_custom_call" | custom-call | flops 1 | bytes 1 | tf_op jit(solution)/shard_map/interior_1_1/pallas_call | solution.py:207
  34.6 0.0 collective-permute-done.3.refs_1_
  34.7 5.3 %collective-permute-start.5 = (bf16[16,16,256]{2,1,0:T(8,128)(2,1)}, bf16[16,16,256]{2,1,0:T(8,128)(2,1)S(1)}, u32[]{:S(2)}, u32[]{:S(2)}) collective-permute-start(bf16[16,16,256]{2,1,0:T(8,128)(2,1)} %get-tuple-element.70), channel_id=1, source_target_pairs={{0,1},{1,2},{2,3},{3,4},{4,5},{5,6},{6,7},{8,9},{9,10},{10,11},{11... | collective-permute-start | bytes 393224 | tf_op jit(solution)/shard_map/ppermute | solution.py:537
  40.0 0.0 collective-permute-done.4.refs_2_
  40.0 1.3 %collective-permute-start.6 = (bf16[16,16,256]{2,1,0:T(8,128)(2,1)}, bf16[16,16,256]{2,1,0:T(8,128)(2,1)S(1)}, u32[]{:S(2)}, u32[]{:S(2)}) collective-permute-start(bf16[16,16,256]{2,1,0:T(8,128)(2,1)} %get-tuple-element.71), channel_id=1, source_target_pairs={{1,0},{2,1},{3,2},{4,3},{5,4},{6,5},{7,6},{9,8},{10,9},{11,10},{12... | collective-permute-start | bytes 393224 | tf_op jit(solution)/shard_map/ppermute | solution.py:537
  41.3 3.4 %collective-permute-done.6.refs_6_ = bf16[16,16,256]{2,1,0:T(8,128)(2,1)S(1)} collective-permute-done((bf16[16,16,256]{2,1,0:T(8,128)(2,1)}, bf16[16,16,256]{2,1,0:T(8,128)(2,1)S(1)}, u32[]{:S(2)}, u32[]{:S(2)}) %collective-permute-start.6) | collective-permute-done | bytes 131104 | tf_op jit(solution)/shard_map/ppermute | solution.py:537
  44.7 0.6 copy-done.5
  45.3 9.1 %rim.1 = (bf16[5,2,32,256]{3,2,1,0:T(8,128)(2,1)}, bf16[5,2,32,256]{3,2,1,0:T(8,128)(2,1)}, bf16[5,2,32,256]{3,2,1,0:T(8,128)(2,1)}, bf16[5,2,32,256]{3,2,1,0:T(8,128)(2,1)}) custom-call(s32[1]{0:T(128)} %bitcast.me_ref, bf16[16,2,32,256]{3,2,1,0:T(8,128)(2,1)} %get-tuple-element.67.refs_0_, bf16[16,16,256]{2,1,0:T(8,128)(2,1)} %copy-done.2, ...), custom_call_target="tpu_custom_call" | custom-call | flops 1 | bytes 1 | tf_op jit(solution)/shard_map/rim/pallas_call | solution.py:322
  54.4 0.0 collective-permute-done.7.refs_6_
  54.4 2.5 %collective-permute-start.10 = (bf16[5,2,32,256]{3,2,1,0:T(8,128)(2,1)}, bf16[5,2,32,256]{3,2,1,0:T(8,128)(2,1)S(1)}, u32[]{:S(2)}, u32[]{:S(2)}) collective-permute-start(bf16[5,2,32,256]{3,2,1,0:T(8,128)(2,1)} %get-tuple-element.79), channel_id=1, source_target_pairs={{0,24},{8,16},{16,8},{24,0},{1,25},{9,17},{17,9},{25,1},{2,26},{10... | collective-permute-start | bytes 491528 | tf_op jit(solution)/shard_map/ppermute | solution.py:549
  56.9 0.5 collective-permute-start.9
  57.4 0.5 collective-permute-start.8
  57.9 6.9 %collective-permute-done.refs_2_ = bf16[5,15,2,16,256]{4,3,2,1,0:T(8,128)(2,1)} collective-permute-done((bf16[5,15,2,16,256]{4,3,2,1,0:T(8,128)(2,1)}, bf16[5,15,2,16,256]{4,3,2,1,0:T(8,128)(2,1)}, u32[]{:S(2)}, u32[]{:S(2)}) %collective-permute-start) | collective-permute-done | bytes 1228832 | tf_op jit(solution)/shard_map/ppermute | solution.py:549
  64.8 0.0 collective-permute-done.13.refs_4_
  64.8 1.5 %collective-permute-start.14 = (bf16[5,6,2,16,256]{4,3,2,1,0:T(8,128)(2,1)}, bf16[5,6,2,16,256]{4,3,2,1,0:T(8,128)(2,1)}, u32[]{:S(2)}, u32[]{:S(2)}) collective-permute-start(bf16[5,6,2,16,256]{4,3,2,1,0:T(8,128)(2,1)} %get-tuple-element.83), channel_id=1, source_target_pairs={{0,16},{8,24},{16,0},{24,8},{1,17},{9,25},{17,1},{25,9},{2,18},{10... | collective-permute-start | bytes 1474568 | tf_op jit(solution)/shard_map/ppermute | solution.py:549
  66.4 1.5 %collective-permute-start.1 = (bf16[5,6,2,16,256]{4,3,2,1,0:T(8,128)(2,1)}, bf16[5,6,2,16,256]{4,3,2,1,0:T(8,128)(2,1)}, u32[]{:S(2)}, u32[]{:S(2)}) collective-permute-start(bf16[5,6,2,16,256]{4,3,2,1,0:T(8,128)(2,1)} %get-tuple-element.64), channel_id=1, source_target_pairs={{0,8},{8,0},{16,24},{24,16},{1,9},{9,1},{17,25},{25,17},{2,10},{10... | collective-permute-start | bytes 1474568 | tf_op jit(solution)/shard_map/ppermute | solution.py:549
  67.9 0.0 collective-permute-done.10
  67.9 2.5 %collective-permute-done.9 = bf16[5,2,32,256]{3,2,1,0:T(8,128)(2,1)S(1)} collective-permute-done((bf16[5,2,32,256]{3,2,1,0:T(8,128)(2,1)}, bf16[5,2,32,256]{3,2,1,0:T(8,128)(2,1)S(1)}, u32[]{:S(2)}, u32[]{:S(2)}) %collective-permute-start.9) | collective-permute-done | bytes 163872 | tf_op jit(solution)/shard_map/ppermute | solution.py:549
  70.4 1.4 %collective-permute-done.8 = bf16[5,2,32,256]{3,2,1,0:T(8,128)(2,1)S(1)} collective-permute-done((bf16[5,2,32,256]{3,2,1,0:T(8,128)(2,1)}, bf16[5,2,32,256]{3,2,1,0:T(8,128)(2,1)S(1)}, u32[]{:S(2)}, u32[]{:S(2)}) %collective-permute-start.8) | collective-permute-done | bytes 163872 | tf_op jit(solution)/shard_map/ppermute | solution.py:549
  71.8 1.4 %collective-permute-start.15 = (bf16[5,6,2,16,256]{4,3,2,1,0:T(8,128)(2,1)}, bf16[5,6,2,16,256]{4,3,2,1,0:T(8,128)(2,1)}, u32[]{:S(2)}, u32[]{:S(2)}) collective-permute-start(bf16[5,6,2,16,256]{4,3,2,1,0:T(8,128)(2,1)} %get-tuple-element.86), channel_id=1, source_target_pairs={{0,24},{8,16},{16,8},{24,0},{1,25},{9,17},{17,9},{25,1},{2,26},{10... | collective-permute-start | bytes 1474568 | tf_op jit(solution)/shard_map/ppermute | solution.py:549
  73.2 1.0 pad_maximum_fusion.own
  74.2 1.3 %collective-permute-start.12 = (bf16[4,5,2,32,256]{4,3,2,1,0:T(8,128)(2,1)S(1)}, bf16[4,5,2,32,256]{4,3,2,1,0:T(8,128)(2,1)}, u32[]{:S(2)}, u32[]{:S(2)}) collective-permute-start(bf16[4,5,2,32,256]{4,3,2,1,0:T(8,128)(2,1)S(1)} %pad_maximum_fusion.own), channel_id=1, source_target_pairs={{1,0},{2,1},{3,2},{4,3},{5,4},{6,5},{7,6},{9,8},{10,9},{11,10},{12... | collective-permute-start | bytes 1966088 | tf_op jit(solution)/shard_map/ppermute | solution.py:537
  75.5 3.9 %collective-permute-start.11 = (bf16[4,5,2,32,256]{4,3,2,1,0:T(8,128)(2,1)S(1)}, bf16[4,5,2,32,256]{4,3,2,1,0:T(8,128)(2,1)}, u32[]{:S(2)}, u32[]{:S(2)}) collective-permute-start(bf16[4,5,2,32,256]{4,3,2,1,0:T(8,128)(2,1)S(1)} %pad_maximum_fusion.own), channel_id=1, source_target_pairs={{0,1},{1,2},{2,3},{3,4},{4,5},{5,6},{6,7},{8,9},{9,10},{10,11},{11... | collective-permute-start | bytes 1966088 | tf_op jit(solution)/shard_map/ppermute | solution.py:537
  79.4 2.3 %collective-permute-done.14.refs_5_ = bf16[5,6,2,16,256]{4,3,2,1,0:T(8,128)(2,1)} collective-permute-done((bf16[5,6,2,16,256]{4,3,2,1,0:T(8,128)(2,1)}, bf16[5,6,2,16,256]{4,3,2,1,0:T(8,128)(2,1)}, u32[]{:S(2)}, u32[]{:S(2)}) %collective-permute-start.14) | collective-permute-done | bytes 491552 | tf_op jit(solution)/shard_map/ppermute | solution.py:549
  81.7 2.0 %collective-permute-start.17 = (bf16[5,6,2,16,256]{4,3,2,1,0:T(8,128)(2,1)}, bf16[5,6,2,16,256]{4,3,2,1,0:T(8,128)(2,1)}, u32[]{:S(2)}, u32[]{:S(2)}) collective-permute-start(bf16[5,6,2,16,256]{4,3,2,1,0:T(8,128)(2,1)} %get-tuple-element.93), channel_id=1, source_target_pairs={{0,16},{8,24},{16,0},{24,8},{1,17},{9,25},{17,1},{25,9},{2,18},{10... | collective-permute-start | bytes 1474568 | tf_op jit(solution)/shard_map/ppermute | solution.py:549
  83.7 0.0 collective-permute-done.1.refs_3_
  83.7 1.5 %collective-permute-start.2 = (bf16[5,6,2,16,256]{4,3,2,1,0:T(8,128)(2,1)}, bf16[5,6,2,16,256]{4,3,2,1,0:T(8,128)(2,1)}, u32[]{:S(2)}, u32[]{:S(2)}) collective-permute-start(bf16[5,6,2,16,256]{4,3,2,1,0:T(8,128)(2,1)} %get-tuple-element.65), channel_id=1, source_target_pairs={{0,8},{8,0},{16,24},{24,16},{1,9},{9,1},{17,25},{25,17},{2,10},{10... | collective-permute-start | bytes 1474568 | tf_op jit(solution)/shard_map/ppermute | solution.py:549
  85.2 7.2 %collective-permute-done.15.refs_7_ = bf16[5,6,2,16,256]{4,3,2,1,0:T(8,128)(2,1)} collective-permute-done((bf16[5,6,2,16,256]{4,3,2,1,0:T(8,128)(2,1)}, bf16[5,6,2,16,256]{4,3,2,1,0:T(8,128)(2,1)}, u32[]{:S(2)}, u32[]{:S(2)}) %collective-permute-start.15) | collective-permute-done | bytes 491552 | tf_op jit(solution)/shard_map/ppermute | solution.py:549
  92.4 3.0 %collective-permute-start.19 = (bf16[5,6,2,16,256]{4,3,2,1,0:T(8,128)(2,1)}, bf16[5,6,2,16,256]{4,3,2,1,0:T(8,128)(2,1)}, u32[]{:S(2)}, u32[]{:S(2)}) collective-permute-start(bf16[5,6,2,16,256]{4,3,2,1,0:T(8,128)(2,1)} %get-tuple-element.97), channel_id=1, source_target_pairs={{0,24},{8,16},{16,8},{24,0},{1,25},{9,17},{17,9},{25,1},{2,26},{10... | collective-permute-start | bytes 1474568 | tf_op jit(solution)/shard_map/ppermute | solution.py:549
  95.4 5.7 %gram_1.1 = (f32[4,16,2,128,128]{4,3,2,1,0:T(8,128)}, f32[4,2,128,128]{3,2,1,0:T(8,128)}, f32[4,2,128,128]{3,2,1,0:T(8,128)}) custom-call(bf16[5,15,2,16,256]{4,3,2,1,0:T(8,128)(2,1)} %get-tuple-element.56.refs_0_, bf16[5,6,2,16,256]{4,3,2,1,0:T(8,128)(2,1)} %get-tuple-element.80.refs_1_, bf16[5,15,2,16,256]{4,3,2,1,0:T(8,128)(2,1)} %collective-permute-done.refs_2_, ...), custom_call_target="tpu_custom_call" | custom-call | flops 1 | bytes 1 | tf_op jit(solution)/shard_map/gram_1/pallas_call | solution.py:513
  101.2 0.0 collective-permute-done.11.before
  101.2 3.8 %rim_gram.1 = (f32[4,16,2,128,128]{4,3,2,1,0:T(8,128)}, f32[4,2,128,128]{3,2,1,0:T(8,128)}) custom-call(s32[1]{0:T(128)} %bitcast.me_ref, bf16[4,5,2,32,256]{4,3,2,1,0:T(8,128)(2,1)} %copy-done.1, bf16[4,5,2,32,256]{4,3,2,1,0:T(8,128)(2,1)} %collective-permute-done.11.before, ...), custom_call_target="tpu_custom_call", output_to_operand_aliasing={{0}: (5, {})} | custom-call | flops 1 | bytes 1 | tf_op jit(solution)/shard_map/rim_gram/pallas_call | solution.py:394
  105.0 0.0 collective-permute-done.17.refs_5_
  105.0 0.6 collective-permute-start.18
  105.6 0.8 collective-permute-start.16
  106.4 7.1 %collective-permute-done.19.refs_7_ = bf16[5,6,2,16,256]{4,3,2,1,0:T(8,128)(2,1)} collective-permute-done((bf16[5,6,2,16,256]{4,3,2,1,0:T(8,128)(2,1)}, bf16[5,6,2,16,256]{4,3,2,1,0:T(8,128)(2,1)}, u32[]{:S(2)}, u32[]{:S(2)}) %collective-permute-start.19) | collective-permute-done | bytes 491552 | tf_op jit(solution)/shard_map/ppermute | solution.py:549
  113.6 3.0 %collective-permute-start.20 = (bf16[5,3,2,16,256]{4,3,2,1,0:T(8,128)(2,1)S(1)}, bf16[5,3,2,16,256]{4,3,2,1,0:T(8,128)(2,1)S(1)}, u32[]{:S(2)}, u32[]{:S(2)}) collective-permute-start(bf16[5,3,2,16,256]{4,3,2,1,0:T(8,128)(2,1)S(1)} %copy-done.6), channel_id=1, source_target_pairs={{0,24},{8,16},{16,8},{24,0},{1,25},{9,17},{17,9},{25,1},{2,26},{10... | collective-permute-start | bytes 737288 | tf_op jit(solution)/shard_map/ppermute | solution.py:549
  116.5 5.6 %gram_7.1 = (f32[4,16,2,128,128]{4,3,2,1,0:T(8,128)}, f32[4,2,128,128]{3,2,1,0:T(8,128)}) custom-call(bf16[5,15,2,16,256]{4,3,2,1,0:T(8,128)(2,1)} %get-tuple-element.56.refs_0_, bf16[5,6,2,16,256]{4,3,2,1,0:T(8,128)(2,1)} %get-tuple-element.99.refs_1_, bf16[5,15,2,16,256]{4,3,2,1,0:T(8,128)(2,1)} %collective-permute-done.refs_2_, ...), custom_call_target="tpu_custom_call", output_to_operand_aliasing={{0}: (10, {})} | custom-call | flops 1 | bytes 1 | tf_op jit(solution)/shard_map/gram_7/pallas_call | solution.py:513
  122.1 0.0 collective-permute-done.16.refs_3_
  122.2 1.0 collective-permute-done.20.refs_7_
  123.2 3.9 %gram_13.1 = (f32[4,16,2,128,128]{4,3,2,1,0:T(8,128)}, f32[4,2,128,128]{3,2,1,0:T(8,128)}) custom-call(bf16[5,15,2,16,256]{4,3,2,1,0:T(8,128)(2,1)} %get-tuple-element.56.refs_0_, bf16[5,3,2,16,256]{4,3,2,1,0:T(8,128)(2,1)} %get-tuple-element.59.refs_1_, bf16[5,15,2,16,256]{4,3,2,1,0:T(8,128)(2,1)} %collective-permute-done.refs_2_, ...), custom_call_target="tpu_custom_call", output_to_operand_aliasing={{0}: (10, {})} | custom-call | flops 1 | bytes 1 | tf_op jit(solution)/shard_map/gram_13/pallas_call | solution.py:513
  (19 shorter events, 0.0 us)
Async XLA Ops:
  5.8 48.6 %collective-permute-start.7 = (bf16[5,15,2,16,256]{4,3,2,1,0:T(8,128)(2,1)}, bf16[5,15,2,16,256]{4,3,2,1,0:T(8,128)(2,1)S(1)}, u32[]{:S(2)}, u32[]{:S(2)}) collective-permute-start(bf16[5,15,2,16,256]{4,3,2,1,0:T(8,128)(2,1)} %interior_0_3.1), channel_id=1, source_target_pairs={{0,24},{8,16},{16,8},{24,0},{1,25},{9,17},{17,9},{25,1},{2,26},{10... | collective-permute-start | bytes 3686408 | tf_op jit(solution)/shard_map/ppermute | solution.py:549
  20.2 44.7 %collective-permute-start = (bf16[5,15,2,16,256]{4,3,2,1,0:T(8,128)(2,1)}, bf16[5,15,2,16,256]{4,3,2,1,0:T(8,128)(2,1)}, u32[]{:S(2)}, u32[]{:S(2)}) collective-permute-start(bf16[5,15,2,16,256]{4,3,2,1,0:T(8,128)(2,1)} %get-tuple-element.60), channel_id=1, source_target_pairs={{0,8},{8,0},{16,24},{24,16},{1,9},{9,1},{17,25},{25,17},{2,10},{10... | collective-permute-start | bytes 3686408 | tf_op jit(solution)/shard_map/ppermute | solution.py:549
  20.8 44.1 %collective-permute-start.13 = (bf16[5,15,2,16,256]{4,3,2,1,0:T(8,128)(2,1)}, bf16[5,15,2,16,256]{4,3,2,1,0:T(8,128)(2,1)}, u32[]{:S(2)}, u32[]{:S(2)}) collective-permute-start(bf16[5,15,2,16,256]{4,3,2,1,0:T(8,128)(2,1)} %get-tuple-element.81), channel_id=1, source_target_pairs={{0,16},{8,24},{16,0},{24,8},{1,17},{9,25},{17,1},{25,9},{2,18},{10... | collective-permute-start | bytes 3686408 | tf_op jit(solution)/shard_map/ppermute | solution.py:549
  20.8 13.8 %collective-permute-start.3 = (bf16[16,16,256]{2,1,0:T(8,128)(2,1)}, bf16[16,16,256]{2,1,0:T(8,128)(2,1)S(1)}, u32[]{:S(2)}, u32[]{:S(2)}) collective-permute-start(bf16[16,16,256]{2,1,0:T(8,128)(2,1)} %get-tuple-element.68), channel_id=1, source_target_pairs={{0,1},{1,2},{2,3},{3,4},{4,5},{5,6},{6,7},{8,9},{9,10},{10,11},{11... | collective-permute-start | bytes 393224 | tf_op jit(solution)/shard_map/ppermute | solution.py:537
  22.1 17.9 %collective-permute-start.4 = (bf16[16,16,256]{2,1,0:T(8,128)(2,1)}, bf16[16,16,256]{2,1,0:T(8,128)(2,1)S(1)}, u32[]{:S(2)}, u32[]{:S(2)}) collective-permute-start(bf16[16,16,256]{2,1,0:T(8,128)(2,1)} %get-tuple-element.57), channel_id=1, source_target_pairs={{1,0},{2,1},{3,2},{4,3},{5,4},{6,5},{7,6},{9,8},{10,9},{11,10},{12... | collective-permute-start | bytes 393224 | tf_op jit(solution)/shard_map/ppermute | solution.py:537
  34.6 10.0 %copy-start.2 = (bf16[16,16,256]{2,1,0:T(8,128)(2,1)}, bf16[16,16,256]{2,1,0:T(8,128)(2,1)S(1)}, u32[]{:S(2)}) copy-start(bf16[16,16,256]{2,1,0:T(8,128)(2,1)S(1)} %collective-permute-done.3.refs_1_) | copy-start | bytes 393220
  34.7 6.6 %collective-permute-start.5 = (bf16[16,16,256]{2,1,0:T(8,128)(2,1)}, bf16[16,16,256]{2,1,0:T(8,128)(2,1)S(1)}, u32[]{:S(2)}, u32[]{:S(2)}) collective-permute-start(bf16[16,16,256]{2,1,0:T(8,128)(2,1)} %get-tuple-element.70), channel_id=1, source_target_pairs={{0,1},{1,2},{2,3},{3,4},{4,5},{5,6},{6,7},{8,9},{9,10},{10,11},{11... | collective-permute-start | bytes 393224 | tf_op jit(solution)/shard_map/ppermute | solution.py:537
  40.0 4.7 %copy-start.3 = (bf16[16,16,256]{2,1,0:T(8,128)(2,1)}, bf16[16,16,256]{2,1,0:T(8,128)(2,1)S(1)}, u32[]{:S(2)}) copy-start(bf16[16,16,256]{2,1,0:T(8,128)(2,1)S(1)} %collective-permute-done.4.refs_2_) | copy-start | bytes 393220
  40.0 4.7 %collective-permute-start.6 = (bf16[16,16,256]{2,1,0:T(8,128)(2,1)}, bf16[16,16,256]{2,1,0:T(8,128)(2,1)S(1)}, u32[]{:S(2)}, u32[]{:S(2)}) collective-permute-start(bf16[16,16,256]{2,1,0:T(8,128)(2,1)} %get-tuple-element.71), channel_id=1, source_target_pairs={{1,0},{2,1},{3,2},{4,3},{5,4},{6,5},{7,6},{9,8},{10,9},{11,10},{12... | collective-permute-start | bytes 393224 | tf_op jit(solution)/shard_map/ppermute | solution.py:537
  41.3 3.4 %copy-start.4 = (bf16[16,16,256]{2,1,0:T(8,128)(2,1)}, bf16[16,16,256]{2,1,0:T(8,128)(2,1)S(1)}, u32[]{:S(2)}) copy-start(bf16[16,16,256]{2,1,0:T(8,128)(2,1)S(1)} %collective-permute-done.5.refs_5_) | copy-start | bytes 393220
  44.7 0.6 copy-start.5
  54.4 41.0 %copy-start = (bf16[5,15,2,16,256]{4,3,2,1,0:T(8,128)(2,1)}, bf16[5,15,2,16,256]{4,3,2,1,0:T(8,128)(2,1)S(1)}, u32[]{:S(2)}) copy-start(bf16[5,15,2,16,256]{4,3,2,1,0:T(8,128)(2,1)S(1)} %collective-permute-done.7.refs_6_) | copy-start | bytes 3686404
  54.4 13.5 %collective-permute-start.10 = (bf16[5,2,32,256]{3,2,1,0:T(8,128)(2,1)}, bf16[5,2,32,256]{3,2,1,0:T(8,128)(2,1)S(1)}, u32[]{:S(2)}, u32[]{:S(2)}) collective-permute-start(bf16[5,2,32,256]{3,2,1,0:T(8,128)(2,1)} %get-tuple-element.79), channel_id=1, source_target_pairs={{0,24},{8,16},{16,8},{24,0},{1,25},{9,17},{17,9},{25,1},{2,26},{10... | collective-permute-start | bytes 491528 | tf_op jit(solution)/shard_map/ppermute | solution.py:549
  56.9 13.5 %collective-permute-start.9 = (bf16[5,2,32,256]{3,2,1,0:T(8,128)(2,1)}, bf16[5,2,32,256]{3,2,1,0:T(8,128)(2,1)S(1)}, u32[]{:S(2)}, u32[]{:S(2)}) collective-permute-start(bf16[5,2,32,256]{3,2,1,0:T(8,128)(2,1)} %get-tuple-element.77), channel_id=1, source_target_pairs={{0,16},{8,24},{16,0},{24,8},{1,17},{9,25},{17,1},{25,9},{2,18},{10... | collective-permute-start | bytes 491528 | tf_op jit(solution)/shard_map/ppermute | solution.py:549
  57.4 14.4 %collective-permute-start.8 = (bf16[5,2,32,256]{3,2,1,0:T(8,128)(2,1)}, bf16[5,2,32,256]{3,2,1,0:T(8,128)(2,1)S(1)}, u32[]{:S(2)}, u32[]{:S(2)}) collective-permute-start(bf16[5,2,32,256]{3,2,1,0:T(8,128)(2,1)} %get-tuple-element.75), channel_id=1, source_target_pairs={{0,8},{8,0},{16,24},{24,16},{1,9},{9,1},{17,25},{25,17},{2,10},{10... | collective-permute-start | bytes 491528 | tf_op jit(solution)/shard_map/ppermute | solution.py:549
  64.8 16.9 %collective-permute-start.14 = (bf16[5,6,2,16,256]{4,3,2,1,0:T(8,128)(2,1)}, bf16[5,6,2,16,256]{4,3,2,1,0:T(8,128)(2,1)}, u32[]{:S(2)}, u32[]{:S(2)}) collective-permute-start(bf16[5,6,2,16,256]{4,3,2,1,0:T(8,128)(2,1)} %get-tuple-element.83), channel_id=1, source_target_pairs={{0,16},{8,24},{16,0},{24,8},{1,17},{9,25},{17,1},{25,9},{2,18},{10... | collective-permute-start | bytes 1474568 | tf_op jit(solution)/shard_map/ppermute | solution.py:549
  66.4 17.4 %collective-permute-start.1 = (bf16[5,6,2,16,256]{4,3,2,1,0:T(8,128)(2,1)}, bf16[5,6,2,16,256]{4,3,2,1,0:T(8,128)(2,1)}, u32[]{:S(2)}, u32[]{:S(2)}) collective-permute-start(bf16[5,6,2,16,256]{4,3,2,1,0:T(8,128)(2,1)} %get-tuple-element.64), channel_id=1, source_target_pairs={{0,8},{8,0},{16,24},{24,16},{1,9},{9,1},{17,25},{25,17},{2,10},{10... | collective-permute-start | bytes 1474568 | tf_op jit(solution)/shard_map/ppermute | solution.py:549
  71.8 20.7 %collective-permute-start.15 = (bf16[5,6,2,16,256]{4,3,2,1,0:T(8,128)(2,1)}, bf16[5,6,2,16,256]{4,3,2,1,0:T(8,128)(2,1)}, u32[]{:S(2)}, u32[]{:S(2)}) collective-permute-start(bf16[5,6,2,16,256]{4,3,2,1,0:T(8,128)(2,1)} %get-tuple-element.86), channel_id=1, source_target_pairs={{0,24},{8,16},{16,8},{24,0},{1,25},{9,17},{17,9},{25,1},{2,26},{10... | collective-permute-start | bytes 1474568 | tf_op jit(solution)/shard_map/ppermute | solution.py:549
  74.2 26.9 %copy-start.1 = (bf16[4,5,2,32,256]{4,3,2,1,0:T(8,128)(2,1)}, bf16[4,5,2,32,256]{4,3,2,1,0:T(8,128)(2,1)S(1)}, u32[]{:S(2)}) copy-start(bf16[4,5,2,32,256]{4,3,2,1,0:T(8,128)(2,1)S(1)} %pad_maximum_fusion.own) | copy-start | bytes 1966084
  74.2 26.9 %collective-permute-start.12 = (bf16[4,5,2,32,256]{4,3,2,1,0:T(8,128)(2,1)S(1)}, bf16[4,5,2,32,256]{4,3,2,1,0:T(8,128)(2,1)}, u32[]{:S(2)}, u32[]{:S(2)}) collective-permute-start(bf16[4,5,2,32,256]{4,3,2,1,0:T(8,128)(2,1)S(1)} %pad_maximum_fusion.own), channel_id=1, source_target_pairs={{1,0},{2,1},{3,2},{4,3},{5,4},{6,5},{7,6},{9,8},{10,9},{11,10},{12... | collective-permute-start | bytes 1966088 | tf_op jit(solution)/shard_map/ppermute | solution.py:537
  75.5 25.6 %collective-permute-start.11 = (bf16[4,5,2,32,256]{4,3,2,1,0:T(8,128)(2,1)S(1)}, bf16[4,5,2,32,256]{4,3,2,1,0:T(8,128)(2,1)}, u32[]{:S(2)}, u32[]{:S(2)}) collective-permute-start(bf16[4,5,2,32,256]{4,3,2,1,0:T(8,128)(2,1)S(1)} %pad_maximum_fusion.own), channel_id=1, source_target_pairs={{0,1},{1,2},{2,3},{3,4},{4,5},{5,6},{6,7},{8,9},{9,10},{10,11},{11... | collective-permute-start | bytes 1966088 | tf_op jit(solution)/shard_map/ppermute | solution.py:537
  81.7 23.3 %collective-permute-start.17 = (bf16[5,6,2,16,256]{4,3,2,1,0:T(8,128)(2,1)}, bf16[5,6,2,16,256]{4,3,2,1,0:T(8,128)(2,1)}, u32[]{:S(2)}, u32[]{:S(2)}) collective-permute-start(bf16[5,6,2,16,256]{4,3,2,1,0:T(8,128)(2,1)} %get-tuple-element.93), channel_id=1, source_target_pairs={{0,16},{8,24},{16,0},{24,8},{1,17},{9,25},{17,1},{25,9},{2,18},{10... | collective-permute-start | bytes 1474568 | tf_op jit(solution)/shard_map/ppermute | solution.py:549
  83.7 21.9 %collective-permute-start.2 = (bf16[5,6,2,16,256]{4,3,2,1,0:T(8,128)(2,1)}, bf16[5,6,2,16,256]{4,3,2,1,0:T(8,128)(2,1)}, u32[]{:S(2)}, u32[]{:S(2)}) collective-permute-start(bf16[5,6,2,16,256]{4,3,2,1,0:T(8,128)(2,1)} %get-tuple-element.65), channel_id=1, source_target_pairs={{0,8},{8,0},{16,24},{24,16},{1,9},{9,1},{17,25},{25,17},{2,10},{10... | collective-permute-start | bytes 1474568 | tf_op jit(solution)/shard_map/ppermute | solution.py:549
  92.4 21.1 %collective-permute-start.19 = (bf16[5,6,2,16,256]{4,3,2,1,0:T(8,128)(2,1)}, bf16[5,6,2,16,256]{4,3,2,1,0:T(8,128)(2,1)}, u32[]{:S(2)}, u32[]{:S(2)}) collective-permute-start(bf16[5,6,2,16,256]{4,3,2,1,0:T(8,128)(2,1)} %get-tuple-element.97), channel_id=1, source_target_pairs={{0,24},{8,16},{16,8},{24,0},{1,25},{9,17},{17,9},{25,1},{2,26},{10... | collective-permute-start | bytes 1474568 | tf_op jit(solution)/shard_map/ppermute | solution.py:549
  101.2 4.4 %copy-start.7 = (bf16[5,3,2,16,256]{4,3,2,1,0:T(8,128)(2,1)S(1)}, bf16[5,3,2,16,256]{4,3,2,1,0:T(8,128)(2,1)}, u32[]{:S(2)}) copy-start(bf16[5,3,2,16,256]{4,3,2,1,0:T(8,128)(2,1)} %get-tuple-element.90) | copy-start | bytes 737284
  101.2 12.4 %copy-start.6 = (bf16[5,3,2,16,256]{4,3,2,1,0:T(8,128)(2,1)S(1)}, bf16[5,3,2,16,256]{4,3,2,1,0:T(8,128)(2,1)}, u32[]{:S(2)}) copy-start(bf16[5,3,2,16,256]{4,3,2,1,0:T(8,128)(2,1)} %get-tuple-element.98) | copy-start | bytes 737284
  105.0 17.1 %collective-permute-start.18 = (bf16[5,3,2,16,256]{4,3,2,1,0:T(8,128)(2,1)}, bf16[5,3,2,16,256]{4,3,2,1,0:T(8,128)(2,1)S(1)}, u32[]{:S(2)}, u32[]{:S(2)}) collective-permute-start(bf16[5,3,2,16,256]{4,3,2,1,0:T(8,128)(2,1)} %get-tuple-element.94), channel_id=1, source_target_pairs={{0,16},{8,24},{16,0},{24,8},{1,17},{9,25},{17,1},{25,9},{2,18},{10... | collective-permute-start | bytes 737288 | tf_op jit(solution)/shard_map/ppermute | solution.py:549
  105.6 16.6 %collective-permute-start.16 = (bf16[5,3,2,16,256]{4,3,2,1,0:T(8,128)(2,1)S(1)}, bf16[5,3,2,16,256]{4,3,2,1,0:T(8,128)(2,1)S(1)}, u32[]{:S(2)}, u32[]{:S(2)}) collective-permute-start(bf16[5,3,2,16,256]{4,3,2,1,0:T(8,128)(2,1)S(1)} %copy-done.7), channel_id=1, source_target_pairs={{0,8},{8,0},{16,24},{24,16},{1,9},{9,1},{17,25},{25,17},{2,10},{10... | collective-permute-start | bytes 737288 | tf_op jit(solution)/shard_map/ppermute | solution.py:549
  113.6 9.6 %collective-permute-start.20 = (bf16[5,3,2,16,256]{4,3,2,1,0:T(8,128)(2,1)S(1)}, bf16[5,3,2,16,256]{4,3,2,1,0:T(8,128)(2,1)S(1)}, u32[]{:S(2)}, u32[]{:S(2)}) collective-permute-start(bf16[5,3,2,16,256]{4,3,2,1,0:T(8,128)(2,1)S(1)} %copy-done.6), channel_id=1, source_target_pairs={{0,24},{8,16},{16,8},{24,0},{1,25},{9,17},{17,9},{25,1},{2,26},{10... | collective-permute-start | bytes 737288 | tf_op jit(solution)/shard_map/ppermute | solution.py:549

commit v6 on v5

--- a/solution.py
+++ b/solution.py
@@ -133,10 +133,9 @@
     lax.fori_loop(0, steps, resample, 0)
 
     masks = group_masks((lines, LANES))
-    copies = [
-        pltpu.make_async_copy(stage[n // n_targets].at[n % n_targets], outs[n], out_sems.at[n])
-        for n in range(len(outs))
-    ]
+    def copy_out(n, j):
+        return pltpu.make_async_copy(stage[n // n_targets].at[n % n_targets, j], outs[n].at[j], out_sems.at[n])
+
 
     for t, k in enumerate(targets):
         base = (me ^ k) * dest_rows
@@ -157,11 +156,11 @@
                                     stage[s][t, j, column - lo, c, :, half * LANES : (half + 1) * LANES] = cols[g][
                                         c * DBLK : (c + 1) * DBLK
                                     ]
+            for s in range(len(spans)):
+                copy_out(s * n_targets + t, j).start()
             return carry
 
         lax.fori_loop(0, row_blocks, blocks, 0)
-        for s in range(len(spans)):
-            copies[s * n_targets + t].start()
 
     pick_row = lax.broadcasted_iota(jnp.int32, (2 * SIDE, n_az), 0)
     pick_col = lax.broadcasted_iota(jnp.int32, (2 * SIDE, n_az), 1)
@@ -180,8 +179,8 @@
 
     if edged:
         lax.fori_loop(0, DBLK // 4, edges, 0)
-    for copy in copies:
-        copy.wait()
+    for n in range(len(outs)):
+        pltpu.make_async_copy(stage[n // n_targets].at[n % n_targets], outs[n], out_sems.at[n]).wait()
 
 
 def interior(me, slc, rk, ak, part, spans, targets, edged, partners):
@@ -423,12 +422,15 @@
     me = lax.axis_index("date").astype(jnp.int32)
     total = pixels.shape[1] // 2
 
+    placed = [n for n in range(parts, partners * parts) if closing and n % parts == parts - 1]
+
     def fetch(column):
         return [
             pltpu.make_async_copy(
                 pieces[n].at[:, offsets[n % parts] + column], blocks[n].at[column], in_sems.at[column, n]
             )
             for n in range(partners * parts)
+            if n not in placed
         ]
 
     def write(window):
@@ -460,7 +462,9 @@
                 for p in range(parts):
                     for c in range(2):
                         at = pl.multiple_of(c * total + (me ^ k) * (parts * DBLK) + p * DBLK, DBLK)
-                        scratch[pl.ds(at, DBLK), :] = blocks[k * parts + p][column, j, c]
+                        n = k * parts + p
+                        here = pieces[n][j, column, c] if n in placed else blocks[n][column, j, c]
+                        scratch[pl.ds(at, DBLK), :] = here
 
         def emit(u, real, imag):
             store_coherence(stage.at[column], (u,), held[u, 0] + real, held[u, 1] + imag)
@@ -512,7 +516,12 @@
     n_out = 2 if opening else 1
     return pl.pallas_call(
         functools.partial(gram_kernel, partners, parts, offsets, columns, first, opening, closing),
-        in_specs=[anywhere] * len(operands),
+        in_specs=[
+            pl.BlockSpec(memory_space=pltpu.VMEM)
+            if closing and parts <= n < partners * parts and n % parts == parts - 1
+            else anywhere
+            for n in range(len(operands))
+        ],
         out_specs=[anywhere] * (1 + n_out),
         out_shape=[out_shape] + [sums] * n_out,
         input_output_aliases=aliases,

time: 127 us -> 127 us (level)
  no operation moved by 1% of the time
where the time goes in v6:
time: 127 us
  Pallas kernels  55.1 us (43%)
  starting transfers between devices  37.8 us (30%)
  waiting for transfers between devices  31.8 us (25%)
    ppermute x15, waiting for transfers between devices, exchange(): got.append(lax.ppermute(block, 'date', [(i, i ^ k) for i in range(n)]))  28.5 us
    pallas_call x3, Pallas kernels, interior(): pl.pallas_call(functools.partial(interior_kernel, spans, targets, edged,...  27.1 us
    ppermute x15, starting transfers between devices, exchange(): got.append(lax.ppermute(block, 'date', [(i, i ^ k) for i in range(n)]))  23.5 us
    pallas_call x3, Pallas kernels, gram(): pl.pallas_call(functools.partial(gram_kernel, partners, parts, offsets, c...  15.2 us
    ppermute x6, starting transfers between devices, shift(): return lax.ppermute(value, axis, pairs)  14.4 us
    pallas_call x1, Pallas kernels, rim(): pl.pallas_call(functools.partial(rim_kernel, dest_rows, parts), grid_spec...  9.07 us
    pallas_call x1, Pallas kernels, rim_gram(): pl.pallas_call(rim_gram_kernel, in_specs=[pl.BlockSpec(memory_space=pltpu...  3.81 us
    ppermute x6, waiting for transfers between devices, shift(): return lax.ppermute(value, axis, pairs)  3.38 us
  transfers between devices with their start and end apart: 21, of which 8 were waited for; matrix products, arithmetic and copies ran while one was open for 1% of the time, Pallas kernels for 36%

profile of v6, /device:TPU:0, one launch (start us, length us, event | category | flops | bytes accessed | tf_op | source)
XLA Modules:
  0.0 126.7 jit_solution(12021573451902950019)
XLA Ops:
  0.0 5.4 %interior_0_3.1 = bf16[5,15,2,16,256]{4,3,2,1,0:T(8,128)(2,1)} custom-call(s32[1]{0:T(128)} %bitcast.me_ref, bf16[2,32,256,256]{3,2,1,0:T(8,128)(2,1)} %slc_any.5, bf16[32,256,256]{2,1,0:T(8,128)(2,1)} %rk_any.5, bf16[32,272,256]{2,1,0:T(8,128)(2,1)} %refs_7_.1), custom_call_target="tpu_custom_call" | custom-call | flops 1 | bytes 1 | tf_op jit(solution)/shard_map/interior_0_3/pallas_call | solution.py:206
  5.4 4.0 %collective-permute-start.7 = (bf16[5,15,2,16,256]{4,3,2,1,0:T(8,128)(2,1)}, bf16[5,15,2,16,256]{4,3,2,1,0:T(8,128)(2,1)S(1)}, u32[]{:S(2)}, u32[]{:S(2)}) collective-permute-start(bf16[5,15,2,16,256]{4,3,2,1,0:T(8,128)(2,1)} %interior_0_3.1), channel_id=1, source_target_pairs={{0,24},{8,16},{16,8},{24,0},{1,25},{9,17},{17,9},{25,1},{2,26},{10... | collective-permute-start | bytes 3686408 | tf_op jit(solution)/shard_map/ppermute | solution.py:558
  9.4 10.4 %interior_0_1.1 = (bf16[16,2,32,256]{3,2,1,0:T(8,128)(2,1)}, bf16[16,16,256]{2,1,0:T(8,128)(2,1)}, bf16[16,16,256]{2,1,0:T(8,128)(2,1)}, bf16[5,15,2,16,256]{4,3...) custom-call(s32[1]{0:T(128)} %bitcast.me_ref, ...), custom_call_target="tpu_custom_call" | custom-call | flops 1 | bytes 1 | tf_op jit(solution)/shard_map/interior_0_1/pallas_call | solution.py:206
  19.8 0.6 collective-permute-start
  20.4 0.1 collective-permute-start.13
  20.5 1.3 %collective-permute-start.3 = (bf16[16,16,256]{2,1,0:T(8,128)(2,1)}, bf16[16,16,256]{2,1,0:T(8,128)(2,1)S(1)}, u32[]{:S(2)}, u32[]{:S(2)}) collective-permute-start(bf16[16,16,256]{2,1,0:T(8,128)(2,1)} %get-tuple-element.68), channel_id=1, source_target_pairs={{0,1},{1,2},{2,3},{3,4},{4,5},{5,6},{6,7},{8,9},{9,10},{10,11},{11... | collective-permute-start | bytes 393224 | tf_op jit(solution)/shard_map/ppermute | solution.py:546
  21.8 1.3 %collective-permute-start.4 = (bf16[16,16,256]{2,1,0:T(8,128)(2,1)}, bf16[16,16,256]{2,1,0:T(8,128)(2,1)S(1)}, u32[]{:S(2)}, u32[]{:S(2)}) collective-permute-start(bf16[16,16,256]{2,1,0:T(8,128)(2,1)} %get-tuple-element.57), channel_id=1, source_target_pairs={{1,0},{2,1},{3,2},{4,3},{5,4},{6,5},{7,6},{9,8},{10,9},{11,10},{12... | collective-permute-start | bytes 393224 | tf_op jit(solution)/shard_map/ppermute | solution.py:546
  23.1 11.2 %interior_1_1.1 = (bf16[16,2,32,256]{3,2,1,0:T(8,128)(2,1)}, bf16[16,16,256]{2,1,0:T(8,128)(2,1)}, bf16[16,16,256]{2,1,0:T(8,128)(2,1)}, bf16[5,6,2,16,256]{4,3,...) custom-call(s32[1]{0:T(128)} %bitcast.me_ref, ...), custom_call_target="tpu_custom_call" | custom-call | flops 1 | bytes 1 | tf_op jit(solution)/shard_map/interior_1_1/pallas_call | solution.py:206
  34.3 0.0 collective-permute-done.3.refs_1_
  34.3 5.3 %collective-permute-start.5 = (bf16[16,16,256]{2,1,0:T(8,128)(2,1)}, bf16[16,16,256]{2,1,0:T(8,128)(2,1)S(1)}, u32[]{:S(2)}, u32[]{:S(2)}) collective-permute-start(bf16[16,16,256]{2,1,0:T(8,128)(2,1)} %get-tuple-element.70), channel_id=1, source_target_pairs={{0,1},{1,2},{2,3},{3,4},{4,5},{5,6},{6,7},{8,9},{9,10},{10,11},{11... | collective-permute-start | bytes 393224 | tf_op jit(solution)/shard_map/ppermute | solution.py:546
  39.6 0.0 collective-permute-done.4.refs_2_
  39.7 1.3 %collective-permute-start.6 = (bf16[16,16,256]{2,1,0:T(8,128)(2,1)}, bf16[16,16,256]{2,1,0:T(8,128)(2,1)S(1)}, u32[]{:S(2)}, u32[]{:S(2)}) collective-permute-start(bf16[16,16,256]{2,1,0:T(8,128)(2,1)} %get-tuple-element.71), channel_id=1, source_target_pairs={{1,0},{2,1},{3,2},{4,3},{5,4},{6,5},{7,6},{9,8},{10,9},{11,10},{12... | collective-permute-start | bytes 393224 | tf_op jit(solution)/shard_map/ppermute | solution.py:546
  41.0 0.0 collective-permute-done.5.refs_5_
  41.0 3.4 %collective-permute-done.6.refs_6_ = bf16[16,16,256]{2,1,0:T(8,128)(2,1)S(1)} collective-permute-done((bf16[16,16,256]{2,1,0:T(8,128)(2,1)}, bf16[16,16,256]{2,1,0:T(8,128)(2,1)S(1)}, u32[]{:S(2)}, u32[]{:S(2)}) %collective-permute-start.6) | collective-permute-done | bytes 131104 | tf_op jit(solution)/shard_map/ppermute | solution.py:546
  44.4 0.6 copy-done.5
  45.0 9.1 %rim.1 = (bf16[5,2,32,256]{3,2,1,0:T(8,128)(2,1)}, bf16[5,2,32,256]{3,2,1,0:T(8,128)(2,1)}, bf16[5,2,32,256]{3,2,1,0:T(8,128)(2,1)}, bf16[5,2,32,256]{3,2,1,0:T(8,128)(2,1)}) custom-call(s32[1]{0:T(128)} %bitcast.me_ref, bf16[16,2,32,256]{3,2,1,0:T(8,128)(2,1)} %get-tuple-element.67.refs_0_, bf16[16,16,256]{2,1,0:T(8,128)(2,1)} %copy-done.2, ...), custom_call_target="tpu_custom_call" | custom-call | flops 1 | bytes 1 | tf_op jit(solution)/shard_map/rim/pallas_call | solution.py:321
  54.1 0.0 collective-permute-done.7.refs_6_
  54.1 2.5 %collective-permute-start.10 = (bf16[5,2,32,256]{3,2,1,0:T(8,128)(2,1)}, bf16[5,2,32,256]{3,2,1,0:T(8,128)(2,1)S(1)}, u32[]{:S(2)}, u32[]{:S(2)}) collective-permute-start(bf16[5,2,32,256]{3,2,1,0:T(8,128)(2,1)} %get-tuple-element.79), channel_id=1, source_target_pairs={{0,24},{8,16},{16,8},{24,0},{1,25},{9,17},{17,9},{25,1},{2,26},{10... | collective-permute-start | bytes 491528 | tf_op jit(solution)/shard_map/ppermute | solution.py:558
  56.6 0.5 collective-permute-start.9
  57.1 0.5 collective-permute-start.8
  57.6 6.9 %collective-permute-done.refs_2_ = bf16[5,15,2,16,256]{4,3,2,1,0:T(8,128)(2,1)} collective-permute-done((bf16[5,15,2,16,256]{4,3,2,1,0:T(8,128)(2,1)}, bf16[5,15,2,16,256]{4,3,2,1,0:T(8,128)(2,1)}, u32[]{:S(2)}, u32[]{:S(2)}) %collective-permute-start) | collective-permute-done | bytes 1228832 | tf_op jit(solution)/shard_map/ppermute | solution.py:558
  64.5 1.5 %collective-permute-start.14 = (bf16[5,6,2,16,256]{4,3,2,1,0:T(8,128)(2,1)}, bf16[5,6,2,16,256]{4,3,2,1,0:T(8,128)(2,1)}, u32[]{:S(2)}, u32[]{:S(2)}) collective-permute-start(bf16[5,6,2,16,256]{4,3,2,1,0:T(8,128)(2,1)} %get-tuple-element.83), channel_id=1, source_target_pairs={{0,16},{8,24},{16,0},{24,8},{1,17},{9,25},{17,1},{25,9},{2,18},{10... | collective-permute-start | bytes 1474568 | tf_op jit(solution)/shard_map/ppermute | solution.py:558
  66.0 1.5 %collective-permute-start.1 = (bf16[5,6,2,16,256]{4,3,2,1,0:T(8,128)(2,1)}, bf16[5,6,2,16,256]{4,3,2,1,0:T(8,128)(2,1)}, u32[]{:S(2)}, u32[]{:S(2)}) collective-permute-start(bf16[5,6,2,16,256]{4,3,2,1,0:T(8,128)(2,1)} %get-tuple-element.64), channel_id=1, source_target_pairs={{0,8},{8,0},{16,24},{24,16},{1,9},{9,1},{17,25},{25,17},{2,10},{10... | collective-permute-start | bytes 1474568 | tf_op jit(solution)/shard_map/ppermute | solution.py:558
  67.5 2.5 %collective-permute-done.9 = bf16[5,2,32,256]{3,2,1,0:T(8,128)(2,1)S(1)} collective-permute-done((bf16[5,2,32,256]{3,2,1,0:T(8,128)(2,1)}, bf16[5,2,32,256]{3,2,1,0:T(8,128)(2,1)S(1)}, u32[]{:S(2)}, u32[]{:S(2)}) %collective-permute-start.9) | collective-permute-done | bytes 163872 | tf_op jit(solution)/shard_map/ppermute | solution.py:558
  70.1 1.4 %collective-permute-done.8 = bf16[5,2,32,256]{3,2,1,0:T(8,128)(2,1)S(1)} collective-permute-done((bf16[5,2,32,256]{3,2,1,0:T(8,128)(2,1)}, bf16[5,2,32,256]{3,2,1,0:T(8,128)(2,1)S(1)}, u32[]{:S(2)}, u32[]{:S(2)}) %collective-permute-start.8) | collective-permute-done | bytes 163872 | tf_op jit(solution)/shard_map/ppermute | solution.py:558
  71.5 1.4 %collective-permute-start.15 = (bf16[5,6,2,16,256]{4,3,2,1,0:T(8,128)(2,1)}, bf16[5,6,2,16,256]{4,3,2,1,0:T(8,128)(2,1)}, u32[]{:S(2)}, u32[]{:S(2)}) collective-permute-start(bf16[5,6,2,16,256]{4,3,2,1,0:T(8,128)(2,1)} %get-tuple-element.86), channel_id=1, source_target_pairs={{0,24},{8,16},{16,8},{24,0},{1,25},{9,17},{17,9},{25,1},{2,26},{10... | collective-permute-start | bytes 1474568 | tf_op jit(solution)/shard_map/ppermute | solution.py:558
  72.9 1.0 pad_maximum_fusion.own
  73.9 1.3 %collective-permute-start.12 = (bf16[4,5,2,32,256]{4,3,2,1,0:T(8,128)(2,1)S(1)}, bf16[4,5,2,32,256]{4,3,2,1,0:T(8,128)(2,1)}, u32[]{:S(2)}, u32[]{:S(2)}) collective-permute-start(bf16[4,5,2,32,256]{4,3,2,1,0:T(8,128)(2,1)S(1)} %pad_maximum_fusion.own), channel_id=1, source_target_pairs={{1,0},{2,1},{3,2},{4,3},{5,4},{6,5},{7,6},{9,8},{10,9},{11,10},{12... | collective-permute-start | bytes 1966088 | tf_op jit(solution)/shard_map/ppermute | solution.py:546
  75.2 3.9 %collective-permute-start.11 = (bf16[4,5,2,32,256]{4,3,2,1,0:T(8,128)(2,1)S(1)}, bf16[4,5,2,32,256]{4,3,2,1,0:T(8,128)(2,1)}, u32[]{:S(2)}, u32[]{:S(2)}) collective-permute-start(bf16[4,5,2,32,256]{4,3,2,1,0:T(8,128)(2,1)S(1)} %pad_maximum_fusion.own), channel_id=1, source_target_pairs={{0,1},{1,2},{2,3},{3,4},{4,5},{5,6},{6,7},{8,9},{9,10},{10,11},{11... | collective-permute-start | bytes 1966088 | tf_op jit(solution)/shard_map/ppermute | solution.py:546
  79.1 2.3 %collective-permute-done.14.refs_5_ = bf16[5,6,2,16,256]{4,3,2,1,0:T(8,128)(2,1)} collective-permute-done((bf16[5,6,2,16,256]{4,3,2,1,0:T(8,128)(2,1)}, bf16[5,6,2,16,256]{4,3,2,1,0:T(8,128)(2,1)}, u32[]{:S(2)}, u32[]{:S(2)}) %collective-permute-start.14) | collective-permute-done | bytes 491552 | tf_op jit(solution)/shard_map/ppermute | solution.py:558
  81.4 2.0 %collective-permute-start.17 = (bf16[5,6,2,16,256]{4,3,2,1,0:T(8,128)(2,1)}, bf16[5,6,2,16,256]{4,3,2,1,0:T(8,128)(2,1)}, u32[]{:S(2)}, u32[]{:S(2)}) collective-permute-start(bf16[5,6,2,16,256]{4,3,2,1,0:T(8,128)(2,1)} %get-tuple-element.93), channel_id=1, source_target_pairs={{0,16},{8,24},{16,0},{24,8},{1,17},{9,25},{17,1},{25,9},{2,18},{10... | collective-permute-start | bytes 1474568 | tf_op jit(solution)/shard_map/ppermute | solution.py:558
  83.4 0.0 collective-permute-done.1.refs_3_
  83.4 1.5 %collective-permute-start.2 = (bf16[5,6,2,16,256]{4,3,2,1,0:T(8,128)(2,1)}, bf16[5,6,2,16,256]{4,3,2,1,0:T(8,128)(2,1)}, u32[]{:S(2)}, u32[]{:S(2)}) collective-permute-start(bf16[5,6,2,16,256]{4,3,2,1,0:T(8,128)(2,1)} %get-tuple-element.65), channel_id=1, source_target_pairs={{0,8},{8,0},{16,24},{24,16},{1,9},{9,1},{17,25},{25,17},{2,10},{10... | collective-permute-start | bytes 1474568 | tf_op jit(solution)/shard_map/ppermute | solution.py:558
  84.9 7.2 %collective-permute-done.15.refs_7_ = bf16[5,6,2,16,256]{4,3,2,1,0:T(8,128)(2,1)} collective-permute-done((bf16[5,6,2,16,256]{4,3,2,1,0:T(8,128)(2,1)}, bf16[5,6,2,16,256]{4,3,2,1,0:T(8,128)(2,1)}, u32[]{:S(2)}, u32[]{:S(2)}) %collective-permute-start.15) | collective-permute-done | bytes 491552 | tf_op jit(solution)/shard_map/ppermute | solution.py:558
  92.1 3.0 %collective-permute-start.19 = (bf16[5,6,2,16,256]{4,3,2,1,0:T(8,128)(2,1)}, bf16[5,6,2,16,256]{4,3,2,1,0:T(8,128)(2,1)}, u32[]{:S(2)}, u32[]{:S(2)}) collective-permute-start(bf16[5,6,2,16,256]{4,3,2,1,0:T(8,128)(2,1)} %get-tuple-element.97), channel_id=1, source_target_pairs={{0,24},{8,16},{16,8},{24,0},{1,25},{9,17},{17,9},{25,1},{2,26},{10... | collective-permute-start | bytes 1474568 | tf_op jit(solution)/shard_map/ppermute | solution.py:558
  95.1 5.7 %gram_1.1 = (f32[4,16,2,128,128]{4,3,2,1,0:T(8,128)}, f32[4,2,128,128]{3,2,1,0:T(8,128)}, f32[4,2,128,128]{3,2,1,0:T(8,128)}) custom-call(bf16[5,15,2,16,256]{4,3,2,1,0:T(8,128)(2,1)} %get-tuple-element.56.refs_0_, bf16[5,6,2,16,256]{4,3,2,1,0:T(8,128)(2,1)} %get-tuple-element.80.refs_1_, bf16[5,15,2,16,256]{4,3,2,1,0:T(8,128)(2,1)} %collective-permute-done.refs_2_, ...), custom_call_target="tpu_custom_call" | custom-call | flops 1 | bytes 1 | tf_op jit(solution)/shard_map/gram_1/pallas_call | solution.py:517
  100.8 0.0 collective-permute-done.12.after
  100.9 3.8 %rim_gram.1 = (f32[4,16,2,128,128]{4,3,2,1,0:T(8,128)}, f32[4,2,128,128]{3,2,1,0:T(8,128)}) custom-call(s32[1]{0:T(128)} %bitcast.me_ref, bf16[4,5,2,32,256]{4,3,2,1,0:T(8,128)(2,1)} %copy-done.1, bf16[4,5,2,32,256]{4,3,2,1,0:T(8,128)(2,1)} %collective-permute-done.11.before, ...), custom_call_target="tpu_custom_call", output_to_operand_aliasing={{0}: (5, {})} | custom-call | flops 1 | bytes 1 | tf_op jit(solution)/shard_map/rim_gram/pallas_call | solution.py:393
  104.7 0.6 collective-permute-start.18
  105.3 0.0 collective-permute-done.2.refs_3_
  105.3 0.8 collective-permute-start.16
  106.1 7.1 %collective-permute-done.19.refs_7_ = bf16[5,6,2,16,256]{4,3,2,1,0:T(8,128)(2,1)} collective-permute-done((bf16[5,6,2,16,256]{4,3,2,1,0:T(8,128)(2,1)}, bf16[5,6,2,16,256]{4,3,2,1,0:T(8,128)(2,1)}, u32[]{:S(2)}, u32[]{:S(2)}) %collective-permute-start.19) | collective-permute-done | bytes 491552 | tf_op jit(solution)/shard_map/ppermute | solution.py:558
  113.2 3.0 %collective-permute-start.20 = (bf16[5,3,2,16,256]{4,3,2,1,0:T(8,128)(2,1)S(1)}, bf16[5,3,2,16,256]{4,3,2,1,0:T(8,128)(2,1)S(1)}, u32[]{:S(2)}, u32[]{:S(2)}) collective-permute-start(bf16[5,3,2,16,256]{4,3,2,1,0:T(8,128)(2,1)S(1)} %copy-done.6), channel_id=1, source_target_pairs={{0,24},{8,16},{16,8},{24,0},{1,25},{9,17},{17,9},{25,1},{2,26},{10... | collective-permute-start | bytes 737288 | tf_op jit(solution)/shard_map/ppermute | solution.py:558
  116.2 5.6 %gram_7.1 = (f32[4,16,2,128,128]{4,3,2,1,0:T(8,128)}, f32[4,2,128,128]{3,2,1,0:T(8,128)}) custom-call(bf16[5,15,2,16,256]{4,3,2,1,0:T(8,128)(2,1)} %get-tuple-element.56.refs_0_, bf16[5,6,2,16,256]{4,3,2,1,0:T(8,128)(2,1)} %get-tuple-element.99.refs_1_, bf16[5,15,2,16,256]{4,3,2,1,0:T(8,128)(2,1)} %collective-permute-done.refs_2_, ...), custom_call_target="tpu_custom_call", output_to_operand_aliasing={{0}: (10, {})} | custom-call | flops 1 | bytes 1 | tf_op jit(solution)/shard_map/gram_7/pallas_call | solution.py:517
  121.8 0.0 collective-permute-done.18.refs_5_
  121.8 0.0 collective-permute-done.16.refs_3_
  121.8 1.0 collective-permute-done.20.refs_7_
  122.8 3.9 %gram_13.1 = (f32[4,16,2,128,128]{4,3,2,1,0:T(8,128)}, f32[4,2,128,128]{3,2,1,0:T(8,128)}) custom-call(bf16[5,15,2,16,256]{4,3,2,1,0:T(8,128)(2,1)} %get-tuple-element.56.refs_0_, bf16[5,3,2,16,256]{4,3,2,1,0:T(8,128)(2,1)} %get-tuple-element.59.refs_1_, bf16[5,15,2,16,256]{4,3,2,1,0:T(8,128)(2,1)} %collective-permute-done.refs_2_, ...), custom_call_target="tpu_custom_call", output_to_operand_aliasing={{0}: (10, {})} | custom-call | flops 1 | bytes 1 | tf_op jit(solution)/shard_map/gram_13/pallas_call | solution.py:517
  (19 shorter events, 0.0 us)
Async XLA Ops:
  5.4 48.6 %collective-permute-start.7 = (bf16[5,15,2,16,256]{4,3,2,1,0:T(8,128)(2,1)}, bf16[5,15,2,16,256]{4,3,2,1,0:T(8,128)(2,1)S(1)}, u32[]{:S(2)}, u32[]{:S(2)}) collective-permute-start(bf16[5,15,2,16,256]{4,3,2,1,0:T(8,128)(2,1)} %interior_0_3.1), channel_id=1, source_target_pairs={{0,24},{8,16},{16,8},{24,0},{1,25},{9,17},{17,9},{25,1},{2,26},{10... | collective-permute-start | bytes 3686408 | tf_op jit(solution)/shard_map/ppermute | solution.py:558
  19.8 44.7 %collective-permute-start = (bf16[5,15,2,16,256]{4,3,2,1,0:T(8,128)(2,1)}, bf16[5,15,2,16,256]{4,3,2,1,0:T(8,128)(2,1)}, u32[]{:S(2)}, u32[]{:S(2)}) collective-permute-start(bf16[5,15,2,16,256]{4,3,2,1,0:T(8,128)(2,1)} %get-tuple-element.60), channel_id=1, source_target_pairs={{0,8},{8,0},{16,24},{24,16},{1,9},{9,1},{17,25},{25,17},{2,10},{10... | collective-permute-start | bytes 3686408 | tf_op jit(solution)/shard_map/ppermute | solution.py:558
  20.4 44.1 %collective-permute-start.13 = (bf16[5,15,2,16,256]{4,3,2,1,0:T(8,128)(2,1)}, bf16[5,15,2,16,256]{4,3,2,1,0:T(8,128)(2,1)}, u32[]{:S(2)}, u32[]{:S(2)}) collective-permute-start(bf16[5,15,2,16,256]{4,3,2,1,0:T(8,128)(2,1)} %get-tuple-element.81), channel_id=1, source_target_pairs={{0,16},{8,24},{16,0},{24,8},{1,17},{9,25},{17,1},{25,9},{2,18},{10... | collective-permute-start | bytes 3686408 | tf_op jit(solution)/shard_map/ppermute | solution.py:558
  20.5 13.8 %collective-permute-start.3 = (bf16[16,16,256]{2,1,0:T(8,128)(2,1)}, bf16[16,16,256]{2,1,0:T(8,128)(2,1)S(1)}, u32[]{:S(2)}, u32[]{:S(2)}) collective-permute-start(bf16[16,16,256]{2,1,0:T(8,128)(2,1)} %get-tuple-element.68), channel_id=1, source_target_pairs={{0,1},{1,2},{2,3},{3,4},{4,5},{5,6},{6,7},{8,9},{9,10},{10,11},{11... | collective-permute-start | bytes 393224 | tf_op jit(solution)/shard_map/ppermute | solution.py:546
  21.8 17.9 %collective-permute-start.4 = (bf16[16,16,256]{2,1,0:T(8,128)(2,1)}, bf16[16,16,256]{2,1,0:T(8,128)(2,1)S(1)}, u32[]{:S(2)}, u32[]{:S(2)}) collective-permute-start(bf16[16,16,256]{2,1,0:T(8,128)(2,1)} %get-tuple-element.57), channel_id=1, source_target_pairs={{1,0},{2,1},{3,2},{4,3},{5,4},{6,5},{7,6},{9,8},{10,9},{11,10},{12... | collective-permute-start | bytes 393224 | tf_op jit(solution)/shard_map/ppermute | solution.py:546
  34.3 10.0 %copy-start.2 = (bf16[16,16,256]{2,1,0:T(8,128)(2,1)}, bf16[16,16,256]{2,1,0:T(8,128)(2,1)S(1)}, u32[]{:S(2)}) copy-start(bf16[16,16,256]{2,1,0:T(8,128)(2,1)S(1)} %collective-permute-done.3.refs_1_) | copy-start | bytes 393220
  34.3 6.6 %collective-permute-start.5 = (bf16[16,16,256]{2,1,0:T(8,128)(2,1)}, bf16[16,16,256]{2,1,0:T(8,128)(2,1)S(1)}, u32[]{:S(2)}, u32[]{:S(2)}) collective-permute-start(bf16[16,16,256]{2,1,0:T(8,128)(2,1)} %get-tuple-element.70), channel_id=1, source_target_pairs={{0,1},{1,2},{2,3},{3,4},{4,5},{5,6},{6,7},{8,9},{9,10},{10,11},{11... | collective-permute-start | bytes 393224 | tf_op jit(solution)/shard_map/ppermute | solution.py:546
  39.7 4.7 %copy-start.3 = (bf16[16,16,256]{2,1,0:T(8,128)(2,1)}, bf16[16,16,256]{2,1,0:T(8,128)(2,1)S(1)}, u32[]{:S(2)}) copy-start(bf16[16,16,256]{2,1,0:T(8,128)(2,1)S(1)} %collective-permute-done.4.refs_2_) | copy-start | bytes 393220
  39.7 4.7 %collective-permute-start.6 = (bf16[16,16,256]{2,1,0:T(8,128)(2,1)}, bf16[16,16,256]{2,1,0:T(8,128)(2,1)S(1)}, u32[]{:S(2)}, u32[]{:S(2)}) collective-permute-start(bf16[16,16,256]{2,1,0:T(8,128)(2,1)} %get-tuple-element.71), channel_id=1, source_target_pairs={{1,0},{2,1},{3,2},{4,3},{5,4},{6,5},{7,6},{9,8},{10,9},{11,10},{12... | collective-permute-start | bytes 393224 | tf_op jit(solution)/shard_map/ppermute | solution.py:546
  41.0 3.4 %copy-start.4 = (bf16[16,16,256]{2,1,0:T(8,128)(2,1)}, bf16[16,16,256]{2,1,0:T(8,128)(2,1)S(1)}, u32[]{:S(2)}) copy-start(bf16[16,16,256]{2,1,0:T(8,128)(2,1)S(1)} %collective-permute-done.5.refs_5_) | copy-start | bytes 393220
  44.4 0.6 copy-start.5
  54.1 41.0 %copy-start = (bf16[5,15,2,16,256]{4,3,2,1,0:T(8,128)(2,1)}, bf16[5,15,2,16,256]{4,3,2,1,0:T(8,128)(2,1)S(1)}, u32[]{:S(2)}) copy-start(bf16[5,15,2,16,256]{4,3,2,1,0:T(8,128)(2,1)S(1)} %collective-permute-done.7.refs_6_) | copy-start | bytes 3686404
  54.1 13.5 %collective-permute-start.10 = (bf16[5,2,32,256]{3,2,1,0:T(8,128)(2,1)}, bf16[5,2,32,256]{3,2,1,0:T(8,128)(2,1)S(1)}, u32[]{:S(2)}, u32[]{:S(2)}) collective-permute-start(bf16[5,2,32,256]{3,2,1,0:T(8,128)(2,1)} %get-tuple-element.79), channel_id=1, source_target_pairs={{0,24},{8,16},{16,8},{24,0},{1,25},{9,17},{17,9},{25,1},{2,26},{10... | collective-permute-start | bytes 491528 | tf_op jit(solution)/shard_map/ppermute | solution.py:558
  56.6 13.5 %collective-permute-start.9 = (bf16[5,2,32,256]{3,2,1,0:T(8,128)(2,1)}, bf16[5,2,32,256]{3,2,1,0:T(8,128)(2,1)S(1)}, u32[]{:S(2)}, u32[]{:S(2)}) collective-permute-start(bf16[5,2,32,256]{3,2,1,0:T(8,128)(2,1)} %get-tuple-element.77), channel_id=1, source_target_pairs={{0,16},{8,24},{16,0},{24,8},{1,17},{9,25},{17,1},{25,9},{2,18},{10... | collective-permute-start | bytes 491528 | tf_op jit(solution)/shard_map/ppermute | solution.py:558
  57.1 14.4 %collective-permute-start.8 = (bf16[5,2,32,256]{3,2,1,0:T(8,128)(2,1)}, bf16[5,2,32,256]{3,2,1,0:T(8,128)(2,1)S(1)}, u32[]{:S(2)}, u32[]{:S(2)}) collective-permute-start(bf16[5,2,32,256]{3,2,1,0:T(8,128)(2,1)} %get-tuple-element.75), channel_id=1, source_target_pairs={{0,8},{8,0},{16,24},{24,16},{1,9},{9,1},{17,25},{25,17},{2,10},{10... | collective-permute-start | bytes 491528 | tf_op jit(solution)/shard_map/ppermute | solution.py:558
  64.5 16.9 %collective-permute-start.14 = (bf16[5,6,2,16,256]{4,3,2,1,0:T(8,128)(2,1)}, bf16[5,6,2,16,256]{4,3,2,1,0:T(8,128)(2,1)}, u32[]{:S(2)}, u32[]{:S(2)}) collective-permute-start(bf16[5,6,2,16,256]{4,3,2,1,0:T(8,128)(2,1)} %get-tuple-element.83), channel_id=1, source_target_pairs={{0,16},{8,24},{16,0},{24,8},{1,17},{9,25},{17,1},{25,9},{2,18},{10... | collective-permute-start | bytes 1474568 | tf_op jit(solution)/shard_map/ppermute | solution.py:558
  66.0 17.4 %collective-permute-start.1 = (bf16[5,6,2,16,256]{4,3,2,1,0:T(8,128)(2,1)}, bf16[5,6,2,16,256]{4,3,2,1,0:T(8,128)(2,1)}, u32[]{:S(2)}, u32[]{:S(2)}) collective-permute-start(bf16[5,6,2,16,256]{4,3,2,1,0:T(8,128)(2,1)} %get-tuple-element.64), channel_id=1, source_target_pairs={{0,8},{8,0},{16,24},{24,16},{1,9},{9,1},{17,25},{25,17},{2,10},{10... | collective-permute-start | bytes 1474568 | tf_op jit(solution)/shard_map/ppermute | solution.py:558
  71.5 20.7 %collective-permute-start.15 = (bf16[5,6,2,16,256]{4,3,2,1,0:T(8,128)(2,1)}, bf16[5,6,2,16,256]{4,3,2,1,0:T(8,128)(2,1)}, u32[]{:S(2)}, u32[]{:S(2)}) collective-permute-start(bf16[5,6,2,16,256]{4,3,2,1,0:T(8,128)(2,1)} %get-tuple-element.86), channel_id=1, source_target_pairs={{0,24},{8,16},{16,8},{24,0},{1,25},{9,17},{17,9},{25,1},{2,26},{10... | collective-permute-start | bytes 1474568 | tf_op jit(solution)/shard_map/ppermute | solution.py:558
  73.9 26.9 %copy-start.1 = (bf16[4,5,2,32,256]{4,3,2,1,0:T(8,128)(2,1)}, bf16[4,5,2,32,256]{4,3,2,1,0:T(8,128)(2,1)S(1)}, u32[]{:S(2)}) copy-start(bf16[4,5,2,32,256]{4,3,2,1,0:T(8,128)(2,1)S(1)} %pad_maximum_fusion.own) | copy-start | bytes 1966084
  73.9 26.9 %collective-permute-start.12 = (bf16[4,5,2,32,256]{4,3,2,1,0:T(8,128)(2,1)S(1)}, bf16[4,5,2,32,256]{4,3,2,1,0:T(8,128)(2,1)}, u32[]{:S(2)}, u32[]{:S(2)}) collective-permute-start(bf16[4,5,2,32,256]{4,3,2,1,0:T(8,128)(2,1)S(1)} %pad_maximum_fusion.own), channel_id=1, source_target_pairs={{1,0},{2,1},{3,2},{4,3},{5,4},{6,5},{7,6},{9,8},{10,9},{11,10},{12... | collective-permute-start | bytes 1966088 | tf_op jit(solution)/shard_map/ppermute | solution.py:546
  75.2 25.6 %collective-permute-start.11 = (bf16[4,5,2,32,256]{4,3,2,1,0:T(8,128)(2,1)S(1)}, bf16[4,5,2,32,256]{4,3,2,1,0:T(8,128)(2,1)}, u32[]{:S(2)}, u32[]{:S(2)}) collective-permute-start(bf16[4,5,2,32,256]{4,3,2,1,0:T(8,128)(2,1)S(1)} %pad_maximum_fusion.own), channel_id=1, source_target_pairs={{0,1},{1,2},{2,3},{3,4},{4,5},{5,6},{6,7},{8,9},{9,10},{10,11},{11... | collective-permute-start | bytes 1966088 | tf_op jit(solution)/shard_map/ppermute | solution.py:546
  81.4 23.3 %collective-permute-start.17 = (bf16[5,6,2,16,256]{4,3,2,1,0:T(8,128)(2,1)}, bf16[5,6,2,16,256]{4,3,2,1,0:T(8,128)(2,1)}, u32[]{:S(2)}, u32[]{:S(2)}) collective-permute-start(bf16[5,6,2,16,256]{4,3,2,1,0:T(8,128)(2,1)} %get-tuple-element.93), channel_id=1, source_target_pairs={{0,16},{8,24},{16,0},{24,8},{1,17},{9,25},{17,1},{25,9},{2,18},{10... | collective-permute-start | bytes 1474568 | tf_op jit(solution)/shard_map/ppermute | solution.py:558
  83.4 21.9 %collective-permute-start.2 = (bf16[5,6,2,16,256]{4,3,2,1,0:T(8,128)(2,1)}, bf16[5,6,2,16,256]{4,3,2,1,0:T(8,128)(2,1)}, u32[]{:S(2)}, u32[]{:S(2)}) collective-permute-start(bf16[5,6,2,16,256]{4,3,2,1,0:T(8,128)(2,1)} %get-tuple-element.65), channel_id=1, source_target_pairs={{0,8},{8,0},{16,24},{24,16},{1,9},{9,1},{17,25},{25,17},{2,10},{10... | collective-permute-start | bytes 1474568 | tf_op jit(solution)/shard_map/ppermute | solution.py:558
  92.1 21.1 %collective-permute-start.19 = (bf16[5,6,2,16,256]{4,3,2,1,0:T(8,128)(2,1)}, bf16[5,6,2,16,256]{4,3,2,1,0:T(8,128)(2,1)}, u32[]{:S(2)}, u32[]{:S(2)}) collective-permute-start(bf16[5,6,2,16,256]{4,3,2,1,0:T(8,128)(2,1)} %get-tuple-element.97), channel_id=1, source_target_pairs={{0,24},{8,16},{16,8},{24,0},{1,25},{9,17},{17,9},{25,1},{2,26},{10... | collective-permute-start | bytes 1474568 | tf_op jit(solution)/shard_map/ppermute | solution.py:558
  100.8 4.4 %copy-start.7 = (bf16[5,3,2,16,256]{4,3,2,1,0:T(8,128)(2,1)S(1)}, bf16[5,3,2,16,256]{4,3,2,1,0:T(8,128)(2,1)}, u32[]{:S(2)}) copy-start(bf16[5,3,2,16,256]{4,3,2,1,0:T(8,128)(2,1)} %get-tuple-element.90) | copy-start | bytes 737284
  100.9 12.4 %copy-start.6 = (bf16[5,3,2,16,256]{4,3,2,1,0:T(8,128)(2,1)S(1)}, bf16[5,3,2,16,256]{4,3,2,1,0:T(8,128)(2,1)}, u32[]{:S(2)}) copy-start(bf16[5,3,2,16,256]{4,3,2,1,0:T(8,128)(2,1)} %get-tuple-element.98) | copy-start | bytes 737284
  104.7 17.1 %collective-permute-start.18 = (bf16[5,3,2,16,256]{4,3,2,1,0:T(8,128)(2,1)}, bf16[5,3,2,16,256]{4,3,2,1,0:T(8,128)(2,1)S(1)}, u32[]{:S(2)}, u32[]{:S(2)}) collective-permute-start(bf16[5,3,2,16,256]{4,3,2,1,0:T(8,128)(2,1)} %get-tuple-element.94), channel_id=1, source_target_pairs={{0,16},{8,24},{16,0},{24,8},{1,17},{9,25},{17,1},{25,9},{2,18},{10... | collective-permute-start | bytes 737288 | tf_op jit(solution)/shard_map/ppermute | solution.py:558
  105.3 16.5 %collective-permute-start.16 = (bf16[5,3,2,16,256]{4,3,2,1,0:T(8,128)(2,1)S(1)}, bf16[5,3,2,16,256]{4,3,2,1,0:T(8,128)(2,1)S(1)}, u32[]{:S(2)}, u32[]{:S(2)}) collective-permute-start(bf16[5,3,2,16,256]{4,3,2,1,0:T(8,128)(2,1)S(1)} %copy-done.7), channel_id=1, source_target_pairs={{0,8},{8,0},{16,24},{24,16},{1,9},{9,1},{17,25},{25,17},{2,10},{10... | collective-permute-start | bytes 737288 | tf_op jit(solution)/shard_map/ppermute | solution.py:558
  113.2 9.6 %collective-permute-start.20 = (bf16[5,3,2,16,256]{4,3,2,1,0:T(8,128)(2,1)S(1)}, bf16[5,3,2,16,256]{4,3,2,1,0:T(8,128)(2,1)S(1)}, u32[]{:S(2)}, u32[]{:S(2)}) collective-permute-start(bf16[5,3,2,16,256]{4,3,2,1,0:T(8,128)(2,1)S(1)} %copy-done.6), channel_id=1, source_target_pairs={{0,24},{8,16},{16,8},{24,0},{1,25},{9,17},{17,9},{25,1},{2,26},{10... | collective-permute-start | bytes 737288 | tf_op jit(solution)/shard_map/ppermute | solution.py:558

commit v7 on v6

--- a/solution.py
+++ b/solution.py
@@ -67,8 +67,8 @@
         there = pl.ds(part * DBLK + step * per_step, per_step)
         return [
             pltpu.make_async_copy(rk_any.at[there, rows_in], rk_ref.at[here, pl.ds(0, taken)], in_sems.at[step, 0]),
-            pltpu.make_async_copy(slc_any.at[0, there, rows_in], slc_ref.at[0, here, rows_in], in_sems.at[step, 1]),
-            pltpu.make_async_copy(slc_any.at[1, there, rows_in], slc_ref.at[1, here, rows_in], in_sems.at[step, 2]),
+            pltpu.make_async_copy(slc_any.at[0, there, rows_in], slc_ref.at[0, here, pl.ds(0, taken)], in_sems.at[step, 1]),
+            pltpu.make_async_copy(slc_any.at[1, there, rows_in], slc_ref.at[1, here, pl.ds(0, taken)], in_sems.at[step, 2]),
             pltpu.make_async_copy(ak_any.at[there], ak_ref.at[here], in_sems.at[step, 3]),
         ]
 
@@ -84,8 +84,11 @@
     def along_range(step):
         for n in range(per_step):
             i = step * per_step + n
+            weights = rk_ref[i, :taken]
+            if taken < n_rows:
+                weights = pltpu.roll(weights.astype(f32), lax.rem(n_rows - top, n_rows), 1).astype(bf16)[:, :taken]
             for c in range(2):
-                value = jnp.dot(rk_ref[i, :taken], slc_ref[c, i], preferred_element_type=f32)
+                value = jnp.dot(weights, slc_ref[c, i, :taken], preferred_element_type=f32)
                 ranged[i, c * taken : (c + 1) * taken, :] = value.astype(bf16)
 
     def prepare(step):
@@ -110,14 +113,6 @@
     for h in range(halves):
         plane[h, : SUB * pitch, :] = zero
         plane[h, (SUB + n_rows) * pitch :, :] = zero
-    if taken < n_rows:
-
-        def clear(n, carry):
-            at = pl.multiple_of(jnp.where(n * SIDE < top, n * SIDE, n * SIDE + taken), SIDE)
-            slc_ref[:, :, pl.ds(at, SIDE), :] = jnp.zeros((2, DBLK, SIDE, n_az), bf16)
-            return carry
-
-        lax.fori_loop(0, (n_rows - taken) // SIDE, clear, 0)
     wait(0)
     along_range(0)
     prepare(0)

time: 127 us -> 127 us (level)
  no operation moved by 1% of the time
where the time goes in v7:
time: 127 us
  Pallas kernels  55 us (43%)
  starting transfers between devices  37.8 us (30%)
  waiting for transfers between devices  31.8 us (25%)
    ppermute x15, waiting for transfers between devices, exchange(): got.append(lax.ppermute(block, 'date', [(i, i ^ k) for i in range(n)]))  28.5 us
    pallas_call x3, Pallas kernels, interior(): pl.pallas_call(functools.partial(interior_kernel, spans, targets, edged,...  27 us
    ppermute x15, starting transfers between devices, exchange(): got.append(lax.ppermute(block, 'date', [(i, i ^ k) for i in range(n)]))  23.4 us
    pallas_call x3, Pallas kernels, gram(): pl.pallas_call(functools.partial(gram_kernel, partners, parts, offsets, c...  15.2 us
    ppermute x6, starting transfers between devices, shift(): return lax.ppermute(value, axis, pairs)  14.4 us
    pallas_call x1, Pallas kernels, rim(): pl.pallas_call(functools.partial(rim_kernel, dest_rows, parts), grid_spec...  9.07 us
    pallas_call x1, Pallas kernels, rim_gram(): pl.pallas_call(rim_gram_kernel, in_specs=[pl.BlockSpec(memory_space=pltpu...  3.81 us
    ppermute x6, waiting for transfers between devices, shift(): return lax.ppermute(value, axis, pairs)  3.38 us
  transfers between devices with their start and end apart: 21, of which 8 were waited for; matrix products, arithmetic and copies ran while one was open for 1% of the time, Pallas kernels for 36%

profile of v7, /device:TPU:0, one launch (start us, length us, event | category | flops | bytes accessed | tf_op | source)
XLA Modules:
  0.0 126.5 jit_solution(3788794365232984345)
XLA Ops:
  0.0 5.3 %interior_0_3.1 = bf16[5,15,2,16,256]{4,3,2,1,0:T(8,128)(2,1)} custom-call(s32[1]{0:T(128)} %bitcast.me_ref, bf16[2,32,256,256]{3,2,1,0:T(8,128)(2,1)} %slc_any.5, bf16[32,256,256]{2,1,0:T(8,128)(2,1)} %rk_any.5, bf16[32,272,256]{2,1,0:T(8,128)(2,1)} %refs_7_.1), custom_call_target="tpu_custom_call" | custom-call | flops 1 | bytes 1 | tf_op jit(solution)/shard_map/interior_0_3/pallas_call | solution.py:201
  5.3 4.0 %collective-permute-start.7 = (bf16[5,15,2,16,256]{4,3,2,1,0:T(8,128)(2,1)}, bf16[5,15,2,16,256]{4,3,2,1,0:T(8,128)(2,1)S(1)}, u32[]{:S(2)}, u32[]{:S(2)}) collective-permute-start(bf16[5,15,2,16,256]{4,3,2,1,0:T(8,128)(2,1)} %interior_0_3.1), channel_id=1, source_target_pairs={{0,24},{8,16},{16,8},{24,0},{1,25},{9,17},{17,9},{25,1},{2,26},{10... | collective-permute-start | bytes 3686408 | tf_op jit(solution)/shard_map/ppermute | solution.py:553
  9.3 10.4 %interior_0_1.1 = (bf16[16,2,32,256]{3,2,1,0:T(8,128)(2,1)}, bf16[16,16,256]{2,1,0:T(8,128)(2,1)}, bf16[16,16,256]{2,1,0:T(8,128)(2,1)}, bf16[5,15,2,16,256]{4,3...) custom-call(s32[1]{0:T(128)} %bitcast.me_ref, ...), custom_call_target="tpu_custom_call" | custom-call | flops 1 | bytes 1 | tf_op jit(solution)/shard_map/interior_0_1/pallas_call | solution.py:201
  19.7 0.6 collective-permute-start
  20.3 0.1 collective-permute-start.13
  20.3 1.3 %collective-permute-start.3 = (bf16[16,16,256]{2,1,0:T(8,128)(2,1)}, bf16[16,16,256]{2,1,0:T(8,128)(2,1)S(1)}, u32[]{:S(2)}, u32[]{:S(2)}) collective-permute-start(bf16[16,16,256]{2,1,0:T(8,128)(2,1)} %get-tuple-element.68), channel_id=1, source_target_pairs={{0,1},{1,2},{2,3},{3,4},{4,5},{5,6},{6,7},{8,9},{9,10},{10,11},{11... | collective-permute-start | bytes 393224 | tf_op jit(solution)/shard_map/ppermute | solution.py:541
  21.6 1.3 %collective-permute-start.4 = (bf16[16,16,256]{2,1,0:T(8,128)(2,1)}, bf16[16,16,256]{2,1,0:T(8,128)(2,1)S(1)}, u32[]{:S(2)}, u32[]{:S(2)}) collective-permute-start(bf16[16,16,256]{2,1,0:T(8,128)(2,1)} %get-tuple-element.57), channel_id=1, source_target_pairs={{1,0},{2,1},{3,2},{4,3},{5,4},{6,5},{7,6},{9,8},{10,9},{11,10},{12... | collective-permute-start | bytes 393224 | tf_op jit(solution)/shard_map/ppermute | solution.py:541
  22.9 11.2 %interior_1_1.1 = (bf16[16,2,32,256]{3,2,1,0:T(8,128)(2,1)}, bf16[16,16,256]{2,1,0:T(8,128)(2,1)}, bf16[16,16,256]{2,1,0:T(8,128)(2,1)}, bf16[5,6,2,16,256]{4,3,...) custom-call(s32[1]{0:T(128)} %bitcast.me_ref, ...), custom_call_target="tpu_custom_call" | custom-call | flops 1 | bytes 1 | tf_op jit(solution)/shard_map/interior_1_1/pallas_call | solution.py:201
  34.2 0.0 collective-permute-done.3.refs_1_
  34.2 5.3 %collective-permute-start.5 = (bf16[16,16,256]{2,1,0:T(8,128)(2,1)}, bf16[16,16,256]{2,1,0:T(8,128)(2,1)S(1)}, u32[]{:S(2)}, u32[]{:S(2)}) collective-permute-start(bf16[16,16,256]{2,1,0:T(8,128)(2,1)} %get-tuple-element.70), channel_id=1, source_target_pairs={{0,1},{1,2},{2,3},{3,4},{4,5},{5,6},{6,7},{8,9},{9,10},{10,11},{11... | collective-permute-start | bytes 393224 | tf_op jit(solution)/shard_map/ppermute | solution.py:541
  39.5 0.0 collective-permute-done.4.refs_2_
  39.5 1.3 %collective-permute-start.6 = (bf16[16,16,256]{2,1,0:T(8,128)(2,1)}, bf16[16,16,256]{2,1,0:T(8,128)(2,1)S(1)}, u32[]{:S(2)}, u32[]{:S(2)}) collective-permute-start(bf16[16,16,256]{2,1,0:T(8,128)(2,1)} %get-tuple-element.71), channel_id=1, source_target_pairs={{1,0},{2,1},{3,2},{4,3},{5,4},{6,5},{7,6},{9,8},{10,9},{11,10},{12... | collective-permute-start | bytes 393224 | tf_op jit(solution)/shard_map/ppermute | solution.py:541
  40.8 0.0 collective-permute-done.5.refs_5_
  40.8 3.4 %collective-permute-done.6.refs_6_ = bf16[16,16,256]{2,1,0:T(8,128)(2,1)S(1)} collective-permute-done((bf16[16,16,256]{2,1,0:T(8,128)(2,1)}, bf16[16,16,256]{2,1,0:T(8,128)(2,1)S(1)}, u32[]{:S(2)}, u32[]{:S(2)}) %collective-permute-start.6) | collective-permute-done | bytes 131104 | tf_op jit(solution)/shard_map/ppermute | solution.py:541
  44.2 0.6 copy-done.5
  44.9 9.1 %rim.1 = (bf16[5,2,32,256]{3,2,1,0:T(8,128)(2,1)}, bf16[5,2,32,256]{3,2,1,0:T(8,128)(2,1)}, bf16[5,2,32,256]{3,2,1,0:T(8,128)(2,1)}, bf16[5,2,32,256]{3,2,1,0:T(8,128)(2,1)}) custom-call(s32[1]{0:T(128)} %bitcast.me_ref, bf16[16,2,32,256]{3,2,1,0:T(8,128)(2,1)} %get-tuple-element.67.refs_0_, bf16[16,16,256]{2,1,0:T(8,128)(2,1)} %copy-done.2, ...), custom_call_target="tpu_custom_call" | custom-call | flops 1 | bytes 1 | tf_op jit(solution)/shard_map/rim/pallas_call | solution.py:316
  53.9 2.5 %collective-permute-start.10 = (bf16[5,2,32,256]{3,2,1,0:T(8,128)(2,1)}, bf16[5,2,32,256]{3,2,1,0:T(8,128)(2,1)S(1)}, u32[]{:S(2)}, u32[]{:S(2)}) collective-permute-start(bf16[5,2,32,256]{3,2,1,0:T(8,128)(2,1)} %get-tuple-element.79), channel_id=1, source_target_pairs={{0,24},{8,16},{16,8},{24,0},{1,25},{9,17},{17,9},{25,1},{2,26},{10... | collective-permute-start | bytes 491528 | tf_op jit(solution)/shard_map/ppermute | solution.py:553
  56.5 0.5 collective-permute-start.9
  57.0 0.5 collective-permute-start.8
  57.5 6.9 %collective-permute-done.refs_2_ = bf16[5,15,2,16,256]{4,3,2,1,0:T(8,128)(2,1)} collective-permute-done((bf16[5,15,2,16,256]{4,3,2,1,0:T(8,128)(2,1)}, bf16[5,15,2,16,256]{4,3,2,1,0:T(8,128)(2,1)}, u32[]{:S(2)}, u32[]{:S(2)}) %collective-permute-start) | collective-permute-done | bytes 1228832 | tf_op jit(solution)/shard_map/ppermute | solution.py:553
  64.4 0.0 collective-permute-done.13.refs_4_
  64.4 1.5 %collective-permute-start.14 = (bf16[5,6,2,16,256]{4,3,2,1,0:T(8,128)(2,1)}, bf16[5,6,2,16,256]{4,3,2,1,0:T(8,128)(2,1)}, u32[]{:S(2)}, u32[]{:S(2)}) collective-permute-start(bf16[5,6,2,16,256]{4,3,2,1,0:T(8,128)(2,1)} %get-tuple-element.83), channel_id=1, source_target_pairs={{0,16},{8,24},{16,0},{24,8},{1,17},{9,25},{17,1},{25,9},{2,18},{10... | collective-permute-start | bytes 1474568 | tf_op jit(solution)/shard_map/ppermute | solution.py:553
  65.9 1.5 %collective-permute-start.1 = (bf16[5,6,2,16,256]{4,3,2,1,0:T(8,128)(2,1)}, bf16[5,6,2,16,256]{4,3,2,1,0:T(8,128)(2,1)}, u32[]{:S(2)}, u32[]{:S(2)}) collective-permute-start(bf16[5,6,2,16,256]{4,3,2,1,0:T(8,128)(2,1)} %get-tuple-element.64), channel_id=1, source_target_pairs={{0,8},{8,0},{16,24},{24,16},{1,9},{9,1},{17,25},{25,17},{2,10},{10... | collective-permute-start | bytes 1474568 | tf_op jit(solution)/shard_map/ppermute | solution.py:553
  67.4 0.0 collective-permute-done.10
  67.4 2.6 %collective-permute-done.9 = bf16[5,2,32,256]{3,2,1,0:T(8,128)(2,1)S(1)} collective-permute-done((bf16[5,2,32,256]{3,2,1,0:T(8,128)(2,1)}, bf16[5,2,32,256]{3,2,1,0:T(8,128)(2,1)S(1)}, u32[]{:S(2)}, u32[]{:S(2)}) %collective-permute-start.9) | collective-permute-done | bytes 163872 | tf_op jit(solution)/shard_map/ppermute | solution.py:553
  69.9 1.4 %collective-permute-done.8 = bf16[5,2,32,256]{3,2,1,0:T(8,128)(2,1)S(1)} collective-permute-done((bf16[5,2,32,256]{3,2,1,0:T(8,128)(2,1)}, bf16[5,2,32,256]{3,2,1,0:T(8,128)(2,1)S(1)}, u32[]{:S(2)}, u32[]{:S(2)}) %collective-permute-start.8) | collective-permute-done | bytes 163872 | tf_op jit(solution)/shard_map/ppermute | solution.py:553
  71.3 1.4 %collective-permute-start.15 = (bf16[5,6,2,16,256]{4,3,2,1,0:T(8,128)(2,1)}, bf16[5,6,2,16,256]{4,3,2,1,0:T(8,128)(2,1)}, u32[]{:S(2)}, u32[]{:S(2)}) collective-permute-start(bf16[5,6,2,16,256]{4,3,2,1,0:T(8,128)(2,1)} %get-tuple-element.86), channel_id=1, source_target_pairs={{0,24},{8,16},{16,8},{24,0},{1,25},{9,17},{17,9},{25,1},{2,26},{10... | collective-permute-start | bytes 1474568 | tf_op jit(solution)/shard_map/ppermute | solution.py:553
  72.8 1.0 pad_maximum_fusion.own
  73.8 1.3 %collective-permute-start.12 = (bf16[4,5,2,32,256]{4,3,2,1,0:T(8,128)(2,1)S(1)}, bf16[4,5,2,32,256]{4,3,2,1,0:T(8,128)(2,1)}, u32[]{:S(2)}, u32[]{:S(2)}) collective-permute-start(bf16[4,5,2,32,256]{4,3,2,1,0:T(8,128)(2,1)S(1)} %pad_maximum_fusion.own), channel_id=1, source_target_pairs={{1,0},{2,1},{3,2},{4,3},{5,4},{6,5},{7,6},{9,8},{10,9},{11,10},{12... | collective-permute-start | bytes 1966088 | tf_op jit(solution)/shard_map/ppermute | solution.py:541
  75.1 3.9 %collective-permute-start.11 = (bf16[4,5,2,32,256]{4,3,2,1,0:T(8,128)(2,1)S(1)}, bf16[4,5,2,32,256]{4,3,2,1,0:T(8,128)(2,1)}, u32[]{:S(2)}, u32[]{:S(2)}) collective-permute-start(bf16[4,5,2,32,256]{4,3,2,1,0:T(8,128)(2,1)S(1)} %pad_maximum_fusion.own), channel_id=1, source_target_pairs={{0,1},{1,2},{2,3},{3,4},{4,5},{5,6},{6,7},{8,9},{9,10},{10,11},{11... | collective-permute-start | bytes 1966088 | tf_op jit(solution)/shard_map/ppermute | solution.py:541
  79.0 2.3 %collective-permute-done.14.refs_5_ = bf16[5,6,2,16,256]{4,3,2,1,0:T(8,128)(2,1)} collective-permute-done((bf16[5,6,2,16,256]{4,3,2,1,0:T(8,128)(2,1)}, bf16[5,6,2,16,256]{4,3,2,1,0:T(8,128)(2,1)}, u32[]{:S(2)}, u32[]{:S(2)}) %collective-permute-start.14) | collective-permute-done | bytes 491552 | tf_op jit(solution)/shard_map/ppermute | solution.py:553
  81.2 2.0 %collective-permute-start.17 = (bf16[5,6,2,16,256]{4,3,2,1,0:T(8,128)(2,1)}, bf16[5,6,2,16,256]{4,3,2,1,0:T(8,128)(2,1)}, u32[]{:S(2)}, u32[]{:S(2)}) collective-permute-start(bf16[5,6,2,16,256]{4,3,2,1,0:T(8,128)(2,1)} %get-tuple-element.93), channel_id=1, source_target_pairs={{0,16},{8,24},{16,0},{24,8},{1,17},{9,25},{17,1},{25,9},{2,18},{10... | collective-permute-start | bytes 1474568 | tf_op jit(solution)/shard_map/ppermute | solution.py:553
  83.3 0.0 collective-permute-done.1.refs_3_
  83.3 1.5 %collective-permute-start.2 = (bf16[5,6,2,16,256]{4,3,2,1,0:T(8,128)(2,1)}, bf16[5,6,2,16,256]{4,3,2,1,0:T(8,128)(2,1)}, u32[]{:S(2)}, u32[]{:S(2)}) collective-permute-start(bf16[5,6,2,16,256]{4,3,2,1,0:T(8,128)(2,1)} %get-tuple-element.65), channel_id=1, source_target_pairs={{0,8},{8,0},{16,24},{24,16},{1,9},{9,1},{17,25},{25,17},{2,10},{10... | collective-permute-start | bytes 1474568 | tf_op jit(solution)/shard_map/ppermute | solution.py:553
  84.7 7.2 %collective-permute-done.15.refs_7_ = bf16[5,6,2,16,256]{4,3,2,1,0:T(8,128)(2,1)} collective-permute-done((bf16[5,6,2,16,256]{4,3,2,1,0:T(8,128)(2,1)}, bf16[5,6,2,16,256]{4,3,2,1,0:T(8,128)(2,1)}, u32[]{:S(2)}, u32[]{:S(2)}) %collective-permute-start.15) | collective-permute-done | bytes 491552 | tf_op jit(solution)/shard_map/ppermute | solution.py:553
  92.0 3.0 %collective-permute-start.19 = (bf16[5,6,2,16,256]{4,3,2,1,0:T(8,128)(2,1)}, bf16[5,6,2,16,256]{4,3,2,1,0:T(8,128)(2,1)}, u32[]{:S(2)}, u32[]{:S(2)}) collective-permute-start(bf16[5,6,2,16,256]{4,3,2,1,0:T(8,128)(2,1)} %get-tuple-element.97), channel_id=1, source_target_pairs={{0,24},{8,16},{16,8},{24,0},{1,25},{9,17},{17,9},{25,1},{2,26},{10... | collective-permute-start | bytes 1474568 | tf_op jit(solution)/shard_map/ppermute | solution.py:553
  94.9 5.7 %gram_1.1 = (f32[4,16,2,128,128]{4,3,2,1,0:T(8,128)}, f32[4,2,128,128]{3,2,1,0:T(8,128)}, f32[4,2,128,128]{3,2,1,0:T(8,128)}) custom-call(bf16[5,15,2,16,256]{4,3,2,1,0:T(8,128)(2,1)} %get-tuple-element.56.refs_0_, bf16[5,6,2,16,256]{4,3,2,1,0:T(8,128)(2,1)} %get-tuple-element.80.refs_1_, bf16[5,15,2,16,256]{4,3,2,1,0:T(8,128)(2,1)} %collective-permute-done.refs_2_, ...), custom_call_target="tpu_custom_call" | custom-call | flops 1 | bytes 1 | tf_op jit(solution)/shard_map/gram_1/pallas_call | solution.py:512
  100.7 0.0 collective-permute-done.12.after
  100.7 3.8 %rim_gram.1 = (f32[4,16,2,128,128]{4,3,2,1,0:T(8,128)}, f32[4,2,128,128]{3,2,1,0:T(8,128)}) custom-call(s32[1]{0:T(128)} %bitcast.me_ref, bf16[4,5,2,32,256]{4,3,2,1,0:T(8,128)(2,1)} %copy-done.1, bf16[4,5,2,32,256]{4,3,2,1,0:T(8,128)(2,1)} %collective-permute-done.11.before, ...), custom_call_target="tpu_custom_call", output_to_operand_aliasing={{0}: (5, {})} | custom-call | flops 1 | bytes 1 | tf_op jit(solution)/shard_map/rim_gram/pallas_call | solution.py:388
  104.6 0.6 collective-permute-start.18
  105.1 0.0 collective-permute-done.2.refs_3_
  105.1 0.8 collective-permute-start.16
  105.9 7.1 %collective-permute-done.19.refs_7_ = bf16[5,6,2,16,256]{4,3,2,1,0:T(8,128)(2,1)} collective-permute-done((bf16[5,6,2,16,256]{4,3,2,1,0:T(8,128)(2,1)}, bf16[5,6,2,16,256]{4,3,2,1,0:T(8,128)(2,1)}, u32[]{:S(2)}, u32[]{:S(2)}) %collective-permute-start.19) | collective-permute-done | bytes 491552 | tf_op jit(solution)/shard_map/ppermute | solution.py:553
  113.1 3.0 %collective-permute-start.20 = (bf16[5,3,2,16,256]{4,3,2,1,0:T(8,128)(2,1)S(1)}, bf16[5,3,2,16,256]{4,3,2,1,0:T(8,128)(2,1)S(1)}, u32[]{:S(2)}, u32[]{:S(2)}) collective-permute-start(bf16[5,3,2,16,256]{4,3,2,1,0:T(8,128)(2,1)S(1)} %copy-done.6), channel_id=1, source_target_pairs={{0,24},{8,16},{16,8},{24,0},{1,25},{9,17},{17,9},{25,1},{2,26},{10... | collective-permute-start | bytes 737288 | tf_op jit(solution)/shard_map/ppermute | solution.py:553
  116.0 5.6 %gram_7.1 = (f32[4,16,2,128,128]{4,3,2,1,0:T(8,128)}, f32[4,2,128,128]{3,2,1,0:T(8,128)}) custom-call(bf16[5,15,2,16,256]{4,3,2,1,0:T(8,128)(2,1)} %get-tuple-element.56.refs_0_, bf16[5,6,2,16,256]{4,3,2,1,0:T(8,128)(2,1)} %get-tuple-element.99.refs_1_, bf16[5,15,2,16,256]{4,3,2,1,0:T(8,128)(2,1)} %collective-permute-done.refs_2_, ...), custom_call_target="tpu_custom_call", output_to_operand_aliasing={{0}: (10, {})} | custom-call | flops 1 | bytes 1 | tf_op jit(solution)/shard_map/gram_7/pallas_call | solution.py:512
  121.7 0.0 collective-permute-done.16.refs_3_
  121.7 1.0 collective-permute-done.20.refs_7_
  122.7 3.9 %gram_13.1 = (f32[4,16,2,128,128]{4,3,2,1,0:T(8,128)}, f32[4,2,128,128]{3,2,1,0:T(8,128)}) custom-call(bf16[5,15,2,16,256]{4,3,2,1,0:T(8,128)(2,1)} %get-tuple-element.56.refs_0_, bf16[5,3,2,16,256]{4,3,2,1,0:T(8,128)(2,1)} %get-tuple-element.59.refs_1_, bf16[5,15,2,16,256]{4,3,2,1,0:T(8,128)(2,1)} %collective-permute-done.refs_2_, ...), custom_call_target="tpu_custom_call", output_to_operand_aliasing={{0}: (10, {})} | custom-call | flops 1 | bytes 1 | tf_op jit(solution)/shard_map/gram_13/pallas_call | solution.py:512
  (19 shorter events, 0.0 us)
Async XLA Ops:
  5.3 48.6 %collective-permute-start.7 = (bf16[5,15,2,16,256]{4,3,2,1,0:T(8,128)(2,1)}, bf16[5,15,2,16,256]{4,3,2,1,0:T(8,128)(2,1)S(1)}, u32[]{:S(2)}, u32[]{:S(2)}) collective-permute-start(bf16[5,15,2,16,256]{4,3,2,1,0:T(8,128)(2,1)} %interior_0_3.1), channel_id=1, source_target_pairs={{0,24},{8,16},{16,8},{24,0},{1,25},{9,17},{17,9},{25,1},{2,26},{10... | collective-permute-start | bytes 3686408 | tf_op jit(solution)/shard_map/ppermute | solution.py:553
  19.7 44.7 %collective-permute-start = (bf16[5,15,2,16,256]{4,3,2,1,0:T(8,128)(2,1)}, bf16[5,15,2,16,256]{4,3,2,1,0:T(8,128)(2,1)}, u32[]{:S(2)}, u32[]{:S(2)}) collective-permute-start(bf16[5,15,2,16,256]{4,3,2,1,0:T(8,128)(2,1)} %get-tuple-element.60), channel_id=1, source_target_pairs={{0,8},{8,0},{16,24},{24,16},{1,9},{9,1},{17,25},{25,17},{2,10},{10... | collective-permute-start | bytes 3686408 | tf_op jit(solution)/shard_map/ppermute | solution.py:553
  20.3 44.1 %collective-permute-start.13 = (bf16[5,15,2,16,256]{4,3,2,1,0:T(8,128)(2,1)}, bf16[5,15,2,16,256]{4,3,2,1,0:T(8,128)(2,1)}, u32[]{:S(2)}, u32[]{:S(2)}) collective-permute-start(bf16[5,15,2,16,256]{4,3,2,1,0:T(8,128)(2,1)} %get-tuple-element.81), channel_id=1, source_target_pairs={{0,16},{8,24},{16,0},{24,8},{1,17},{9,25},{17,1},{25,9},{2,18},{10... | collective-permute-start | bytes 3686408 | tf_op jit(solution)/shard_map/ppermute | solution.py:553
  20.3 13.8 %collective-permute-start.3 = (bf16[16,16,256]{2,1,0:T(8,128)(2,1)}, bf16[16,16,256]{2,1,0:T(8,128)(2,1)S(1)}, u32[]{:S(2)}, u32[]{:S(2)}) collective-permute-start(bf16[16,16,256]{2,1,0:T(8,128)(2,1)} %get-tuple-element.68), channel_id=1, source_target_pairs={{0,1},{1,2},{2,3},{3,4},{4,5},{5,6},{6,7},{8,9},{9,10},{10,11},{11... | collective-permute-start | bytes 393224 | tf_op jit(solution)/shard_map/ppermute | solution.py:541
  21.6 17.9 %collective-permute-start.4 = (bf16[16,16,256]{2,1,0:T(8,128)(2,1)}, bf16[16,16,256]{2,1,0:T(8,128)(2,1)S(1)}, u32[]{:S(2)}, u32[]{:S(2)}) collective-permute-start(bf16[16,16,256]{2,1,0:T(8,128)(2,1)} %get-tuple-element.57), channel_id=1, source_target_pairs={{1,0},{2,1},{3,2},{4,3},{5,4},{6,5},{7,6},{9,8},{10,9},{11,10},{12... | collective-permute-start | bytes 393224 | tf_op jit(solution)/shard_map/ppermute | solution.py:541
  34.2 10.0 %copy-start.2 = (bf16[16,16,256]{2,1,0:T(8,128)(2,1)}, bf16[16,16,256]{2,1,0:T(8,128)(2,1)S(1)}, u32[]{:S(2)}) copy-start(bf16[16,16,256]{2,1,0:T(8,128)(2,1)S(1)} %collective-permute-done.3.refs_1_) | copy-start | bytes 393220
  34.2 6.6 %collective-permute-start.5 = (bf16[16,16,256]{2,1,0:T(8,128)(2,1)}, bf16[16,16,256]{2,1,0:T(8,128)(2,1)S(1)}, u32[]{:S(2)}, u32[]{:S(2)}) collective-permute-start(bf16[16,16,256]{2,1,0:T(8,128)(2,1)} %get-tuple-element.70), channel_id=1, source_target_pairs={{0,1},{1,2},{2,3},{3,4},{4,5},{5,6},{6,7},{8,9},{9,10},{10,11},{11... | collective-permute-start | bytes 393224 | tf_op jit(solution)/shard_map/ppermute | solution.py:541
  39.5 4.7 %copy-start.3 = (bf16[16,16,256]{2,1,0:T(8,128)(2,1)}, bf16[16,16,256]{2,1,0:T(8,128)(2,1)S(1)}, u32[]{:S(2)}) copy-start(bf16[16,16,256]{2,1,0:T(8,128)(2,1)S(1)} %collective-permute-done.4.refs_2_) | copy-start | bytes 393220
  39.5 4.7 %collective-permute-start.6 = (bf16[16,16,256]{2,1,0:T(8,128)(2,1)}, bf16[16,16,256]{2,1,0:T(8,128)(2,1)S(1)}, u32[]{:S(2)}, u32[]{:S(2)}) collective-permute-start(bf16[16,16,256]{2,1,0:T(8,128)(2,1)} %get-tuple-element.71), channel_id=1, source_target_pairs={{1,0},{2,1},{3,2},{4,3},{5,4},{6,5},{7,6},{9,8},{10,9},{11,10},{12... | collective-permute-start | bytes 393224 | tf_op jit(solution)/shard_map/ppermute | solution.py:541
  40.8 3.4 %copy-start.4 = (bf16[16,16,256]{2,1,0:T(8,128)(2,1)}, bf16[16,16,256]{2,1,0:T(8,128)(2,1)S(1)}, u32[]{:S(2)}) copy-start(bf16[16,16,256]{2,1,0:T(8,128)(2,1)S(1)} %collective-permute-done.5.refs_5_) | copy-start | bytes 393220
  44.2 0.6 copy-start.5
  53.9 41.0 %copy-start = (bf16[5,15,2,16,256]{4,3,2,1,0:T(8,128)(2,1)}, bf16[5,15,2,16,256]{4,3,2,1,0:T(8,128)(2,1)S(1)}, u32[]{:S(2)}) copy-start(bf16[5,15,2,16,256]{4,3,2,1,0:T(8,128)(2,1)S(1)} %collective-permute-done.7.refs_6_) | copy-start | bytes 3686404
  53.9 13.4 %collective-permute-start.10 = (bf16[5,2,32,256]{3,2,1,0:T(8,128)(2,1)}, bf16[5,2,32,256]{3,2,1,0:T(8,128)(2,1)S(1)}, u32[]{:S(2)}, u32[]{:S(2)}) collective-permute-start(bf16[5,2,32,256]{3,2,1,0:T(8,128)(2,1)} %get-tuple-element.79), channel_id=1, source_target_pairs={{0,24},{8,16},{16,8},{24,0},{1,25},{9,17},{17,9},{25,1},{2,26},{10... | collective-permute-start | bytes 491528 | tf_op jit(solution)/shard_map/ppermute | solution.py:553
  56.5 13.5 %collective-permute-start.9 = (bf16[5,2,32,256]{3,2,1,0:T(8,128)(2,1)}, bf16[5,2,32,256]{3,2,1,0:T(8,128)(2,1)S(1)}, u32[]{:S(2)}, u32[]{:S(2)}) collective-permute-start(bf16[5,2,32,256]{3,2,1,0:T(8,128)(2,1)} %get-tuple-element.77), channel_id=1, source_target_pairs={{0,16},{8,24},{16,0},{24,8},{1,17},{9,25},{17,1},{25,9},{2,18},{10... | collective-permute-start | bytes 491528 | tf_op jit(solution)/shard_map/ppermute | solution.py:553
  57.0 14.4 %collective-permute-start.8 = (bf16[5,2,32,256]{3,2,1,0:T(8,128)(2,1)}, bf16[5,2,32,256]{3,2,1,0:T(8,128)(2,1)S(1)}, u32[]{:S(2)}, u32[]{:S(2)}) collective-permute-start(bf16[5,2,32,256]{3,2,1,0:T(8,128)(2,1)} %get-tuple-element.75), channel_id=1, source_target_pairs={{0,8},{8,0},{16,24},{24,16},{1,9},{9,1},{17,25},{25,17},{2,10},{10... | collective-permute-start | bytes 491528 | tf_op jit(solution)/shard_map/ppermute | solution.py:553
  64.4 16.9 %collective-permute-start.14 = (bf16[5,6,2,16,256]{4,3,2,1,0:T(8,128)(2,1)}, bf16[5,6,2,16,256]{4,3,2,1,0:T(8,128)(2,1)}, u32[]{:S(2)}, u32[]{:S(2)}) collective-permute-start(bf16[5,6,2,16,256]{4,3,2,1,0:T(8,128)(2,1)} %get-tuple-element.83), channel_id=1, source_target_pairs={{0,16},{8,24},{16,0},{24,8},{1,17},{9,25},{17,1},{25,9},{2,18},{10... | collective-permute-start | bytes 1474568 | tf_op jit(solution)/shard_map/ppermute | solution.py:553
  65.9 17.4 %collective-permute-start.1 = (bf16[5,6,2,16,256]{4,3,2,1,0:T(8,128)(2,1)}, bf16[5,6,2,16,256]{4,3,2,1,0:T(8,128)(2,1)}, u32[]{:S(2)}, u32[]{:S(2)}) collective-permute-start(bf16[5,6,2,16,256]{4,3,2,1,0:T(8,128)(2,1)} %get-tuple-element.64), channel_id=1, source_target_pairs={{0,8},{8,0},{16,24},{24,16},{1,9},{9,1},{17,25},{25,17},{2,10},{10... | collective-permute-start | bytes 1474568 | tf_op jit(solution)/shard_map/ppermute | solution.py:553
  71.3 20.6 %collective-permute-start.15 = (bf16[5,6,2,16,256]{4,3,2,1,0:T(8,128)(2,1)}, bf16[5,6,2,16,256]{4,3,2,1,0:T(8,128)(2,1)}, u32[]{:S(2)}, u32[]{:S(2)}) collective-permute-start(bf16[5,6,2,16,256]{4,3,2,1,0:T(8,128)(2,1)} %get-tuple-element.86), channel_id=1, source_target_pairs={{0,24},{8,16},{16,8},{24,0},{1,25},{9,17},{17,9},{25,1},{2,26},{10... | collective-permute-start | bytes 1474568 | tf_op jit(solution)/shard_map/ppermute | solution.py:553
  73.8 26.9 %copy-start.1 = (bf16[4,5,2,32,256]{4,3,2,1,0:T(8,128)(2,1)}, bf16[4,5,2,32,256]{4,3,2,1,0:T(8,128)(2,1)S(1)}, u32[]{:S(2)}) copy-start(bf16[4,5,2,32,256]{4,3,2,1,0:T(8,128)(2,1)S(1)} %pad_maximum_fusion.own) | copy-start | bytes 1966084
  73.8 26.9 %collective-permute-start.12 = (bf16[4,5,2,32,256]{4,3,2,1,0:T(8,128)(2,1)S(1)}, bf16[4,5,2,32,256]{4,3,2,1,0:T(8,128)(2,1)}, u32[]{:S(2)}, u32[]{:S(2)}) collective-permute-start(bf16[4,5,2,32,256]{4,3,2,1,0:T(8,128)(2,1)S(1)} %pad_maximum_fusion.own), channel_id=1, source_target_pairs={{1,0},{2,1},{3,2},{4,3},{5,4},{6,5},{7,6},{9,8},{10,9},{11,10},{12... | collective-permute-start | bytes 1966088 | tf_op jit(solution)/shard_map/ppermute | solution.py:541
  75.1 25.6 %collective-permute-start.11 = (bf16[4,5,2,32,256]{4,3,2,1,0:T(8,128)(2,1)S(1)}, bf16[4,5,2,32,256]{4,3,2,1,0:T(8,128)(2,1)}, u32[]{:S(2)}, u32[]{:S(2)}) collective-permute-start(bf16[4,5,2,32,256]{4,3,2,1,0:T(8,128)(2,1)S(1)} %pad_maximum_fusion.own), channel_id=1, source_target_pairs={{0,1},{1,2},{2,3},{3,4},{4,5},{5,6},{6,7},{8,9},{9,10},{10,11},{11... | collective-permute-start | bytes 1966088 | tf_op jit(solution)/shard_map/ppermute | solution.py:541
  81.2 23.3 %collective-permute-start.17 = (bf16[5,6,2,16,256]{4,3,2,1,0:T(8,128)(2,1)}, bf16[5,6,2,16,256]{4,3,2,1,0:T(8,128)(2,1)}, u32[]{:S(2)}, u32[]{:S(2)}) collective-permute-start(bf16[5,6,2,16,256]{4,3,2,1,0:T(8,128)(2,1)} %get-tuple-element.93), channel_id=1, source_target_pairs={{0,16},{8,24},{16,0},{24,8},{1,17},{9,25},{17,1},{25,9},{2,18},{10... | collective-permute-start | bytes 1474568 | tf_op jit(solution)/shard_map/ppermute | solution.py:553
  83.3 21.9 %collective-permute-start.2 = (bf16[5,6,2,16,256]{4,3,2,1,0:T(8,128)(2,1)}, bf16[5,6,2,16,256]{4,3,2,1,0:T(8,128)(2,1)}, u32[]{:S(2)}, u32[]{:S(2)}) collective-permute-start(bf16[5,6,2,16,256]{4,3,2,1,0:T(8,128)(2,1)} %get-tuple-element.65), channel_id=1, source_target_pairs={{0,8},{8,0},{16,24},{24,16},{1,9},{9,1},{17,25},{25,17},{2,10},{10... | collective-permute-start | bytes 1474568 | tf_op jit(solution)/shard_map/ppermute | solution.py:553
  92.0 21.1 %collective-permute-start.19 = (bf16[5,6,2,16,256]{4,3,2,1,0:T(8,128)(2,1)}, bf16[5,6,2,16,256]{4,3,2,1,0:T(8,128)(2,1)}, u32[]{:S(2)}, u32[]{:S(2)}) collective-permute-start(bf16[5,6,2,16,256]{4,3,2,1,0:T(8,128)(2,1)} %get-tuple-element.97), channel_id=1, source_target_pairs={{0,24},{8,16},{16,8},{24,0},{1,25},{9,17},{17,9},{25,1},{2,26},{10... | collective-permute-start | bytes 1474568 | tf_op jit(solution)/shard_map/ppermute | solution.py:553
  100.7 4.4 %copy-start.7 = (bf16[5,3,2,16,256]{4,3,2,1,0:T(8,128)(2,1)S(1)}, bf16[5,3,2,16,256]{4,3,2,1,0:T(8,128)(2,1)}, u32[]{:S(2)}) copy-start(bf16[5,3,2,16,256]{4,3,2,1,0:T(8,128)(2,1)} %get-tuple-element.90) | copy-start | bytes 737284
  100.7 12.4 %copy-start.6 = (bf16[5,3,2,16,256]{4,3,2,1,0:T(8,128)(2,1)S(1)}, bf16[5,3,2,16,256]{4,3,2,1,0:T(8,128)(2,1)}, u32[]{:S(2)}) copy-start(bf16[5,3,2,16,256]{4,3,2,1,0:T(8,128)(2,1)} %get-tuple-element.98) | copy-start | bytes 737284
  104.6 17.1 %collective-permute-start.18 = (bf16[5,3,2,16,256]{4,3,2,1,0:T(8,128)(2,1)}, bf16[5,3,2,16,256]{4,3,2,1,0:T(8,128)(2,1)S(1)}, u32[]{:S(2)}, u32[]{:S(2)}) collective-permute-start(bf16[5,3,2,16,256]{4,3,2,1,0:T(8,128)(2,1)} %get-tuple-element.94), channel_id=1, source_target_pairs={{0,16},{8,24},{16,0},{24,8},{1,17},{9,25},{17,1},{25,9},{2,18},{10... | collective-permute-start | bytes 737288 | tf_op jit(solution)/shard_map/ppermute | solution.py:553
  105.1 16.5 %collective-permute-start.16 = (bf16[5,3,2,16,256]{4,3,2,1,0:T(8,128)(2,1)S(1)}, bf16[5,3,2,16,256]{4,3,2,1,0:T(8,128)(2,1)S(1)}, u32[]{:S(2)}, u32[]{:S(2)}) collective-permute-start(bf16[5,3,2,16,256]{4,3,2,1,0:T(8,128)(2,1)S(1)} %copy-done.7), channel_id=1, source_target_pairs={{0,8},{8,0},{16,24},{24,16},{1,9},{9,1},{17,25},{25,17},{2,10},{10... | collective-permute-start | bytes 737288 | tf_op jit(solution)/shard_map/ppermute | solution.py:553
  113.1 9.6 %collective-permute-start.20 = (bf16[5,3,2,16,256]{4,3,2,1,0:T(8,128)(2,1)S(1)}, bf16[5,3,2,16,256]{4,3,2,1,0:T(8,128)(2,1)S(1)}, u32[]{:S(2)}, u32[]{:S(2)}) collective-permute-start(bf16[5,3,2,16,256]{4,3,2,1,0:T(8,128)(2,1)S(1)} %copy-done.6), channel_id=1, source_target_pairs={{0,24},{8,16},{16,8},{24,0},{1,25},{9,17},{17,9},{25,1},{2,26},{10... | collective-permute-start | bytes 737288 | tf_op jit(solution)/shard_map/ppermute | solution.py:553

commit v8 on v7

--- a/solution.py
+++ b/solution.py
@@ -567,7 +567,7 @@
     columns = n_az // SIDE
     me = lax.axis_index("date").astype(jnp.int32).reshape(1)
     parts = n_dates // DBLK
-    bounds = [1, 7, 13, columns]
+    bounds = [1, 6, 13, columns]
     spans = list(zip(bounds[:-1], bounds[1:]))
 
     dest_windows = n_rows // partners // SIDE

time: 127 us -> 127 us (level)
  transfers between devices with their start and end apart: 21 -> 21, of which waited for: 8 -> 10; matrix products, arithmetic and copies ran while one was open for 1% -> 1% of each run, Pallas kernels for 36% -> 36%
where the time goes in v8:
time: 127 us
  Pallas kernels  55 us (43%)
  starting transfers between devices  36.7 us (29%)
  waiting for transfers between devices  32.9 us (26%)
    ppermute x15, waiting for transfers between devices, exchange(): got.append(lax.ppermute(block, 'date', [(i, i ^ k) for i in range(n)]))  29.5 us
    pallas_call x3, Pallas kernels, interior(): pl.pallas_call(functools.partial(interior_kernel, spans, targets, edged,...  27 us
    ppermute x15, starting transfers between devices, exchange(): got.append(lax.ppermute(block, 'date', [(i, i ^ k) for i in range(n)]))  22.4 us
    pallas_call x3, Pallas kernels, gram(): pl.pallas_call(functools.partial(gram_kernel, partners, parts, offsets, c...  15.1 us
    ppermute x6, starting transfers between devices, shift(): return lax.ppermute(value, axis, pairs)  14.4 us
    pallas_call x1, Pallas kernels, rim(): pl.pallas_call(functools.partial(rim_kernel, dest_rows, parts), grid_spec...  9.07 us
    pallas_call x1, Pallas kernels, rim_gram(): pl.pallas_call(rim_gram_kernel, in_specs=[pl.BlockSpec(memory_space=pltpu...  3.83 us
    ppermute x6, waiting for transfers between devices, shift(): return lax.ppermute(value, axis, pairs)  3.38 us
  transfers between devices with their start and end apart: 21, of which 10 were waited for; matrix products, arithmetic and copies ran while one was open for 1% of the time, Pallas kernels for 36%

profile of v8, /device:TPU:0, one launch (start us, length us, event | category | flops | bytes accessed | tf_op | source)
XLA Modules:
  0.0 126.5 jit_solution(5241492088535885944)
XLA Ops:
  0.0 5.3 %interior_0_3.1 = bf16[5,15,2,16,256]{4,3,2,1,0:T(8,128)(2,1)} custom-call(s32[1]{0:T(128)} %bitcast.me_ref, bf16[2,32,256,256]{3,2,1,0:T(8,128)(2,1)} %slc_any.5, bf16[32,256,256]{2,1,0:T(8,128)(2,1)} %rk_any.5, bf16[32,272,256]{2,1,0:T(8,128)(2,1)} %refs_7_.1), custom_call_target="tpu_custom_call" | custom-call | flops 1 | bytes 1 | tf_op jit(solution)/shard_map/interior_0_3/pallas_call | solution.py:201
  5.3 4.0 %collective-permute-start.7 = (bf16[5,15,2,16,256]{4,3,2,1,0:T(8,128)(2,1)}, bf16[5,15,2,16,256]{4,3,2,1,0:T(8,128)(2,1)S(1)}, u32[]{:S(2)}, u32[]{:S(2)}) collective-permute-start(bf16[5,15,2,16,256]{4,3,2,1,0:T(8,128)(2,1)} %interior_0_3.1), channel_id=1, source_target_pairs={{0,24},{8,16},{16,8},{24,0},{1,25},{9,17},{17,9},{25,1},{2,26},{10... | collective-permute-start | bytes 3686408 | tf_op jit(solution)/shard_map/ppermute | solution.py:553
  9.3 10.5 %interior_0_1.1 = (bf16[16,2,32,256]{3,2,1,0:T(8,128)(2,1)}, bf16[16,16,256]{2,1,0:T(8,128)(2,1)}, bf16[16,16,256]{2,1,0:T(8,128)(2,1)}, bf16[5,15,2,16,256]{4,3...) custom-call(s32[1]{0:T(128)} %bitcast.me_ref, ...), custom_call_target="tpu_custom_call" | custom-call | flops 1 | bytes 1 | tf_op jit(solution)/shard_map/interior_0_1/pallas_call | solution.py:201
  19.7 0.6 collective-permute-start
  20.3 0.1 collective-permute-start.13
  20.4 1.3 %collective-permute-start.3 = (bf16[16,16,256]{2,1,0:T(8,128)(2,1)}, bf16[16,16,256]{2,1,0:T(8,128)(2,1)S(1)}, u32[]{:S(2)}, u32[]{:S(2)}) collective-permute-start(bf16[16,16,256]{2,1,0:T(8,128)(2,1)} %get-tuple-element.68), channel_id=1, source_target_pairs={{0,1},{1,2},{2,3},{3,4},{4,5},{5,6},{6,7},{8,9},{9,10},{10,11},{11... | collective-permute-start | bytes 393224 | tf_op jit(solution)/shard_map/ppermute | solution.py:541
  21.7 1.3 %collective-permute-start.4 = (bf16[16,16,256]{2,1,0:T(8,128)(2,1)}, bf16[16,16,256]{2,1,0:T(8,128)(2,1)S(1)}, u32[]{:S(2)}, u32[]{:S(2)}) collective-permute-start(bf16[16,16,256]{2,1,0:T(8,128)(2,1)} %get-tuple-element.57), channel_id=1, source_target_pairs={{1,0},{2,1},{3,2},{4,3},{5,4},{6,5},{7,6},{9,8},{10,9},{11,10},{12... | collective-permute-start | bytes 393224 | tf_op jit(solution)/shard_map/ppermute | solution.py:541
  23.0 11.2 %interior_1_1.1 = (bf16[16,2,32,256]{3,2,1,0:T(8,128)(2,1)}, bf16[16,16,256]{2,1,0:T(8,128)(2,1)}, bf16[16,16,256]{2,1,0:T(8,128)(2,1)}, bf16[5,5,2,16,256]{4,3,...) custom-call(s32[1]{0:T(128)} %bitcast.me_ref, ...), custom_call_target="tpu_custom_call" | custom-call | flops 1 | bytes 1 | tf_op jit(solution)/shard_map/interior_1_1/pallas_call | solution.py:201
  34.2 0.0 collective-permute-done.3.refs_1_
  34.2 5.3 %collective-permute-start.5 = (bf16[16,16,256]{2,1,0:T(8,128)(2,1)}, bf16[16,16,256]{2,1,0:T(8,128)(2,1)S(1)}, u32[]{:S(2)}, u32[]{:S(2)}) collective-permute-start(bf16[16,16,256]{2,1,0:T(8,128)(2,1)} %get-tuple-element.70), channel_id=1, source_target_pairs={{0,1},{1,2},{2,3},{3,4},{4,5},{5,6},{6,7},{8,9},{9,10},{10,11},{11... | collective-permute-start | bytes 393224 | tf_op jit(solution)/shard_map/ppermute | solution.py:541
  39.5 0.0 collective-permute-done.4.refs_2_
  39.5 1.3 %collective-permute-start.6 = (bf16[16,16,256]{2,1,0:T(8,128)(2,1)}, bf16[16,16,256]{2,1,0:T(8,128)(2,1)S(1)}, u32[]{:S(2)}, u32[]{:S(2)}) collective-permute-start(bf16[16,16,256]{2,1,0:T(8,128)(2,1)} %get-tuple-element.71), channel_id=1, source_target_pairs={{1,0},{2,1},{3,2},{4,3},{5,4},{6,5},{7,6},{9,8},{10,9},{11,10},{12... | collective-permute-start | bytes 393224 | tf_op jit(solution)/shard_map/ppermute | solution.py:541
  40.8 0.0 collective-permute-done.5.refs_5_
  40.9 3.4 %collective-permute-done.6.refs_6_ = bf16[16,16,256]{2,1,0:T(8,128)(2,1)S(1)} collective-permute-done((bf16[16,16,256]{2,1,0:T(8,128)(2,1)}, bf16[16,16,256]{2,1,0:T(8,128)(2,1)S(1)}, u32[]{:S(2)}, u32[]{:S(2)}) %collective-permute-start.6) | collective-permute-done | bytes 131104 | tf_op jit(solution)/shard_map/ppermute | solution.py:541
  44.2 0.6 copy-done.5
  44.9 9.1 %rim.1 = (bf16[5,2,32,256]{3,2,1,0:T(8,128)(2,1)}, bf16[5,2,32,256]{3,2,1,0:T(8,128)(2,1)}, bf16[5,2,32,256]{3,2,1,0:T(8,128)(2,1)}, bf16[5,2,32,256]{3,2,1,0:T(8,128)(2,1)}) custom-call(s32[1]{0:T(128)} %bitcast.me_ref, bf16[16,2,32,256]{3,2,1,0:T(8,128)(2,1)} %get-tuple-element.67.refs_0_, bf16[16,16,256]{2,1,0:T(8,128)(2,1)} %copy-done.2, ...), custom_call_target="tpu_custom_call" | custom-call | flops 1 | bytes 1 | tf_op jit(solution)/shard_map/rim/pallas_call | solution.py:316
  54.0 0.0 collective-permute-done.7.refs_6_
  54.0 2.5 %collective-permute-start.10 = (bf16[5,2,32,256]{3,2,1,0:T(8,128)(2,1)}, bf16[5,2,32,256]{3,2,1,0:T(8,128)(2,1)S(1)}, u32[]{:S(2)}, u32[]{:S(2)}) collective-permute-start(bf16[5,2,32,256]{3,2,1,0:T(8,128)(2,1)} %get-tuple-element.79), channel_id=1, source_target_pairs={{0,24},{8,16},{16,8},{24,0},{1,25},{9,17},{17,9},{25,1},{2,26},{10... | collective-permute-start | bytes 491528 | tf_op jit(solution)/shard_map/ppermute | solution.py:553
  56.5 0.5 collective-permute-start.9
  57.0 0.5 collective-permute-start.8
  57.5 6.8 %collective-permute-done.refs_2_ = bf16[5,15,2,16,256]{4,3,2,1,0:T(8,128)(2,1)} collective-permute-done((bf16[5,15,2,16,256]{4,3,2,1,0:T(8,128)(2,1)}, bf16[5,15,2,16,256]{4,3,2,1,0:T(8,128)(2,1)}, u32[]{:S(2)}, u32[]{:S(2)}) %collective-permute-start) | collective-permute-done | bytes 1228832 | tf_op jit(solution)/shard_map/ppermute | solution.py:553
  64.4 1.5 %collective-permute-start.1 = (bf16[5,5,2,16,256]{4,3,2,1,0:T(8,128)(2,1)}, bf16[5,5,2,16,256]{4,3,2,1,0:T(8,128)(2,1)}, u32[]{:S(2)}, u32[]{:S(2)}) collective-permute-start(bf16[5,5,2,16,256]{4,3,2,1,0:T(8,128)(2,1)} %get-tuple-element.64), channel_id=1, source_target_pairs={{0,8},{8,0},{16,24},{24,16},{1,9},{9,1},{17,25},{25,17},{2,10},{10... | collective-permute-start | bytes 1228808 | tf_op jit(solution)/shard_map/ppermute | solution.py:553
  65.9 0.0 collective-permute-done.13.refs_4_
  65.9 0.5 collective-permute-start.14
  66.4 0.9 collective-permute-done.10
  67.2 2.7 %collective-permute-done.9 = bf16[5,2,32,256]{3,2,1,0:T(8,128)(2,1)S(1)} collective-permute-done((bf16[5,2,32,256]{3,2,1,0:T(8,128)(2,1)}, bf16[5,2,32,256]{3,2,1,0:T(8,128)(2,1)S(1)}, u32[]{:S(2)}, u32[]{:S(2)}) %collective-permute-start.9) | collective-permute-done | bytes 163872 | tf_op jit(solution)/shard_map/ppermute | solution.py:553
  69.9 1.4 %collective-permute-done.8 = bf16[5,2,32,256]{3,2,1,0:T(8,128)(2,1)S(1)} collective-permute-done((bf16[5,2,32,256]{3,2,1,0:T(8,128)(2,1)}, bf16[5,2,32,256]{3,2,1,0:T(8,128)(2,1)S(1)}, u32[]{:S(2)}, u32[]{:S(2)}) %collective-permute-start.8) | collective-permute-done | bytes 163872 | tf_op jit(solution)/shard_map/ppermute | solution.py:553
  71.3 1.4 %collective-permute-start.15 = (bf16[5,5,2,16,256]{4,3,2,1,0:T(8,128)(2,1)}, bf16[5,5,2,16,256]{4,3,2,1,0:T(8,128)(2,1)}, u32[]{:S(2)}, u32[]{:S(2)}) collective-permute-start(bf16[5,5,2,16,256]{4,3,2,1,0:T(8,128)(2,1)} %get-tuple-element.86), channel_id=1, source_target_pairs={{0,24},{8,16},{16,8},{24,0},{1,25},{9,17},{17,9},{25,1},{2,26},{10... | collective-permute-start | bytes 1228808 | tf_op jit(solution)/shard_map/ppermute | solution.py:553
  72.8 1.0 pad_maximum_fusion.own
  73.8 1.3 %collective-permute-start.12 = (bf16[4,5,2,32,256]{4,3,2,1,0:T(8,128)(2,1)S(1)}, bf16[4,5,2,32,256]{4,3,2,1,0:T(8,128)(2,1)}, u32[]{:S(2)}, u32[]{:S(2)}) collective-permute-start(bf16[4,5,2,32,256]{4,3,2,1,0:T(8,128)(2,1)S(1)} %pad_maximum_fusion.own), channel_id=1, source_target_pairs={{1,0},{2,1},{3,2},{4,3},{5,4},{6,5},{7,6},{9,8},{10,9},{11,10},{12... | collective-permute-start | bytes 1966088 | tf_op jit(solution)/shard_map/ppermute | solution.py:541
  75.1 3.9 %collective-permute-start.11 = (bf16[4,5,2,32,256]{4,3,2,1,0:T(8,128)(2,1)S(1)}, bf16[4,5,2,32,256]{4,3,2,1,0:T(8,128)(2,1)}, u32[]{:S(2)}, u32[]{:S(2)}) collective-permute-start(bf16[4,5,2,32,256]{4,3,2,1,0:T(8,128)(2,1)S(1)} %pad_maximum_fusion.own), channel_id=1, source_target_pairs={{0,1},{1,2},{2,3},{3,4},{4,5},{5,6},{6,7},{8,9},{9,10},{10,11},{11... | collective-permute-start | bytes 1966088 | tf_op jit(solution)/shard_map/ppermute | solution.py:541
  79.0 1.2 collective-permute-done.1.refs_3_
  80.2 1.5 %collective-permute-start.2 = (bf16[5,7,2,16,256]{4,3,2,1,0:T(8,128)(2,1)}, bf16[5,7,2,16,256]{4,3,2,1,0:T(8,128)(2,1)}, u32[]{:S(2)}, u32[]{:S(2)}) collective-permute-start(bf16[5,7,2,16,256]{4,3,2,1,0:T(8,128)(2,1)} %get-tuple-element.65), channel_id=1, source_target_pairs={{0,8},{8,0},{16,24},{24,16},{1,9},{9,1},{17,25},{25,17},{2,10},{10... | collective-permute-start | bytes 1720328 | tf_op jit(solution)/shard_map/ppermute | solution.py:553
  81.7 0.0 collective-permute-done.14.refs_5_
  81.7 0.5 collective-permute-start.17
  82.2 6.3 %collective-permute-done.15.refs_7_ = bf16[5,5,2,16,256]{4,3,2,1,0:T(8,128)(2,1)} collective-permute-done((bf16[5,5,2,16,256]{4,3,2,1,0:T(8,128)(2,1)}, bf16[5,5,2,16,256]{4,3,2,1,0:T(8,128)(2,1)}, u32[]{:S(2)}, u32[]{:S(2)}) %collective-permute-start.15) | collective-permute-done | bytes 409632 | tf_op jit(solution)/shard_map/ppermute | solution.py:553
  88.5 3.0 %collective-permute-start.19 = (bf16[5,7,2,16,256]{4,3,2,1,0:T(8,128)(2,1)}, bf16[5,7,2,16,256]{4,3,2,1,0:T(8,128)(2,1)}, u32[]{:S(2)}, u32[]{:S(2)}) collective-permute-start(bf16[5,7,2,16,256]{4,3,2,1,0:T(8,128)(2,1)} %get-tuple-element.97), channel_id=1, source_target_pairs={{0,24},{8,16},{16,8},{24,0},{1,25},{9,17},{17,9},{25,1},{2,26},{10... | collective-permute-start | bytes 1720328 | tf_op jit(solution)/shard_map/ppermute | solution.py:553
  91.4 5.1 %gram_1.1 = (f32[4,16,2,128,128]{4,3,2,1,0:T(8,128)}, f32[4,2,128,128]{3,2,1,0:T(8,128)}, f32[4,2,128,128]{3,2,1,0:T(8,128)}) custom-call(bf16[5,15,2,16,256]{4,3,2,1,0:T(8,128)(2,1)} %get-tuple-element.56.refs_0_, bf16[5,5,2,16,256]{4,3,2,1,0:T(8,128)(2,1)} %get-tuple-element.80.refs_1_, bf16[5,15,2,16,256]{4,3,2,1,0:T(8,128)(2,1)} %collective-permute-done.refs_2_, ...), custom_call_target="tpu_custom_call" | custom-call | flops 1 | bytes 1 | tf_op jit(solution)/shard_map/gram_1/pallas_call | solution.py:512
  96.6 3.8 %rim_gram.1 = (f32[4,16,2,128,128]{4,3,2,1,0:T(8,128)}, f32[4,2,128,128]{3,2,1,0:T(8,128)}) custom-call(s32[1]{0:T(128)} %bitcast.me_ref, bf16[4,5,2,32,256]{4,3,2,1,0:T(8,128)(2,1)} %copy-done.1, bf16[4,5,2,32,256]{4,3,2,1,0:T(8,128)(2,1)} %collective-permute-done.11.before, ...), custom_call_target="tpu_custom_call", output_to_operand_aliasing={{0}: (5, {})} | custom-call | flops 1 | bytes 1 | tf_op jit(solution)/shard_map/rim_gram/pallas_call | solution.py:388
  100.4 0.9 collective-permute-done.2.refs_3_
  101.3 1.4 %collective-permute-start.18 = (bf16[5,3,2,16,256]{4,3,2,1,0:T(8,128)(2,1)}, bf16[5,3,2,16,256]{4,3,2,1,0:T(8,128)(2,1)S(1)}, u32[]{:S(2)}, u32[]{:S(2)}) collective-permute-start(bf16[5,3,2,16,256]{4,3,2,1,0:T(8,128)(2,1)} %get-tuple-element.94), channel_id=1, source_target_pairs={{0,16},{8,24},{16,0},{24,8},{1,17},{9,25},{17,1},{25,9},{2,18},{10... | collective-permute-start | bytes 737288 | tf_op jit(solution)/shard_map/ppermute | solution.py:553
  102.7 1.5 %collective-permute-start.16 = (bf16[5,3,2,16,256]{4,3,2,1,0:T(8,128)(2,1)S(1)}, bf16[5,3,2,16,256]{4,3,2,1,0:T(8,128)(2,1)S(1)}, u32[]{:S(2)}, u32[]{:S(2)}) collective-permute-start(bf16[5,3,2,16,256]{4,3,2,1,0:T(8,128)(2,1)S(1)} %copy-done.7), channel_id=1, source_target_pairs={{0,8},{8,0},{16,24},{24,16},{1,9},{9,1},{17,25},{25,17},{2,10},{10... | collective-permute-start | bytes 737288 | tf_op jit(solution)/shard_map/ppermute | solution.py:553
  104.2 8.9 %collective-permute-done.19.refs_7_ = bf16[5,7,2,16,256]{4,3,2,1,0:T(8,128)(2,1)} collective-permute-done((bf16[5,7,2,16,256]{4,3,2,1,0:T(8,128)(2,1)}, bf16[5,7,2,16,256]{4,3,2,1,0:T(8,128)(2,1)}, u32[]{:S(2)}, u32[]{:S(2)}) %collective-permute-start.19) | collective-permute-done | bytes 573472 | tf_op jit(solution)/shard_map/ppermute | solution.py:553
  113.1 3.0 %collective-permute-start.20 = (bf16[5,3,2,16,256]{4,3,2,1,0:T(8,128)(2,1)S(1)}, bf16[5,3,2,16,256]{4,3,2,1,0:T(8,128)(2,1)S(1)}, u32[]{:S(2)}, u32[]{:S(2)}) collective-permute-start(bf16[5,3,2,16,256]{4,3,2,1,0:T(8,128)(2,1)S(1)} %copy-done.6), channel_id=1, source_target_pairs={{0,24},{8,16},{16,8},{24,0},{1,25},{9,17},{17,9},{25,1},{2,26},{10... | collective-permute-start | bytes 737288 | tf_op jit(solution)/shard_map/ppermute | solution.py:553
  116.0 6.2 %gram_6.1 = (f32[4,16,2,128,128]{4,3,2,1,0:T(8,128)}, f32[4,2,128,128]{3,2,1,0:T(8,128)}) custom-call(bf16[5,15,2,16,256]{4,3,2,1,0:T(8,128)(2,1)} %get-tuple-element.56.refs_0_, bf16[5,7,2,16,256]{4,3,2,1,0:T(8,128)(2,1)} %get-tuple-element.99.refs_1_, bf16[5,15,2,16,256]{4,3,2,1,0:T(8,128)(2,1)} %collective-permute-done.refs_2_, ...), custom_call_target="tpu_custom_call", output_to_operand_aliasing={{0}: (10, {})} | custom-call | flops 1 | bytes 1 | tf_op jit(solution)/shard_map/gram_6/pallas_call | solution.py:512
  122.2 0.0 collective-permute-done.18.refs_5_
  122.3 0.4 collective-permute-done.20.refs_7_
  122.7 3.9 %gram_13.1 = (f32[4,16,2,128,128]{4,3,2,1,0:T(8,128)}, f32[4,2,128,128]{3,2,1,0:T(8,128)}) custom-call(bf16[5,15,2,16,256]{4,3,2,1,0:T(8,128)(2,1)} %get-tuple-element.56.refs_0_, bf16[5,3,2,16,256]{4,3,2,1,0:T(8,128)(2,1)} %get-tuple-element.59.refs_1_, bf16[5,15,2,16,256]{4,3,2,1,0:T(8,128)(2,1)} %collective-permute-done.refs_2_, ...), custom_call_target="tpu_custom_call", output_to_operand_aliasing={{0}: (10, {})} | custom-call | flops 1 | bytes 1 | tf_op jit(solution)/shard_map/gram_13/pallas_call | solution.py:512
  (19 shorter events, 0.0 us)
Async XLA Ops:
  5.3 48.7 %collective-permute-start.7 = (bf16[5,15,2,16,256]{4,3,2,1,0:T(8,128)(2,1)}, bf16[5,15,2,16,256]{4,3,2,1,0:T(8,128)(2,1)S(1)}, u32[]{:S(2)}, u32[]{:S(2)}) collective-permute-start(bf16[5,15,2,16,256]{4,3,2,1,0:T(8,128)(2,1)} %interior_0_3.1), channel_id=1, source_target_pairs={{0,24},{8,16},{16,8},{24,0},{1,25},{9,17},{17,9},{25,1},{2,26},{10... | collective-permute-start | bytes 3686408 | tf_op jit(solution)/shard_map/ppermute | solution.py:553
  19.7 44.6 %collective-permute-start = (bf16[5,15,2,16,256]{4,3,2,1,0:T(8,128)(2,1)}, bf16[5,15,2,16,256]{4,3,2,1,0:T(8,128)(2,1)}, u32[]{:S(2)}, u32[]{:S(2)}) collective-permute-start(bf16[5,15,2,16,256]{4,3,2,1,0:T(8,128)(2,1)} %get-tuple-element.60), channel_id=1, source_target_pairs={{0,8},{8,0},{16,24},{24,16},{1,9},{9,1},{17,25},{25,17},{2,10},{10... | collective-permute-start | bytes 3686408 | tf_op jit(solution)/shard_map/ppermute | solution.py:553
  20.3 45.5 %collective-permute-start.13 = (bf16[5,15,2,16,256]{4,3,2,1,0:T(8,128)(2,1)}, bf16[5,15,2,16,256]{4,3,2,1,0:T(8,128)(2,1)}, u32[]{:S(2)}, u32[]{:S(2)}) collective-permute-start(bf16[5,15,2,16,256]{4,3,2,1,0:T(8,128)(2,1)} %get-tuple-element.81), channel_id=1, source_target_pairs={{0,16},{8,24},{16,0},{24,8},{1,17},{9,25},{17,1},{25,9},{2,18},{10... | collective-permute-start | bytes 3686408 | tf_op jit(solution)/shard_map/ppermute | solution.py:553
  20.4 13.8 %collective-permute-start.3 = (bf16[16,16,256]{2,1,0:T(8,128)(2,1)}, bf16[16,16,256]{2,1,0:T(8,128)(2,1)S(1)}, u32[]{:S(2)}, u32[]{:S(2)}) collective-permute-start(bf16[16,16,256]{2,1,0:T(8,128)(2,1)} %get-tuple-element.68), channel_id=1, source_target_pairs={{0,1},{1,2},{2,3},{3,4},{4,5},{5,6},{6,7},{8,9},{9,10},{10,11},{11... | collective-permute-start | bytes 393224 | tf_op jit(solution)/shard_map/ppermute | solution.py:541
  21.7 17.8 %collective-permute-start.4 = (bf16[16,16,256]{2,1,0:T(8,128)(2,1)}, bf16[16,16,256]{2,1,0:T(8,128)(2,1)S(1)}, u32[]{:S(2)}, u32[]{:S(2)}) collective-permute-start(bf16[16,16,256]{2,1,0:T(8,128)(2,1)} %get-tuple-element.57), channel_id=1, source_target_pairs={{1,0},{2,1},{3,2},{4,3},{5,4},{6,5},{7,6},{9,8},{10,9},{11,10},{12... | collective-permute-start | bytes 393224 | tf_op jit(solution)/shard_map/ppermute | solution.py:541
  34.2 10.0 %copy-start.2 = (bf16[16,16,256]{2,1,0:T(8,128)(2,1)}, bf16[16,16,256]{2,1,0:T(8,128)(2,1)S(1)}, u32[]{:S(2)}) copy-start(bf16[16,16,256]{2,1,0:T(8,128)(2,1)S(1)} %collective-permute-done.3.refs_1_) | copy-start | bytes 393220
  34.2 6.6 %collective-permute-start.5 = (bf16[16,16,256]{2,1,0:T(8,128)(2,1)}, bf16[16,16,256]{2,1,0:T(8,128)(2,1)S(1)}, u32[]{:S(2)}, u32[]{:S(2)}) collective-permute-start(bf16[16,16,256]{2,1,0:T(8,128)(2,1)} %get-tuple-element.70), channel_id=1, source_target_pairs={{0,1},{1,2},{2,3},{3,4},{4,5},{5,6},{6,7},{8,9},{9,10},{10,11},{11... | collective-permute-start | bytes 393224 | tf_op jit(solution)/shard_map/ppermute | solution.py:541
  39.5 4.7 %copy-start.3 = (bf16[16,16,256]{2,1,0:T(8,128)(2,1)}, bf16[16,16,256]{2,1,0:T(8,128)(2,1)S(1)}, u32[]{:S(2)}) copy-start(bf16[16,16,256]{2,1,0:T(8,128)(2,1)S(1)} %collective-permute-done.4.refs_2_) | copy-start | bytes 393220
  39.5 4.7 %collective-permute-start.6 = (bf16[16,16,256]{2,1,0:T(8,128)(2,1)}, bf16[16,16,256]{2,1,0:T(8,128)(2,1)S(1)}, u32[]{:S(2)}, u32[]{:S(2)}) collective-permute-start(bf16[16,16,256]{2,1,0:T(8,128)(2,1)} %get-tuple-element.71), channel_id=1, source_target_pairs={{1,0},{2,1},{3,2},{4,3},{5,4},{6,5},{7,6},{9,8},{10,9},{11,10},{12... | collective-permute-start | bytes 393224 | tf_op jit(solution)/shard_map/ppermute | solution.py:541
  40.8 3.4 %copy-start.4 = (bf16[16,16,256]{2,1,0:T(8,128)(2,1)}, bf16[16,16,256]{2,1,0:T(8,128)(2,1)S(1)}, u32[]{:S(2)}) copy-start(bf16[16,16,256]{2,1,0:T(8,128)(2,1)S(1)} %collective-permute-done.5.refs_5_) | copy-start | bytes 393220
  44.2 0.7 copy-start.5
  54.0 37.5 %copy-start = (bf16[5,15,2,16,256]{4,3,2,1,0:T(8,128)(2,1)}, bf16[5,15,2,16,256]{4,3,2,1,0:T(8,128)(2,1)S(1)}, u32[]{:S(2)}) copy-start(bf16[5,15,2,16,256]{4,3,2,1,0:T(8,128)(2,1)S(1)} %collective-permute-done.7.refs_6_) | copy-start | bytes 3686404
  54.0 13.3 %collective-permute-start.10 = (bf16[5,2,32,256]{3,2,1,0:T(8,128)(2,1)}, bf16[5,2,32,256]{3,2,1,0:T(8,128)(2,1)S(1)}, u32[]{:S(2)}, u32[]{:S(2)}) collective-permute-start(bf16[5,2,32,256]{3,2,1,0:T(8,128)(2,1)} %get-tuple-element.79), channel_id=1, source_target_pairs={{0,24},{8,16},{16,8},{24,0},{1,25},{9,17},{17,9},{25,1},{2,26},{10... | collective-permute-start | bytes 491528 | tf_op jit(solution)/shard_map/ppermute | solution.py:553
  56.5 13.5 %collective-permute-start.9 = (bf16[5,2,32,256]{3,2,1,0:T(8,128)(2,1)}, bf16[5,2,32,256]{3,2,1,0:T(8,128)(2,1)S(1)}, u32[]{:S(2)}, u32[]{:S(2)}) collective-permute-start(bf16[5,2,32,256]{3,2,1,0:T(8,128)(2,1)} %get-tuple-element.77), channel_id=1, source_target_pairs={{0,16},{8,24},{16,0},{24,8},{1,17},{9,25},{17,1},{25,9},{2,18},{10... | collective-permute-start | bytes 491528 | tf_op jit(solution)/shard_map/ppermute | solution.py:553
  57.0 14.3 %collective-permute-start.8 = (bf16[5,2,32,256]{3,2,1,0:T(8,128)(2,1)}, bf16[5,2,32,256]{3,2,1,0:T(8,128)(2,1)S(1)}, u32[]{:S(2)}, u32[]{:S(2)}) collective-permute-start(bf16[5,2,32,256]{3,2,1,0:T(8,128)(2,1)} %get-tuple-element.75), channel_id=1, source_target_pairs={{0,8},{8,0},{16,24},{24,16},{1,9},{9,1},{17,25},{25,17},{2,10},{10... | collective-permute-start | bytes 491528 | tf_op jit(solution)/shard_map/ppermute | solution.py:553
  64.4 15.8 %collective-permute-start.1 = (bf16[5,5,2,16,256]{4,3,2,1,0:T(8,128)(2,1)}, bf16[5,5,2,16,256]{4,3,2,1,0:T(8,128)(2,1)}, u32[]{:S(2)}, u32[]{:S(2)}) collective-permute-start(bf16[5,5,2,16,256]{4,3,2,1,0:T(8,128)(2,1)} %get-tuple-element.64), channel_id=1, source_target_pairs={{0,8},{8,0},{16,24},{24,16},{1,9},{9,1},{17,25},{25,17},{2,10},{10... | collective-permute-start | bytes 1228808 | tf_op jit(solution)/shard_map/ppermute | solution.py:553
  65.9 15.8 %collective-permute-start.14 = (bf16[5,5,2,16,256]{4,3,2,1,0:T(8,128)(2,1)}, bf16[5,5,2,16,256]{4,3,2,1,0:T(8,128)(2,1)}, u32[]{:S(2)}, u32[]{:S(2)}) collective-permute-start(bf16[5,5,2,16,256]{4,3,2,1,0:T(8,128)(2,1)} %get-tuple-element.83), channel_id=1, source_target_pairs={{0,16},{8,24},{16,0},{24,8},{1,17},{9,25},{17,1},{25,9},{2,18},{10... | collective-permute-start | bytes 1228808 | tf_op jit(solution)/shard_map/ppermute | solution.py:553
  71.3 17.1 %collective-permute-start.15 = (bf16[5,5,2,16,256]{4,3,2,1,0:T(8,128)(2,1)}, bf16[5,5,2,16,256]{4,3,2,1,0:T(8,128)(2,1)}, u32[]{:S(2)}, u32[]{:S(2)}) collective-permute-start(bf16[5,5,2,16,256]{4,3,2,1,0:T(8,128)(2,1)} %get-tuple-element.86), channel_id=1, source_target_pairs={{0,24},{8,16},{16,8},{24,0},{1,25},{9,17},{17,9},{25,1},{2,26},{10... | collective-permute-start | bytes 1228808 | tf_op jit(solution)/shard_map/ppermute | solution.py:553
  73.8 22.8 %copy-start.1 = (bf16[4,5,2,32,256]{4,3,2,1,0:T(8,128)(2,1)}, bf16[4,5,2,32,256]{4,3,2,1,0:T(8,128)(2,1)S(1)}, u32[]{:S(2)}) copy-start(bf16[4,5,2,32,256]{4,3,2,1,0:T(8,128)(2,1)S(1)} %pad_maximum_fusion.own) | copy-start | bytes 1966084
  73.8 22.8 %collective-permute-start.12 = (bf16[4,5,2,32,256]{4,3,2,1,0:T(8,128)(2,1)S(1)}, bf16[4,5,2,32,256]{4,3,2,1,0:T(8,128)(2,1)}, u32[]{:S(2)}, u32[]{:S(2)}) collective-permute-start(bf16[4,5,2,32,256]{4,3,2,1,0:T(8,128)(2,1)S(1)} %pad_maximum_fusion.own), channel_id=1, source_target_pairs={{1,0},{2,1},{3,2},{4,3},{5,4},{6,5},{7,6},{9,8},{10,9},{11,10},{12... | collective-permute-start | bytes 1966088 | tf_op jit(solution)/shard_map/ppermute | solution.py:541
  75.1 21.5 %collective-permute-start.11 = (bf16[4,5,2,32,256]{4,3,2,1,0:T(8,128)(2,1)S(1)}, bf16[4,5,2,32,256]{4,3,2,1,0:T(8,128)(2,1)}, u32[]{:S(2)}, u32[]{:S(2)}) collective-permute-start(bf16[4,5,2,32,256]{4,3,2,1,0:T(8,128)(2,1)S(1)} %pad_maximum_fusion.own), channel_id=1, source_target_pairs={{0,1},{1,2},{2,3},{3,4},{4,5},{5,6},{6,7},{8,9},{9,10},{10,11},{11... | collective-permute-start | bytes 1966088 | tf_op jit(solution)/shard_map/ppermute | solution.py:541
  80.2 21.1 %collective-permute-start.2 = (bf16[5,7,2,16,256]{4,3,2,1,0:T(8,128)(2,1)}, bf16[5,7,2,16,256]{4,3,2,1,0:T(8,128)(2,1)}, u32[]{:S(2)}, u32[]{:S(2)}) collective-permute-start(bf16[5,7,2,16,256]{4,3,2,1,0:T(8,128)(2,1)} %get-tuple-element.65), channel_id=1, source_target_pairs={{0,8},{8,0},{16,24},{24,16},{1,9},{9,1},{17,25},{25,17},{2,10},{10... | collective-permute-start | bytes 1720328 | tf_op jit(solution)/shard_map/ppermute | solution.py:553
  81.7 19.6 %collective-permute-start.17 = (bf16[5,7,2,16,256]{4,3,2,1,0:T(8,128)(2,1)}, bf16[5,7,2,16,256]{4,3,2,1,0:T(8,128)(2,1)}, u32[]{:S(2)}, u32[]{:S(2)}) collective-permute-start(bf16[5,7,2,16,256]{4,3,2,1,0:T(8,128)(2,1)} %get-tuple-element.93), channel_id=1, source_target_pairs={{0,16},{8,24},{16,0},{24,8},{1,17},{9,25},{17,1},{25,9},{2,18},{10... | collective-permute-start | bytes 1720328 | tf_op jit(solution)/shard_map/ppermute | solution.py:553
  88.5 24.6 %collective-permute-start.19 = (bf16[5,7,2,16,256]{4,3,2,1,0:T(8,128)(2,1)}, bf16[5,7,2,16,256]{4,3,2,1,0:T(8,128)(2,1)}, u32[]{:S(2)}, u32[]{:S(2)}) collective-permute-start(bf16[5,7,2,16,256]{4,3,2,1,0:T(8,128)(2,1)} %get-tuple-element.97), channel_id=1, source_target_pairs={{0,24},{8,16},{16,8},{24,0},{1,25},{9,17},{17,9},{25,1},{2,26},{10... | collective-permute-start | bytes 1720328 | tf_op jit(solution)/shard_map/ppermute | solution.py:553
  96.6 6.1 %copy-start.7 = (bf16[5,3,2,16,256]{4,3,2,1,0:T(8,128)(2,1)S(1)}, bf16[5,3,2,16,256]{4,3,2,1,0:T(8,128)(2,1)}, u32[]{:S(2)}) copy-start(bf16[5,3,2,16,256]{4,3,2,1,0:T(8,128)(2,1)} %get-tuple-element.90) | copy-start | bytes 737284
  96.6 16.5 %copy-start.6 = (bf16[5,3,2,16,256]{4,3,2,1,0:T(8,128)(2,1)S(1)}, bf16[5,3,2,16,256]{4,3,2,1,0:T(8,128)(2,1)}, u32[]{:S(2)}) copy-start(bf16[5,3,2,16,256]{4,3,2,1,0:T(8,128)(2,1)} %get-tuple-element.98) | copy-start | bytes 737284
  101.3 20.9 %collective-permute-start.18 = (bf16[5,3,2,16,256]{4,3,2,1,0:T(8,128)(2,1)}, bf16[5,3,2,16,256]{4,3,2,1,0:T(8,128)(2,1)S(1)}, u32[]{:S(2)}, u32[]{:S(2)}) collective-permute-start(bf16[5,3,2,16,256]{4,3,2,1,0:T(8,128)(2,1)} %get-tuple-element.94), channel_id=1, source_target_pairs={{0,16},{8,24},{16,0},{24,8},{1,17},{9,25},{17,1},{25,9},{2,18},{10... | collective-permute-start | bytes 737288 | tf_op jit(solution)/shard_map/ppermute | solution.py:553
  102.7 19.5 %collective-permute-start.16 = (bf16[5,3,2,16,256]{4,3,2,1,0:T(8,128)(2,1)S(1)}, bf16[5,3,2,16,256]{4,3,2,1,0:T(8,128)(2,1)S(1)}, u32[]{:S(2)}, u32[]{:S(2)}) collective-permute-start(bf16[5,3,2,16,256]{4,3,2,1,0:T(8,128)(2,1)S(1)} %copy-done.7), channel_id=1, source_target_pairs={{0,8},{8,0},{16,24},{24,16},{1,9},{9,1},{17,25},{25,17},{2,10},{10... | collective-permute-start | bytes 737288 | tf_op jit(solution)/shard_map/ppermute | solution.py:553
  113.1 9.6 %collective-permute-start.20 = (bf16[5,3,2,16,256]{4,3,2,1,0:T(8,128)(2,1)S(1)}, bf16[5,3,2,16,256]{4,3,2,1,0:T(8,128)(2,1)S(1)}, u32[]{:S(2)}, u32[]{:S(2)}) collective-permute-start(bf16[5,3,2,16,256]{4,3,2,1,0:T(8,128)(2,1)S(1)} %copy-done.6), channel_id=1, source_target_pairs={{0,24},{8,16},{16,8},{24,0},{1,25},{9,17},{17,9},{25,1},{2,26},{10... | collective-permute-start | bytes 737288 | tf_op jit(solution)/shard_map/ppermute | solution.py:553
